TPU v7x, 32 devices: a whole 2x2x4 slice. The times are simulated.
32 devices in a mesh: grp: 2 (over y), rcv: 16 (over z, x, core).
Axes of the slice: x: 2, y: 2, z: 4, core: 2. Of those that a mesh axis runs over, the one named last changes fastest.
Arguments:
- traces: bfloat16 [2, 3072, 5376], P(None, ('grp', 'rcv')), parts along dimension 1, may hold values from -17 to 17, as said below
- sketch: bfloat16 [2, 96, 5376], P(None, None, 'rcv'), may hold values from -0.0625 to 0.0625
Outputs:
- basis: float32 [2, 3072, 96], P(None, ('grp', 'rcv')), parts along dimension 1
- coeffs: float32 [2, 192, 5376], P(None, 'grp', 'rcv'), parts along dimension 1
There are 2 independent parts, one for each index of `grp`. A program takes and returns all parts, laid end to end along the dimension named above; an argument that names none is the same for every part. Nothing has to cross between parts.
Inputs may be any that keep to these rules, and one draw needn't show every extreme that they name: `traces`: complex data, real part at index 0 and imaginary part at index 1 of the first dimension.
All inputs are finite; a program needn't handle non-finite values.
Results may differ from a plain program's by a relative error of at most 0.0015.
Values may be sent and summed in bfloat16 or wider, within the bound.
No kernel may reach another device: no remote copies, remote signals or barrier semaphores. Data moves between devices by JAX's collectives and lax.ppermute only.
A program may use at most 64 MiB of HBM per device.

v0:
```python
import math

import jax
import jax.numpy as jnp
from jax import lax
from jax.sharding import PartitionSpec as P


def precise_dot(left, right):
    return jnp.dot(left, right, precision=lax.Precision.HIGHEST, preferred_element_type=jnp.float32)


def complex_product(left, right):
    return (
        precise_dot(left[0], right[0]) - precise_dot(left[1], right[1]),
        precise_dot(left[0], right[1]) + precise_dot(left[1], right[0]),
    )


def inner_rows(left, right):
    return lax.dot_general(
        left,
        right,
        (((0,), (0,)), ((), ())),
        precision=lax.Precision.HIGHEST,
        preferred_element_type=jnp.float32,
    )


def coarse_rows(left, right):
    return lax.dot_general(
        left, right, (((0,), (0,)), ((), ())), preferred_element_type=jnp.float32
    )


def across_sources(left, right):
    return lax.dot_general(
        left, right, (((1,), (1,)), ((), ())), preferred_element_type=jnp.float32
    )


def factor(gram):
    count = gram[0].shape[0]
    embed = jnp.stack(
        [jnp.stack([gram[0], -gram[1]], axis=-1), jnp.stack([gram[1], gram[0]], axis=-1)], axis=1
    )
    embed = embed.reshape(2 * count, 2 * count)
    lower = jnp.linalg.cholesky(embed)
    ident = jnp.eye(2 * count, dtype=jnp.float32)
    lower_inv = jax.scipy.linalg.solve_triangular(lower, ident, lower=True)
    low_re = lower[0::2, 0::2]
    low_im = lower[1::2, 0::2]
    linv_re = lower_inv[0::2, 0::2]
    linv_im = lower_inv[1::2, 0::2]
    return (low_re.T, -low_im.T, linv_re.T, -linv_im.T)


def per_device(traces, sketch):
    rows = traces.shape[1]
    width = sketch.shape[1]
    piece = lax.all_gather(sketch, "rcv", axis=2, tiled=True)
    columns = traces
    sum_re = across_sources(columns[0], piece[0]) - across_sources(columns[1], piece[1])
    sum_im = across_sources(columns[0], piece[1]) + across_sources(columns[1], piece[0])
    gram_re = inner_rows(sum_re, sum_re) + inner_rows(sum_im, sum_im)
    gram_im = inner_rows(sum_re, sum_im) - inner_rows(sum_im, sum_re)
    total_re, total_im = lax.psum((gram_re, gram_im), "rcv")
    factors = factor((total_re, total_im))
    ortho_re, ortho_im = complex_product((sum_re, sum_im), (factors[2], factors[3]))
    scale = math.sqrt(rows * lax.axis_size("rcv"))
    basis = jnp.stack([ortho_re * scale, ortho_im * scale])
    rounded_re = ortho_re.astype(jnp.bfloat16)
    rounded_im = ortho_im.astype(jnp.bfloat16)
    share = traces.shape[2] // lax.axis_size("rcv")
    columns = traces
    block_re = coarse_rows(columns[0], rounded_re) + coarse_rows(columns[1], rounded_im)
    block_im = coarse_rows(columns[1], rounded_re) - coarse_rows(columns[0], rounded_im)
    summed = lax.psum_scatter(
        jnp.concatenate([block_re, block_im], axis=1), "rcv", scatter_dimension=0, tiled=True
    )
    coeffs = jnp.transpose(summed.reshape(share, 2, width), (1, 2, 0))
    return (basis, coeffs)


def solution(mesh):
    return jax.shard_map(
        per_device,
        mesh=mesh,
        in_specs=(P(None, ("grp", "rcv"), None), P(None, None, "rcv")),
        out_specs=(P(None, ("grp", "rcv"), None), P(None, "grp", "rcv")),
        check_vma=False,
    )
```

profile of v0, /device:TPU:0, one launch (start us, length us, event | category | flops | bytes accessed | tf_op | source)
XLA Modules:
  0.0 336.9 jit_solution(4600300290485290631)
XLA Ops:
  7.2 1.7 copy.14
  9.1 48.3 %all-gather.2.cloned.1.call-done = bf16[2,96,5376]{1,0,2:T(2,128)(2,1)} async-done(((bf16[2,96,336]{1,0,2:T(2,128)(2,1)}), bf16[2,96,5376]{1,0,2:T(2,128)(2,1)}) %all-gather.2.cloned.1.call-update) | async-done | bytes 2064400 | tf_op jit(solution)/shard_map/all_gather | solution.py:61
  57.3 8.1 %fusion.43 = (bf16[1,96,5376]{1,0,2:T(2,128)(2,1)}, bf16[1,96,5376]{1,0,2:T(2,128)(2,1)S(1)}) fusion(bf16[2,96,5376]{1,0,2:T(2,128)(2,1)} %all-gather.2.cloned.1.call-done), kind=kLoop, calls=%fused_computation.84 | loop fusion | bytes 4128768 | tf_op jit(solution)/shard_map/slice | solution.py:63
  65.4 6.5 %copy.24 = bf16[1,96,5376]{2,1,0:T(8,128)(2,1)} copy(bf16[1,96,5376]{1,0,2:T(2,128)(2,1)} %get-tuple-element.24) | data formatting | bytes 2064384
  71.9 4.7 %copy.23 = bf16[1,96,5376]{2,1,0:T(8,128)(2,1)} copy(bf16[1,96,5376]{1,0,2:T(2,128)(2,1)S(1)} %get-tuple-element.25) | data formatting | bytes 2064384
  76.6 2.1 fusion.3
  78.8 1.7 fusion.12
  80.5 0.4 convolution_add_fusion.3
  81.9 0.9 convolution_subtract_fusion.3
  82.8 0.9 fusion.2
  84.0 85.9 %all-reduce.6.cloned.1.call-done = (f32[96,96,1]{1,0,2:T(8,128)}, f32[96,96]{1,0:T(8,128)}) async-done(((f32[96,96,1]{1,0,2:T(8,128)}, f32[96,96]{1,0:T(8,128)}), (f32[96,96,1]{1,0,2:T(8,128)}, f32[96,96]{1,0:T(8,128)})) %all-reduce.6.cloned.1.call-update) | async-done | bytes 73744 | tf_op jit(solution)/shard_map/psum | solution.py:67
  169.9 0.8 negate_bitcast_fusion
  170.7 0.9 maximum_bitcast_fusion
  171.6 5.1 %copy.17 = f32[96,2,96,2]{3,2,1,0:T(8,128)} copy(f32[96,2,96,2]{2,0,3,1:T(8,128)S(1)} %pad_maximum_fusion.1) | data formatting | bytes 294912 | tf_op jit(solution)/shard_map/stack | solution.py:44
  176.7 7.7 %reshape.33 = f32[192,192]{1,0:T(8,128)S(1)} reshape(f32[96,2,96,2]{3,2,1,0:T(8,128)} %copy.17) | data formatting | bytes 294912 | tf_op jit(solution)/shard_map/reshape | solution.py:47
  184.6 11.7 %cholesky.51 = f32[128,128]{1,0:T(8,128)S(1)} custom-call(f32[128,128]{1,0:T(8,128)S(1)} %cholesky.124), custom_call_target="Cholesky" | custom-call | tf_op jit(solution)/shard_map/jit(cholesky)/cholesky | solution.py:48
  196.3 9.8 %custom-call.15 = f32[1,128,128]{1,2,0:T(8,128)S(1)} custom-call(f32[1,128,128]{2,1,0:T(8,128)S(1)} %get-tuple-element.27), custom_call_target="InvertDiagBlocksLowerTriangular" | custom-call | tf_op jit(solution)/shard_map/jit(cholesky)/cholesky | solution.py:48
  206.5 5.8 %cholesky.110 = f32[64,64]{1,0:T(8,128)S(1)} custom-call(f32[64,64]{1,0:T(8,128)S(1)} %convolution_subtract_fusion.5), custom_call_target="Cholesky" | custom-call | tf_op jit(solution)/shard_map/jit(cholesky)/cholesky | solution.py:48
  212.4 0.6 compare_reduce_fusion
  213.0 0.6 compare_reduce_fusion.1
  215.1 19.9 %custom-call.16 = f32[2,128,128]{1,2,0:T(8,128)S(1)} custom-call(f32[2,128,128]{2,1,0:T(8,128)S(1)} %pad_maximum_fusion.3), custom_call_target="InvertDiagBlocksLowerTriangular" | custom-call | tf_op jit(solution)/shard_map/jit(_solve_triangular)/triangular_solve | solution.py:50
  236.0 1.3 slice.81
  237.3 1.3 slice.82
  239.2 0.5 fusion.15
  239.6 0.5 fusion.6
  240.3 0.5 fusion
  240.8 0.5 fusion.1
  241.2 2.3 pad_maximum_fusion
  243.5 5.7 %copy.21 = f32[5376,192]{1,0:T(8,128)} copy(f32[5376,192]{0,1:T(8,128)} %pad_maximum_fusion) | data formatting | bytes 8257536
  249.3 0.7 pad_maximum_fusion.4
  250.0 78.5 %reduce-scatter.4.cloned.1.call-done = f32[336,192]{1,0:T(8,128)} async-done(((f32[5376,192]{1,0:T(8,128)}), f32[336,192]{1,0:T(8,128)}) %reduce-scatter.4.cloned.1.call-update) | async-done | bytes 258064
  328.5 1.8 copy.22
  (41 shorter events, 3.9 us)
Async XLA Ops:
  7.2 50.1 %all-gather.2.cloned.1.call-start = ((), (), s32[]{:S(2)}) async-start(), calls=%async_computation.1 | async-start | bytes 2924544 | tf_op jit(solution)/shard_map/all_gather | solution.py:61
  9.0 160.9 %all-reduce.6.cloned.1.call-start = ((), (), s32[]{:S(2)}) async-start(), calls=%async_computation.3 | async-start | bytes 196608 | tf_op jit(solution)/shard_map/psum | solution.py:67
  76.6 2.2 copy-start
  76.6 3.9 %copy-start.2 = (bf16[1,96,5376]{2,1,0:T(8,128)(2,1)S(1)}, bf16[1,96,5376]{2,1,0:T(8,128)(2,1)}, u32[]{:S(2)}) copy-start(bf16[1,96,5376]{2,1,0:T(8,128)(2,1)} %copy.23) | copy-start | bytes 3096580
  78.8 2.2 copy-start.1
  83.7 244.8 %reduce-scatter.4.cloned.1.call-start = ((), (), s32[]{:S(2)}) async-start(), calls=%async_computation.2 | async-start | bytes 5849088
Sparse Core Ops, SparseCore 0:
  10.9 46.4 all-gather.1
  83.8 85.9 all-reduce.5
  249.4 79.0 reduce-scatter.3
where the time goes:
time: 338 us; the launch traced here: 337 us
  waiting for transfers between devices  213 us (63%)
  other arithmetic  53.5 us (16%)
  local copies, waits for them, and re-layouts  44.2 us (13%)
  between operations  15.3 us (5%)
  matrix products  10.8 us (3%)
    psum x1, waiting for transfers between devices, per_device(): total_re, total_im = lax.psum((gram_re, gram_im), 'rcv')  85.9 us
    unnamed x4, waiting for transfers between devices  78.6 us
    all_gather x1, waiting for transfers between devices, per_device(): piece = lax.all_gather(sketch, 'rcv', axis=2, tiled=True)  48.3 us
    another operation x7, other arithmetic, factor(): lower = jnp.linalg.cholesky(embed)  28.7 us
    unnamed x11, local copies, waits for them, and re-layouts  20.6 us
    another operation x7, other arithmetic, factor(): lower_inv = jax.scipy.linalg.solve_triangular(lower, ident, lower=True)  20 us
    slice x1, local copies, waits for them, and re-layouts, per_device(): piece[1]  8.06 us
    reshape x2, local copies, waits for them, and re-layouts, factor(): embed = embed.reshape(2 * count, 2 * count)  7.84 us
  transfers between devices with their start and end apart: 3, of which 3 were waited for; matrix products, arithmetic and copies ran while one was open for 0% of the time, Pallas kernels for 0%

commit v1 on v0

v1 whole, which is shorter than its diff:
```python
import functools
import math

import jax
import jax.numpy as jnp
from jax import lax
from jax.experimental import pallas as pl
from jax.experimental.pallas import tpu as pltpu
from jax.sharding import PartitionSpec as P

LANES = 128
ROWS = 8


def axis_masks(size):
    masks = []
    for bit in range(size.bit_length() - 1):
        masks.append(1 << bit if bit < 3 else 3 << (bit - 1))
    return masks


def slot_owner(slot, masks):
    owner = 0
    for bit, mask in enumerate(masks):
        if slot >> bit & 1:
            owner ^= mask
    return owner


def swap(value, mask, size):
    return lax.ppermute(value, "rcv", [(i, i ^ mask) for i in range(size)])


def rotated(items, shift):
    shift = shift % len(items) if items else 0
    return items[shift:] + items[:shift]


def gather_slots(piece, masks, size):
    far = list(range(1, len(masks)))
    ways = max(len(far), 1)
    rows = piece.shape[0]
    cuts = [rows * p // ways // 16 * 16 for p in range(ways)] + [rows]
    parts = [piece[None, cuts[p] : cuts[p + 1]] for p in range(ways)]
    held = [[0] for _ in range(ways)]
    for step in range(len(far)):
        got = []
        for p in range(ways):
            bit = rotated(far, p)[step]
            got.append(swap(parts[p], masks[bit], size))
        for p in range(ways):
            bit = rotated(far, p)[step]
            parts[p] = jnp.concatenate([parts[p], got[p]])
            held[p] = held[p] + [slot | 1 << bit for slot in held[p]]
    if masks:
        for p in range(ways):
            parts[p] = jnp.concatenate([parts[p], swap(parts[p], masks[0], size)])
            held[p] = held[p] + [slot | 1 for slot in held[p]]
    return parts, held


def sketch_kernel(ways, slots, held, owner_ref, data_ref, *refs):
    part_refs, (out_ref, gram_ref) = refs[:ways], refs[ways:]
    count = out_ref.shape[2]
    total = None
    place = [{slot: at for at, slot in enumerate(h)} for h in held]
    for slot in range(slots):
        block = jnp.concatenate([part_refs[p][place[p][slot]] for p in range(ways)], axis=0)
        term = lax.dot_general(
            data_ref[owner_ref[slot]],
            block,
            (((1,), (1,)), ((), ())),
            preferred_element_type=jnp.float32,
        )
        total = term if total is None else total + term
    rows = total.shape[0] // 2
    real = total[:rows, :count] - total[rows:, count:]
    imag = total[:rows, count:] + total[rows:, :count]
    out_ref[0] = real
    out_ref[1] = imag
    exact = functools.partial(
        lax.dot_general,
        dimension_numbers=(((0,), (0,)), ((), ())),
        precision=lax.Precision.HIGHEST,
        preferred_element_type=jnp.float32,
    )
    gram_re = exact(real, real) + exact(imag, imag)
    gram_im = exact(real, imag) - exact(imag, real)
    row = lax.broadcasted_iota(jnp.int32, gram_re.shape, 0)
    column = lax.broadcasted_iota(jnp.int32, gram_re.shape, 1)
    gram_ref[...] = jnp.where(row <= column, gram_re, gram_im)


def eliminate(real, imag):
    count, width = real.shape
    lane = lax.broadcasted_iota(jnp.int32, (ROWS, width), 1)
    row = lax.broadcasted_iota(jnp.int32, (ROWS, width), 0)
    blocks = count // ROWS
    re = [real[ROWS * i : ROWS * (i + 1)] for i in range(blocks)]
    im = [imag[ROWS * i : ROWS * (i + 1)] for i in range(blocks)]
    for b in range(blocks):
        col_re, col_im = [], []
        for o in range(ROWS):
            k = ROWS * b + o
            col_re.append([jnp.broadcast_to(re[i][:, k : k + 1], (ROWS, width)) for i in range(b, blocks)])
            col_im.append([jnp.broadcast_to(im[i][:, k : k + 1], (ROWS, width)) for i in range(b, blocks)])
        for o in range(ROWS):
            hit = lane == ROWS * b + o
            scale = lax.rsqrt(col_re[o][0][o : o + 1])
            pivot_re = jnp.where(hit[:1], scale, re[b][o : o + 1] * scale)
            pivot_im = jnp.where(hit[:1], 0.0, im[b][o : o + 1] * scale)
            by_re = [v * scale for v in col_re[o]]
            by_im = [v * scale for v in col_im[o]]
            for j in range(o + 1, ROWS):
                x_re, x_im = by_re[0][j : j + 1], by_im[0][j : j + 1]
                for q in range(blocks - b):
                    col_re[j][q] = col_re[j][q] - (by_re[q] * x_re + by_im[q] * x_im)
                    col_im[j][q] = col_im[j][q] - (by_im[q] * x_re - by_re[q] * x_im)
            for q, i in enumerate(range(b, blocks)):
                new_re = jnp.where(hit, 0.0, re[i]) - (by_re[q] * pivot_re - by_im[q] * pivot_im)
                new_im = jnp.where(hit, 0.0, im[i]) - (by_re[q] * pivot_im + by_im[q] * pivot_re)
                if i == b:
                    new_re = jnp.where(row > o, new_re, jnp.where(row == o, pivot_re, re[i]))
                    new_im = jnp.where(row > o, new_im, jnp.where(row == o, pivot_im, im[i]))
                re[i], im[i] = new_re, new_im
    return jnp.concatenate(re, axis=0), jnp.concatenate(im, axis=0)


def basis_kernel(scale, gram_ref, sketched_ref, basis_ref, weight_ref):
    packed = gram_ref[...]
    count = packed.shape[0]
    flipped = packed.T
    row = lax.broadcasted_iota(jnp.int32, packed.shape, 0)
    column = lax.broadcasted_iota(jnp.int32, packed.shape, 1)
    gram_re = jnp.where(row <= column, packed, flipped)
    gram_im = jnp.where(row > column, packed, jnp.where(row < column, -flipped, 0.0))
    low_re, low_im = eliminate(gram_re, gram_im)
    low_re = jnp.where(row >= column, low_re, 0.0)
    low_im = jnp.where(row >= column, low_im, 0.0)
    exact = functools.partial(
        lax.dot_general,
        dimension_numbers=(((1,), (1,)), ((), ())),
        precision=lax.Precision.HIGHEST,
        preferred_element_type=jnp.float32,
    )
    real, imag = sketched_ref[0], sketched_ref[1]
    ortho_re = exact(real, low_re) + exact(imag, low_im)
    ortho_im = exact(imag, low_re) - exact(real, low_im)
    basis_ref[0] = ortho_re * scale
    basis_ref[1] = ortho_im * scale
    top = jnp.concatenate([ortho_re.T, ortho_im.T], axis=1)
    low = jnp.concatenate([-ortho_im.T, ortho_re.T], axis=1)
    weight_ref[...] = jnp.concatenate([top, low], axis=0).astype(weight_ref.dtype)


def project_kernel(slots, owner_ref, weight_ref, data_ref, out_ref):
    weight = weight_ref[...]
    for slot in range(slots):
        out_ref[slot] = jnp.dot(
            weight, data_ref[owner_ref[slot]], preferred_element_type=jnp.float32
        )


def scatter_slots(held, masks, size, factor):
    send = lambda value: (value * factor).astype(jnp.float16)
    back = lambda value: value.astype(jnp.float32) / factor
    far = list(range(1, len(masks)))
    ways = max(len(far), 1)
    rows = held.shape[1]
    if masks:
        near = held.reshape((-1, 2) + held.shape[1:])
        held = near[:, 0] + back(swap(send(near[:, 1]), masks[0], size))
    cuts = [rows * p // ways // 16 * 16 for p in range(ways)] + [rows]
    parts = []
    for p in range(ways):
        parts.append(held[:, cuts[p] : cuts[p + 1]].reshape((2,) * len(far) + (cuts[p + 1] - cuts[p], -1)))
    left = [list(reversed(far)) for _ in range(ways)]
    for step in range(len(far)):
        got = []
        for p in range(ways):
            bit = rotated(far, p)[step]
            at = left[p].index(bit)
            got.append(swap(send(lax.index_in_dim(parts[p], 1, at, keepdims=False)), masks[bit], size))
        for p in range(ways):
            bit = rotated(far, p)[step]
            at = left[p].index(bit)
            parts[p] = lax.index_in_dim(parts[p], 0, at, keepdims=False) + back(got[p])
            left[p].remove(bit)
    return jnp.concatenate([part.reshape((-1, part.shape[-1])) for part in parts])


def per_device(traces, sketch):
    size = lax.axis_size("rcv")
    me = lax.axis_index("rcv")
    masks = axis_masks(size)
    rows, sources = traces.shape[1:]
    count, share = sketch.shape[1:]
    vmem = pl.BlockSpec(memory_space=pltpu.VMEM)
    smem = pl.BlockSpec(memory_space=pltpu.SMEM)
    params = pltpu.CompilerParams(vmem_limit_bytes=40 * 1024 * 1024)
    owners = me ^ jnp.array([slot_owner(slot, masks) for slot in range(size)], jnp.int32)

    data = jnp.transpose(traces.reshape(2 * rows, size, share), (1, 0, 2))
    parts, held = gather_slots(sketch.reshape(2 * count, share), masks, size)
    sketched, gram = pl.pallas_call(
        functools.partial(sketch_kernel, len(parts), size, held),
        out_shape=(
            jax.ShapeDtypeStruct((2, rows, count), jnp.float32),
            jax.ShapeDtypeStruct((count, count), jnp.float32),
        ),
        in_specs=[smem] + [vmem] * (1 + len(parts)),
        out_specs=(vmem, vmem),
        compiler_params=params,
        name="sketch_rows",
    )(owners, data, *parts)
    for mask in masks:
        gram = gram + swap(gram, mask, size)
    basis, weight = pl.pallas_call(
        functools.partial(basis_kernel, math.sqrt(rows * size)),
        out_shape=(
            jax.ShapeDtypeStruct((2, rows, count), jnp.float32),
            jax.ShapeDtypeStruct((2 * count, 2 * rows), jnp.bfloat16),
        ),
        in_specs=[vmem, vmem],
        out_specs=(vmem, vmem),
        compiler_params=params,
        name="orthonormal_basis",
    )(gram, sketched)
    terms = pl.pallas_call(
        functools.partial(project_kernel, size),
        out_shape=jax.ShapeDtypeStruct((size, 2 * count, share), jnp.float32),
        in_specs=[smem, vmem, vmem],
        out_specs=vmem,
        compiler_params=params,
        name="project_rows",
    )(owners, weight, data)
    coeffs = scatter_slots(terms, masks, size, jnp.float32(1.0))
    return basis, coeffs.reshape(2, count, share)


def solution(mesh):
    return jax.shard_map(
        per_device,
        mesh=mesh,
        in_specs=(P(None, ("grp", "rcv"), None), P(None, None, "rcv")),
        out_specs=(P(None, ("grp", "rcv"), None), P(None, "grp", "rcv")),
        check_vma=False,
    )
```

time: 338 us -> 91.4 us (0.27)
  waiting for transfers between devices: 213 us -> 40.6 us
  other arithmetic: 53.5 us -> 2.82 us
  local copies, waits for them, and re-layouts: 44.2 us -> 10.4 us
  starting transfers between devices: 0.3 us -> 26.6 us
  between operations: 15.3 us -> 0.99 us
  matrix products: 10.8 us -> 0 us
  Pallas kernels: 0 us -> 9.62 us
    psum x1 -> x0, waiting for transfers between devices: 85.9 us -> none  [per_device(): total_re, total_im = lax.psum((gram_re, gram_im), 'rcv')]
    unnamed x4 -> x0, waiting for transfers between devices: 78.6 us -> none
    another operation x20 -> x1, other arithmetic: 51.1 us -> 0.05 us  [the longest x7 28.7 us: factor(): lower = jnp.linalg.cholesky(embed)]
    all_gather x1 -> x0, waiting for transfers between devices: 48.3 us -> none  [per_device(): piece = lax.all_gather(sketch, 'rcv', axis=2, tiled=True)]
    ppermute x0 -> x26, waiting for transfers between devices: none -> 40.6 us  [swap(): return lax.ppermute(value, 'rcv', [(i, i ^ mask) for i in range(size)])]
    ppermute x0 -> x26, starting transfers between devices: none -> 26.6 us  [swap(): return lax.ppermute(value, 'rcv', [(i, i ^ mask) for i in range(size)])]
    unnamed x11 -> x10, local copies, waits for them, and re-layouts: 20.6 us -> 1.05 us
    slice x3, local copies, waits for them, and re-layouts: 10.6 us -> 0.21 us  [the longest x2 0.11 us: scatter_slots(): lax.index_in_dim(parts[p], 1, at, keepdims=False)]
  transfers between devices with their start and end apart: 3 -> 26, of which waited for: 3 -> 18; matrix products, arithmetic and copies ran while one was open for 0% -> 12% of each run, Pallas kernels for 0% -> 0%
where the time goes in v1:
time: 91.4 us; the launch traced here: 91 us
  waiting for transfers between devices  40.6 us (44%)
  starting transfers between devices  26.6 us (29%)
  local copies, waits for them, and re-layouts  10.4 us (11%)
  Pallas kernels  9.62 us (11%)
  other arithmetic  2.82 us (3%)
  between operations  0.99 us (1%)
    ppermute x26, waiting for transfers between devices, swap(): return lax.ppermute(value, 'rcv', [(i, i ^ mask) for i in range(size)])  40.6 us
    ppermute x26, starting transfers between devices, swap(): return lax.ppermute(value, 'rcv', [(i, i ^ mask) for i in range(size)])  26.6 us
    reshape x2, local copies, waits for them, and re-layouts, per_device(): data = jnp.transpose(traces.reshape(2 * rows, size, share), (1, 0, 2))  8.05 us
    pallas_call x1, Pallas kernels, per_device(): pl.pallas_call(functools.partial(basis_kernel, math.sqrt(rows * size)), o...  5.78 us
    pallas_call x1, Pallas kernels, per_device(): pl.pallas_call(functools.partial(sketch_kernel, len(parts), size, held),...  2.32 us
  transfers between devices with their start and end apart: 26, of which 18 were waited for; matrix products, arithmetic and copies ran while one was open for 12% of the time, Pallas kernels for 0%

profile of v1, /device:TPU:0, one launch (start us, length us, event | category | flops | bytes accessed | tf_op | source)
XLA Modules:
  0.0 91.0 jit_solution(3162342419733407299)
XLA Ops:
  1.5 5.1 %collective-permute-start.8 = (bf16[1,64,336]{2,1,0:T(8,128)(2,1)S(1)}, bf16[1,64,336]{2,1,0:T(8,128)(2,1)S(1)}, u32[]{:S(2)}, u32[]{:S(2)}) collective-permute-start(bf16[1,64,336]{2,1,0:T(8,128)(2,1)S(1)} %get-tuple-element.18), channel_id=1, source_target_pairs={{0,12},{1,13},{2,14},{3,15},{4,8},{5,9},{6,10},{7,11},{8,4},{9,5},... | collective-permute-start | bytes 129032 | tf_op jit(solution)/shard_map/ppermute | solution.py:31
  6.6 1.5 %collective-permute-start = (bf16[1,64,336]{2,1,0:T(8,128)(2,1)S(1)}, bf16[1,64,336]{2,1,0:T(8,128)(2,1)S(1)}, u32[]{:S(2)}, u32[]{:S(2)}) collective-permute-start(bf16[1,64,336]{2,1,0:T(8,128)(2,1)S(1)} %get-tuple-element.20), channel_id=1, source_target_pairs={{0,2},{1,3},{2,0},{3,1},{4,6},{5,7},{6,4},{7,5},{8,10},{9,11},{10,... | collective-permute-start | bytes 129032 | tf_op jit(solution)/shard_map/ppermute | solution.py:31
  9.6 5.8 %reshape.37 = bf16[192,16,336]{2,1,0:T(8,128)(2,1)} reshape(bf16[2,96,5376]{2,1,0:T(8,128)(2,1)} %param.3) | data formatting | bytes 4128768 | tf_op jit(solution)/shard_map/reshape | solution.py:203
  15.5 2.2 %copy.39 = bf16[192,16,336]{2,0,1:T(8,128)(2,1)S(1)} copy(bf16[192,16,336]{2,1,0:T(8,128)(2,1)} %reshape.37) | data formatting | bytes 4128768 | tf_op jit(solution)/shard_map/reshape | solution.py:203
  18.4 1.0 %collective-permute-start.5 = (bf16[2,64,336]{2,1,0:T(8,128)(2,1)S(1)}, bf16[2,64,336]{2,1,0:T(8,128)(2,1)S(1)}, u32[]{:S(2)}, u32[]{:S(2)}) collective-permute-start(bf16[2,64,336]{2,1,0:T(8,128)(2,1)S(1)} %pad_maximum_fusion.8), channel_id=1, source_target_pairs={{0,12},{1,13},{2,14},{3,15},{4,8},{5,9},{6,10},{7,11},{8,4},{9,5},... | collective-permute-start | bytes 258056 | tf_op jit(solution)/shard_map/ppermute | solution.py:31
  19.4 1.2 %collective-permute-start.1 = (bf16[2,64,336]{2,1,0:T(8,128)(2,1)S(1)}, bf16[2,64,336]{2,1,0:T(8,128)(2,1)S(1)}, u32[]{:S(2)}, u32[]{:S(2)}) collective-permute-start(bf16[2,64,336]{2,1,0:T(8,128)(2,1)S(1)} %pad_maximum_fusion.7), channel_id=1, source_target_pairs={{0,4},{1,5},{2,6},{3,7},{4,0},{5,1},{6,2},{7,3},{8,12},{9,13},{10,... | collective-permute-start | bytes 258056 | tf_op jit(solution)/shard_map/ppermute | solution.py:31
  20.6 1.8 %collective-permute-done.9 = bf16[2,64,336]{2,1,0:T(8,128)(2,1)S(1)} collective-permute-done((bf16[2,64,336]{2,1,0:T(8,128)(2,1)S(1)}, bf16[2,64,336]{2,1,0:T(8,128)(2,1)S(1)}, u32[]{:S(2)}, u32[]{:S(2)}) %collective-permute-start.9) | collective-permute-done | bytes 86048 | tf_op jit(solution)/shard_map/ppermute | solution.py:31
  22.5 2.1 %collective-permute-start.10 = (bf16[4,64,336]{2,1,0:T(8,128)(2,1)S(1)}, bf16[4,64,336]{2,1,0:T(8,128)(2,1)S(1)}, u32[]{:S(2)}, u32[]{:S(2)}) collective-permute-start(bf16[4,64,336]{2,1,0:T(8,128)(2,1)S(1)} %pad_maximum_fusion.6), channel_id=1, source_target_pairs={{0,4},{1,5},{2,6},{3,7},{4,0},{5,1},{6,2},{7,3},{8,12},{9,13},{10,... | collective-permute-start | bytes 516104 | tf_op jit(solution)/shard_map/ppermute | solution.py:31
  24.6 1.4 %collective-permute-done.5 = bf16[2,64,336]{2,1,0:T(8,128)(2,1)S(1)} collective-permute-done((bf16[2,64,336]{2,1,0:T(8,128)(2,1)S(1)}, bf16[2,64,336]{2,1,0:T(8,128)(2,1)S(1)}, u32[]{:S(2)}, u32[]{:S(2)}) %collective-permute-start.5) | collective-permute-done | bytes 86048 | tf_op jit(solution)/shard_map/ppermute | solution.py:31
  26.0 1.6 %collective-permute-start.6 = (bf16[4,64,336]{2,1,0:T(8,128)(2,1)S(1)}, bf16[4,64,336]{2,1,0:T(8,128)(2,1)S(1)}, u32[]{:S(2)}, u32[]{:S(2)}) collective-permute-start(bf16[4,64,336]{2,1,0:T(8,128)(2,1)S(1)} %pad_maximum_fusion.5), channel_id=1, source_target_pairs={{0,2},{1,3},{2,0},{3,1},{4,6},{5,7},{6,4},{7,5},{8,10},{9,11},{10,... | collective-permute-start | bytes 516104 | tf_op jit(solution)/shard_map/ppermute | solution.py:31
  28.3 1.6 %collective-permute-done.10 = bf16[4,64,336]{2,1,0:T(8,128)(2,1)S(1)} collective-permute-done((bf16[4,64,336]{2,1,0:T(8,128)(2,1)S(1)}, bf16[4,64,336]{2,1,0:T(8,128)(2,1)S(1)}, u32[]{:S(2)}, u32[]{:S(2)}) %collective-permute-start.10) | collective-permute-done | bytes 172064 | tf_op jit(solution)/shard_map/ppermute | solution.py:31
  30.0 1.7 %collective-permute-done.6 = bf16[4,64,336]{2,1,0:T(8,128)(2,1)S(1)} collective-permute-done((bf16[4,64,336]{2,1,0:T(8,128)(2,1)S(1)}, bf16[4,64,336]{2,1,0:T(8,128)(2,1)S(1)}, u32[]{:S(2)}, u32[]{:S(2)}) %collective-permute-start.6) | collective-permute-done | bytes 172064 | tf_op jit(solution)/shard_map/ppermute | solution.py:31
  31.9 3.3 %collective-permute-done.2 = bf16[4,64,336]{2,1,0:T(8,128)(2,1)S(1)} collective-permute-done((bf16[4,64,336]{2,1,0:T(8,128)(2,1)S(1)}, bf16[4,64,336]{2,1,0:T(8,128)(2,1)S(1)}, u32[]{:S(2)}, u32[]{:S(2)}) %collective-permute-start.2) | collective-permute-done | bytes 172064 | tf_op jit(solution)/shard_map/ppermute | solution.py:31
  35.7 1.4 %collective-permute-done.3 = bf16[8,64,336]{2,1,0:T(8,128)(2,1)S(1)} collective-permute-done((bf16[8,64,336]{2,1,0:T(8,128)(2,1)S(1)}, bf16[8,64,336]{2,1,0:T(8,128)(2,1)S(1)}, u32[]{:S(2)}, u32[]{:S(2)}) %collective-permute-start.3) | collective-permute-done | bytes 344096 | tf_op jit(solution)/shard_map/ppermute | solution.py:31
  37.2 2.3 %sketch_rows.1 = (f32[2,96,96]{2,1,0:T(8,128)S(1)}, f32[96,96]{1,0:T(8,128)S(1)}) custom-call(s32[16]{0:T(128)S(1)} %broadcast_xor_fusion.owner_ref, bf16[16,192,336]{2,1,0:T(8,128)(2,1)S(1)} %bitcast.78, bf16[16,64,336]{2,1,0:T(8,128)(2,1)S(1)} %constant_dynamic-update-slice_fusion.refs_0_, ...), custom_call_target="tpu_custom_call" | custom-call | tf_op jit(solution)/shard_map/sketch_rows/pallas_call | solution.py:205
  39.7 1.1 %collective-permute-done.12 = f32[96,96]{1,0:T(8,128)S(1)} collective-permute-done((f32[96,96]{1,0:T(8,128)S(1)}, f32[96,96]{1,0:T(8,128)S(1)}, u32[]{:S(2)}, u32[]{:S(2)}) %collective-permute-start.12) | collective-permute-done | bytes 36896 | tf_op jit(solution)/shard_map/ppermute | solution.py:31
  41.7 3.2 %collective-permute-done.13 = f32[96,96]{1,0:T(8,128)S(1)} collective-permute-done((f32[96,96]{1,0:T(8,128)S(1)}, f32[96,96]{1,0:T(8,128)S(1)}, u32[]{:S(2)}, u32[]{:S(2)}) %collective-permute-start.13) | collective-permute-done | bytes 36896 | tf_op jit(solution)/shard_map/ppermute | solution.py:31
  45.0 1.3 %collective-permute-start.14 = (f32[96,96]{1,0:T(8,128)S(1)}, f32[96,96]{1,0:T(8,128)S(1)}, u32[]{:S(2)}, u32[]{:S(2)}) collective-permute-start(f32[96,96]{1,0:T(8,128)S(1)} %add.43), channel_id=1, source_target_pairs={{0,4},{1,5},{2,6},{3,7},{4,0},{5,1},{6,2},{7,3},{8,12},{9,13},{10,... | collective-permute-start | bytes 110600 | tf_op jit(solution)/shard_map/ppermute | solution.py:31
  46.3 2.9 %collective-permute-done.14 = f32[96,96]{1,0:T(8,128)S(1)} collective-permute-done((f32[96,96]{1,0:T(8,128)S(1)}, f32[96,96]{1,0:T(8,128)S(1)}, u32[]{:S(2)}, u32[]{:S(2)}) %collective-permute-start.14) | collective-permute-done | bytes 36896 | tf_op jit(solution)/shard_map/ppermute | solution.py:31
  49.9 5.2 %collective-permute-done.15 = f32[96,96]{1,0:T(8,128)S(1)} collective-permute-done((f32[96,96]{1,0:T(8,128)S(1)}, f32[96,96]{1,0:T(8,128)S(1)}, u32[]{:S(2)}, u32[]{:S(2)}) %collective-permute-start.15) | collective-permute-done | bytes 36896 | tf_op jit(solution)/shard_map/ppermute | solution.py:31
  55.1 5.8 %orthonormal_basis.1 = (f32[2,96,96]{2,1,0:T(8,128)}, bf16[192,192]{1,0:T(8,128)(2,1)S(1)}) custom-call(f32[96,96]{1,0:T(8,128)S(1)} %add.45.gram_ref, f32[2,96,96]{2,1,0:T(8,128)S(1)} %get-tuple-element.7.sketched_ref), custom_call_target="tpu_custom_call" | custom-call | tf_op jit(solution)/shard_map/orthonormal_basis/pallas_call | solution.py:218
  60.9 1.5 %project_rows.1 = f32[16,192,336]{2,1,0:T(8,128)S(1)} custom-call(s32[16]{0:T(128)S(1)} %broadcast_xor_fusion.owner_ref, bf16[192,192]{1,0:T(8,128)(2,1)S(1)} %get-tuple-element.9.weight_ref, bf16[16,192,336]{2,1,0:T(8,128)(2,1)S(1)} %bitcast.79), custom_call_target="tpu_custom_call" | custom-call | tf_op jit(solution)/shard_map/project_rows/pallas_call | solution.py:229
  62.7 2.8 %collective-permute-done.16 = f16[8,192,336]{2,1,0:T(8,128)(2,1)S(1)} collective-permute-done((f16[8,192,336]{2,1,0:T(8,128)(2,1)S(1)}, f16[8,192,336]{2,1,0:T(8,128)(2,1)S(1)}, u32[]{:S(2)}, u32[]{:S(2)}) %collective-permute-start.16) | collective-permute-done | bytes 1032224 | tf_op jit(solution)/shard_map/ppermute | solution.py:31
  67.2 2.1 %collective-permute-start.23 = (f16[2,2,64,336]{3,2,0,1:T(8,128)(2,1)S(1)}, f16[2,2,64,336]{3,2,0,1:T(8,128)(2,1)S(1)}, u32[]{:S(2)}, u32[]{:S(2)}) collective-permute-start(f16[2,2,64,336]{3,2,0,1:T(8,128)(2,1)S(1)} %copy.18), channel_id=1, source_target_pairs={{0,12},{1,13},{2,14},{3,15},{4,8},{5,9},{6,10},{7,11},{8,4},{9,5},... | collective-permute-start | bytes 516104 | tf_op jit(solution)/shard_map/ppermute | solution.py:31
  69.3 3.9 %collective-permute-done.17 = f16[2,2,64,336]{3,2,0,1:T(8,128)(2,1)S(1)} collective-permute-done((f16[2,2,64,336]{3,2,0,1:T(8,128)(2,1)S(1)}, f16[2,2,64,336]{3,2,0,1:T(8,128)(2,1)S(1)}, u32[]{:S(2)}, u32[]{:S(2)}) %collective-permute-start.17) | collective-permute-done | bytes 172064 | tf_op jit(solution)/shard_map/ppermute | solution.py:31
  73.4 1.5 %collective-permute-done.20 = f16[2,2,64,336]{3,2,1,0:T(8,128)(2,1)S(1)} collective-permute-done((f16[2,2,64,336]{3,2,1,0:T(8,128)(2,1)S(1)}, f16[2,2,64,336]{3,2,1,0:T(8,128)(2,1)S(1)}, u32[]{:S(2)}, u32[]{:S(2)}) %collective-permute-start.20) | collective-permute-done | bytes 172064 | tf_op jit(solution)/shard_map/ppermute | solution.py:31
  75.7 3.7 %collective-permute-done.23 = f16[2,2,64,336]{3,2,0,1:T(8,128)(2,1)S(1)} collective-permute-done((f16[2,2,64,336]{3,2,0,1:T(8,128)(2,1)S(1)}, f16[2,2,64,336]{3,2,0,1:T(8,128)(2,1)S(1)}, u32[]{:S(2)}, u32[]{:S(2)}) %collective-permute-start.23) | collective-permute-done | bytes 172064 | tf_op jit(solution)/shard_map/ppermute | solution.py:31
  80.0 1.9 %collective-permute-done.18 = f16[2,64,336]{2,1,0:T(8,128)(2,1)S(1)} collective-permute-done((f16[2,64,336]{2,1,0:T(8,128)(2,1)S(1)}, f16[2,64,336]{2,1,0:T(8,128)(2,1)S(1)}, u32[]{:S(2)}, u32[]{:S(2)}) %collective-permute-start.18) | collective-permute-done | bytes 86048 | tf_op jit(solution)/shard_map/ppermute | solution.py:31
  82.0 1.6 %collective-permute-start.19 = (f16[64,336]{1,0:T(8,128)(2,1)S(1)}, f16[64,336]{1,0:T(8,128)(2,1)S(1)}, u32[]{:S(2)}, u32[]{:S(2)}) collective-permute-start(f16[64,336]{1,0:T(8,128)(2,1)S(1)} %fusion.15), channel_id=1, source_target_pairs={{0,12},{1,13},{2,14},{3,15},{4,8},{5,9},{6,10},{7,11},{8,4},{9,5},... | collective-permute-start | bytes 129032 | tf_op jit(solution)/shard_map/ppermute | solution.py:31
  83.7 2.4 %collective-permute-start.22 = (f16[64,336]{1,0:T(8,128)(2,1)S(1)}, f16[64,336]{1,0:T(8,128)(2,1)S(1)}, u32[]{:S(2)}, u32[]{:S(2)}) collective-permute-start(f16[64,336]{1,0:T(8,128)(2,1)S(1)} %fusion.16), channel_id=1, source_target_pairs={{0,2},{1,3},{2,0},{3,1},{4,6},{5,7},{6,4},{7,5},{8,10},{9,11},{10,... | collective-permute-start | bytes 129032 | tf_op jit(solution)/shard_map/ppermute | solution.py:31
  86.1 1.0 %collective-permute-start.25 = (f16[64,336]{1,0:T(8,128)(2,1)S(1)}, f16[64,336]{1,0:T(8,128)(2,1)S(1)}, u32[]{:S(2)}, u32[]{:S(2)}) collective-permute-start(f16[64,336]{1,0:T(8,128)(2,1)S(1)} %fusion.17), channel_id=1, source_target_pairs={{0,4},{1,5},{2,6},{3,7},{4,0},{5,1},{6,2},{7,3},{8,12},{9,13},{10,... | collective-permute-start | bytes 129032 | tf_op jit(solution)/shard_map/ppermute | solution.py:31
  88.2 2.1 %collective-permute-done.25 = f16[64,336]{1,0:T(8,128)(2,1)S(1)} collective-permute-done((f16[64,336]{1,0:T(8,128)(2,1)S(1)}, f16[64,336]{1,0:T(8,128)(2,1)S(1)}, u32[]{:S(2)}, u32[]{:S(2)}) %collective-permute-start.25) | collective-permute-done | bytes 43040 | tf_op jit(solution)/shard_map/ppermute | solution.py:31
  (78 shorter events, 11.8 us)
Async XLA Ops:
  1.5 16.2 %collective-permute-start.8 = (bf16[1,64,336]{2,1,0:T(8,128)(2,1)S(1)}, bf16[1,64,336]{2,1,0:T(8,128)(2,1)S(1)}, u32[]{:S(2)}, u32[]{:S(2)}) collective-permute-start(bf16[1,64,336]{2,1,0:T(8,128)(2,1)S(1)} %get-tuple-element.18), channel_id=1, source_target_pairs={{0,12},{1,13},{2,14},{3,15},{4,8},{5,9},{6,10},{7,11},{8,4},{9,5},... | collective-permute-start | bytes 129032 | tf_op jit(solution)/shard_map/ppermute | solution.py:31
  6.6 11.7 %collective-permute-start.4 = (bf16[1,64,336]{2,1,0:T(8,128)(2,1)S(1)}, bf16[1,64,336]{2,1,0:T(8,128)(2,1)S(1)}, u32[]{:S(2)}, u32[]{:S(2)}) collective-permute-start(bf16[1,64,336]{2,1,0:T(8,128)(2,1)S(1)} %get-tuple-element.19), channel_id=1, source_target_pairs={{0,4},{1,5},{2,6},{3,7},{4,0},{5,1},{6,2},{7,3},{8,12},{9,13},{10,... | collective-permute-start | bytes 129032 | tf_op jit(solution)/shard_map/ppermute | solution.py:31
  6.6 12.7 %collective-permute-start = (bf16[1,64,336]{2,1,0:T(8,128)(2,1)S(1)}, bf16[1,64,336]{2,1,0:T(8,128)(2,1)S(1)}, u32[]{:S(2)}, u32[]{:S(2)}) collective-permute-start(bf16[1,64,336]{2,1,0:T(8,128)(2,1)S(1)} %get-tuple-element.20), channel_id=1, source_target_pairs={{0,2},{1,3},{2,0},{3,1},{4,6},{5,7},{6,4},{7,5},{8,10},{9,11},{10,... | collective-permute-start | bytes 129032 | tf_op jit(solution)/shard_map/ppermute | solution.py:31
  17.7 4.7 %collective-permute-start.9 = (bf16[2,64,336]{2,1,0:T(8,128)(2,1)S(1)}, bf16[2,64,336]{2,1,0:T(8,128)(2,1)S(1)}, u32[]{:S(2)}, u32[]{:S(2)}) collective-permute-start(bf16[2,64,336]{2,1,0:T(8,128)(2,1)S(1)} %pad_maximum_fusion.9), channel_id=1, source_target_pairs={{0,2},{1,3},{2,0},{3,1},{4,6},{5,7},{6,4},{7,5},{8,10},{9,11},{10,... | collective-permute-start | bytes 258056 | tf_op jit(solution)/shard_map/ppermute | solution.py:31
  18.4 7.6 %collective-permute-start.5 = (bf16[2,64,336]{2,1,0:T(8,128)(2,1)S(1)}, bf16[2,64,336]{2,1,0:T(8,128)(2,1)S(1)}, u32[]{:S(2)}, u32[]{:S(2)}) collective-permute-start(bf16[2,64,336]{2,1,0:T(8,128)(2,1)S(1)} %pad_maximum_fusion.8), channel_id=1, source_target_pairs={{0,12},{1,13},{2,14},{3,15},{4,8},{5,9},{6,10},{7,11},{8,4},{9,5},... | collective-permute-start | bytes 258056 | tf_op jit(solution)/shard_map/ppermute | solution.py:31
  19.4 8.2 %collective-permute-start.1 = (bf16[2,64,336]{2,1,0:T(8,128)(2,1)S(1)}, bf16[2,64,336]{2,1,0:T(8,128)(2,1)S(1)}, u32[]{:S(2)}, u32[]{:S(2)}) collective-permute-start(bf16[2,64,336]{2,1,0:T(8,128)(2,1)S(1)} %pad_maximum_fusion.7), channel_id=1, source_target_pairs={{0,4},{1,5},{2,6},{3,7},{4,0},{5,1},{6,2},{7,3},{8,12},{9,13},{10,... | collective-permute-start | bytes 258056 | tf_op jit(solution)/shard_map/ppermute | solution.py:31
  22.5 7.4 %collective-permute-start.10 = (bf16[4,64,336]{2,1,0:T(8,128)(2,1)S(1)}, bf16[4,64,336]{2,1,0:T(8,128)(2,1)S(1)}, u32[]{:S(2)}, u32[]{:S(2)}) collective-permute-start(bf16[4,64,336]{2,1,0:T(8,128)(2,1)S(1)} %pad_maximum_fusion.6), channel_id=1, source_target_pairs={{0,4},{1,5},{2,6},{3,7},{4,0},{5,1},{6,2},{7,3},{8,12},{9,13},{10,... | collective-permute-start | bytes 516104 | tf_op jit(solution)/shard_map/ppermute | solution.py:31
  26.0 5.7 %collective-permute-start.6 = (bf16[4,64,336]{2,1,0:T(8,128)(2,1)S(1)}, bf16[4,64,336]{2,1,0:T(8,128)(2,1)S(1)}, u32[]{:S(2)}, u32[]{:S(2)}) collective-permute-start(bf16[4,64,336]{2,1,0:T(8,128)(2,1)S(1)} %pad_maximum_fusion.5), channel_id=1, source_target_pairs={{0,2},{1,3},{2,0},{3,1},{4,6},{5,7},{6,4},{7,5},{8,10},{9,11},{10,... | collective-permute-start | bytes 516104 | tf_op jit(solution)/shard_map/ppermute | solution.py:31
  27.6 7.6 %collective-permute-start.2 = (bf16[4,64,336]{2,1,0:T(8,128)(2,1)S(1)}, bf16[4,64,336]{2,1,0:T(8,128)(2,1)S(1)}, u32[]{:S(2)}, u32[]{:S(2)}) collective-permute-start(bf16[4,64,336]{2,1,0:T(8,128)(2,1)S(1)} %pad_maximum_fusion.4), channel_id=1, source_target_pairs={{0,12},{1,13},{2,14},{3,15},{4,8},{5,9},{6,10},{7,11},{8,4},{9,5},... | collective-permute-start | bytes 516104 | tf_op jit(solution)/shard_map/ppermute | solution.py:31
  29.9 5.6 %collective-permute-start.11 = (bf16[8,64,336]{2,1,0:T(8,128)(2,1)S(1)}, bf16[8,64,336]{2,1,0:T(8,128)(2,1)S(1)}, u32[]{:S(2)}, u32[]{:S(2)}) collective-permute-start(bf16[8,64,336]{2,1,0:T(8,128)(2,1)S(1)} %pad_maximum_fusion.2), channel_id=1, source_target_pairs={{0,1},{1,0},{2,3},{3,2},{4,5},{5,4},{6,7},{7,6},{8,9},{9,8},{10,11... | collective-permute-start | bytes 1032200 | tf_op jit(solution)/shard_map/ppermute | solution.py:31
  31.8 3.8 %collective-permute-start.7 = (bf16[8,64,336]{2,1,0:T(8,128)(2,1)S(1)}, bf16[8,64,336]{2,1,0:T(8,128)(2,1)S(1)}, u32[]{:S(2)}, u32[]{:S(2)}) collective-permute-start(bf16[8,64,336]{2,1,0:T(8,128)(2,1)S(1)} %pad_maximum_fusion.1), channel_id=1, source_target_pairs={{0,1},{1,0},{2,3},{3,2},{4,5},{5,4},{6,7},{7,6},{8,9},{9,8},{10,11... | collective-permute-start | bytes 1032200 | tf_op jit(solution)/shard_map/ppermute | solution.py:31
  35.3 1.8 %collective-permute-start.3 = (bf16[8,64,336]{2,1,0:T(8,128)(2,1)S(1)}, bf16[8,64,336]{2,1,0:T(8,128)(2,1)S(1)}, u32[]{:S(2)}, u32[]{:S(2)}) collective-permute-start(bf16[8,64,336]{2,1,0:T(8,128)(2,1)S(1)} %pad_maximum_fusion), channel_id=1, source_target_pairs={{0,1},{1,0},{2,3},{3,2},{4,5},{5,4},{6,7},{7,6},{8,9},{9,8},{10,11... | collective-permute-start | bytes 1032200 | tf_op jit(solution)/shard_map/ppermute | solution.py:31
  39.5 1.3 %collective-permute-start.12 = (f32[96,96]{1,0:T(8,128)S(1)}, f32[96,96]{1,0:T(8,128)S(1)}, u32[]{:S(2)}, u32[]{:S(2)}) collective-permute-start(f32[96,96]{1,0:T(8,128)S(1)} %get-tuple-element.6), channel_id=1, source_target_pairs={{0,1},{1,0},{2,3},{3,2},{4,5},{5,4},{6,7},{7,6},{8,9},{9,8},{10,11... | collective-permute-start | bytes 110600 | tf_op jit(solution)/shard_map/ppermute | solution.py:31
  40.8 4.2 %collective-permute-start.13 = (f32[96,96]{1,0:T(8,128)S(1)}, f32[96,96]{1,0:T(8,128)S(1)}, u32[]{:S(2)}, u32[]{:S(2)}) collective-permute-start(f32[96,96]{1,0:T(8,128)S(1)} %add.42), channel_id=1, source_target_pairs={{0,2},{1,3},{2,0},{3,1},{4,6},{5,7},{6,4},{7,5},{8,10},{9,11},{10,... | collective-permute-start | bytes 110600 | tf_op jit(solution)/shard_map/ppermute | solution.py:31
  45.0 4.2 %collective-permute-start.14 = (f32[96,96]{1,0:T(8,128)S(1)}, f32[96,96]{1,0:T(8,128)S(1)}, u32[]{:S(2)}, u32[]{:S(2)}) collective-permute-start(f32[96,96]{1,0:T(8,128)S(1)} %add.43), channel_id=1, source_target_pairs={{0,4},{1,5},{2,6},{3,7},{4,0},{5,1},{6,2},{7,3},{8,12},{9,13},{10,... | collective-permute-start | bytes 110600 | tf_op jit(solution)/shard_map/ppermute | solution.py:31
  49.1 5.9 %collective-permute-start.15 = (f32[96,96]{1,0:T(8,128)S(1)}, f32[96,96]{1,0:T(8,128)S(1)}, u32[]{:S(2)}, u32[]{:S(2)}) collective-permute-start(f32[96,96]{1,0:T(8,128)S(1)} %add.44), channel_id=1, source_target_pairs={{0,12},{1,13},{2,14},{3,15},{4,8},{5,9},{6,10},{7,11},{8,4},{9,5},... | collective-permute-start | bytes 110600 | tf_op jit(solution)/shard_map/ppermute | solution.py:31
  62.6 2.9 %collective-permute-start.16 = (f16[8,192,336]{2,1,0:T(8,128)(2,1)S(1)}, f16[8,192,336]{2,1,0:T(8,128)(2,1)S(1)}, u32[]{:S(2)}, u32[]{:S(2)}) collective-permute-start(f16[8,192,336]{2,1,0:T(8,128)(2,1)S(1)} %fusion.1), channel_id=1, source_target_pairs={{0,1},{1,0},{2,3},{3,2},{4,5},{5,4},{6,7},{7,6},{8,9},{9,8},{10,11... | collective-permute-start | bytes 3096584 | tf_op jit(solution)/shard_map/ppermute | solution.py:31
  66.2 7.0 %collective-permute-start.17 = (f16[2,2,64,336]{3,2,0,1:T(8,128)(2,1)S(1)}, f16[2,2,64,336]{3,2,0,1:T(8,128)(2,1)S(1)}, u32[]{:S(2)}, u32[]{:S(2)}) collective-permute-start(f16[2,2,64,336]{3,2,0,1:T(8,128)(2,1)S(1)} %fusion.4), channel_id=1, source_target_pairs={{0,2},{1,3},{2,0},{3,1},{4,6},{5,7},{6,4},{7,5},{8,10},{9,11},{10,... | collective-permute-start | bytes 516104 | tf_op jit(solution)/shard_map/ppermute | solution.py:31
  67.2 7.8 %collective-permute-start.20 = (f16[2,2,64,336]{3,2,1,0:T(8,128)(2,1)S(1)}, f16[2,2,64,336]{3,2,1,0:T(8,128)(2,1)S(1)}, u32[]{:S(2)}, u32[]{:S(2)}) collective-permute-start(f16[2,2,64,336]{3,2,1,0:T(8,128)(2,1)S(1)} %fusion.5), channel_id=1, source_target_pairs={{0,4},{1,5},{2,6},{3,7},{4,0},{5,1},{6,2},{7,3},{8,12},{9,13},{10,... | collective-permute-start | bytes 516104 | tf_op jit(solution)/shard_map/ppermute | solution.py:31
  67.2 12.1 %collective-permute-start.23 = (f16[2,2,64,336]{3,2,0,1:T(8,128)(2,1)S(1)}, f16[2,2,64,336]{3,2,0,1:T(8,128)(2,1)S(1)}, u32[]{:S(2)}, u32[]{:S(2)}) collective-permute-start(f16[2,2,64,336]{3,2,0,1:T(8,128)(2,1)S(1)} %copy.18), channel_id=1, source_target_pairs={{0,12},{1,13},{2,14},{3,15},{4,8},{5,9},{6,10},{7,11},{8,4},{9,5},... | collective-permute-start | bytes 516104 | tf_op jit(solution)/shard_map/ppermute | solution.py:31
  73.3 8.6 %collective-permute-start.18 = (f16[2,64,336]{2,1,0:T(8,128)(2,1)S(1)}, f16[2,64,336]{2,1,0:T(8,128)(2,1)S(1)}, u32[]{:S(2)}, u32[]{:S(2)}) collective-permute-start(f16[2,64,336]{2,1,0:T(8,128)(2,1)S(1)} %fusion.9), channel_id=1, source_target_pairs={{0,4},{1,5},{2,6},{3,7},{4,0},{5,1},{6,2},{7,3},{8,12},{9,13},{10,... | collective-permute-start | bytes 258056 | tf_op jit(solution)/shard_map/ppermute | solution.py:31
  75.0 8.6 %collective-permute-start.21 = (f16[2,64,336]{2,1,0:T(8,128)(2,1)S(1)}, f16[2,64,336]{2,1,0:T(8,128)(2,1)S(1)}, u32[]{:S(2)}, u32[]{:S(2)}) collective-permute-start(f16[2,64,336]{2,1,0:T(8,128)(2,1)S(1)} %fusion.10), channel_id=1, source_target_pairs={{0,12},{1,13},{2,14},{3,15},{4,8},{5,9},{6,10},{7,11},{8,4},{9,5},... | collective-permute-start | bytes 258056 | tf_op jit(solution)/shard_map/ppermute | solution.py:31
  79.4 6.6 %collective-permute-start.24 = (f16[2,64,336]{2,1,0:T(8,128)(2,1)S(1)}, f16[2,64,336]{2,1,0:T(8,128)(2,1)S(1)}, u32[]{:S(2)}, u32[]{:S(2)}) collective-permute-start(f16[2,64,336]{2,1,0:T(8,128)(2,1)S(1)} %fusion.11), channel_id=1, source_target_pairs={{0,2},{1,3},{2,0},{3,1},{4,6},{5,7},{6,4},{7,5},{8,10},{9,11},{10,... | collective-permute-start | bytes 258056 | tf_op jit(solution)/shard_map/ppermute | solution.py:31
  82.0 6.0 %collective-permute-start.19 = (f16[64,336]{1,0:T(8,128)(2,1)S(1)}, f16[64,336]{1,0:T(8,128)(2,1)S(1)}, u32[]{:S(2)}, u32[]{:S(2)}) collective-permute-start(f16[64,336]{1,0:T(8,128)(2,1)S(1)} %fusion.15), channel_id=1, source_target_pairs={{0,12},{1,13},{2,14},{3,15},{4,8},{5,9},{6,10},{7,11},{8,4},{9,5},... | collective-permute-start | bytes 129032 | tf_op jit(solution)/shard_map/ppermute | solution.py:31
  83.7 4.5 %collective-permute-start.22 = (f16[64,336]{1,0:T(8,128)(2,1)S(1)}, f16[64,336]{1,0:T(8,128)(2,1)S(1)}, u32[]{:S(2)}, u32[]{:S(2)}) collective-permute-start(f16[64,336]{1,0:T(8,128)(2,1)S(1)} %fusion.16), channel_id=1, source_target_pairs={{0,2},{1,3},{2,0},{3,1},{4,6},{5,7},{6,4},{7,5},{8,10},{9,11},{10,... | collective-permute-start | bytes 129032 | tf_op jit(solution)/shard_map/ppermute | solution.py:31
  86.1 4.2 %collective-permute-start.25 = (f16[64,336]{1,0:T(8,128)(2,1)S(1)}, f16[64,336]{1,0:T(8,128)(2,1)S(1)}, u32[]{:S(2)}, u32[]{:S(2)}) collective-permute-start(f16[64,336]{1,0:T(8,128)(2,1)S(1)} %fusion.17), channel_id=1, source_target_pairs={{0,4},{1,5},{2,6},{3,7},{4,0},{5,1},{6,2},{7,3},{8,12},{9,13},{10,... | collective-permute-start | bytes 129032 | tf_op jit(solution)/shard_map/ppermute | solution.py:31

commit v2 on v1

v2 whole, which is shorter than its diff:
```python
import functools
import math

import jax
import jax.numpy as jnp
from jax import lax
from jax.experimental import pallas as pl
from jax.experimental.pallas import tpu as pltpu
from jax.sharding import PartitionSpec as P

ROWS = 8
NEAR = 2
TOP = 32768.0
VMEM = pl.BlockSpec(memory_space=pltpu.VMEM)
SMEM = pl.BlockSpec(memory_space=pltpu.SMEM)
PARAMS = pltpu.CompilerParams(vmem_limit_bytes=40 * 1024 * 1024)


def axis_masks(size):
    masks = []
    for bit in range(size.bit_length() - 1):
        masks.append(1 << bit if bit < 3 else 3 << (bit - 1))
    return masks


def slot_mask(slot, masks):
    away = 0
    for bit, mask in enumerate(masks):
        if slot >> bit & 1:
            away ^= mask
    return away


def swap(value, mask, size):
    return lax.ppermute(value, "rcv", [(i, i ^ mask) for i in range(size)])


def rotated(items, shift):
    return items[shift:] + items[:shift]


def exact(left, right, dims):
    return lax.dot_general(
        left,
        right,
        ((dims[0], dims[1]), ((), ())),
        precision=lax.Precision.HIGHEST,
        preferred_element_type=jnp.float32,
    )


def chunk_kernel(masks, share, me_ref, traces_ref, out_ref, peak_ref):
    rows, sources = traces_ref.shape[1:]
    me = me_ref[0]
    for owner in range(sources // share):
        away = me ^ owner
        slot = 0
        for bit in reversed(range(len(masks))):
            set_ = (away >> bit) & 1
            slot = slot | (set_ << bit)
            away = away ^ (set_ * masks[bit])
        group = slot & ((1 << NEAR) - 1)
        for part in range(2):
            out_ref[group, slot >> NEAR, rows * part : rows * (part + 1), :] = traces_ref[
                part, :, owner * share : (owner + 1) * share
            ]
    peak_ref[...] = jnp.max(jnp.abs(traces_ref[...].astype(jnp.float32)), axis=(0, 1), keepdims=True)[0]


def sketch_kernel(slots, held, data_ref, peak_ref, *refs):
    pieces, (out_ref, gram_ref) = refs[:-2], refs[-2:]
    count = out_ref.shape[2]
    total = None
    for slot in range(slots):
        block = jnp.concatenate([pieces[which][at] for which, at in held[slot]], axis=0)
        term = lax.dot_general(
            data_ref[slot & ((1 << NEAR) - 1), slot >> NEAR],
            block,
            (((1,), (1,)), ((), ())),
            preferred_element_type=jnp.float32,
        )
        total = term if total is None else total + term
    rows = total.shape[0] // 2
    real = total[:rows, :count] - total[rows:, count:]
    imag = total[:rows, count:] + total[rows:, :count]
    out_ref[0] = real
    out_ref[1] = imag
    gram_re = exact(real, real, ((0,), (0,))) + exact(imag, imag, ((0,), (0,)))
    gram_im = exact(real, imag, ((0,), (0,))) - exact(imag, real, ((0,), (0,)))
    row = lax.broadcasted_iota(jnp.int32, gram_re.shape, 0)
    column = lax.broadcasted_iota(jnp.int32, gram_re.shape, 1)
    gram_ref[:, :count] = jnp.where(row <= column, gram_re, gram_im)
    peak = jnp.max(peak_ref[...], axis=1, keepdims=True)
    gram_ref[:, count:] = jnp.broadcast_to(peak, (count, gram_ref.shape[1] - count))


def eliminate(real, imag):
    count, width = real.shape
    lane = lax.broadcasted_iota(jnp.int32, (ROWS, width), 1)
    row = lax.broadcasted_iota(jnp.int32, (ROWS, width), 0)
    blocks = count // ROWS
    re = [real[ROWS * i : ROWS * (i + 1)] for i in range(blocks)]
    im = [imag[ROWS * i : ROWS * (i + 1)] for i in range(blocks)]
    for b in range(blocks):
        col_re, col_im = [], []
        for o in range(ROWS):
            k = ROWS * b + o
            col_re.append([jnp.broadcast_to(re[i][:, k : k + 1], (ROWS, width)) for i in range(b, blocks)])
            col_im.append([jnp.broadcast_to(im[i][:, k : k + 1], (ROWS, width)) for i in range(b, blocks)])
        for o in range(ROWS):
            hit = lane == ROWS * b + o
            scale = lax.rsqrt(col_re[o][0][o : o + 1])
            pivot_re = jnp.where(hit[:1], scale, re[b][o : o + 1] * scale)
            pivot_im = jnp.where(hit[:1], 0.0, im[b][o : o + 1] * scale)
            by_re = [v * scale for v in col_re[o]]
            by_im = [v * scale for v in col_im[o]]
            for j in range(o + 1, ROWS):
                x_re, x_im = by_re[0][j : j + 1], by_im[0][j : j + 1]
                for q in range(blocks - b):
                    col_re[j][q] = col_re[j][q] - (by_re[q] * x_re + by_im[q] * x_im)
                    col_im[j][q] = col_im[j][q] - (by_im[q] * x_re - by_re[q] * x_im)
            for q, i in enumerate(range(b, blocks)):
                new_re = jnp.where(hit, 0.0, re[i]) - (by_re[q] * pivot_re - by_im[q] * pivot_im)
                new_im = jnp.where(hit, 0.0, im[i]) - (by_re[q] * pivot_im + by_im[q] * pivot_re)
                if i == b:
                    new_re = jnp.where(row > o, new_re, jnp.where(row == o, pivot_re, re[i]))
                    new_im = jnp.where(row > o, new_im, jnp.where(row == o, pivot_im, im[i]))
                re[i], im[i] = new_re, new_im
    return jnp.concatenate(re, axis=0), jnp.concatenate(im, axis=0)


def finish_kernel(groups, scale, bound, ways, gram_ref, *refs):
    sketched, data, (basis_ref, *outs) = refs[:groups], refs[groups : 2 * groups], refs[2 * groups :]
    count = gram_ref.shape[0]
    packed = gram_ref[:, :count]
    factor = TOP / (gram_ref[:1, count : count + 1] * bound)
    flipped = packed.T
    row = lax.broadcasted_iota(jnp.int32, packed.shape, 0)
    column = lax.broadcasted_iota(jnp.int32, packed.shape, 1)
    gram_re = jnp.where(row <= column, packed, flipped)
    gram_im = jnp.where(row > column, packed, jnp.where(row < column, -flipped, 0.0))
    low_re, low_im = eliminate(gram_re, gram_im)
    low_re = jnp.where(row >= column, low_re, 0.0)
    low_im = jnp.where(row >= column, low_im, 0.0)
    weights = []
    for group in range(groups):
        real, imag = sketched[group][0], sketched[group][1]
        ortho_re = exact(real, low_re, ((1,), (1,))) + exact(imag, low_im, ((1,), (1,)))
        ortho_im = exact(imag, low_re, ((1,), (1,))) - exact(real, low_im, ((1,), (1,)))
        if group == 0:
            basis_ref[0] = ortho_re * scale
            basis_ref[1] = ortho_im * scale
        flat_re, flat_im = ortho_re.T, ortho_im.T
        top = jnp.concatenate([flat_re, flat_im], axis=1)
        low = jnp.concatenate([-flat_im, flat_re], axis=1)
        weights.append(jnp.concatenate([top, low], axis=0).astype(jnp.bfloat16))
    slots = data[0].shape[0]
    far = list(range(slots.bit_length() - 1))
    rows = 2 * count
    for slot in range(slots):
        total = None
        for group in range(groups):
            term = jnp.dot(weights[group], data[group][slot], preferred_element_type=jnp.float32)
            total = term if total is None else total + term
        for p, (first, last, bit) in enumerate(ways):
            block = total[first:last]
            if bit is None:
                outs[p][0] = block
                continue
            at = (slot >> bit + 1 << bit) | (slot & (1 << bit) - 1)
            if slot >> bit & 1:
                outs[2 * p + 1][at] = block * factor
            else:
                outs[2 * p][at] = block


def per_device(traces, sketch):
    size = lax.axis_size("rcv")
    me = lax.axis_index("rcv")
    masks = axis_masks(size)
    near, far = masks[:NEAR], masks[NEAR:]
    rows, sources = traces.shape[1:]
    count, share = sketch.shape[1:]
    groups, zones = 1 << len(near), 1 << len(far)

    whole = sketch.reshape(1, 2 * count, share)
    whole_slots = [0]
    for bit in range(1, len(near)):
        whole = jnp.concatenate([whole, swap(whole, masks[bit], size)])
        whole_slots = whole_slots + [slot | 1 << bit for slot in whole_slots]

    data, peak = pl.pallas_call(
        functools.partial(chunk_kernel, masks, share),
        out_shape=(
            jax.ShapeDtypeStruct((groups, zones, 2 * rows, share), traces.dtype),
            jax.ShapeDtypeStruct((1, sources), jnp.float32),
        ),
        in_specs=[SMEM, VMEM],
        out_specs=(VMEM, VMEM),
        compiler_params=PARAMS,
        name="source_chunks",
    )(me.reshape(1), traces)
    traded = [data[0]] + [swap(data[g], slot_mask(g, masks), size) for g in range(1, groups)]

    ways = max(len(far), 1)
    cuts = [2 * count * p // ways // 16 * 16 for p in range(ways)] + [2 * count]
    pieces, held = [], [[None] * ways for _ in range(size)]
    parts = [whole[:, cuts[p] : cuts[p + 1]] for p in range(ways)]
    owns = [list(whole_slots) for _ in range(ways)]
    order = [rotated(list(range(NEAR, len(masks))), p) if far else [] for p in range(ways)]

    def settle(p, piece, slots):
        for which, extra in ((piece, 0), (swap(piece, masks[0], size), 1)) if masks else ((piece, 0),):
            for at, slot in enumerate(slots):
                held[slot | extra][p] = (len(pieces), at)
            pieces.append(which)

    for step in range(len(far)):
        got = [swap(parts[p], masks[order[p][step]], size) for p in range(ways)]
        for p in range(ways):
            bit = order[p][step]
            fresh = [slot | 1 << bit for slot in owns[p]]
            if step == len(far) - 1:
                settle(p, parts[p], owns[p])
                settle(p, got[p], fresh)
            else:
                parts[p] = jnp.concatenate([parts[p], got[p]])
            owns[p] = owns[p] + fresh
    if not far:
        settle(0, parts[0], owns[0])

    sketched, gram = pl.pallas_call(
        functools.partial(sketch_kernel, size, held),
        out_shape=(
            jax.ShapeDtypeStruct((2, rows, count), jnp.float32),
            jax.ShapeDtypeStruct((count, count + 1), jnp.float32),
        ),
        in_specs=[VMEM] * (2 + len(pieces)),
        out_specs=(VMEM, VMEM),
        compiler_params=PARAMS,
        name="sketch_rows",
    )(data, peak, *pieces)
    known = [sketched] + [swap(sketched, slot_mask(g, masks), size) for g in range(1, groups)]
    for mask in masks[:1] + masks[:0:-1]:
        gram = gram + swap(gram, mask, size)

    bound = 1.01 * math.sqrt(2 * rows * size)
    plan = [(cuts[p], cuts[p + 1], order[p][0] - NEAR if far else None) for p in range(ways)]
    shapes = []
    for first, last, bit in plan:
        shape = (max(zones // 2, 1), last - first, share)
        shapes.append(jax.ShapeDtypeStruct(shape, jnp.float32))
        if bit is not None:
            shapes.append(jax.ShapeDtypeStruct(shape, jnp.float32))
    basis, *sums = pl.pallas_call(
        functools.partial(finish_kernel, groups, math.sqrt(rows * size), bound, plan),
        out_shape=(jax.ShapeDtypeStruct((2, rows, count), jnp.float32), *shapes),
        in_specs=[VMEM] * (1 + 2 * groups),
        out_specs=(VMEM,) * (1 + len(shapes)),
        compiler_params=PARAMS,
        name="basis_and_projection",
    )(gram, *known, *traded)

    if far:
        level = gram[0, count] * bound
        factor, back = TOP / level, level / TOP
        keep, send = list(sums[0::2]), [v.astype(jnp.float16) for v in sums[1::2]]
        left = [sorted(order[p][1:], reverse=True) for p in range(ways)]
        for step in range(len(far)):
            got = [swap(send[p], masks[order[p][step]], size) for p in range(ways)]
            for p in range(ways):
                total = keep[p] + got[p].astype(jnp.float32) * back
                if step < len(far) - 1:
                    bit = order[p][step + 1]
                    at = left[p].index(bit)
                    shape = total.shape
                    halves = total.reshape((2 ** at, 2, -1) + shape[1:])
                    keep[p] = halves[:, 0].reshape((-1,) + shape[1:])
                    send[p] = (halves[:, 1].reshape((-1,) + shape[1:]) * factor).astype(jnp.float16)
                    left[p].remove(bit)
                else:
                    keep[p] = total
        sums = keep
    coeffs = jnp.concatenate([part[0] for part in sums]) if len(sums) > 1 else sums[0][0]
    return basis, coeffs.reshape(2, count, share)


def solution(mesh):
    return jax.shard_map(
        per_device,
        mesh=mesh,
        in_specs=(P(None, ("grp", "rcv"), None), P(None, None, "rcv")),
        out_specs=(P(None, ("grp", "rcv"), None), P(None, "grp", "rcv")),
        check_vma=False,
    )
```

time: 91.4 us -> 85.9 us (0.940)
  local copies, waits for them, and re-layouts: 10.4 us -> 2.42 us
  starting transfers between devices: 26.6 us -> 33.8 us
  waiting for transfers between devices: 40.6 us -> 34.7 us
  between operations: 0.99 us -> 2.12 us
  Pallas kernels: 9.62 us -> 10.6 us
    reshape x2 -> x0, local copies, waits for them, and re-layouts: 8.05 us -> none  [per_device(): data = jnp.transpose(traces.reshape(2 * rows, size, share), (1, 0, 2))]
    ppermute x26 -> x23, starting transfers between devices: 26.6 us -> 33.8 us  [swap(): return lax.ppermute(value, 'rcv', [(i, i ^ mask) for i in range(size)])]
    ppermute x26 -> x23, waiting for transfers between devices: 40.6 us -> 34.7 us  [swap(): return lax.ppermute(value, 'rcv', [(i, i ^ mask) for i in range(size)])]
    pallas_call x3, Pallas kernels: 9.62 us -> 10.6 us  [the longest x1 7.95 us: per_device(): pl.pallas_call(functools.partial(finish_kernel, groups, math.sqrt(rows *...]
  transfers between devices with their start and end apart: 26 -> 23, of which waited for: 18 -> 14; matrix products, arithmetic and copies ran while one was open for 12% -> 1% of each run, Pallas kernels for 0% -> 3%
where the time goes in v2:
time: 85.9 us; the launch traced here: 85.7 us
  waiting for transfers between devices  34.7 us (40%)
  starting transfers between devices  33.8 us (39%)
  Pallas kernels  10.6 us (12%)
  local copies, waits for them, and re-layouts  2.42 us (3%)
  between operations  2.12 us (2%)
  other arithmetic  2.03 us (2%)
    ppermute x23, waiting for transfers between devices, swap(): return lax.ppermute(value, 'rcv', [(i, i ^ mask) for i in range(size)])  34.7 us
    ppermute x23, starting transfers between devices, swap(): return lax.ppermute(value, 'rcv', [(i, i ^ mask) for i in range(size)])  33.8 us
    pallas_call x1, Pallas kernels, per_device(): pl.pallas_call(functools.partial(finish_kernel, groups, math.sqrt(rows *...  7.95 us
    pallas_call x1, Pallas kernels, per_device(): pl.pallas_call(functools.partial(sketch_kernel, size, held), out_shape=(j...  1.78 us
  transfers between devices with their start and end apart: 23, of which 14 were waited for; matrix products, arithmetic and copies ran while one was open for 1% of the time, Pallas kernels for 3%

profile of v2, /device:TPU:0, one launch (start us, length us, event | category | flops | bytes accessed | tf_op | source)
XLA Modules:
  0.0 85.7 jit_solution(8564400829067290086)
XLA Ops:
  0.6 3.0 %collective-permute-start = (bf16[1,192,336]{2,1,0:T(8,128)(2,1)}, bf16[1,192,336]{2,1,0:T(8,128)(2,1)S(1)}, u32[]{:S(2)}, u32[]{:S(2)}) collective-permute-start(bf16[1,192,336]{2,1,0:T(8,128)(2,1)} %bitcast.42), channel_id=1, source_target_pairs={{0,2},{1,3},{2,0},{3,1},{4,6},{5,7},{6,4},{7,5},{8,10},{9,11},{10,... | collective-permute-start | bytes 387080 | tf_op jit(solution)/shard_map/ppermute | solution.py:35
  3.6 4.1 %collective-permute-done = bf16[1,192,336]{2,1,0:T(8,128)(2,1)S(1)} collective-permute-done((bf16[1,192,336]{2,1,0:T(8,128)(2,1)}, bf16[1,192,336]{2,1,0:T(8,128)(2,1)S(1)}, u32[]{:S(2)}, u32[]{:S(2)}) %collective-permute-start) | collective-permute-done | bytes 129056 | tf_op jit(solution)/shard_map/ppermute | solution.py:35
  7.7 1.0 %pad_maximum_fusion.3 = (bf16[2,96,336]{2,1,0:T(8,128)(2,1)S(1)}, bf16[2,96,336]{2,1,0:T(8,128)(2,1)S(1)}) fusion(bf16[1,192,336]{2,1,0:T(8,128)(2,1)S(1)} %collective-permute-done, bf16[1,192,336]{2,1,0:T(8,128)(2,1)} %bitcast.43), kind=kLoop, calls=%fused_computation.24 | loop fusion | flops 516096 | bytes 516096 | tf_op jit(solution)/shard_map/concatenate | solution.py:189
  8.6 1.9 %collective-permute-start.1 = (bf16[2,96,336]{2,1,0:T(8,128)(2,1)S(1)}, bf16[2,96,336]{2,1,0:T(8,128)(2,1)S(1)}, u32[]{:S(2)}, u32[]{:S(2)}) collective-permute-start(bf16[2,96,336]{2,1,0:T(8,128)(2,1)S(1)} %get-tuple-element.27), channel_id=1, source_target_pairs={{0,4},{1,5},{2,6},{3,7},{4,0},{5,1},{6,2},{7,3},{8,12},{9,13},{10,... | collective-permute-start | bytes 387080 | tf_op jit(solution)/shard_map/ppermute | solution.py:35
  10.5 2.5 %collective-permute-start.5 = (bf16[2,96,336]{2,1,0:T(8,128)(2,1)S(1)}, bf16[2,96,336]{2,1,0:T(8,128)(2,1)S(1)}, u32[]{:S(2)}, u32[]{:S(2)}) collective-permute-start(bf16[2,96,336]{2,1,0:T(8,128)(2,1)S(1)} %get-tuple-element.26), channel_id=1, source_target_pairs={{0,12},{1,13},{2,14},{3,15},{4,8},{5,9},{6,10},{7,11},{8,4},{9,5},... | collective-permute-start | bytes 387080 | tf_op jit(solution)/shard_map/ppermute | solution.py:35
  13.0 1.6 %copy-done = bf16[2,96,5376]{2,1,0:T(8,128)(2,1)S(1)} copy-done((bf16[2,96,5376]{2,1,0:T(8,128)(2,1)S(1)}, bf16[2,96,5376]{2,1,0:T(8,128)(2,1)}, u32[]{:S(2)}) %copy-start) | copy-done | bytes 2064408
  14.6 0.9 %source_chunks.1 = (bf16[4,4,192,336]{3,2,1,0:T(8,128)(2,1)S(1)}, f32[1,5376]{1,0:T(1,128)S(1)}) custom-call(s32[1]{0:T(128)} %bitcast.me_ref, bf16[2,96,5376]{2,1,0:T(8,128)(2,1)S(1)} %copy-done), custom_call_target="tpu_custom_call" | custom-call | tf_op jit(solution)/shard_map/source_chunks/pallas_call | solution.py:192
  15.6 8.6 %collective-permute-start.3 = (bf16[4,96,336]{2,1,0:T(8,128)(2,1)S(1)}, bf16[4,96,336]{2,1,0:T(8,128)(2,1)S(1)}, u32[]{:S(2)}, u32[]{:S(2)}) collective-permute-start(bf16[4,96,336]{2,1,0:T(8,128)(2,1)S(1)} %pad_maximum_fusion.refs_0_), channel_id=1, source_target_pairs={{0,12},{1,13},{2,14},{3,15},{4,8},{5,9},{6,10},{7,11},{8,4},{9,5},... | collective-permute-start | bytes 774152 | tf_op jit(solution)/shard_map/ppermute | solution.py:35
  25.1 1.2 %collective-permute-start.18 = (bf16[4,192,336]{2,1,0:T(8,128)(2,1)S(1)}, bf16[4,192,336]{2,1,0:T(8,128)(2,1)S(1)}, u32[]{:S(2)}, u32[]{:S(2)}) collective-permute-start(bf16[4,192,336]{2,1,0:T(8,128)(2,1)S(1)} %get-tuple-element.20), channel_id=1, source_target_pairs={{0,3},{1,2},{2,1},{3,0},{4,7},{5,6},{6,5},{7,4},{8,11},{9,10},{10,... | collective-permute-start | bytes 1548296 | tf_op jit(solution)/shard_map/ppermute | solution.py:35
  26.3 5.7 %collective-permute-done.3.refs_2_ = bf16[4,96,336]{2,1,0:T(8,128)(2,1)S(1)} collective-permute-done((bf16[4,96,336]{2,1,0:T(8,128)(2,1)S(1)}, bf16[4,96,336]{2,1,0:T(8,128)(2,1)S(1)}, u32[]{:S(2)}, u32[]{:S(2)}) %collective-permute-start.3) | collective-permute-done | bytes 258080 | tf_op jit(solution)/shard_map/ppermute | solution.py:35
  32.0 1.5 %collective-permute-start.17 = (bf16[4,192,336]{2,1,0:T(8,128)(2,1)S(1)}, bf16[4,192,336]{2,1,0:T(8,128)(2,1)S(1)}, u32[]{:S(2)}, u32[]{:S(2)}) collective-permute-start(bf16[4,192,336]{2,1,0:T(8,128)(2,1)S(1)} %get-tuple-element.21), channel_id=1, source_target_pairs={{0,2},{1,3},{2,0},{3,1},{4,6},{5,7},{6,4},{7,5},{8,10},{9,11},{10,... | collective-permute-start | bytes 1548296 | tf_op jit(solution)/shard_map/ppermute | solution.py:35
  33.5 2.5 %collective-permute-done.7.refs_6_ = bf16[4,96,336]{2,1,0:T(8,128)(2,1)S(1)} collective-permute-done((bf16[4,96,336]{2,1,0:T(8,128)(2,1)S(1)}, bf16[4,96,336]{2,1,0:T(8,128)(2,1)S(1)}, u32[]{:S(2)}, u32[]{:S(2)}) %collective-permute-start.7) | collective-permute-done | bytes 258080 | tf_op jit(solution)/shard_map/ppermute | solution.py:35
  36.5 1.1 %collective-permute-done.4.refs_3_ = bf16[4,96,336]{2,1,0:T(8,128)(2,1)S(1)} collective-permute-done((bf16[4,96,336]{2,1,0:T(8,128)(2,1)S(1)}, bf16[4,96,336]{2,1,0:T(8,128)(2,1)S(1)}, u32[]{:S(2)}, u32[]{:S(2)}) %collective-permute-start.4) | collective-permute-done | bytes 258080 | tf_op jit(solution)/shard_map/ppermute | solution.py:35
  38.0 1.8 %sketch_rows.1 = (f32[2,96,96]{2,1,0:T(8,128)S(1)}, f32[96,97]{1,0:T(8,128)S(1)}) custom-call(bf16[4,4,192,336]{3,2,1,0:T(8,128)(2,1)S(1)} %get-tuple-element.11.data_ref, f32[1,5376]{1,0:T(1,128)S(1)} %get-tuple-element.12.peak_ref, bf16[4,96,336]{2,1,0:T(8,128)(2,1)S(1)} %pad_maximum_fusion.refs_0_, ...), custom_call_target="tpu_custom_call" | custom-call | tf_op jit(solution)/shard_map/sketch_rows/pallas_call | solution.py:232
  40.0 1.1 %collective-permute-done.9 = f32[96,97]{1,0:T(8,128)S(1)} collective-permute-done((f32[96,97]{1,0:T(8,128)S(1)}, f32[96,97]{1,0:T(8,128)S(1)}, u32[]{:S(2)}, u32[]{:S(2)}) %collective-permute-start.9) | collective-permute-done | bytes 37280 | tf_op jit(solution)/shard_map/ppermute | solution.py:35
  41.1 2.3 %collective-permute-start.10 = (f32[96,97]{1,0:T(8,128)S(1)}, f32[96,97]{1,0:T(8,128)S(1)}, u32[]{:S(2)}, u32[]{:S(2)}) collective-permute-start(f32[96,97]{1,0:T(8,128)S(1)} %add.24), channel_id=1, source_target_pairs={{0,12},{1,13},{2,14},{3,15},{4,8},{5,9},{6,10},{7,11},{8,4},{9,5},... | collective-permute-start | bytes 111752 | tf_op jit(solution)/shard_map/ppermute | solution.py:35
  43.4 3.7 %collective-permute-done.10 = f32[96,97]{1,0:T(8,128)S(1)} collective-permute-done((f32[96,97]{1,0:T(8,128)S(1)}, f32[96,97]{1,0:T(8,128)S(1)}, u32[]{:S(2)}, u32[]{:S(2)}) %collective-permute-start.10) | collective-permute-done | bytes 37280 | tf_op jit(solution)/shard_map/ppermute | solution.py:35
  47.1 4.1 %collective-permute-done.11 = f32[96,97]{1,0:T(8,128)S(1)} collective-permute-done((f32[96,97]{1,0:T(8,128)S(1)}, f32[96,97]{1,0:T(8,128)S(1)}, u32[]{:S(2)}, u32[]{:S(2)}) %collective-permute-start.11) | collective-permute-done | bytes 37280 | tf_op jit(solution)/shard_map/ppermute | solution.py:35
  51.2 1.6 %collective-permute-start.12 = (f32[96,97]{1,0:T(8,128)S(1)}, f32[96,97]{1,0:T(8,128)S(1)}, u32[]{:S(2)}, u32[]{:S(2)}) collective-permute-start(f32[96,97]{1,0:T(8,128)S(1)} %add.26), channel_id=1, source_target_pairs={{0,2},{1,3},{2,0},{3,1},{4,6},{5,7},{6,4},{7,5},{8,10},{9,11},{10,... | collective-permute-start | bytes 111752 | tf_op jit(solution)/shard_map/ppermute | solution.py:35
  53.3 2.0 %collective-permute-done.12 = f32[96,97]{1,0:T(8,128)S(1)} collective-permute-done((f32[96,97]{1,0:T(8,128)S(1)}, f32[96,97]{1,0:T(8,128)S(1)}, u32[]{:S(2)}, u32[]{:S(2)}) %collective-permute-start.12) | collective-permute-done | bytes 37280 | tf_op jit(solution)/shard_map/ppermute | solution.py:35
  55.4 2.5 %collective-permute-done.15.refs_3_ = f32[2,96,96]{2,1,0:T(8,128)S(1)} collective-permute-done((f32[2,96,96]{2,1,0:T(8,128)S(1)}, f32[2,96,96]{2,1,0:T(8,128)S(1)}, u32[]{:S(2)}, u32[]{:S(2)}) %collective-permute-start.15) | collective-permute-done | bytes 73760 | tf_op jit(solution)/shard_map/ppermute | solution.py:35
  57.8 1.3 %collective-permute-done.14.refs_2_ = f32[2,96,96]{2,1,0:T(8,128)S(1)} collective-permute-done((f32[2,96,96]{2,1,0:T(8,128)S(1)}, f32[2,96,96]{2,1,0:T(8,128)S(1)}, u32[]{:S(2)}, u32[]{:S(2)}) %collective-permute-start.14) | collective-permute-done | bytes 73760 | tf_op jit(solution)/shard_map/ppermute | solution.py:35
  59.2 8.0 %basis_and_projection.1 = (f32[2,96,96]{2,1,0:T(8,128)}, f32[2,96,336]{2,1,0:T(8,128)S(1)}, f32[2,96,336]{2,1,0:T(8,128)S(1)}, f32[2,96,336]{2,1,0:T(8,128)S(1)}, f32[2,96,336]{2,1,0:T(8,128)S(1)}) custom-call(f32[96,97]{1,0:T(8,128)S(1)} %add.27.gram_ref, f32[2,96,96]{2,1,0:T(8,128)S(1)} %get-tuple-element.14.refs_0_, ...), custom_call_target="tpu_custom_call" | custom-call | tf_op jit(solution)/shard_map/basis_and_projection/pallas_call | solution.py:255
  67.2 1.3 %collective-permute-start.19 = (f16[2,96,336]{2,1,0:T(8,128)(2,1)S(1)}, f16[2,96,336]{2,1,0:T(8,128)(2,1)S(1)}, u32[]{:S(2)}, u32[]{:S(2)}) collective-permute-start(f16[2,96,336]{2,1,0:T(8,128)(2,1)S(1)} %convert_element_type.46), channel_id=1, source_target_pairs={{0,4},{1,5},{2,6},{3,7},{4,0},{5,1},{6,2},{7,3},{8,12},{9,13},{10,... | collective-permute-start | bytes 387080 | tf_op jit(solution)/shard_map/ppermute | solution.py:35
  68.5 0.6 slice.46
  70.4 1.4 %collective-permute-start.21 = (f16[2,96,336]{2,1,0:T(8,128)(2,1)S(1)}, f16[2,96,336]{2,1,0:T(8,128)(2,1)S(1)}, u32[]{:S(2)}, u32[]{:S(2)}) collective-permute-start(f16[2,96,336]{2,1,0:T(8,128)(2,1)S(1)} %convert_element_type.51), channel_id=1, source_target_pairs={{0,12},{1,13},{2,14},{3,15},{4,8},{5,9},{6,10},{7,11},{8,4},{9,5},... | collective-permute-start | bytes 387080 | tf_op jit(solution)/shard_map/ppermute | solution.py:35
  71.8 1.4 %collective-permute-done.19 = f16[2,96,336]{2,1,0:T(8,128)(2,1)S(1)} collective-permute-done((f16[2,96,336]{2,1,0:T(8,128)(2,1)S(1)}, f16[2,96,336]{2,1,0:T(8,128)(2,1)S(1)}, u32[]{:S(2)}, u32[]{:S(2)}) %collective-permute-start.19) | collective-permute-done | bytes 129056 | tf_op jit(solution)/shard_map/ppermute | solution.py:35
  73.3 2.0 %collective-permute-start.20 = (f16[1,96,336]{2,1,0:T(8,128)(2,1)S(1)}, f16[1,96,336]{2,1,0:T(8,128)(2,1)S(1)}, u32[]{:S(2)}, u32[]{:S(2)}) collective-permute-start(f16[1,96,336]{2,1,0:T(8,128)(2,1)S(1)} %fusion.9), channel_id=1, source_target_pairs={{0,12},{1,13},{2,14},{3,15},{4,8},{5,9},{6,10},{7,11},{8,4},{9,5},... | collective-permute-start | bytes 193544 | tf_op jit(solution)/shard_map/ppermute | solution.py:35
  75.2 2.6 %collective-permute-done.21 = f16[2,96,336]{2,1,0:T(8,128)(2,1)S(1)} collective-permute-done((f16[2,96,336]{2,1,0:T(8,128)(2,1)S(1)}, f16[2,96,336]{2,1,0:T(8,128)(2,1)S(1)}, u32[]{:S(2)}, u32[]{:S(2)}) %collective-permute-start.21) | collective-permute-done | bytes 129056 | tf_op jit(solution)/shard_map/ppermute | solution.py:35
  77.9 4.7 %collective-permute-start.22 = (f16[1,96,336]{2,1,0:T(8,128)(2,1)S(1)}, f16[1,96,336]{2,1,0:T(8,128)(2,1)S(1)}, u32[]{:S(2)}, u32[]{:S(2)}) collective-permute-start(f16[1,96,336]{2,1,0:T(8,128)(2,1)S(1)} %fusion.10), channel_id=1, source_target_pairs={{0,4},{1,5},{2,6},{3,7},{4,0},{5,1},{6,2},{7,3},{8,12},{9,13},{10,... | collective-permute-start | bytes 193544 | tf_op jit(solution)/shard_map/ppermute | solution.py:35
  82.6 2.3 %collective-permute-done.22 = f16[1,96,336]{2,1,0:T(8,128)(2,1)S(1)} collective-permute-done((f16[1,96,336]{2,1,0:T(8,128)(2,1)S(1)}, f16[1,96,336]{2,1,0:T(8,128)(2,1)S(1)}, u32[]{:S(2)}, u32[]{:S(2)}) %collective-permute-start.22) | collective-permute-done | bytes 64544 | tf_op jit(solution)/shard_map/ppermute | solution.py:35
  84.9 0.7 pad_maximum_fusion.2
  (37 shorter events, 3.0 us)
Async XLA Ops:
  0.6 7.1 %collective-permute-start = (bf16[1,192,336]{2,1,0:T(8,128)(2,1)}, bf16[1,192,336]{2,1,0:T(8,128)(2,1)S(1)}, u32[]{:S(2)}, u32[]{:S(2)}) collective-permute-start(bf16[1,192,336]{2,1,0:T(8,128)(2,1)} %bitcast.42), channel_id=1, source_target_pairs={{0,2},{1,3},{2,0},{3,1},{4,6},{5,7},{6,4},{7,5},{8,10},{9,11},{10,... | collective-permute-start | bytes 387080 | tf_op jit(solution)/shard_map/ppermute | solution.py:35
  8.6 6.9 %collective-permute-start.1 = (bf16[2,96,336]{2,1,0:T(8,128)(2,1)S(1)}, bf16[2,96,336]{2,1,0:T(8,128)(2,1)S(1)}, u32[]{:S(2)}, u32[]{:S(2)}) collective-permute-start(bf16[2,96,336]{2,1,0:T(8,128)(2,1)S(1)} %get-tuple-element.27), channel_id=1, source_target_pairs={{0,4},{1,5},{2,6},{3,7},{4,0},{5,1},{6,2},{7,3},{8,12},{9,13},{10,... | collective-permute-start | bytes 387080 | tf_op jit(solution)/shard_map/ppermute | solution.py:35
  10.5 13.6 %collective-permute-start.5 = (bf16[2,96,336]{2,1,0:T(8,128)(2,1)S(1)}, bf16[2,96,336]{2,1,0:T(8,128)(2,1)S(1)}, u32[]{:S(2)}, u32[]{:S(2)}) collective-permute-start(bf16[2,96,336]{2,1,0:T(8,128)(2,1)S(1)} %get-tuple-element.26), channel_id=1, source_target_pairs={{0,12},{1,13},{2,14},{3,15},{4,8},{5,9},{6,10},{7,11},{8,4},{9,5},... | collective-permute-start | bytes 387080 | tf_op jit(solution)/shard_map/ppermute | solution.py:35
  13.0 1.6 %copy-start = (bf16[2,96,5376]{2,1,0:T(8,128)(2,1)S(1)}, bf16[2,96,5376]{2,1,0:T(8,128)(2,1)}, u32[]{:S(2)}) copy-start(bf16[2,96,5376]{2,1,0:T(8,128)(2,1)} %traces_ref.1) | copy-start | bytes 6193156
  15.6 16.4 %collective-permute-start.3 = (bf16[4,96,336]{2,1,0:T(8,128)(2,1)S(1)}, bf16[4,96,336]{2,1,0:T(8,128)(2,1)S(1)}, u32[]{:S(2)}, u32[]{:S(2)}) collective-permute-start(bf16[4,96,336]{2,1,0:T(8,128)(2,1)S(1)} %pad_maximum_fusion.refs_0_), channel_id=1, source_target_pairs={{0,12},{1,13},{2,14},{3,15},{4,8},{5,9},{6,10},{7,11},{8,4},{9,5},... | collective-permute-start | bytes 774152 | tf_op jit(solution)/shard_map/ppermute | solution.py:35
  24.1 9.3 %collective-permute-start.2 = (bf16[4,96,336]{2,1,0:T(8,128)(2,1)S(1)}, bf16[4,96,336]{2,1,0:T(8,128)(2,1)S(1)}, u32[]{:S(2)}, u32[]{:S(2)}) collective-permute-start(bf16[4,96,336]{2,1,0:T(8,128)(2,1)S(1)} %pad_maximum_fusion.refs_0_), channel_id=1, source_target_pairs={{0,1},{1,0},{2,3},{3,2},{4,5},{5,4},{6,7},{7,6},{8,9},{9,8},{10,11... | collective-permute-start | bytes 774152 | tf_op jit(solution)/shard_map/ppermute | solution.py:35
  24.2 11.8 %collective-permute-start.7 = (bf16[4,96,336]{2,1,0:T(8,128)(2,1)S(1)}, bf16[4,96,336]{2,1,0:T(8,128)(2,1)S(1)}, u32[]{:S(2)}, u32[]{:S(2)}) collective-permute-start(bf16[4,96,336]{2,1,0:T(8,128)(2,1)S(1)} %pad_maximum_fusion.1.refs_4_), channel_id=1, source_target_pairs={{0,4},{1,5},{2,6},{3,7},{4,0},{5,1},{6,2},{7,3},{8,12},{9,13},{10,... | collective-permute-start | bytes 774152 | tf_op jit(solution)/shard_map/ppermute | solution.py:35
  24.3 11.7 %collective-permute-start.6 = (bf16[4,96,336]{2,1,0:T(8,128)(2,1)S(1)}, bf16[4,96,336]{2,1,0:T(8,128)(2,1)S(1)}, u32[]{:S(2)}, u32[]{:S(2)}) collective-permute-start(bf16[4,96,336]{2,1,0:T(8,128)(2,1)S(1)} %pad_maximum_fusion.1.refs_4_), channel_id=1, source_target_pairs={{0,1},{1,0},{2,3},{3,2},{4,5},{5,4},{6,7},{7,6},{8,9},{9,8},{10,11... | collective-permute-start | bytes 774152 | tf_op jit(solution)/shard_map/ppermute | solution.py:35
  25.1 27.6 %collective-permute-start.18 = (bf16[4,192,336]{2,1,0:T(8,128)(2,1)S(1)}, bf16[4,192,336]{2,1,0:T(8,128)(2,1)S(1)}, u32[]{:S(2)}, u32[]{:S(2)}) collective-permute-start(bf16[4,192,336]{2,1,0:T(8,128)(2,1)S(1)} %get-tuple-element.20), channel_id=1, source_target_pairs={{0,3},{1,2},{2,1},{3,0},{4,7},{5,6},{6,5},{7,4},{8,11},{9,10},{10,... | collective-permute-start | bytes 1548296 | tf_op jit(solution)/shard_map/ppermute | solution.py:35
  32.0 23.4 %collective-permute-start.17 = (bf16[4,192,336]{2,1,0:T(8,128)(2,1)S(1)}, bf16[4,192,336]{2,1,0:T(8,128)(2,1)S(1)}, u32[]{:S(2)}, u32[]{:S(2)}) collective-permute-start(bf16[4,192,336]{2,1,0:T(8,128)(2,1)S(1)} %get-tuple-element.21), channel_id=1, source_target_pairs={{0,2},{1,3},{2,0},{3,1},{4,6},{5,7},{6,4},{7,5},{8,10},{9,11},{10,... | collective-permute-start | bytes 1548296 | tf_op jit(solution)/shard_map/ppermute | solution.py:35
  33.5 21.9 %collective-permute-start.16 = (bf16[4,192,336]{2,1,0:T(8,128)(2,1)S(1)}, bf16[4,192,336]{2,1,0:T(8,128)(2,1)S(1)}, u32[]{:S(2)}, u32[]{:S(2)}) collective-permute-start(bf16[4,192,336]{2,1,0:T(8,128)(2,1)S(1)} %get-tuple-element.22), channel_id=1, source_target_pairs={{0,1},{1,0},{2,3},{3,2},{4,5},{5,4},{6,7},{7,6},{8,9},{9,8},{10,11... | collective-permute-start | bytes 1548296 | tf_op jit(solution)/shard_map/ppermute | solution.py:35
  36.0 1.6 %collective-permute-start.4 = (bf16[4,96,336]{2,1,0:T(8,128)(2,1)S(1)}, bf16[4,96,336]{2,1,0:T(8,128)(2,1)S(1)}, u32[]{:S(2)}, u32[]{:S(2)}) collective-permute-start(bf16[4,96,336]{2,1,0:T(8,128)(2,1)S(1)} %collective-permute-done.3.refs_2_), channel_id=1, source_target_pairs={{0,1},{1,0},{2,3},{3,2},{4,5},{5,4},{6,7},{7,6},{8,9},{9,8},{10,11... | collective-permute-start | bytes 774152 | tf_op jit(solution)/shard_map/ppermute | solution.py:35
  36.0 2.0 %collective-permute-start.8 = (bf16[4,96,336]{2,1,0:T(8,128)(2,1)S(1)}, bf16[4,96,336]{2,1,0:T(8,128)(2,1)S(1)}, u32[]{:S(2)}, u32[]{:S(2)}) collective-permute-start(bf16[4,96,336]{2,1,0:T(8,128)(2,1)S(1)} %collective-permute-done.7.refs_6_), channel_id=1, source_target_pairs={{0,1},{1,0},{2,3},{3,2},{4,5},{5,4},{6,7},{7,6},{8,9},{9,8},{10,11... | collective-permute-start | bytes 774152 | tf_op jit(solution)/shard_map/ppermute | solution.py:35
  39.8 1.3 %collective-permute-start.9 = (f32[96,97]{1,0:T(8,128)S(1)}, f32[96,97]{1,0:T(8,128)S(1)}, u32[]{:S(2)}, u32[]{:S(2)}) collective-permute-start(f32[96,97]{1,0:T(8,128)S(1)} %get-tuple-element.13), channel_id=1, source_target_pairs={{0,1},{1,0},{2,3},{3,2},{4,5},{5,4},{6,7},{7,6},{8,9},{9,8},{10,11... | collective-permute-start | bytes 111752 | tf_op jit(solution)/shard_map/ppermute | solution.py:35
  41.1 5.9 %collective-permute-start.10 = (f32[96,97]{1,0:T(8,128)S(1)}, f32[96,97]{1,0:T(8,128)S(1)}, u32[]{:S(2)}, u32[]{:S(2)}) collective-permute-start(f32[96,97]{1,0:T(8,128)S(1)} %add.24), channel_id=1, source_target_pairs={{0,12},{1,13},{2,14},{3,15},{4,8},{5,9},{6,10},{7,11},{8,4},{9,5},... | collective-permute-start | bytes 111752 | tf_op jit(solution)/shard_map/ppermute | solution.py:35
  47.0 4.2 %collective-permute-start.11 = (f32[96,97]{1,0:T(8,128)S(1)}, f32[96,97]{1,0:T(8,128)S(1)}, u32[]{:S(2)}, u32[]{:S(2)}) collective-permute-start(f32[96,97]{1,0:T(8,128)S(1)} %add.25), channel_id=1, source_target_pairs={{0,4},{1,5},{2,6},{3,7},{4,0},{5,1},{6,2},{7,3},{8,12},{9,13},{10,... | collective-permute-start | bytes 111752 | tf_op jit(solution)/shard_map/ppermute | solution.py:35
  51.2 4.2 %collective-permute-start.12 = (f32[96,97]{1,0:T(8,128)S(1)}, f32[96,97]{1,0:T(8,128)S(1)}, u32[]{:S(2)}, u32[]{:S(2)}) collective-permute-start(f32[96,97]{1,0:T(8,128)S(1)} %add.26), channel_id=1, source_target_pairs={{0,2},{1,3},{2,0},{3,1},{4,6},{5,7},{6,4},{7,5},{8,10},{9,11},{10,... | collective-permute-start | bytes 111752 | tf_op jit(solution)/shard_map/ppermute | solution.py:35
  52.8 5.1 %collective-permute-start.15 = (f32[2,96,96]{2,1,0:T(8,128)S(1)}, f32[2,96,96]{2,1,0:T(8,128)S(1)}, u32[]{:S(2)}, u32[]{:S(2)}) collective-permute-start(f32[2,96,96]{2,1,0:T(8,128)S(1)} %get-tuple-element.14.refs_0_), channel_id=1, source_target_pairs={{0,3},{1,2},{2,1},{3,0},{4,7},{5,6},{6,5},{7,4},{8,11},{9,10},{10,... | collective-permute-start | bytes 221192 | tf_op jit(solution)/shard_map/ppermute | solution.py:35
  52.8 6.4 %collective-permute-start.14 = (f32[2,96,96]{2,1,0:T(8,128)S(1)}, f32[2,96,96]{2,1,0:T(8,128)S(1)}, u32[]{:S(2)}, u32[]{:S(2)}) collective-permute-start(f32[2,96,96]{2,1,0:T(8,128)S(1)} %get-tuple-element.14.refs_0_), channel_id=1, source_target_pairs={{0,2},{1,3},{2,0},{3,1},{4,6},{5,7},{6,4},{7,5},{8,10},{9,11},{10,... | collective-permute-start | bytes 221192 | tf_op jit(solution)/shard_map/ppermute | solution.py:35
  55.4 3.8 %collective-permute-start.13 = (f32[2,96,96]{2,1,0:T(8,128)S(1)}, f32[2,96,96]{2,1,0:T(8,128)S(1)}, u32[]{:S(2)}, u32[]{:S(2)}) collective-permute-start(f32[2,96,96]{2,1,0:T(8,128)S(1)} %get-tuple-element.14.refs_0_), channel_id=1, source_target_pairs={{0,1},{1,0},{2,3},{3,2},{4,5},{5,4},{6,7},{7,6},{8,9},{9,8},{10,11... | collective-permute-start | bytes 221192 | tf_op jit(solution)/shard_map/ppermute | solution.py:35
  67.2 6.0 %collective-permute-start.19 = (f16[2,96,336]{2,1,0:T(8,128)(2,1)S(1)}, f16[2,96,336]{2,1,0:T(8,128)(2,1)S(1)}, u32[]{:S(2)}, u32[]{:S(2)}) collective-permute-start(f16[2,96,336]{2,1,0:T(8,128)(2,1)S(1)} %convert_element_type.46), channel_id=1, source_target_pairs={{0,4},{1,5},{2,6},{3,7},{4,0},{5,1},{6,2},{7,3},{8,12},{9,13},{10,... | collective-permute-start | bytes 387080 | tf_op jit(solution)/shard_map/ppermute | solution.py:35
  70.4 7.4 %collective-permute-start.21 = (f16[2,96,336]{2,1,0:T(8,128)(2,1)S(1)}, f16[2,96,336]{2,1,0:T(8,128)(2,1)S(1)}, u32[]{:S(2)}, u32[]{:S(2)}) collective-permute-start(f16[2,96,336]{2,1,0:T(8,128)(2,1)S(1)} %convert_element_type.51), channel_id=1, source_target_pairs={{0,12},{1,13},{2,14},{3,15},{4,8},{5,9},{6,10},{7,11},{8,4},{9,5},... | collective-permute-start | bytes 387080 | tf_op jit(solution)/shard_map/ppermute | solution.py:35
  73.3 9.3 %collective-permute-start.20 = (f16[1,96,336]{2,1,0:T(8,128)(2,1)S(1)}, f16[1,96,336]{2,1,0:T(8,128)(2,1)S(1)}, u32[]{:S(2)}, u32[]{:S(2)}) collective-permute-start(f16[1,96,336]{2,1,0:T(8,128)(2,1)S(1)} %fusion.9), channel_id=1, source_target_pairs={{0,12},{1,13},{2,14},{3,15},{4,8},{5,9},{6,10},{7,11},{8,4},{9,5},... | collective-permute-start | bytes 193544 | tf_op jit(solution)/shard_map/ppermute | solution.py:35
  77.9 7.0 %collective-permute-start.22 = (f16[1,96,336]{2,1,0:T(8,128)(2,1)S(1)}, f16[1,96,336]{2,1,0:T(8,128)(2,1)S(1)}, u32[]{:S(2)}, u32[]{:S(2)}) collective-permute-start(f16[1,96,336]{2,1,0:T(8,128)(2,1)S(1)} %fusion.10), channel_id=1, source_target_pairs={{0,4},{1,5},{2,6},{3,7},{4,0},{5,1},{6,2},{7,3},{8,12},{9,13},{10,... | collective-permute-start | bytes 193544 | tf_op jit(solution)/shard_map/ppermute | solution.py:35

commit v3 on v2

v3 whole, which is shorter than its diff:
```python
import functools
import math

import jax
import jax.numpy as jnp
from jax import lax
from jax.experimental import pallas as pl
from jax.experimental.pallas import tpu as pltpu
from jax.sharding import PartitionSpec as P

ROWS = 8
NEAR = 2
TOP = 32768.0
VMEM = pl.BlockSpec(memory_space=pltpu.VMEM)
SMEM = pl.BlockSpec(memory_space=pltpu.SMEM)
PARAMS = pltpu.CompilerParams(vmem_limit_bytes=40 * 1024 * 1024)


def swap(value, mask, size):
    return lax.ppermute(value, "rcv", [(i, i ^ mask) for i in range(size)])


def exact(left, right, dims):
    return lax.dot_general(
        left,
        right,
        ((dims[0], dims[1]), ((), ())),
        precision=lax.Precision.HIGHEST,
        preferred_element_type=jnp.float32,
    )


def chunk_kernel(share, me_ref, traces_ref, *refs):
    groups, peak_ref = refs[:-1], refs[-1]
    rows, sources = traces_ref.shape[1:]
    me = me_ref[0]
    near = len(groups)
    for block in range(sources // share // near):
        for member in range(near):
            owner = block * near + member
            away = member ^ (me & (near - 1))
            slot = block ^ (me // near)
            for group in range(near):

                @pl.when(away == group)
                def _(group=group, owner=owner, slot=slot):
                    for part in range(2):
                        groups[group][slot, rows * part : rows * (part + 1), :] = traces_ref[
                            part, :, owner * share : (owner + 1) * share
                        ]

    peak_ref[...] = jnp.max(jnp.abs(traces_ref[...].astype(jnp.float32)), axis=(0, 1), keepdims=True)[0]


def sketch_kernel(slots, groups, held, *refs):
    data, peak_ref, pieces, (out_ref, gram_ref) = refs[:groups], refs[groups], refs[groups + 1 : -2], refs[-2:]
    count = out_ref.shape[2]
    total = None
    for slot in range(slots):
        which, at = held[slot]
        term = lax.dot_general(
            data[slot % groups][slot // groups],
            pieces[which][at],
            (((1,), (1,)), ((), ())),
            preferred_element_type=jnp.float32,
        )
        total = term if total is None else total + term
    rows = total.shape[0] // 2
    real = total[:rows, :count] - total[rows:, count:]
    imag = total[:rows, count:] + total[rows:, :count]
    out_ref[0] = real
    out_ref[1] = imag
    gram_re = exact(real, real, ((0,), (0,))) + exact(imag, imag, ((0,), (0,)))
    gram_im = exact(real, imag, ((0,), (0,))) - exact(imag, real, ((0,), (0,)))
    row = lax.broadcasted_iota(jnp.int32, gram_re.shape, 0)
    column = lax.broadcasted_iota(jnp.int32, gram_re.shape, 1)
    gram_ref[:, :count] = jnp.where(row <= column, gram_re, gram_im)
    peak = jnp.max(peak_ref[...], axis=1, keepdims=True)
    gram_ref[:, count:] = jnp.broadcast_to(peak, (count, gram_ref.shape[1] - count))


def eliminate(real, imag):
    count, width = real.shape
    lane = lax.broadcasted_iota(jnp.int32, (ROWS, width), 1)
    row = lax.broadcasted_iota(jnp.int32, (ROWS, width), 0)
    blocks = count // ROWS
    re = [real[ROWS * i : ROWS * (i + 1)] for i in range(blocks)]
    im = [imag[ROWS * i : ROWS * (i + 1)] for i in range(blocks)]
    for b in range(blocks):
        col_re, col_im = [], []
        for o in range(ROWS):
            k = ROWS * b + o
            col_re.append([jnp.broadcast_to(re[i][:, k : k + 1], (ROWS, width)) for i in range(b, blocks)])
            col_im.append([jnp.broadcast_to(im[i][:, k : k + 1], (ROWS, width)) for i in range(b, blocks)])
        for o in range(ROWS):
            hit = lane == ROWS * b + o
            scale = lax.rsqrt(col_re[o][0][o : o + 1])
            pivot_re = jnp.where(hit[:1], scale, re[b][o : o + 1] * scale)
            pivot_im = jnp.where(hit[:1], 0.0, im[b][o : o + 1] * scale)
            by_re = [v * scale for v in col_re[o]]
            by_im = [v * scale for v in col_im[o]]
            for j in range(o + 1, ROWS):
                x_re, x_im = by_re[0][j : j + 1], by_im[0][j : j + 1]
                for q in range(blocks - b):
                    col_re[j][q] = col_re[j][q] - (by_re[q] * x_re + by_im[q] * x_im)
                    col_im[j][q] = col_im[j][q] - (by_im[q] * x_re - by_re[q] * x_im)
            for q, i in enumerate(range(b, blocks)):
                new_re = jnp.where(hit, 0.0, re[i]) - (by_re[q] * pivot_re - by_im[q] * pivot_im)
                new_im = jnp.where(hit, 0.0, im[i]) - (by_re[q] * pivot_im + by_im[q] * pivot_re)
                if i == b:
                    new_re = jnp.where(row > o, new_re, jnp.where(row == o, pivot_re, re[i]))
                    new_im = jnp.where(row > o, new_im, jnp.where(row == o, pivot_im, im[i]))
                re[i], im[i] = new_re, new_im
    return jnp.concatenate(re, axis=0), jnp.concatenate(im, axis=0)


def finish_kernel(groups, scale, bound, gram_ref, *refs):
    sketched, data, (basis_ref, *outs) = refs[:groups], refs[groups : 2 * groups], refs[2 * groups :]
    count = gram_ref.shape[0]
    packed = gram_ref[:, :count]
    factor = TOP / (gram_ref[:1, count : count + 1] * bound)
    flipped = packed.T
    row = lax.broadcasted_iota(jnp.int32, packed.shape, 0)
    column = lax.broadcasted_iota(jnp.int32, packed.shape, 1)
    gram_re = jnp.where(row <= column, packed, flipped)
    gram_im = jnp.where(row > column, packed, jnp.where(row < column, -flipped, 0.0))
    low_re, low_im = eliminate(gram_re, gram_im)
    low_re = jnp.where(row >= column, low_re, 0.0)
    low_im = jnp.where(row >= column, low_im, 0.0)
    stacked = jnp.concatenate([ref[part] for ref in sketched for part in range(2)], axis=0)
    by_re = exact(stacked, low_re, ((1,), (1,)))
    by_im = exact(stacked, low_im, ((1,), (1,)))
    rows = stacked.shape[0] // groups // 2
    weights = []
    for group in range(groups):
        real = slice(2 * rows * group, 2 * rows * group + rows)
        imag = slice(2 * rows * group + rows, 2 * rows * (group + 1))
        ortho_re = by_re[real] + by_im[imag]
        ortho_im = by_re[imag] - by_im[real]
        if group == 0:
            basis_ref[0] = ortho_re * scale
            basis_ref[1] = ortho_im * scale
        flat_re, flat_im = ortho_re.T, ortho_im.T
        top = jnp.concatenate([flat_re, flat_im], axis=1)
        low = jnp.concatenate([-flat_im, flat_re], axis=1)
        weights.append(jnp.concatenate([top, low], axis=0).astype(jnp.bfloat16))
    for slot in range(data[0].shape[0]):
        total = None
        for group in range(groups):
            term = jnp.dot(weights[group], data[group][slot], preferred_element_type=jnp.float32)
            total = term if total is None else total + term
        outs[slot][...] = total if slot == 0 else total * factor


def tied(first, second):
    first, second = list(first), list(second)
    both = lax.optimization_barrier(tuple(first + second))
    return list(both[: len(first)]), list(both[len(first) :])


def gather_slots(piece, size):
    bits = size.bit_length() - 1
    direct = range(1, min(bits, 4))
    have = {0: piece}
    for level in range(1, len(direct) + 1):
        for slot in range(0, 1 << (direct.stop if bits > 1 else 1), 2):
            if slot.bit_count() == level:
                low = slot & -slot
                have[slot] = swap(have[slot ^ low], low, size)
    pieces = [(have[slot], [slot]) for slot in sorted(have, key=lambda slot: (slot.bit_count(), slot))]
    for bit in range(4, bits):
        whole = jnp.concatenate([value for value, _ in pieces])
        slots = [slot for _, held in pieces for slot in held]
        pieces = [(whole, slots), (swap(whole, 1 << bit, size), [slot | 1 << bit for slot in slots])]
    if bits:
        pieces += [(swap(value, 1, size), [slot | 1 for slot in slots]) for value, slots in pieces]
    return pieces


def sum_all(value, size, tie):
    bits = size.bit_length() - 1
    steps = [[1]] if bits else []
    if bits > 2:
        steps.append([2, 4])
    steps += [[1 << bit] for bit in range(3 if bits > 2 else 1, bits)]
    for at, step in enumerate(steps):
        if at == len(steps) - 1:
            value = tie(value)
        if len(step) == 2:
            first, second = step
            near = value + swap(value, first, size)
            value = near + (swap(value, second, size) + swap(value, first | second, size))
        else:
            value = value + swap(value, step[0], size)
    return value


def per_device(traces, sketch):
    size = lax.axis_size("rcv")
    me = lax.axis_index("rcv")
    rows, sources = traces.shape[1:]
    count, share = sketch.shape[1:]
    groups = min(1 << NEAR, size)
    zones = size // groups

    pieces = gather_slots(sketch.reshape(1, 2 * count, share), size)
    *data, peak = pl.pallas_call(
        functools.partial(chunk_kernel, share),
        out_shape=(jax.ShapeDtypeStruct((zones, 2 * rows, share), traces.dtype),) * groups
        + (jax.ShapeDtypeStruct((1, sources), jnp.float32),),
        in_specs=[SMEM, VMEM],
        out_specs=(VMEM,) * (groups + 1),
        compiler_params=PARAMS,
        name="source_chunks",
    )(me.astype(jnp.int32).reshape(1), traces)
    traded = [swap(data[group], group, size) for group in range(1, groups)]

    values, traded[:2] = tied([value for value, _ in pieces], traded[:2])
    held = {slot: (which, at) for which, (_, slots) in enumerate(pieces) for at, slot in enumerate(slots)}
    sketched, gram = pl.pallas_call(
        functools.partial(sketch_kernel, size, groups, held),
        out_shape=(
            jax.ShapeDtypeStruct((2, rows, count), jnp.float32),
            jax.ShapeDtypeStruct((count, count + 1), jnp.float32),
        ),
        in_specs=[VMEM] * (groups + 1 + len(values)),
        out_specs=(VMEM, VMEM),
        compiler_params=PARAMS,
        name="sketch_rows",
    )(*data, peak, *values)
    known = [swap(sketched, group, size) for group in range(1, groups)]

    def tie(value):
        nonlocal known, traded
        (value,), rest = tied([value], known + traded)
        known, traded = rest[: len(known)], rest[len(known) :]
        return value

    gram = sum_all(gram, size, tie)

    bound = 1.01 * math.sqrt(2 * rows * size)
    basis, *terms = pl.pallas_call(
        functools.partial(finish_kernel, groups, math.sqrt(rows * size), bound),
        out_shape=(jax.ShapeDtypeStruct((2, rows, count), jnp.float32),)
        + (jax.ShapeDtypeStruct((2 * count, share), jnp.float32),) * zones,
        in_specs=[VMEM] * (1 + 2 * groups),
        out_specs=(VMEM,) * (1 + zones),
        compiler_params=PARAMS,
        name="basis_and_projection",
    )(gram, sketched, *known, data[0], *traded)

    level = gram[0, count] * bound
    total = terms[0]
    if zones <= 4:
        parts = [swap(terms[zone].astype(jnp.float16), zone * groups, size) for zone in range(1, zones)]
    else:
        held_terms = jnp.stack([total * (TOP / level)] + terms[1:])
        parts = []
        for bit in reversed(range(zones.bit_length() - 1)):
            low, high = jnp.split(held_terms, 2)
            got = swap(high.astype(jnp.float16), groups << bit, size)
            held_terms = low + got.astype(jnp.float32)
        total = held_terms[0] * (level / TOP)
    if parts:
        total = total + sum(part.astype(jnp.float32) for part in parts) * (level / TOP)
    return basis, total.reshape(2, count, share)


def solution(mesh):
    return jax.shard_map(
        per_device,
        mesh=mesh,
        in_specs=(P(None, ("grp", "rcv"), None), P(None, None, "rcv")),
        out_specs=(P(None, ("grp", "rcv"), None), P(None, "grp", "rcv")),
        check_vma=False,
    )
```

time: 85.9 us -> 92.6 us (1.078)
  waiting for transfers between devices: 34.7 us -> 45.2 us
  starting transfers between devices: 33.8 us -> 30 us
  Pallas kernels: 10.6 us -> 12.8 us
  other arithmetic: 2.03 us -> 0.88 us
    ppermute x23 -> x29, waiting for transfers between devices: 34.7 us -> 45.2 us  [swap(): return lax.ppermute(value, 'rcv', [(i, i ^ mask) for i in range(size)])]
    ppermute x23 -> x29, starting transfers between devices: 33.8 us -> 30 us  [swap(): return lax.ppermute(value, 'rcv', [(i, i ^ mask) for i in range(size)])]
    concatenate x4 -> x0, other arithmetic: 1.8 us -> none  [the longest x1 0.96 us: per_device(): whole = jnp.concatenate([whole, swap(whole, masks[bit], size)])]
    pallas_call x2, Pallas kernels: 2.68 us -> 4.06 us  [the longest x1 2.26 us: per_device(): pl.pallas_call(functools.partial(chunk_kernel, share), out_shape=(jax.Sha...]
  transfers between devices with their start and end apart: 23 -> 29, of which waited for: 14 -> 14; matrix products, arithmetic and copies ran while one was open for 1% -> 1% of each run, Pallas kernels for 3% -> 4%
where the time goes in v3:
time: 92.6 us; the launch traced here: 92.4 us
  waiting for transfers between devices  45.2 us (49%)
  starting transfers between devices  30 us (32%)
  Pallas kernels  12.8 us (14%)
  local copies, waits for them, and re-layouts  2.16 us (2%)
  between operations  1.37 us (1%)
    ppermute x29, waiting for transfers between devices, swap(): return lax.ppermute(value, 'rcv', [(i, i ^ mask) for i in range(size)])  45.2 us
    ppermute x29, starting transfers between devices, swap(): return lax.ppermute(value, 'rcv', [(i, i ^ mask) for i in range(size)])  30 us
    pallas_call x1, Pallas kernels, per_device(): pl.pallas_call(functools.partial(finish_kernel, groups, math.sqrt(rows *...  8.69 us
    pallas_call x1, Pallas kernels, per_device(): pl.pallas_call(functools.partial(chunk_kernel, share), out_shape=(jax.Sha...  2.26 us
  transfers between devices with their start and end apart: 29, of which 14 were waited for; matrix products, arithmetic and copies ran while one was open for 1% of the time, Pallas kernels for 4%

profile of v3, /device:TPU:0, one launch (start us, length us, event | category | flops | bytes accessed | tf_op | source)
XLA Modules:
  0.0 92.4 jit_solution(3069859065646381414)
XLA Ops:
  0.6 4.1 %collective-permute-start.2 = (bf16[1,192,336]{2,1,0:T(8,128)(2,1)}, bf16[1,192,336]{2,1,0:T(8,128)(2,1)S(1)}, u32[]{:S(2)}, u32[]{:S(2)}) collective-permute-start(bf16[1,192,336]{2,1,0:T(8,128)(2,1)} %bitcast.4), channel_id=1, source_target_pairs={{0,8},{1,9},{2,10},{3,11},{4,12},{5,13},{6,14},{7,15},{8,0},{9,1},... | collective-permute-start | bytes 387080 | tf_op jit(solution)/shard_map/ppermute | solution.py:20
  4.7 1.6 %collective-permute-start.1 = (bf16[1,192,336]{2,1,0:T(8,128)(2,1)}, bf16[1,192,336]{2,1,0:T(8,128)(2,1)S(1)}, u32[]{:S(2)}, u32[]{:S(2)}) collective-permute-start(bf16[1,192,336]{2,1,0:T(8,128)(2,1)} %bitcast.6), channel_id=1, source_target_pairs={{0,4},{1,5},{2,6},{3,7},{4,0},{5,1},{6,2},{7,3},{8,12},{9,13},{10,... | collective-permute-start | bytes 387080 | tf_op jit(solution)/shard_map/ppermute | solution.py:20
  6.3 1.5 %collective-permute-start = (bf16[1,192,336]{2,1,0:T(8,128)(2,1)}, bf16[1,192,336]{2,1,0:T(8,128)(2,1)S(1)}, u32[]{:S(2)}, u32[]{:S(2)}) collective-permute-start(bf16[1,192,336]{2,1,0:T(8,128)(2,1)} %bitcast.7), channel_id=1, source_target_pairs={{0,2},{1,3},{2,0},{3,1},{4,6},{5,7},{6,4},{7,5},{8,10},{9,11},{10,... | collective-permute-start | bytes 387080 | tf_op jit(solution)/shard_map/ppermute | solution.py:20
  7.8 4.3 %collective-permute-done.2.refs_8_ = bf16[1,192,336]{2,1,0:T(8,128)(2,1)S(1)} collective-permute-done((bf16[1,192,336]{2,1,0:T(8,128)(2,1)}, bf16[1,192,336]{2,1,0:T(8,128)(2,1)S(1)}, u32[]{:S(2)}, u32[]{:S(2)}) %collective-permute-start.2) | collective-permute-done | bytes 129056 | tf_op jit(solution)/shard_map/ppermute | solution.py:20
  12.1 1.6 %copy-done = bf16[2,96,5376]{2,1,0:T(8,128)(2,1)S(1)} copy-done((bf16[2,96,5376]{2,1,0:T(8,128)(2,1)S(1)}, bf16[2,96,5376]{2,1,0:T(8,128)(2,1)}, u32[]{:S(2)}) %copy-start) | copy-done | bytes 2064408
  13.6 2.3 %source_chunks.1 = (bf16[4,192,336]{2,1,0:T(8,128)(2,1)S(1)}, bf16[4,192,336]{2,1,0:T(8,128)(2,1)S(1)}, bf16[4,192,336]{2,1,0:T(8,128)(2,1)S(1)}, bf16[4,192,336]{2,1,0:T(8,128)(2,1)S(1)}, f32[1,5376]{1,0:T(1,128)S(1)}) custom-call(s32[1]{0:T(128)} %bitcast.me_ref, bf16[2,96,5376]{2,1,0:T(8,128)(2,1)S(1)} %copy-done), custom_call_target="tpu_custom_call" | custom-call | tf_op jit(solution)/shard_map/source_chunks/pallas_call | solution.py:207
  15.9 0.8 collective-permute-start.5
  16.8 1.5 %collective-permute-start.4 = (bf16[1,192,336]{2,1,0:T(8,128)(2,1)S(1)}, bf16[1,192,336]{2,1,0:T(8,128)(2,1)S(1)}, u32[]{:S(2)}, u32[]{:S(2)}) collective-permute-start(bf16[1,192,336]{2,1,0:T(8,128)(2,1)S(1)} %collective-permute-done.2.refs_8_), channel_id=1, source_target_pairs={{0,2},{1,3},{2,0},{3,1},{4,6},{5,7},{6,4},{7,5},{8,10},{9,11},{10,... | collective-permute-start | bytes 387080 | tf_op jit(solution)/shard_map/ppermute | solution.py:20
  19.0 3.2 %collective-permute-done.5.refs_11_ = bf16[1,192,336]{2,1,0:T(8,128)(2,1)S(1)} collective-permute-done((bf16[1,192,336]{2,1,0:T(8,128)(2,1)S(1)}, bf16[1,192,336]{2,1,0:T(8,128)(2,1)S(1)}, u32[]{:S(2)}, u32[]{:S(2)}) %collective-permute-start.5) | collective-permute-done | bytes 129056 | tf_op jit(solution)/shard_map/ppermute | solution.py:20
  22.2 1.5 %collective-permute-start.3 = (bf16[1,192,336]{2,1,0:T(8,128)(2,1)S(1)}, bf16[1,192,336]{2,1,0:T(8,128)(2,1)S(1)}, u32[]{:S(2)}, u32[]{:S(2)}) collective-permute-start(bf16[1,192,336]{2,1,0:T(8,128)(2,1)S(1)} %collective-permute-done.1.refs_7_), channel_id=1, source_target_pairs={{0,2},{1,3},{2,0},{3,1},{4,6},{5,7},{6,4},{7,5},{8,10},{9,11},{10,... | collective-permute-start | bytes 387080 | tf_op jit(solution)/shard_map/ppermute | solution.py:20
  24.3 14.2 %collective-permute-done.3.refs_9_ = bf16[1,192,336]{2,1,0:T(8,128)(2,1)S(1)} collective-permute-done((bf16[1,192,336]{2,1,0:T(8,128)(2,1)S(1)}, bf16[1,192,336]{2,1,0:T(8,128)(2,1)S(1)}, u32[]{:S(2)}, u32[]{:S(2)}) %collective-permute-start.3) | collective-permute-done | bytes 129056 | tf_op jit(solution)/shard_map/ppermute | solution.py:20
  38.5 1.5 %collective-permute-start.6 = (bf16[1,192,336]{2,1,0:T(8,128)(2,1)S(1)}, bf16[1,192,336]{2,1,0:T(8,128)(2,1)S(1)}, u32[]{:S(2)}, u32[]{:S(2)}) collective-permute-start(bf16[1,192,336]{2,1,0:T(8,128)(2,1)S(1)} %collective-permute-done.5.refs_11_), channel_id=1, source_target_pairs={{0,2},{1,3},{2,0},{3,1},{4,6},{5,7},{6,4},{7,5},{8,10},{9,11},{10,... | collective-permute-start | bytes 387080 | tf_op jit(solution)/shard_map/ppermute | solution.py:20
  40.6 3.6 %collective-permute-done.6.refs_12_ = bf16[1,192,336]{2,1,0:T(8,128)(2,1)S(1)} collective-permute-done((bf16[1,192,336]{2,1,0:T(8,128)(2,1)S(1)}, bf16[1,192,336]{2,1,0:T(8,128)(2,1)S(1)}, u32[]{:S(2)}, u32[]{:S(2)}) %collective-permute-start.6) | collective-permute-done | bytes 129056 | tf_op jit(solution)/shard_map/ppermute | solution.py:20
  44.8 0.9 collective-permute-done.11.refs_17_
  45.8 1.8 %sketch_rows.1 = (f32[2,96,96]{2,1,0:T(8,128)S(1)}, f32[96,97]{1,0:T(8,128)S(1)}) custom-call(bf16[4,192,336]{2,1,0:T(8,128)(2,1)S(1)} %get-tuple-element.39.refs_0_.refs_4_, bf16[4,192,336]{2,1,0:T(8,128)(2,1)S(1)} %get-tuple-element.40.refs_1_, bf16[4,192,336]{2,1,0:T(8,128)(2,1)S(1)} %get-tuple-element.41.refs_2_, ...), custom_call_target="tpu_custom_call" | custom-call | tf_op jit(solution)/shard_map/sketch_rows/pallas_call | solution.py:220
  48.0 0.9 %collective-permute-done.17 = f32[96,97]{1,0:T(8,128)S(1)} collective-permute-done((f32[96,97]{1,0:T(8,128)S(1)}, f32[96,97]{1,0:T(8,128)S(1)}, u32[]{:S(2)}, u32[]{:S(2)}) %collective-permute-start.17) | collective-permute-done | bytes 37280 | tf_op jit(solution)/shard_map/ppermute | solution.py:20
  48.9 3.3 %collective-permute-start.20 = (f32[96,97]{1,0:T(8,128)S(1)}, f32[96,97]{1,0:T(8,128)S(1)}, u32[]{:S(2)}, u32[]{:S(2)}) collective-permute-start(f32[96,97]{1,0:T(8,128)S(1)} %add.24), channel_id=1, source_target_pairs={{0,6},{1,7},{2,4},{3,5},{4,2},{5,3},{6,0},{7,1},{8,14},{9,15},{10,... | collective-permute-start | bytes 111752 | tf_op jit(solution)/shard_map/ppermute | solution.py:20
  52.2 0.7 collective-permute-start.19
  52.9 1.1 %collective-permute-start.23 = (f32[2,96,96]{2,1,0:T(8,128)S(1)}, f32[2,96,96]{2,1,0:T(8,128)S(1)}, u32[]{:S(2)}, u32[]{:S(2)}) collective-permute-start(f32[2,96,96]{2,1,0:T(8,128)S(1)} %get-tuple-element.61.refs_0_), channel_id=1, source_target_pairs={{0,3},{1,2},{2,1},{3,0},{4,7},{5,6},{6,5},{7,4},{8,11},{9,10},{10,... | collective-permute-start | bytes 221192 | tf_op jit(solution)/shard_map/ppermute | solution.py:20
  54.0 0.7 collective-permute-done.20
  54.7 1.9 %collective-permute-start.22 = (f32[2,96,96]{2,1,0:T(8,128)S(1)}, f32[2,96,96]{2,1,0:T(8,128)S(1)}, u32[]{:S(2)}, u32[]{:S(2)}) collective-permute-start(f32[2,96,96]{2,1,0:T(8,128)S(1)} %get-tuple-element.61.refs_0_), channel_id=1, source_target_pairs={{0,2},{1,3},{2,0},{3,1},{4,6},{5,7},{6,4},{7,5},{8,10},{9,11},{10,... | collective-permute-start | bytes 221192 | tf_op jit(solution)/shard_map/ppermute | solution.py:20
  56.6 2.4 %collective-permute-done.18 = f32[96,97]{1,0:T(8,128)S(1)} collective-permute-done((f32[96,97]{1,0:T(8,128)S(1)}, f32[96,97]{1,0:T(8,128)S(1)}, u32[]{:S(2)}, u32[]{:S(2)}) %collective-permute-start.18) | collective-permute-done | bytes 37280 | tf_op jit(solution)/shard_map/ppermute | solution.py:20
  59.0 1.5 %collective-permute-done.23.refs_3_ = f32[2,96,96]{2,1,0:T(8,128)S(1)} collective-permute-done((f32[2,96,96]{2,1,0:T(8,128)S(1)}, f32[2,96,96]{2,1,0:T(8,128)S(1)}, u32[]{:S(2)}, u32[]{:S(2)}) %collective-permute-start.23) | collective-permute-done | bytes 73760 | tf_op jit(solution)/shard_map/ppermute | solution.py:20
  60.5 2.1 %collective-permute-done.22.refs_2_ = f32[2,96,96]{2,1,0:T(8,128)S(1)} collective-permute-done((f32[2,96,96]{2,1,0:T(8,128)S(1)}, f32[2,96,96]{2,1,0:T(8,128)S(1)}, u32[]{:S(2)}, u32[]{:S(2)}) %collective-permute-start.22) | collective-permute-done | bytes 73760 | tf_op jit(solution)/shard_map/ppermute | solution.py:20
  62.6 3.3 %collective-permute-start.25 = (f32[96,97]{1,0:T(8,128)S(1)}, f32[96,97]{1,0:T(8,128)S(1)}, u32[]{:S(2)}, u32[]{:S(2)}) collective-permute-start(f32[96,97]{1,0:T(8,128)S(1)} %add_add_fusion), channel_id=1, source_target_pairs={{0,8},{1,9},{2,10},{3,11},{4,12},{5,13},{6,14},{7,15},{8,0},{9,1},... | collective-permute-start | bytes 111752 | tf_op jit(solution)/shard_map/ppermute | solution.py:20
  65.9 2.6 %collective-permute-done.25 = f32[96,97]{1,0:T(8,128)S(1)} collective-permute-done((f32[96,97]{1,0:T(8,128)S(1)}, f32[96,97]{1,0:T(8,128)S(1)}, u32[]{:S(2)}, u32[]{:S(2)}) %collective-permute-start.25) | collective-permute-done | bytes 37280 | tf_op jit(solution)/shard_map/ppermute | solution.py:20
  68.5 8.7 %basis_and_projection.1 = (f32[2,96,96]{2,1,0:T(8,128)}, f32[192,336]{1,0:T(8,128)S(1)}, f32[192,336]{1,0:T(8,128)S(1)}, f32[192,336]{1,0:T(8,128)S(1)}, f32[192,336]{1,0:T(8,128)S(1)}) custom-call(f32[96,97]{1,0:T(8,128)S(1)} %add.28.gram_ref, f32[2,96,96]{2,1,0:T(8,128)S(1)} %get-tuple-element.61.refs_0_, ...), custom_call_target="tpu_custom_call" | custom-call | tf_op jit(solution)/shard_map/basis_and_projection/pallas_call | solution.py:242
  77.3 2.6 %collective-permute-start.28 = (f16[192,336]{1,0:T(8,128)(2,1)S(1)}, f16[192,336]{1,0:T(8,128)(2,1)S(1)}, u32[]{:S(2)}, u32[]{:S(2)}) collective-permute-start(f16[192,336]{1,0:T(8,128)(2,1)S(1)} %convert_element_type.22), channel_id=1, source_target_pairs={{0,12},{1,13},{2,14},{3,15},{4,8},{5,9},{6,10},{7,11},{8,4},{9,5},... | collective-permute-start | bytes 387080 | tf_op jit(solution)/shard_map/ppermute | solution.py:20
  79.9 1.9 %collective-permute-start.26 = (f16[192,336]{1,0:T(8,128)(2,1)S(1)}, f16[192,336]{1,0:T(8,128)(2,1)S(1)}, u32[]{:S(2)}, u32[]{:S(2)}) collective-permute-start(f16[192,336]{1,0:T(8,128)(2,1)S(1)} %convert_element_type.18), channel_id=1, source_target_pairs={{0,4},{1,5},{2,6},{3,7},{4,0},{5,1},{6,2},{7,3},{8,12},{9,13},{10,... | collective-permute-start | bytes 387080 | tf_op jit(solution)/shard_map/ppermute | solution.py:20
  83.0 3.0 %collective-permute-done.28 = f16[192,336]{1,0:T(8,128)(2,1)S(1)} collective-permute-done((f16[192,336]{1,0:T(8,128)(2,1)S(1)}, f16[192,336]{1,0:T(8,128)(2,1)S(1)}, u32[]{:S(2)}, u32[]{:S(2)}) %collective-permute-start.28) | collective-permute-done | bytes 129056 | tf_op jit(solution)/shard_map/ppermute | solution.py:20
  86.0 5.7 %collective-permute-done.27 = f16[192,336]{1,0:T(8,128)(2,1)S(1)} collective-permute-done((f16[192,336]{1,0:T(8,128)(2,1)S(1)}, f16[192,336]{1,0:T(8,128)(2,1)S(1)}, u32[]{:S(2)}, u32[]{:S(2)}) %collective-permute-start.27) | collective-permute-done | bytes 129056 | tf_op jit(solution)/shard_map/ppermute | solution.py:20
  91.6 0.8 multiply_add_fusion
  (41 shorter events, 3.8 us)
Async XLA Ops:
  0.6 11.4 %collective-permute-start.2 = (bf16[1,192,336]{2,1,0:T(8,128)(2,1)}, bf16[1,192,336]{2,1,0:T(8,128)(2,1)S(1)}, u32[]{:S(2)}, u32[]{:S(2)}) collective-permute-start(bf16[1,192,336]{2,1,0:T(8,128)(2,1)} %bitcast.4), channel_id=1, source_target_pairs={{0,8},{1,9},{2,10},{3,11},{4,12},{5,13},{6,14},{7,15},{8,0},{9,1},... | collective-permute-start | bytes 387080 | tf_op jit(solution)/shard_map/ppermute | solution.py:20
  4.7 12.0 %collective-permute-start.7 = (bf16[1,192,336]{2,1,0:T(8,128)(2,1)}, bf16[1,192,336]{2,1,0:T(8,128)(2,1)S(1)}, u32[]{:S(2)}, u32[]{:S(2)}) collective-permute-start(bf16[1,192,336]{2,1,0:T(8,128)(2,1)} %bitcast.5), channel_id=1, source_target_pairs={{0,1},{1,0},{2,3},{3,2},{4,5},{5,4},{6,7},{7,6},{8,9},{9,8},{10,11... | collective-permute-start | bytes 387080 | tf_op jit(solution)/shard_map/ppermute | solution.py:20
  4.7 13.5 %collective-permute-start.1 = (bf16[1,192,336]{2,1,0:T(8,128)(2,1)}, bf16[1,192,336]{2,1,0:T(8,128)(2,1)S(1)}, u32[]{:S(2)}, u32[]{:S(2)}) collective-permute-start(bf16[1,192,336]{2,1,0:T(8,128)(2,1)} %bitcast.6), channel_id=1, source_target_pairs={{0,4},{1,5},{2,6},{3,7},{4,0},{5,1},{6,2},{7,3},{8,12},{9,13},{10,... | collective-permute-start | bytes 387080 | tf_op jit(solution)/shard_map/ppermute | solution.py:20
  6.3 11.9 %collective-permute-start = (bf16[1,192,336]{2,1,0:T(8,128)(2,1)}, bf16[1,192,336]{2,1,0:T(8,128)(2,1)S(1)}, u32[]{:S(2)}, u32[]{:S(2)}) collective-permute-start(bf16[1,192,336]{2,1,0:T(8,128)(2,1)} %bitcast.7), channel_id=1, source_target_pairs={{0,2},{1,3},{2,0},{3,1},{4,6},{5,7},{6,4},{7,5},{8,10},{9,11},{10,... | collective-permute-start | bytes 387080 | tf_op jit(solution)/shard_map/ppermute | solution.py:20
  12.1 6.8 %collective-permute-start.10 = (bf16[1,192,336]{2,1,0:T(8,128)(2,1)S(1)}, bf16[1,192,336]{2,1,0:T(8,128)(2,1)S(1)}, u32[]{:S(2)}, u32[]{:S(2)}) collective-permute-start(bf16[1,192,336]{2,1,0:T(8,128)(2,1)S(1)} %collective-permute-done.2.refs_8_), channel_id=1, source_target_pairs={{0,1},{1,0},{2,3},{3,2},{4,5},{5,4},{6,7},{7,6},{8,9},{9,8},{10,11... | collective-permute-start | bytes 387080 | tf_op jit(solution)/shard_map/ppermute | solution.py:20
  12.1 1.6 %copy-start = (bf16[2,96,5376]{2,1,0:T(8,128)(2,1)S(1)}, bf16[2,96,5376]{2,1,0:T(8,128)(2,1)}, u32[]{:S(2)}) copy-start(bf16[2,96,5376]{2,1,0:T(8,128)(2,1)} %traces_ref.1) | copy-start | bytes 6193156
  13.6 32.2 %copy-start.1 = (bf16[2,96,336]{2,1,0:T(8,128)(2,1)S(1)}, bf16[2,96,336]{2,1,0:T(8,128)(2,1)}, u32[]{:S(2)}) copy-start(bf16[2,96,336]{2,1,0:T(8,128)(2,1)} %param.3) | copy-start | bytes 387076
  15.9 6.3 %collective-permute-start.5 = (bf16[1,192,336]{2,1,0:T(8,128)(2,1)S(1)}, bf16[1,192,336]{2,1,0:T(8,128)(2,1)S(1)}, u32[]{:S(2)}, u32[]{:S(2)}) collective-permute-start(bf16[1,192,336]{2,1,0:T(8,128)(2,1)S(1)} %collective-permute-done.2.refs_8_), channel_id=1, source_target_pairs={{0,4},{1,5},{2,6},{3,7},{4,0},{5,1},{6,2},{7,3},{8,12},{9,13},{10,... | collective-permute-start | bytes 387080 | tf_op jit(solution)/shard_map/ppermute | solution.py:20
  16.8 7.0 %collective-permute-start.4 = (bf16[1,192,336]{2,1,0:T(8,128)(2,1)S(1)}, bf16[1,192,336]{2,1,0:T(8,128)(2,1)S(1)}, u32[]{:S(2)}, u32[]{:S(2)}) collective-permute-start(bf16[1,192,336]{2,1,0:T(8,128)(2,1)S(1)} %collective-permute-done.2.refs_8_), channel_id=1, source_target_pairs={{0,2},{1,3},{2,0},{3,1},{4,6},{5,7},{6,4},{7,5},{8,10},{9,11},{10,... | collective-permute-start | bytes 387080 | tf_op jit(solution)/shard_map/ppermute | solution.py:20
  18.2 27.6 %collective-permute-start.15 = (bf16[4,192,336]{2,1,0:T(8,128)(2,1)S(1)}, bf16[4,192,336]{2,1,0:T(8,128)(2,1)S(1)}, u32[]{:S(2)}, u32[]{:S(2)}) collective-permute-start(bf16[4,192,336]{2,1,0:T(8,128)(2,1)S(1)} %get-tuple-element.40.refs_1_), channel_id=1, source_target_pairs={{0,1},{1,0},{2,3},{3,2},{4,5},{5,4},{6,7},{7,6},{8,9},{9,8},{10,11... | collective-permute-start | bytes 1548296 | tf_op jit(solution)/shard_map/ppermute | solution.py:20
  18.3 27.6 %collective-permute-start.16 = (bf16[4,192,336]{2,1,0:T(8,128)(2,1)S(1)}, bf16[4,192,336]{2,1,0:T(8,128)(2,1)S(1)}, u32[]{:S(2)}, u32[]{:S(2)}) collective-permute-start(bf16[4,192,336]{2,1,0:T(8,128)(2,1)S(1)} %get-tuple-element.41.refs_2_), channel_id=1, source_target_pairs={{0,2},{1,3},{2,0},{3,1},{4,6},{5,7},{6,4},{7,5},{8,10},{9,11},{10,... | collective-permute-start | bytes 1548296 | tf_op jit(solution)/shard_map/ppermute | solution.py:20
  18.9 4.9 %collective-permute-start.9 = (bf16[1,192,336]{2,1,0:T(8,128)(2,1)S(1)}, bf16[1,192,336]{2,1,0:T(8,128)(2,1)S(1)}, u32[]{:S(2)}, u32[]{:S(2)}) collective-permute-start(bf16[1,192,336]{2,1,0:T(8,128)(2,1)S(1)} %collective-permute-done.1.refs_7_), channel_id=1, source_target_pairs={{0,1},{1,0},{2,3},{3,2},{4,5},{5,4},{6,7},{7,6},{8,9},{9,8},{10,11... | collective-permute-start | bytes 387080 | tf_op jit(solution)/shard_map/ppermute | solution.py:20
  22.2 16.3 %collective-permute-start.3 = (bf16[1,192,336]{2,1,0:T(8,128)(2,1)S(1)}, bf16[1,192,336]{2,1,0:T(8,128)(2,1)S(1)}, u32[]{:S(2)}, u32[]{:S(2)}) collective-permute-start(bf16[1,192,336]{2,1,0:T(8,128)(2,1)S(1)} %collective-permute-done.1.refs_7_), channel_id=1, source_target_pairs={{0,2},{1,3},{2,0},{3,1},{4,6},{5,7},{6,4},{7,5},{8,10},{9,11},{10,... | collective-permute-start | bytes 387080 | tf_op jit(solution)/shard_map/ppermute | solution.py:20
  23.7 16.2 %collective-permute-start.8 = (bf16[1,192,336]{2,1,0:T(8,128)(2,1)S(1)}, bf16[1,192,336]{2,1,0:T(8,128)(2,1)S(1)}, u32[]{:S(2)}, u32[]{:S(2)}) collective-permute-start(bf16[1,192,336]{2,1,0:T(8,128)(2,1)S(1)} %collective-permute-done.refs_6_), channel_id=1, source_target_pairs={{0,1},{1,0},{2,3},{3,2},{4,5},{5,4},{6,7},{7,6},{8,9},{9,8},{10,11... | collective-permute-start | bytes 387080 | tf_op jit(solution)/shard_map/ppermute | solution.py:20
  23.8 16.2 %collective-permute-start.13 = (bf16[1,192,336]{2,1,0:T(8,128)(2,1)S(1)}, bf16[1,192,336]{2,1,0:T(8,128)(2,1)S(1)}, u32[]{:S(2)}, u32[]{:S(2)}) collective-permute-start(bf16[1,192,336]{2,1,0:T(8,128)(2,1)S(1)} %collective-permute-done.5.refs_11_), channel_id=1, source_target_pairs={{0,1},{1,0},{2,3},{3,2},{4,5},{5,4},{6,7},{7,6},{8,9},{9,8},{10,11... | collective-permute-start | bytes 387080 | tf_op jit(solution)/shard_map/ppermute | solution.py:20
  38.5 5.7 %collective-permute-start.6 = (bf16[1,192,336]{2,1,0:T(8,128)(2,1)S(1)}, bf16[1,192,336]{2,1,0:T(8,128)(2,1)S(1)}, u32[]{:S(2)}, u32[]{:S(2)}) collective-permute-start(bf16[1,192,336]{2,1,0:T(8,128)(2,1)S(1)} %collective-permute-done.5.refs_11_), channel_id=1, source_target_pairs={{0,2},{1,3},{2,0},{3,1},{4,6},{5,7},{6,4},{7,5},{8,10},{9,11},{10,... | collective-permute-start | bytes 387080 | tf_op jit(solution)/shard_map/ppermute | solution.py:20
  40.0 4.3 %collective-permute-start.12 = (bf16[1,192,336]{2,1,0:T(8,128)(2,1)S(1)}, bf16[1,192,336]{2,1,0:T(8,128)(2,1)S(1)}, u32[]{:S(2)}, u32[]{:S(2)}) collective-permute-start(bf16[1,192,336]{2,1,0:T(8,128)(2,1)S(1)} %collective-permute-done.4.refs_10_), channel_id=1, source_target_pairs={{0,1},{1,0},{2,3},{3,2},{4,5},{5,4},{6,7},{7,6},{8,9},{9,8},{10,11... | collective-permute-start | bytes 387080 | tf_op jit(solution)/shard_map/ppermute | solution.py:20
  40.0 19.0 %collective-permute-start.24 = (bf16[4,192,336]{2,1,0:T(8,128)(2,1)S(1)}, bf16[4,192,336]{2,1,0:T(8,128)(2,1)S(1)}, u32[]{:S(2)}, u32[]{:S(2)}) collective-permute-start(bf16[4,192,336]{2,1,0:T(8,128)(2,1)S(1)} %get-tuple-element.42.refs_3_), channel_id=1, source_target_pairs={{0,3},{1,2},{2,1},{3,0},{4,7},{5,6},{6,5},{7,4},{8,11},{9,10},{10,... | collective-permute-start | bytes 1548296 | tf_op jit(solution)/shard_map/ppermute | solution.py:20
  44.2 1.4 %collective-permute-start.11 = (bf16[1,192,336]{2,1,0:T(8,128)(2,1)S(1)}, bf16[1,192,336]{2,1,0:T(8,128)(2,1)S(1)}, u32[]{:S(2)}, u32[]{:S(2)}) collective-permute-start(bf16[1,192,336]{2,1,0:T(8,128)(2,1)S(1)} %collective-permute-done.3.refs_9_), channel_id=1, source_target_pairs={{0,1},{1,0},{2,3},{3,2},{4,5},{5,4},{6,7},{7,6},{8,9},{9,8},{10,11... | collective-permute-start | bytes 387080 | tf_op jit(solution)/shard_map/ppermute | solution.py:20
  44.2 1.6 %collective-permute-start.14 = (bf16[1,192,336]{2,1,0:T(8,128)(2,1)S(1)}, bf16[1,192,336]{2,1,0:T(8,128)(2,1)S(1)}, u32[]{:S(2)}, u32[]{:S(2)}) collective-permute-start(bf16[1,192,336]{2,1,0:T(8,128)(2,1)S(1)} %collective-permute-done.6.refs_12_), channel_id=1, source_target_pairs={{0,1},{1,0},{2,3},{3,2},{4,5},{5,4},{6,7},{7,6},{8,9},{9,8},{10,11... | collective-permute-start | bytes 387080 | tf_op jit(solution)/shard_map/ppermute | solution.py:20
  47.6 1.3 %collective-permute-start.17 = (f32[96,97]{1,0:T(8,128)S(1)}, f32[96,97]{1,0:T(8,128)S(1)}, u32[]{:S(2)}, u32[]{:S(2)}) collective-permute-start(f32[96,97]{1,0:T(8,128)S(1)} %get-tuple-element.60), channel_id=1, source_target_pairs={{0,1},{1,0},{2,3},{3,2},{4,5},{5,4},{6,7},{7,6},{8,9},{9,8},{10,11... | collective-permute-start | bytes 111752 | tf_op jit(solution)/shard_map/ppermute | solution.py:20
  48.9 5.8 %collective-permute-start.20 = (f32[96,97]{1,0:T(8,128)S(1)}, f32[96,97]{1,0:T(8,128)S(1)}, u32[]{:S(2)}, u32[]{:S(2)}) collective-permute-start(f32[96,97]{1,0:T(8,128)S(1)} %add.24), channel_id=1, source_target_pairs={{0,6},{1,7},{2,4},{3,5},{4,2},{5,3},{6,0},{7,1},{8,14},{9,15},{10,... | collective-permute-start | bytes 111752 | tf_op jit(solution)/shard_map/ppermute | solution.py:20
  52.2 4.4 %collective-permute-start.19 = (f32[96,97]{1,0:T(8,128)S(1)}, f32[96,97]{1,0:T(8,128)S(1)}, u32[]{:S(2)}, u32[]{:S(2)}) collective-permute-start(f32[96,97]{1,0:T(8,128)S(1)} %add.24), channel_id=1, source_target_pairs={{0,4},{1,5},{2,6},{3,7},{4,0},{5,1},{6,2},{7,3},{8,12},{9,13},{10,... | collective-permute-start | bytes 111752 | tf_op jit(solution)/shard_map/ppermute | solution.py:20
  52.9 6.1 %collective-permute-start.18 = (f32[96,97]{1,0:T(8,128)S(1)}, f32[96,97]{1,0:T(8,128)S(1)}, u32[]{:S(2)}, u32[]{:S(2)}) collective-permute-start(f32[96,97]{1,0:T(8,128)S(1)} %add.24), channel_id=1, source_target_pairs={{0,2},{1,3},{2,0},{3,1},{4,6},{5,7},{6,4},{7,5},{8,10},{9,11},{10,... | collective-permute-start | bytes 111752 | tf_op jit(solution)/shard_map/ppermute | solution.py:20
  52.9 7.7 %collective-permute-start.23 = (f32[2,96,96]{2,1,0:T(8,128)S(1)}, f32[2,96,96]{2,1,0:T(8,128)S(1)}, u32[]{:S(2)}, u32[]{:S(2)}) collective-permute-start(f32[2,96,96]{2,1,0:T(8,128)S(1)} %get-tuple-element.61.refs_0_), channel_id=1, source_target_pairs={{0,3},{1,2},{2,1},{3,0},{4,7},{5,6},{6,5},{7,4},{8,11},{9,10},{10,... | collective-permute-start | bytes 221192 | tf_op jit(solution)/shard_map/ppermute | solution.py:20
  54.7 7.9 %collective-permute-start.22 = (f32[2,96,96]{2,1,0:T(8,128)S(1)}, f32[2,96,96]{2,1,0:T(8,128)S(1)}, u32[]{:S(2)}, u32[]{:S(2)}) collective-permute-start(f32[2,96,96]{2,1,0:T(8,128)S(1)} %get-tuple-element.61.refs_0_), channel_id=1, source_target_pairs={{0,2},{1,3},{2,0},{3,1},{4,6},{5,7},{6,4},{7,5},{8,10},{9,11},{10,... | collective-permute-start | bytes 221192 | tf_op jit(solution)/shard_map/ppermute | solution.py:20
  56.6 6.0 %collective-permute-start.21 = (f32[2,96,96]{2,1,0:T(8,128)S(1)}, f32[2,96,96]{2,1,0:T(8,128)S(1)}, u32[]{:S(2)}, u32[]{:S(2)}) collective-permute-start(f32[2,96,96]{2,1,0:T(8,128)S(1)} %get-tuple-element.61.refs_0_), channel_id=1, source_target_pairs={{0,1},{1,0},{2,3},{3,2},{4,5},{5,4},{6,7},{7,6},{8,9},{9,8},{10,11... | collective-permute-start | bytes 221192 | tf_op jit(solution)/shard_map/ppermute | solution.py:20
  62.6 5.9 %collective-permute-start.25 = (f32[96,97]{1,0:T(8,128)S(1)}, f32[96,97]{1,0:T(8,128)S(1)}, u32[]{:S(2)}, u32[]{:S(2)}) collective-permute-start(f32[96,97]{1,0:T(8,128)S(1)} %add_add_fusion), channel_id=1, source_target_pairs={{0,8},{1,9},{2,10},{3,11},{4,12},{5,13},{6,14},{7,15},{8,0},{9,1},... | collective-permute-start | bytes 111752 | tf_op jit(solution)/shard_map/ppermute | solution.py:20
  77.3 8.7 %collective-permute-start.28 = (f16[192,336]{1,0:T(8,128)(2,1)S(1)}, f16[192,336]{1,0:T(8,128)(2,1)S(1)}, u32[]{:S(2)}, u32[]{:S(2)}) collective-permute-start(f16[192,336]{1,0:T(8,128)(2,1)S(1)} %convert_element_type.22), channel_id=1, source_target_pairs={{0,12},{1,13},{2,14},{3,15},{4,8},{5,9},{6,10},{7,11},{8,4},{9,5},... | collective-permute-start | bytes 387080 | tf_op jit(solution)/shard_map/ppermute | solution.py:20
  79.9 11.7 %collective-permute-start.27 = (f16[192,336]{1,0:T(8,128)(2,1)S(1)}, f16[192,336]{1,0:T(8,128)(2,1)S(1)}, u32[]{:S(2)}, u32[]{:S(2)}) collective-permute-start(f16[192,336]{1,0:T(8,128)(2,1)S(1)} %convert_element_type.20), channel_id=1, source_target_pairs={{0,8},{1,9},{2,10},{3,11},{4,12},{5,13},{6,14},{7,15},{8,0},{9,1},... | collective-permute-start | bytes 387080 | tf_op jit(solution)/shard_map/ppermute | solution.py:20
  79.9 11.7 %collective-permute-start.26 = (f16[192,336]{1,0:T(8,128)(2,1)S(1)}, f16[192,336]{1,0:T(8,128)(2,1)S(1)}, u32[]{:S(2)}, u32[]{:S(2)}) collective-permute-start(f16[192,336]{1,0:T(8,128)(2,1)S(1)} %convert_element_type.18), channel_id=1, source_target_pairs={{0,4},{1,5},{2,6},{3,7},{4,0},{5,1},{6,2},{7,3},{8,12},{9,13},{10,... | collective-permute-start | bytes 387080 | tf_op jit(solution)/shard_map/ppermute | solution.py:20

commit v4 on v3

v4 whole, which is shorter than its diff:
```python
import functools
import math

import jax
import jax.numpy as jnp
from jax import lax
from jax.experimental import pallas as pl
from jax.experimental.pallas import tpu as pltpu
from jax.sharding import PartitionSpec as P

ROWS = 8
GROUPS = 4
TOP = 32768.0
VMEM = pl.BlockSpec(memory_space=pltpu.VMEM)
SMEM = pl.BlockSpec(memory_space=pltpu.SMEM)
PARAMS = pltpu.CompilerParams(vmem_limit_bytes=40 * 1024 * 1024)


def swap(value, mask, size):
    return lax.ppermute(value, "rcv", [(i, i ^ mask) for i in range(size)])


def exact(left, right, dims):
    return lax.dot_general(
        left,
        right,
        ((dims[0], dims[1]), ((), ())),
        precision=lax.Precision.HIGHEST,
        preferred_element_type=jnp.float32,
    )


def chunk_kernel(share, me_ref, traces_ref, stay_ref, core_ref, near_ref, far_ref, cross_ref, peak_ref, held_ref):
    rows, sources = traces_ref.shape[1:]
    me = me_ref[0]
    for owner in range(sources // share):
        away = owner ^ me
        for part in range(2):
            held_ref[away % GROUPS, away // GROUPS, rows * part : rows * (part + 1), :] = traces_ref[
                part, :, owner * share : (owner + 1) * share
            ]
    zones = stay_ref.shape[0]
    half = zones // 2
    stay_ref[...] = held_ref[0]
    core_ref[:zones] = held_ref[1]
    core_ref[zones:] = held_ref[3, :half]
    near_ref[...] = held_ref[2, :half]
    far_ref[...] = held_ref[2, half:]
    cross_ref[...] = held_ref[3, half:]
    peak = jnp.maximum(
        jnp.max(jnp.abs(traces_ref[0]), axis=0, keepdims=True),
        jnp.max(jnp.abs(traces_ref[1]), axis=0, keepdims=True),
    )
    peak_ref[...] = peak.astype(jnp.float32)


def sketch_kernel(held, stay_ref, core_ref, near_ref, far_ref, cross_ref, peak_ref, *refs):
    pieces, (out_ref, gram_ref) = refs[:-2], refs[-2:]
    count = out_ref.shape[2]
    zones = stay_ref.shape[0]
    half = zones // 2
    total = None
    for slot in range(GROUPS * zones):
        group, zone = slot % GROUPS, slot // GROUPS
        if group < 2:
            data = (stay_ref, core_ref)[group][zone]
        elif zone < half:
            data = near_ref[zone] if group == 2 else core_ref[zones + zone]
        else:
            data = (far_ref, cross_ref)[group - 2][zone - half]
        which, at = held[slot]
        term = lax.dot_general(
            data, pieces[which][at], (((1,), (1,)), ((), ())), preferred_element_type=jnp.float32
        )
        total = term if total is None else total + term
    rows = total.shape[0] // 2
    real = total[:rows, :count] - total[rows:, count:]
    imag = total[:rows, count:] + total[rows:, :count]
    out_ref[0] = real
    out_ref[1] = imag
    gram_re = exact(real, real, ((0,), (0,))) + exact(imag, imag, ((0,), (0,)))
    gram_im = exact(real, imag, ((0,), (0,))) - exact(imag, real, ((0,), (0,)))
    row = lax.broadcasted_iota(jnp.int32, gram_re.shape, 0)
    column = lax.broadcasted_iota(jnp.int32, gram_re.shape, 1)
    gram_ref[:, :count] = jnp.where(row <= column, gram_re, gram_im)
    peak = jnp.max(peak_ref[...], axis=1, keepdims=True)
    gram_ref[:, count:] = jnp.broadcast_to(peak, (count, gram_ref.shape[1] - count))


def eliminate(real, imag):
    count, width = real.shape
    lane = lax.broadcasted_iota(jnp.int32, (ROWS, width), 1)
    row = lax.broadcasted_iota(jnp.int32, (ROWS, width), 0)
    blocks = count // ROWS
    re = [real[ROWS * i : ROWS * (i + 1)] for i in range(blocks)]
    im = [imag[ROWS * i : ROWS * (i + 1)] for i in range(blocks)]
    for b in range(blocks):
        col_re, col_im = [], []
        for o in range(ROWS):
            k = ROWS * b + o
            col_re.append([jnp.broadcast_to(re[i][:, k : k + 1], (ROWS, width)) for i in range(b, blocks)])
            col_im.append([jnp.broadcast_to(im[i][:, k : k + 1], (ROWS, width)) for i in range(b, blocks)])
        for o in range(ROWS):
            hit = lane == ROWS * b + o
            scale = lax.rsqrt(col_re[o][0][o : o + 1])
            pivot_re = jnp.where(hit[:1], scale, re[b][o : o + 1] * scale)
            pivot_im = jnp.where(hit[:1], 0.0, im[b][o : o + 1] * scale)
            by_re = [v * scale for v in col_re[o]]
            by_im = [v * scale for v in col_im[o]]
            for j in range(o + 1, ROWS):
                x_re, x_im = by_re[0][j : j + 1], by_im[0][j : j + 1]
                for q in range(blocks - b):
                    col_re[j][q] = col_re[j][q] - (by_re[q] * x_re + by_im[q] * x_im)
                    col_im[j][q] = col_im[j][q] - (by_im[q] * x_re - by_re[q] * x_im)
            for q, i in enumerate(range(b, blocks)):
                new_re = jnp.where(hit, 0.0, re[i]) - (by_re[q] * pivot_re - by_im[q] * pivot_im)
                new_im = jnp.where(hit, 0.0, im[i]) - (by_re[q] * pivot_im + by_im[q] * pivot_re)
                if i == b:
                    new_re = jnp.where(row > o, new_re, jnp.where(row == o, pivot_re, re[i]))
                    new_im = jnp.where(row > o, new_im, jnp.where(row == o, pivot_im, im[i]))
                re[i], im[i] = new_re, new_im
    return jnp.concatenate(re, axis=0), jnp.concatenate(im, axis=0)


def basis_kernel(scale, gram_ref, *refs):
    sketched, basis_ref, weights = refs[:GROUPS], refs[GROUPS], refs[GROUPS + 1 :]
    count = gram_ref.shape[0]
    packed = gram_ref[:, :count]
    flipped = packed.T
    row = lax.broadcasted_iota(jnp.int32, packed.shape, 0)
    column = lax.broadcasted_iota(jnp.int32, packed.shape, 1)
    gram_re = jnp.where(row <= column, packed, flipped)
    gram_im = jnp.where(row > column, packed, jnp.where(row < column, -flipped, 0.0))
    low_re, low_im = eliminate(gram_re, gram_im)
    low_re = jnp.where(row >= column, low_re, 0.0)
    low_im = jnp.where(row >= column, low_im, 0.0)
    stacked = jnp.concatenate([ref[part] for ref in sketched for part in range(2)], axis=0)
    by_re = exact(stacked, low_re, ((1,), (1,)))
    by_im = exact(stacked, low_im, ((1,), (1,)))
    rows = stacked.shape[0] // GROUPS // 2
    for group in range(GROUPS):
        real = slice(2 * rows * group, 2 * rows * group + rows)
        imag = slice(2 * rows * group + rows, 2 * rows * (group + 1))
        ortho_re = by_re[real] + by_im[imag]
        ortho_im = by_re[imag] - by_im[real]
        if group == 0:
            basis_ref[0] = ortho_re * scale
            basis_ref[1] = ortho_im * scale
        flat_re, flat_im = ortho_re.T, ortho_im.T
        top = jnp.concatenate([flat_re, flat_im], axis=1)
        low = jnp.concatenate([-flat_im, flat_re], axis=1)
        weights[group][...] = jnp.concatenate([top, low], axis=0).astype(jnp.bfloat16)


def project_kernel(bound, gram_ref, *refs):
    weights, (stay_ref, core_ref, near_ref, far_ref, cross_ref) = refs[:GROUPS], refs[GROUPS : GROUPS + 5]
    own_ref, side_ref, *far_outs = refs[GROUPS + 5 :]
    count = gram_ref.shape[0]
    factor = TOP / (gram_ref[:1, count : count + 1] * bound)
    half = near_ref.shape[0]
    zones = 2 * half

    def project(*data):
        total = None
        for weight_ref, block in zip(weights, data):
            term = jnp.dot(weight_ref[...], block, preferred_element_type=jnp.float32)
            total = term if total is None else total + term
        return total * factor

    for zone in range(half):
        far_outs[zone][...] = project(stay_ref[half + zone], core_ref[half + zone], far_ref[zone], cross_ref[zone])
    for zone in range(half):
        side_ref[zone] = project(near_ref[zone], core_ref[zones + zone])
        own_ref[zone] = project(stay_ref[zone], core_ref[zone])


def tied(first, second):
    first, second = list(first), list(second)
    both = lax.optimization_barrier(tuple(first + second))
    return list(both[: len(first)]), list(both[len(first) :])


def gather_slots(piece, size, ahead):
    bits = size.bit_length() - 1
    direct = min(bits, 4)
    have = {0: piece}
    for level in range(1, direct):
        if level == 2:
            (have[1 << direct - 1],), _ = tied([have[1 << direct - 1]], [ahead])
        for slot in reversed(range(0, 1 << direct, 2)):
            if slot.bit_count() == level:
                along = slot & -slot if slot >> direct - 1 else 1 << slot.bit_length() - 1
                have[slot] = swap(have[slot ^ along], along, size)
    pieces = [(have[slot], [slot]) for slot in sorted(have, key=lambda slot: (slot.bit_count(), slot))]
    for bit in range(4, bits):
        whole = jnp.concatenate([value for value, _ in pieces])
        slots = [slot for _, held in pieces for slot in held]
        pieces = [(whole, slots), (swap(whole, 1 << bit, size), [slot | 1 << bit for slot in slots])]
    return pieces + [(swap(value, 1, size), [slot | 1 for slot in slots]) for value, slots in pieces]


def per_device(traces, sketch):
    size = lax.axis_size("rcv")
    me = lax.axis_index("rcv")
    rows, sources = traces.shape[1:]
    count, share = sketch.shape[1:]
    zones = size // GROUPS
    half = zones // 2
    bits = size.bit_length() - 1
    chunk = lambda slots: jax.ShapeDtypeStruct((slots, 2 * rows, share), traces.dtype)

    stay, core, near, far, cross, peak = pl.pallas_call(
        functools.partial(chunk_kernel, share),
        out_shape=(
            chunk(zones),
            chunk(zones + half),
            chunk(half),
            chunk(half),
            chunk(half),
            jax.ShapeDtypeStruct((1, sources), jnp.float32),
        ),
        in_specs=[SMEM, VMEM],
        out_specs=(VMEM,) * 6,
        scratch_shapes=[pltpu.VMEM((GROUPS, zones, 2 * rows, share), traces.dtype)],
        compiler_params=PARAMS,
        name="source_chunks",
    )(me.astype(jnp.int32).reshape(1), traces)
    pieces = gather_slots(sketch.reshape(1, 2 * count, share), size, stay)
    values = [value for value, _ in pieces]
    held = {slot: (which, at) for which, (_, slots) in enumerate(pieces) for at, slot in enumerate(slots)}
    sketched, gram = pl.pallas_call(
        functools.partial(sketch_kernel, held),
        out_shape=(
            jax.ShapeDtypeStruct((2, rows, count), jnp.float32),
            jax.ShapeDtypeStruct((count, count + 1), jnp.float32),
        ),
        in_specs=[VMEM] * (6 + len(values)),
        out_specs=(VMEM, VMEM),
        compiler_params=PARAMS,
        name="sketch_rows",
    )(stay, core, near, far, cross, peak, *values)

    core_in = swap(core, 1, size)
    gram = gram + swap(gram, 1, size)
    beside = swap(gram, 2, size)
    known = [swap(sketched, group, size) for group in range(1, GROUPS)]
    (far_out, cross_out), _ = tied([far, cross], [beside, *known])
    far_in, cross_in = swap(far_out, 2, size), swap(cross_out, 3, size)
    gram = gram + beside
    for bit in range(2, bits):
        gram = gram + swap(gram, 1 << bit, size)

    basis, *weights = pl.pallas_call(
        functools.partial(basis_kernel, math.sqrt(rows * size)),
        out_shape=(jax.ShapeDtypeStruct((2, rows, count), jnp.float32),)
        + (jax.ShapeDtypeStruct((2 * count, 2 * rows), jnp.bfloat16),) * GROUPS,
        in_specs=[VMEM] * (1 + GROUPS),
        out_specs=(VMEM,) * (1 + GROUPS),
        compiler_params=PARAMS,
        name="orthonormal_basis",
    )(gram, sketched, *known)
    bound = 1.01 * math.sqrt(2 * rows * size)
    own, side, *away = pl.pallas_call(
        functools.partial(project_kernel, bound),
        out_shape=(
            jax.ShapeDtypeStruct((half, 2 * count, share), jnp.float32),
            jax.ShapeDtypeStruct((half, 2 * count, share), jnp.float32),
        )
        + (jax.ShapeDtypeStruct((2 * count, share), jnp.float32),) * half,
        in_specs=[VMEM] * (1 + GROUPS + 5),
        out_specs=(VMEM,) * (2 + half),
        compiler_params=PARAMS,
        name="project_rows",
    )(gram, *weights, stay, core_in, near, far_in, cross_in)

    send = lambda value, mask: swap(value.astype(jnp.float16), mask, size).astype(jnp.float32)
    if zones <= 4:
        total = sum(send(value, GROUPS * (half + zone)) for zone, value in enumerate(away))
        side = send(side, 2)
        for zone in range(1, half):
            total = total + send(own[zone] + side[zone], GROUPS * zone)
        total = total + (own[0] + side[0])
    else:
        total = own + send(side, 2) + send(jnp.stack(away), GROUPS * half)
        while total.shape[0] > 1:
            low, high = jnp.split(total, 2)
            total = low + send(high, GROUPS * low.shape[0])
        total = total[0]
    level = gram[0, count] * bound
    return basis, (total * (level / TOP)).reshape(2, count, share)


def solution(mesh):
    return jax.shard_map(
        per_device,
        mesh=mesh,
        in_specs=(P(None, ("grp", "rcv"), None), P(None, None, "rcv")),
        out_specs=(P(None, ("grp", "rcv"), None), P(None, "grp", "rcv")),
        check_vma=False,
    )
```

time: 92.6 us -> 72 us (0.78)
  waiting for transfers between devices: 45.2 us -> 27.4 us
  Pallas kernels: 12.8 us -> 10.7 us
    ppermute x29, waiting for transfers between devices: 45.2 us -> 27.4 us  [swap(): return lax.ppermute(value, 'rcv', [(i, i ^ mask) for i in range(size)])]
    pallas_call x3 -> x4, Pallas kernels: 12.8 us -> 10.7 us  [the longest x1 6.38 us: per_device(): pl.pallas_call(functools.partial(basis_kernel, math.sqrt(rows * size)), o...]
  transfers between devices with their start and end apart: 29 -> 29, of which waited for: 14 -> 13; matrix products, arithmetic and copies ran while one was open for 1% -> 1% of each run, Pallas kernels for 4% -> 14%
where the time goes in v4:
time: 72 us; the launch traced here: 71.8 us
  starting transfers between devices  29.2 us (41%)
  waiting for transfers between devices  27.4 us (38%)
  Pallas kernels  10.7 us (15%)
  local copies, waits for them, and re-layouts  2.16 us (3%)
  between operations  1.41 us (2%)
  other arithmetic  0.98 us (1%)
    ppermute x29, starting transfers between devices, swap(): return lax.ppermute(value, 'rcv', [(i, i ^ mask) for i in range(size)])  29.2 us
    ppermute x29, waiting for transfers between devices, swap(): return lax.ppermute(value, 'rcv', [(i, i ^ mask) for i in range(size)])  27.4 us
    pallas_call x1, Pallas kernels, per_device(): pl.pallas_call(functools.partial(basis_kernel, math.sqrt(rows * size)), o...  6.38 us
    pallas_call x1, Pallas kernels, per_device(): pl.pallas_call(functools.partial(sketch_kernel, held), out_shape=(jax.Sha...  1.78 us
    unnamed x4, local copies, waits for them, and re-layouts  1.58 us
    pallas_call x1, Pallas kernels, per_device(): pl.pallas_call(functools.partial(chunk_kernel, share), out_shape=(chunk(z...  1.53 us
  transfers between devices with their start and end apart: 29, of which 13 were waited for; matrix products, arithmetic and copies ran while one was open for 1% of the time, Pallas kernels for 14%

profile of v4, /device:TPU:0, one launch (start us, length us, event | category | flops | bytes accessed | tf_op | source)
XLA Modules:
  0.0 71.8 jit_solution(13874042393586892038)
XLA Ops:
  0.6 4.1 %collective-permute-start.2 = (bf16[1,192,336]{2,1,0:T(8,128)(2,1)}, bf16[1,192,336]{2,1,0:T(8,128)(2,1)S(1)}, u32[]{:S(2)}, u32[]{:S(2)}) collective-permute-start(bf16[1,192,336]{2,1,0:T(8,128)(2,1)} %bitcast.12), channel_id=1, source_target_pairs={{0,8},{1,9},{2,10},{3,11},{4,12},{5,13},{6,14},{7,15},{8,0},{9,1},... | collective-permute-start | bytes 387080 | tf_op jit(solution)/shard_map/ppermute | solution.py:20
  4.7 1.6 %collective-permute-start.1 = (bf16[1,192,336]{2,1,0:T(8,128)(2,1)}, bf16[1,192,336]{2,1,0:T(8,128)(2,1)S(1)}, u32[]{:S(2)}, u32[]{:S(2)}) collective-permute-start(bf16[1,192,336]{2,1,0:T(8,128)(2,1)} %bitcast.13), channel_id=1, source_target_pairs={{0,4},{1,5},{2,6},{3,7},{4,0},{5,1},{6,2},{7,3},{8,12},{9,13},{10,... | collective-permute-start | bytes 387080 | tf_op jit(solution)/shard_map/ppermute | solution.py:20
  6.3 1.5 %collective-permute-start = (bf16[1,192,336]{2,1,0:T(8,128)(2,1)}, bf16[1,192,336]{2,1,0:T(8,128)(2,1)S(1)}, u32[]{:S(2)}, u32[]{:S(2)}) collective-permute-start(bf16[1,192,336]{2,1,0:T(8,128)(2,1)} %bitcast.14), channel_id=1, source_target_pairs={{0,2},{1,3},{2,0},{3,1},{4,6},{5,7},{6,4},{7,5},{8,10},{9,11},{10,... | collective-permute-start | bytes 387080 | tf_op jit(solution)/shard_map/ppermute | solution.py:20
  7.8 1.6 %copy-done = bf16[2,96,5376]{2,1,0:T(8,128)(2,1)S(1)} copy-done((bf16[2,96,5376]{2,1,0:T(8,128)(2,1)S(1)}, bf16[2,96,5376]{2,1,0:T(8,128)(2,1)}, u32[]{:S(2)}) %copy-start) | copy-done | bytes 2064408
  9.4 1.5 %source_chunks.1 = (bf16[4,192,336]{2,1,0:T(8,128)(2,1)S(1)}, bf16[6,192,336]{2,1,0:T(8,128)(2,1)S(1)}, bf16[2,192,336]{2,1,0:T(8,128)(2,1)S(1)}, bf16[2,192,336...) custom-call(s32[1]{0:T(128)} %bitcast.me_ref, bf16[2,96,5376]{2,1,0:T(8,128)(2,1)S(1)} %copy-done), custom_call_target="tpu_custom_call" | custom-call | tf_op jit(solution)/shard_map/source_chunks/pallas_call | solution.py:212
  12.8 1.5 %collective-permute-start.5 = (bf16[1,192,336]{2,1,0:T(8,128)(2,1)S(1)}, bf16[1,192,336]{2,1,0:T(8,128)(2,1)S(1)}, u32[]{:S(2)}, u32[]{:S(2)}) collective-permute-start(bf16[1,192,336]{2,1,0:T(8,128)(2,1)S(1)} %collective-permute-done.2.refs_3_), channel_id=1, source_target_pairs={{0,4},{1,5},{2,6},{3,7},{4,0},{5,1},{6,2},{7,3},{8,12},{9,13},{10,... | collective-permute-start | bytes 387080 | tf_op jit(solution)/shard_map/ppermute | solution.py:20
  14.8 1.6 %collective-permute-start.4 = (bf16[1,192,336]{2,1,0:T(8,128)(2,1)S(1)}, bf16[1,192,336]{2,1,0:T(8,128)(2,1)S(1)}, u32[]{:S(2)}, u32[]{:S(2)}) collective-permute-start(bf16[1,192,336]{2,1,0:T(8,128)(2,1)S(1)} %collective-permute-done.2.refs_3_), channel_id=1, source_target_pairs={{0,2},{1,3},{2,0},{3,1},{4,6},{5,7},{6,4},{7,5},{8,10},{9,11},{10,... | collective-permute-start | bytes 387080 | tf_op jit(solution)/shard_map/ppermute | solution.py:20
  16.4 3.1 %collective-permute-done.5.refs_6_ = bf16[1,192,336]{2,1,0:T(8,128)(2,1)S(1)} collective-permute-done((bf16[1,192,336]{2,1,0:T(8,128)(2,1)S(1)}, bf16[1,192,336]{2,1,0:T(8,128)(2,1)S(1)}, u32[]{:S(2)}, u32[]{:S(2)}) %collective-permute-start.5) | collective-permute-done | bytes 129056 | tf_op jit(solution)/shard_map/ppermute | solution.py:20
  19.5 1.5 %collective-permute-start.6 = (bf16[1,192,336]{2,1,0:T(8,128)(2,1)S(1)}, bf16[1,192,336]{2,1,0:T(8,128)(2,1)S(1)}, u32[]{:S(2)}, u32[]{:S(2)}) collective-permute-start(bf16[1,192,336]{2,1,0:T(8,128)(2,1)S(1)} %collective-permute-done.5.refs_6_), channel_id=1, source_target_pairs={{0,2},{1,3},{2,0},{3,1},{4,6},{5,7},{6,4},{7,5},{8,10},{9,11},{10,... | collective-permute-start | bytes 387080 | tf_op jit(solution)/shard_map/ppermute | solution.py:20
  21.0 0.7 collective-permute-done.3.refs_4_
  22.3 2.4 %collective-permute-done.6.refs_7_ = bf16[1,192,336]{2,1,0:T(8,128)(2,1)S(1)} collective-permute-done((bf16[1,192,336]{2,1,0:T(8,128)(2,1)S(1)}, bf16[1,192,336]{2,1,0:T(8,128)(2,1)S(1)}, u32[]{:S(2)}, u32[]{:S(2)}) %collective-permute-start.6) | collective-permute-done | bytes 129056 | tf_op jit(solution)/shard_map/ppermute | solution.py:20
  24.6 1.3 %collective-permute-done.14.refs_15_ = bf16[1,192,336]{2,1,0:T(8,128)(2,1)S(1)} collective-permute-done((bf16[1,192,336]{2,1,0:T(8,128)(2,1)S(1)}, bf16[1,192,336]{2,1,0:T(8,128)(2,1)S(1)}, u32[]{:S(2)}, u32[]{:S(2)}) %collective-permute-start.14) | collective-permute-done | bytes 129056 | tf_op jit(solution)/shard_map/ppermute | solution.py:20
  26.0 1.8 %sketch_rows.1 = (f32[2,96,96]{2,1,0:T(8,128)S(1)}, f32[96,97]{1,0:T(8,128)S(1)}) custom-call(bf16[4,192,336]{2,1,0:T(8,128)(2,1)S(1)} %get-tuple-element.22.stay_ref.refs_4_, bf16[6,192,336]{2,1,0:T(8,128)(2,1)S(1)} %get-tuple-element.23.core_ref, bf16[2,192,336]{2,1,0:T(8,128)(2,1)S(1)} %get-tuple-element.24.near_ref.refs_6_, ...), custom_call_target="tpu_custom_call" | custom-call | tf_op jit(solution)/shard_map/sketch_rows/pallas_call | solution.py:231
  28.0 1.5 %collective-permute-start.21 = (f32[2,96,96]{2,1,0:T(8,128)S(1)}, f32[2,96,96]{2,1,0:T(8,128)S(1)}, u32[]{:S(2)}, u32[]{:S(2)}) collective-permute-start(f32[2,96,96]{2,1,0:T(8,128)S(1)} %get-tuple-element.30.refs_0_), channel_id=1, source_target_pairs={{0,3},{1,2},{2,1},{3,0},{4,7},{5,6},{6,5},{7,4},{8,11},{9,10},{10,... | collective-permute-start | bytes 221192 | tf_op jit(solution)/shard_map/ppermute | solution.py:20
  30.0 1.6 %collective-permute-start.16 = (f32[96,97]{1,0:T(8,128)S(1)}, f32[96,97]{1,0:T(8,128)S(1)}, u32[]{:S(2)}, u32[]{:S(2)}) collective-permute-start(f32[96,97]{1,0:T(8,128)S(1)} %add.31), channel_id=1, source_target_pairs={{0,2},{1,3},{2,0},{3,1},{4,6},{5,7},{6,4},{7,5},{8,10},{9,11},{10,... | collective-permute-start | bytes 111752 | tf_op jit(solution)/shard_map/ppermute | solution.py:20
  31.6 1.0 %collective-permute-done.21.refs_3_ = f32[2,96,96]{2,1,0:T(8,128)S(1)} collective-permute-done((f32[2,96,96]{2,1,0:T(8,128)S(1)}, f32[2,96,96]{2,1,0:T(8,128)S(1)}, u32[]{:S(2)}, u32[]{:S(2)}) %collective-permute-start.21) | collective-permute-done | bytes 73760 | tf_op jit(solution)/shard_map/ppermute | solution.py:20
  32.6 3.0 %collective-permute-done.20.refs_2_ = f32[2,96,96]{2,1,0:T(8,128)S(1)} collective-permute-done((f32[2,96,96]{2,1,0:T(8,128)S(1)}, f32[2,96,96]{2,1,0:T(8,128)S(1)}, u32[]{:S(2)}, u32[]{:S(2)}) %collective-permute-start.20) | collective-permute-done | bytes 73760 | tf_op jit(solution)/shard_map/ppermute | solution.py:20
  35.7 0.6 collective-permute-done.16
  36.3 1.5 %collective-permute-start.23 = (bf16[2,192,336]{2,1,0:T(8,128)(2,1)S(1)}, bf16[2,192,336]{2,1,0:T(8,128)(2,1)S(1)}, u32[]{:S(2)}, u32[]{:S(2)}) collective-permute-start(bf16[2,192,336]{2,1,0:T(8,128)(2,1)S(1)} %get-tuple-element.36.far_ref), channel_id=1, source_target_pairs={{0,2},{1,3},{2,0},{3,1},{4,6},{5,7},{6,4},{7,5},{8,10},{9,11},{10,... | collective-permute-start | bytes 774152 | tf_op jit(solution)/shard_map/ppermute | solution.py:20
  37.8 1.5 %collective-permute-start.17 = (f32[96,97]{1,0:T(8,128)S(1)}, f32[96,97]{1,0:T(8,128)S(1)}, u32[]{:S(2)}, u32[]{:S(2)}) collective-permute-start(f32[96,97]{1,0:T(8,128)S(1)} %add.32), channel_id=1, source_target_pairs={{0,4},{1,5},{2,6},{3,7},{4,0},{5,1},{6,2},{7,3},{8,12},{9,13},{10,... | collective-permute-start | bytes 111752 | tf_op jit(solution)/shard_map/ppermute | solution.py:20
  39.3 2.7 %collective-permute-done.17 = f32[96,97]{1,0:T(8,128)S(1)} collective-permute-done((f32[96,97]{1,0:T(8,128)S(1)}, f32[96,97]{1,0:T(8,128)S(1)}, u32[]{:S(2)}, u32[]{:S(2)}) %collective-permute-start.17) | collective-permute-done | bytes 37280 | tf_op jit(solution)/shard_map/ppermute | solution.py:20
  42.1 2.1 %collective-permute-start.18 = (f32[96,97]{1,0:T(8,128)S(1)}, f32[96,97]{1,0:T(8,128)S(1)}, u32[]{:S(2)}, u32[]{:S(2)}) collective-permute-start(f32[96,97]{1,0:T(8,128)S(1)} %add.33), channel_id=1, source_target_pairs={{0,8},{1,9},{2,10},{3,11},{4,12},{5,13},{6,14},{7,15},{8,0},{9,1},... | collective-permute-start | bytes 111752 | tf_op jit(solution)/shard_map/ppermute | solution.py:20
  44.2 3.2 %collective-permute-done.18 = f32[96,97]{1,0:T(8,128)S(1)} collective-permute-done((f32[96,97]{1,0:T(8,128)S(1)}, f32[96,97]{1,0:T(8,128)S(1)}, u32[]{:S(2)}, u32[]{:S(2)}) %collective-permute-start.18) | collective-permute-done | bytes 37280 | tf_op jit(solution)/shard_map/ppermute | solution.py:20
  47.4 6.4 %orthonormal_basis.1 = (f32[2,96,96]{2,1,0:T(8,128)}, bf16[192,192]{1,0:T(8,128)(2,1)S(1)}, bf16[192,192]{1,0:T(8,128)(2,1)S(1)}, bf16[192,192]{1,0:T(8,128)(2,1)S(1)}, bf16[192,192]{1,0:T(8,128)(2,1)S(1)}) custom-call(f32[96,97]{1,0:T(8,128)S(1)} %add.34.gram_ref, f32[2,96,96]{2,1,0:T(8,128)S(1)} %get-tuple-element.30.refs_0_, ...), custom_call_target="tpu_custom_call" | custom-call | tf_op jit(solution)/shard_map/orthonormal_basis/pallas_call | solution.py:253
  53.8 1.0 %project_rows.1 = (f32[2,192,336]{2,1,0:T(8,128)S(1)}, f32[2,192,336]{2,1,0:T(8,128)S(1)}, f32[192,336]{1,0:T(8,128)S(1)}, f32[192,336]{1,0:T(8,128)S(1)}) custom-call(f32[96,97]{1,0:T(8,128)S(1)} %add.34.gram_ref, bf16[192,192]{1,0:T(8,128)(2,1)S(1)} %get-tuple-element.32.refs_0_, bf16[192,192]{1,0:T(8,128)(2,1)S(1)} %get-tuple-element.33.refs_1_, ...), custom_call_target="tpu_custom_call" | custom-call | tf_op jit(solution)/shard_map/project_rows/pallas_call | solution.py:263
  54.9 2.0 %collective-permute-start.27 = (f16[2,192,336]{2,1,0:T(8,128)(2,1)S(1)}, f16[2,192,336]{2,1,0:T(8,128)(2,1)S(1)}, u32[]{:S(2)}, u32[]{:S(2)}) collective-permute-start(f16[2,192,336]{2,1,0:T(8,128)(2,1)S(1)} %convert_element_type.31), channel_id=1, source_target_pairs={{0,2},{1,3},{2,0},{3,1},{4,6},{5,7},{6,4},{7,5},{8,10},{9,11},{10,... | collective-permute-start | bytes 774152 | tf_op jit(solution)/shard_map/ppermute | solution.py:20
  56.9 2.5 %collective-permute-start.26 = (f16[192,336]{1,0:T(8,128)(2,1)S(1)}, f16[192,336]{1,0:T(8,128)(2,1)S(1)}, u32[]{:S(2)}, u32[]{:S(2)}) collective-permute-start(f16[192,336]{1,0:T(8,128)(2,1)S(1)} %convert_element_type.29), channel_id=1, source_target_pairs={{0,12},{1,13},{2,14},{3,15},{4,8},{5,9},{6,10},{7,11},{8,4},{9,5},... | collective-permute-start | bytes 387080 | tf_op jit(solution)/shard_map/ppermute | solution.py:20
  59.5 2.7 %collective-permute-done.27 = f16[2,192,336]{2,1,0:T(8,128)(2,1)S(1)} collective-permute-done((f16[2,192,336]{2,1,0:T(8,128)(2,1)S(1)}, f16[2,192,336]{2,1,0:T(8,128)(2,1)S(1)}, u32[]{:S(2)}, u32[]{:S(2)}) %collective-permute-start.27) | collective-permute-done | bytes 258080 | tf_op jit(solution)/shard_map/ppermute | solution.py:20
  62.3 1.6 %collective-permute-start.28 = (f16[192,336]{1,0:T(8,128)(2,1)S(1)}, f16[192,336]{1,0:T(8,128)(2,1)S(1)}, u32[]{:S(2)}, u32[]{:S(2)}) collective-permute-start(f16[192,336]{1,0:T(8,128)(2,1)S(1)} %fusion.4), channel_id=1, source_target_pairs={{0,4},{1,5},{2,6},{3,7},{4,0},{5,1},{6,2},{7,3},{8,12},{9,13},{10,... | collective-permute-start | bytes 387080 | tf_op jit(solution)/shard_map/ppermute | solution.py:20
  63.9 0.6 slice.22
  65.1 5.9 %collective-permute-done.25 = f16[192,336]{1,0:T(8,128)(2,1)S(1)} collective-permute-done((f16[192,336]{1,0:T(8,128)(2,1)S(1)}, f16[192,336]{1,0:T(8,128)(2,1)S(1)}, u32[]{:S(2)}, u32[]{:S(2)}) %collective-permute-start.25) | collective-permute-done | bytes 129056 | tf_op jit(solution)/shard_map/ppermute | solution.py:20
  71.0 0.8 %fusion.2 = f32[192,336]{1,0:T(8,128)} fusion(f32[2,192,336]{2,1,0:T(8,128)S(1)} %convert_element_type.32, f32[2,192,336]{2,1,0:T(8,128)S(1)} %get-tuple-element.40, f16[192,336]{1,0:T(8,128)(2,1)S(1)} %collective-permute-done.28, f16[192,336]{1,0:T(8,128)(2,1)S(1)} %collective-permute-done.26, f16[192,336]{1,0:T(8,128)(2,1)S(1)} %collective-permute-done.25, ...), kind=kLoop, calls=%fused_computation.3 | loop fusion | flops 516096 | bytes 1161220 | tf_op jit(solution)/shard_map/mul | solution.py:290
  (45 shorter events, 3.9 us)
Async XLA Ops:
  0.6 11.4 %collective-permute-start.2 = (bf16[1,192,336]{2,1,0:T(8,128)(2,1)}, bf16[1,192,336]{2,1,0:T(8,128)(2,1)S(1)}, u32[]{:S(2)}, u32[]{:S(2)}) collective-permute-start(bf16[1,192,336]{2,1,0:T(8,128)(2,1)} %bitcast.12), channel_id=1, source_target_pairs={{0,8},{1,9},{2,10},{3,11},{4,12},{5,13},{6,14},{7,15},{8,0},{9,1},... | collective-permute-start | bytes 387080 | tf_op jit(solution)/shard_map/ppermute | solution.py:20
  4.7 7.5 %collective-permute-start.1 = (bf16[1,192,336]{2,1,0:T(8,128)(2,1)}, bf16[1,192,336]{2,1,0:T(8,128)(2,1)S(1)}, u32[]{:S(2)}, u32[]{:S(2)}) collective-permute-start(bf16[1,192,336]{2,1,0:T(8,128)(2,1)} %bitcast.13), channel_id=1, source_target_pairs={{0,4},{1,5},{2,6},{3,7},{4,0},{5,1},{6,2},{7,3},{8,12},{9,13},{10,... | collective-permute-start | bytes 387080 | tf_op jit(solution)/shard_map/ppermute | solution.py:20
  6.3 5.9 %collective-permute-start = (bf16[1,192,336]{2,1,0:T(8,128)(2,1)}, bf16[1,192,336]{2,1,0:T(8,128)(2,1)S(1)}, u32[]{:S(2)}, u32[]{:S(2)}) collective-permute-start(bf16[1,192,336]{2,1,0:T(8,128)(2,1)} %bitcast.14), channel_id=1, source_target_pairs={{0,2},{1,3},{2,0},{3,1},{4,6},{5,7},{6,4},{7,5},{8,10},{9,11},{10,... | collective-permute-start | bytes 387080 | tf_op jit(solution)/shard_map/ppermute | solution.py:20
  7.8 1.6 %copy-start = (bf16[2,96,5376]{2,1,0:T(8,128)(2,1)S(1)}, bf16[2,96,5376]{2,1,0:T(8,128)(2,1)}, u32[]{:S(2)}) copy-start(bf16[2,96,5376]{2,1,0:T(8,128)(2,1)} %traces_ref.1) | copy-start | bytes 6193156
  9.4 1.6 %copy-start.1 = (bf16[2,96,336]{2,1,0:T(8,128)(2,1)S(1)}, bf16[2,96,336]{2,1,0:T(8,128)(2,1)}, u32[]{:S(2)}) copy-start(bf16[2,96,336]{2,1,0:T(8,128)(2,1)} %param.3) | copy-start | bytes 387076
  10.9 42.9 %collective-permute-start.22 = (bf16[6,192,336]{2,1,0:T(8,128)(2,1)S(1)}, bf16[6,192,336]{2,1,0:T(8,128)(2,1)S(1)}, u32[]{:S(2)}, u32[]{:S(2)}) collective-permute-start(bf16[6,192,336]{2,1,0:T(8,128)(2,1)S(1)} %get-tuple-element.23.core_ref), channel_id=1, source_target_pairs={{0,1},{1,0},{2,3},{3,2},{4,5},{5,4},{6,7},{7,6},{8,9},{9,8},{10,11... | collective-permute-start | bytes 2322440 | tf_op jit(solution)/shard_map/ppermute | solution.py:20
  11.0 3.2 %collective-permute-start.7 = (bf16[1,192,336]{2,1,0:T(8,128)(2,1)S(1)}, bf16[1,192,336]{2,1,0:T(8,128)(2,1)S(1)}, u32[]{:S(2)}, u32[]{:S(2)}) collective-permute-start(bf16[1,192,336]{2,1,0:T(8,128)(2,1)S(1)} %bitcast.15), channel_id=1, source_target_pairs={{0,1},{1,0},{2,3},{3,2},{4,5},{5,4},{6,7},{7,6},{8,9},{9,8},{10,11... | collective-permute-start | bytes 387080 | tf_op jit(solution)/shard_map/ppermute | solution.py:20
  12.2 2.5 %collective-permute-start.9 = (bf16[1,192,336]{2,1,0:T(8,128)(2,1)S(1)}, bf16[1,192,336]{2,1,0:T(8,128)(2,1)S(1)}, u32[]{:S(2)}, u32[]{:S(2)}) collective-permute-start(bf16[1,192,336]{2,1,0:T(8,128)(2,1)S(1)} %collective-permute-done.1.refs_2_), channel_id=1, source_target_pairs={{0,1},{1,0},{2,3},{3,2},{4,5},{5,4},{6,7},{7,6},{8,9},{9,8},{10,11... | collective-permute-start | bytes 387080 | tf_op jit(solution)/shard_map/ppermute | solution.py:20
  12.3 2.5 %collective-permute-start.8 = (bf16[1,192,336]{2,1,0:T(8,128)(2,1)S(1)}, bf16[1,192,336]{2,1,0:T(8,128)(2,1)S(1)}, u32[]{:S(2)}, u32[]{:S(2)}) collective-permute-start(bf16[1,192,336]{2,1,0:T(8,128)(2,1)S(1)} %collective-permute-done.refs_1_), channel_id=1, source_target_pairs={{0,1},{1,0},{2,3},{3,2},{4,5},{5,4},{6,7},{7,6},{8,9},{9,8},{10,11... | collective-permute-start | bytes 387080 | tf_op jit(solution)/shard_map/ppermute | solution.py:20
  12.8 6.7 %collective-permute-start.5 = (bf16[1,192,336]{2,1,0:T(8,128)(2,1)S(1)}, bf16[1,192,336]{2,1,0:T(8,128)(2,1)S(1)}, u32[]{:S(2)}, u32[]{:S(2)}) collective-permute-start(bf16[1,192,336]{2,1,0:T(8,128)(2,1)S(1)} %collective-permute-done.2.refs_3_), channel_id=1, source_target_pairs={{0,4},{1,5},{2,6},{3,7},{4,0},{5,1},{6,2},{7,3},{8,12},{9,13},{10,... | collective-permute-start | bytes 387080 | tf_op jit(solution)/shard_map/ppermute | solution.py:20
  14.3 7.4 %collective-permute-start.3 = (bf16[1,192,336]{2,1,0:T(8,128)(2,1)S(1)}, bf16[1,192,336]{2,1,0:T(8,128)(2,1)S(1)}, u32[]{:S(2)}, u32[]{:S(2)}) collective-permute-start(bf16[1,192,336]{2,1,0:T(8,128)(2,1)S(1)} %collective-permute-done.refs_1_), channel_id=1, source_target_pairs={{0,4},{1,5},{2,6},{3,7},{4,0},{5,1},{6,2},{7,3},{8,12},{9,13},{10,... | collective-permute-start | bytes 387080 | tf_op jit(solution)/shard_map/ppermute | solution.py:20
  14.8 6.9 %collective-permute-start.10 = (bf16[1,192,336]{2,1,0:T(8,128)(2,1)S(1)}, bf16[1,192,336]{2,1,0:T(8,128)(2,1)S(1)}, u32[]{:S(2)}, u32[]{:S(2)}) collective-permute-start(bf16[1,192,336]{2,1,0:T(8,128)(2,1)S(1)} %collective-permute-done.2.refs_3_), channel_id=1, source_target_pairs={{0,1},{1,0},{2,3},{3,2},{4,5},{5,4},{6,7},{7,6},{8,9},{9,8},{10,11... | collective-permute-start | bytes 387080 | tf_op jit(solution)/shard_map/ppermute | solution.py:20
  14.8 7.4 %collective-permute-start.4 = (bf16[1,192,336]{2,1,0:T(8,128)(2,1)S(1)}, bf16[1,192,336]{2,1,0:T(8,128)(2,1)S(1)}, u32[]{:S(2)}, u32[]{:S(2)}) collective-permute-start(bf16[1,192,336]{2,1,0:T(8,128)(2,1)S(1)} %collective-permute-done.2.refs_3_), channel_id=1, source_target_pairs={{0,2},{1,3},{2,0},{3,1},{4,6},{5,7},{6,4},{7,5},{8,10},{9,11},{10,... | collective-permute-start | bytes 387080 | tf_op jit(solution)/shard_map/ppermute | solution.py:20
  19.5 5.1 %collective-permute-start.6 = (bf16[1,192,336]{2,1,0:T(8,128)(2,1)S(1)}, bf16[1,192,336]{2,1,0:T(8,128)(2,1)S(1)}, u32[]{:S(2)}, u32[]{:S(2)}) collective-permute-start(bf16[1,192,336]{2,1,0:T(8,128)(2,1)S(1)} %collective-permute-done.5.refs_6_), channel_id=1, source_target_pairs={{0,2},{1,3},{2,0},{3,1},{4,6},{5,7},{6,4},{7,5},{8,10},{9,11},{10,... | collective-permute-start | bytes 387080 | tf_op jit(solution)/shard_map/ppermute | solution.py:20
  21.7 3.0 %collective-permute-start.13 = (bf16[1,192,336]{2,1,0:T(8,128)(2,1)S(1)}, bf16[1,192,336]{2,1,0:T(8,128)(2,1)S(1)}, u32[]{:S(2)}, u32[]{:S(2)}) collective-permute-start(bf16[1,192,336]{2,1,0:T(8,128)(2,1)S(1)} %collective-permute-done.5.refs_6_), channel_id=1, source_target_pairs={{0,1},{1,0},{2,3},{3,2},{4,5},{5,4},{6,7},{7,6},{8,9},{9,8},{10,11... | collective-permute-start | bytes 387080 | tf_op jit(solution)/shard_map/ppermute | solution.py:20
  21.7 2.9 %collective-permute-start.11 = (bf16[1,192,336]{2,1,0:T(8,128)(2,1)S(1)}, bf16[1,192,336]{2,1,0:T(8,128)(2,1)S(1)}, u32[]{:S(2)}, u32[]{:S(2)}) collective-permute-start(bf16[1,192,336]{2,1,0:T(8,128)(2,1)S(1)} %collective-permute-done.3.refs_4_), channel_id=1, source_target_pairs={{0,1},{1,0},{2,3},{3,2},{4,5},{5,4},{6,7},{7,6},{8,9},{9,8},{10,11... | collective-permute-start | bytes 387080 | tf_op jit(solution)/shard_map/ppermute | solution.py:20
  22.2 2.4 %collective-permute-start.12 = (bf16[1,192,336]{2,1,0:T(8,128)(2,1)S(1)}, bf16[1,192,336]{2,1,0:T(8,128)(2,1)S(1)}, u32[]{:S(2)}, u32[]{:S(2)}) collective-permute-start(bf16[1,192,336]{2,1,0:T(8,128)(2,1)S(1)} %collective-permute-done.4.refs_5_), channel_id=1, source_target_pairs={{0,1},{1,0},{2,3},{3,2},{4,5},{5,4},{6,7},{7,6},{8,9},{9,8},{10,11... | collective-permute-start | bytes 387080 | tf_op jit(solution)/shard_map/ppermute | solution.py:20
  24.6 1.4 %collective-permute-start.14 = (bf16[1,192,336]{2,1,0:T(8,128)(2,1)S(1)}, bf16[1,192,336]{2,1,0:T(8,128)(2,1)S(1)}, u32[]{:S(2)}, u32[]{:S(2)}) collective-permute-start(bf16[1,192,336]{2,1,0:T(8,128)(2,1)S(1)} %collective-permute-done.6.refs_7_), channel_id=1, source_target_pairs={{0,1},{1,0},{2,3},{3,2},{4,5},{5,4},{6,7},{7,6},{8,9},{9,8},{10,11... | collective-permute-start | bytes 387080 | tf_op jit(solution)/shard_map/ppermute | solution.py:20
  27.8 2.2 %collective-permute-start.15 = (f32[96,97]{1,0:T(8,128)S(1)}, f32[96,97]{1,0:T(8,128)S(1)}, u32[]{:S(2)}, u32[]{:S(2)}) collective-permute-start(f32[96,97]{1,0:T(8,128)S(1)} %get-tuple-element.29), channel_id=1, source_target_pairs={{0,1},{1,0},{2,3},{3,2},{4,5},{5,4},{6,7},{7,6},{8,9},{9,8},{10,11... | collective-permute-start | bytes 111752 | tf_op jit(solution)/shard_map/ppermute | solution.py:20
  28.0 4.6 %collective-permute-start.21 = (f32[2,96,96]{2,1,0:T(8,128)S(1)}, f32[2,96,96]{2,1,0:T(8,128)S(1)}, u32[]{:S(2)}, u32[]{:S(2)}) collective-permute-start(f32[2,96,96]{2,1,0:T(8,128)S(1)} %get-tuple-element.30.refs_0_), channel_id=1, source_target_pairs={{0,3},{1,2},{2,1},{3,0},{4,7},{5,6},{6,5},{7,4},{8,11},{9,10},{10,... | collective-permute-start | bytes 221192 | tf_op jit(solution)/shard_map/ppermute | solution.py:20
  29.5 6.2 %collective-permute-start.20 = (f32[2,96,96]{2,1,0:T(8,128)S(1)}, f32[2,96,96]{2,1,0:T(8,128)S(1)}, u32[]{:S(2)}, u32[]{:S(2)}) collective-permute-start(f32[2,96,96]{2,1,0:T(8,128)S(1)} %get-tuple-element.30.refs_0_), channel_id=1, source_target_pairs={{0,2},{1,3},{2,0},{3,1},{4,6},{5,7},{6,4},{7,5},{8,10},{9,11},{10,... | collective-permute-start | bytes 221192 | tf_op jit(solution)/shard_map/ppermute | solution.py:20
  30.0 5.7 %collective-permute-start.19 = (f32[2,96,96]{2,1,0:T(8,128)S(1)}, f32[2,96,96]{2,1,0:T(8,128)S(1)}, u32[]{:S(2)}, u32[]{:S(2)}) collective-permute-start(f32[2,96,96]{2,1,0:T(8,128)S(1)} %get-tuple-element.30.refs_0_), channel_id=1, source_target_pairs={{0,1},{1,0},{2,3},{3,2},{4,5},{5,4},{6,7},{7,6},{8,9},{9,8},{10,11... | collective-permute-start | bytes 221192 | tf_op jit(solution)/shard_map/ppermute | solution.py:20
  30.0 6.3 %collective-permute-start.16 = (f32[96,97]{1,0:T(8,128)S(1)}, f32[96,97]{1,0:T(8,128)S(1)}, u32[]{:S(2)}, u32[]{:S(2)}) collective-permute-start(f32[96,97]{1,0:T(8,128)S(1)} %add.31), channel_id=1, source_target_pairs={{0,2},{1,3},{2,0},{3,1},{4,6},{5,7},{6,4},{7,5},{8,10},{9,11},{10,... | collective-permute-start | bytes 111752 | tf_op jit(solution)/shard_map/ppermute | solution.py:20
  36.3 17.5 %collective-permute-start.23 = (bf16[2,192,336]{2,1,0:T(8,128)(2,1)S(1)}, bf16[2,192,336]{2,1,0:T(8,128)(2,1)S(1)}, u32[]{:S(2)}, u32[]{:S(2)}) collective-permute-start(bf16[2,192,336]{2,1,0:T(8,128)(2,1)S(1)} %get-tuple-element.36.far_ref), channel_id=1, source_target_pairs={{0,2},{1,3},{2,0},{3,1},{4,6},{5,7},{6,4},{7,5},{8,10},{9,11},{10,... | collective-permute-start | bytes 774152 | tf_op jit(solution)/shard_map/ppermute | solution.py:20
  37.8 16.0 %collective-permute-start.24 = (bf16[2,192,336]{2,1,0:T(8,128)(2,1)S(1)}, bf16[2,192,336]{2,1,0:T(8,128)(2,1)S(1)}, u32[]{:S(2)}, u32[]{:S(2)}) collective-permute-start(bf16[2,192,336]{2,1,0:T(8,128)(2,1)S(1)} %get-tuple-element.37.cross_ref), channel_id=1, source_target_pairs={{0,3},{1,2},{2,1},{3,0},{4,7},{5,6},{6,5},{7,4},{8,11},{9,10},{10,... | collective-permute-start | bytes 774152 | tf_op jit(solution)/shard_map/ppermute | solution.py:20
  37.8 4.2 %collective-permute-start.17 = (f32[96,97]{1,0:T(8,128)S(1)}, f32[96,97]{1,0:T(8,128)S(1)}, u32[]{:S(2)}, u32[]{:S(2)}) collective-permute-start(f32[96,97]{1,0:T(8,128)S(1)} %add.32), channel_id=1, source_target_pairs={{0,4},{1,5},{2,6},{3,7},{4,0},{5,1},{6,2},{7,3},{8,12},{9,13},{10,... | collective-permute-start | bytes 111752 | tf_op jit(solution)/shard_map/ppermute | solution.py:20
  42.1 5.3 %collective-permute-start.18 = (f32[96,97]{1,0:T(8,128)S(1)}, f32[96,97]{1,0:T(8,128)S(1)}, u32[]{:S(2)}, u32[]{:S(2)}) collective-permute-start(f32[96,97]{1,0:T(8,128)S(1)} %add.33), channel_id=1, source_target_pairs={{0,8},{1,9},{2,10},{3,11},{4,12},{5,13},{6,14},{7,15},{8,0},{9,1},... | collective-permute-start | bytes 111752 | tf_op jit(solution)/shard_map/ppermute | solution.py:20
  54.9 7.3 %collective-permute-start.27 = (f16[2,192,336]{2,1,0:T(8,128)(2,1)S(1)}, f16[2,192,336]{2,1,0:T(8,128)(2,1)S(1)}, u32[]{:S(2)}, u32[]{:S(2)}) collective-permute-start(f16[2,192,336]{2,1,0:T(8,128)(2,1)S(1)} %convert_element_type.31), channel_id=1, source_target_pairs={{0,2},{1,3},{2,0},{3,1},{4,6},{5,7},{6,4},{7,5},{8,10},{9,11},{10,... | collective-permute-start | bytes 774152 | tf_op jit(solution)/shard_map/ppermute | solution.py:20
  56.9 8.2 %collective-permute-start.26 = (f16[192,336]{1,0:T(8,128)(2,1)S(1)}, f16[192,336]{1,0:T(8,128)(2,1)S(1)}, u32[]{:S(2)}, u32[]{:S(2)}) collective-permute-start(f16[192,336]{1,0:T(8,128)(2,1)S(1)} %convert_element_type.29), channel_id=1, source_target_pairs={{0,12},{1,13},{2,14},{3,15},{4,8},{5,9},{6,10},{7,11},{8,4},{9,5},... | collective-permute-start | bytes 387080 | tf_op jit(solution)/shard_map/ppermute | solution.py:20
  59.5 11.6 %collective-permute-start.25 = (f16[192,336]{1,0:T(8,128)(2,1)S(1)}, f16[192,336]{1,0:T(8,128)(2,1)S(1)}, u32[]{:S(2)}, u32[]{:S(2)}) collective-permute-start(f16[192,336]{1,0:T(8,128)(2,1)S(1)} %convert_element_type.27), channel_id=1, source_target_pairs={{0,8},{1,9},{2,10},{3,11},{4,12},{5,13},{6,14},{7,15},{8,0},{9,1},... | collective-permute-start | bytes 387080 | tf_op jit(solution)/shard_map/ppermute | solution.py:20
  62.3 8.8 %collective-permute-start.28 = (f16[192,336]{1,0:T(8,128)(2,1)S(1)}, f16[192,336]{1,0:T(8,128)(2,1)S(1)}, u32[]{:S(2)}, u32[]{:S(2)}) collective-permute-start(f16[192,336]{1,0:T(8,128)(2,1)S(1)} %fusion.4), channel_id=1, source_target_pairs={{0,4},{1,5},{2,6},{3,7},{4,0},{5,1},{6,2},{7,3},{8,12},{9,13},{10,... | collective-permute-start | bytes 387080 | tf_op jit(solution)/shard_map/ppermute | solution.py:20

commit v5 on v4

--- a/solution.py
+++ b/solution.py
@@ -10,6 +10,7 @@
 
 ROWS = 8
 GROUPS = 4
+PARTS = 4
 TOP = 32768.0
 VMEM = pl.BlockSpec(memory_space=pltpu.VMEM)
 SMEM = pl.BlockSpec(memory_space=pltpu.SMEM)
@@ -30,7 +31,8 @@
     )
 
 
-def chunk_kernel(share, me_ref, traces_ref, stay_ref, core_ref, near_ref, far_ref, cross_ref, peak_ref, held_ref):
+def chunk_kernel(share, me_ref, traces_ref, stay_ref, near_ref, far_ref, cross_ref, peak_ref, *refs):
+    core, held_ref = refs[:-1], refs[-1]
     rows, sources = traces_ref.shape[1:]
     me = me_ref[0]
     for owner in range(sources // share):
@@ -39,11 +41,11 @@
             held_ref[away % GROUPS, away // GROUPS, rows * part : rows * (part + 1), :] = traces_ref[
                 part, :, owner * share : (owner + 1) * share
             ]
-    zones = stay_ref.shape[0]
-    half = zones // 2
+    zones, half = stay_ref.shape[0], near_ref.shape[0]
+    for at, ref in enumerate(core):
+        first = at % PARTS * ref.shape[0]
+        ref[...] = held_ref[1 + at // PARTS * 2, first : first + ref.shape[0]]
     stay_ref[...] = held_ref[0]
-    core_ref[:zones] = held_ref[1]
-    core_ref[zones:] = held_ref[3, :half]
     near_ref[...] = held_ref[2, :half]
     far_ref[...] = held_ref[2, half:]
     cross_ref[...] = held_ref[3, half:]
@@ -54,37 +56,55 @@
     peak_ref[...] = peak.astype(jnp.float32)
 
 
-def sketch_kernel(held, stay_ref, core_ref, near_ref, far_ref, cross_ref, peak_ref, *refs):
-    pieces, (out_ref, gram_ref) = refs[:-2], refs[-2:]
-    count = out_ref.shape[2]
-    zones = stay_ref.shape[0]
-    half = zones // 2
-    total = None
-    for slot in range(GROUPS * zones):
-        group, zone = slot % GROUPS, slot // GROUPS
-        if group < 2:
-            data = (stay_ref, core_ref)[group][zone]
-        elif zone < half:
-            data = near_ref[zone] if group == 2 else core_ref[zones + zone]
+def of_core(core, beside, zone):
+    each = core[0].shape[0]
+    return core[beside * PARTS + zone // each][zone % each]
+
+
+def sketch_kernel(held, peak_ref, stay_ref, near_ref, far_ref, *refs):
+    core, pieces, out_ref = refs[: 2 * PARTS], refs[2 * PARTS : -1], refs[-1]
+    count = out_ref.shape[-1] - 1
+    zones, half = stay_ref.shape[0], near_ref.shape[0]
+    totals = [None, None]
+    for slot in range(0, GROUPS * zones, 2):
+        beside, zone = slot % GROUPS // 2, slot // GROUPS
+        if beside:
+            own = near_ref[zone] if zone < half else far_ref[zone - half]
         else:
-            data = (far_ref, cross_ref)[group - 2][zone - half]
+            own = stay_ref[zone]
         which, at = held[slot]
-        term = lax.dot_general(
-            data, pieces[which][at], (((1,), (1,)), ((), ())), preferred_element_type=jnp.float32
-        )
-        total = term if total is None else total + term
-    rows = total.shape[0] // 2
-    real = total[:rows, :count] - total[rows:, count:]
-    imag = total[:rows, count:] + total[rows:, :count]
-    out_ref[0] = real
-    out_ref[1] = imag
-    gram_re = exact(real, real, ((0,), (0,))) + exact(imag, imag, ((0,), (0,)))
-    gram_im = exact(real, imag, ((0,), (0,))) - exact(imag, real, ((0,), (0,)))
+        for rows, data in enumerate((own, of_core(core, beside, zone))):
+            term = lax.dot_general(
+                data, pieces[which][at], (((1,), (1,)), ((), ())), preferred_element_type=jnp.float32
+            )
+            totals[rows] = term if totals[rows] is None else totals[rows] + term
+    for part, total in enumerate(totals):
+        rows = total.shape[0] // 2
+        out_ref[part, 0, :, :count] = total[:rows, :count] - total[rows:, count:]
+        out_ref[part, 1, :, :count] = total[:rows, count:] + total[rows:, :count]
+    peak = jnp.max(peak_ref[...], axis=1, keepdims=True)
+    out_ref[:, :, :, count:] = jnp.broadcast_to(peak[None, None], out_ref.shape[:3] + (1,))
+
+
+def gram_kernel(part_ref, other_ref, own_ref, core_ref):
+    count = part_ref.shape[-1] - 1
+    rows = part_ref.shape[2]
+    products = []
+    for which, out_ref in enumerate((own_ref, core_ref)):
+        real = (part_ref[which, 0] + other_ref[1 - which, 0])[:, :count]
+        imag = (part_ref[which, 1] + other_ref[1 - which, 1])[:, :count]
+        out_ref[count : count + rows, :count] = real
+        out_ref[count + rows :, :count] = imag
+        both = jnp.concatenate([real, imag], axis=1)
+        products.append(exact(both, both, ((0,), (0,))))
+    product = products[0] + products[1]
+    gram_re = product[:count, :count] + product[count:, count:]
+    gram_im = product[:count, count:] - product[count:, :count]
     row = lax.broadcasted_iota(jnp.int32, gram_re.shape, 0)
     column = lax.broadcasted_iota(jnp.int32, gram_re.shape, 1)
-    gram_ref[:, :count] = jnp.where(row <= column, gram_re, gram_im)
-    peak = jnp.max(peak_ref[...], axis=1, keepdims=True)
-    gram_ref[:, count:] = jnp.broadcast_to(peak, (count, gram_ref.shape[1] - count))
+    own_ref[:count, :count] = jnp.where(row <= column, gram_re, gram_im)
+    peak = part_ref[0, 0, :1, count:] + other_ref[0, 0, :1, count:]
+    own_ref[:, count:] = jnp.broadcast_to(peak, (own_ref.shape[0], 1))
 
 
 def eliminate(real, imag):
@@ -122,9 +142,10 @@
     return jnp.concatenate(re, axis=0), jnp.concatenate(im, axis=0)
 
 
-def basis_kernel(scale, gram_ref, *refs):
-    sketched, basis_ref, weights = refs[:GROUPS], refs[GROUPS], refs[GROUPS + 1 :]
+def basis_kernel(scale, *refs):
+    sketched, gram_ref, basis_ref, weights = refs[:GROUPS], refs[GROUPS], refs[GROUPS + 1], refs[GROUPS + 2 :]
     count = gram_ref.shape[0]
+    rows = basis_ref.shape[1]
     packed = gram_ref[:, :count]
     flipped = packed.T
     row = lax.broadcasted_iota(jnp.int32, packed.shape, 0)
@@ -134,10 +155,9 @@
     low_re, low_im = eliminate(gram_re, gram_im)
     low_re = jnp.where(row >= column, low_re, 0.0)
     low_im = jnp.where(row >= column, low_im, 0.0)
-    stacked = jnp.concatenate([ref[part] for ref in sketched for part in range(2)], axis=0)
+    stacked = jnp.concatenate([ref[count:, :count] for ref in sketched], axis=0)
     by_re = exact(stacked, low_re, ((1,), (1,)))
     by_im = exact(stacked, low_im, ((1,), (1,)))
-    rows = stacked.shape[0] // GROUPS // 2
     for group in range(GROUPS):
         real = slice(2 * rows * group, 2 * rows * group + rows)
         imag = slice(2 * rows * group + rows, 2 * rows * (group + 1))
@@ -153,12 +173,11 @@
 
 
 def project_kernel(bound, gram_ref, *refs):
-    weights, (stay_ref, core_ref, near_ref, far_ref, cross_ref) = refs[:GROUPS], refs[GROUPS : GROUPS + 5]
-    own_ref, side_ref, *far_outs = refs[GROUPS + 5 :]
+    weights, (stay_ref, near_ref, far_ref, cross_ref) = refs[:GROUPS], refs[GROUPS : GROUPS + 4]
+    core, (own_ref, side_ref, *far_outs) = refs[GROUPS + 4 : GROUPS + 4 + 2 * PARTS], refs[GROUPS + 4 + 2 * PARTS :]
     count = gram_ref.shape[0]
     factor = TOP / (gram_ref[:1, count : count + 1] * bound)
     half = near_ref.shape[0]
-    zones = 2 * half
 
     def project(*data):
         total = None
@@ -168,10 +187,12 @@
         return total * factor
 
     for zone in range(half):
-        far_outs[zone][...] = project(stay_ref[half + zone], core_ref[half + zone], far_ref[zone], cross_ref[zone])
+        far_outs[zone][...] = project(
+            stay_ref[half + zone], of_core(core, 0, half + zone), far_ref[zone], cross_ref[zone]
+        )
     for zone in range(half):
-        side_ref[zone] = project(near_ref[zone], core_ref[zones + zone])
-        own_ref[zone] = project(stay_ref[zone], core_ref[zone])
+        side_ref[zone] = project(near_ref[zone], of_core(core, 1, zone))
+        own_ref[zone] = project(stay_ref[zone], of_core(core, 0, zone))
 
 
 def tied(first, second):
@@ -187,7 +208,7 @@
     for level in range(1, direct):
         if level == 2:
             (have[1 << direct - 1],), _ = tied([have[1 << direct - 1]], [ahead])
-        for slot in reversed(range(0, 1 << direct, 2)):
+        for slot in range(0, 1 << direct, 2):
             if slot.bit_count() == level:
                 along = slot & -slot if slot >> direct - 1 else 1 << slot.bit_length() - 1
                 have[slot] = swap(have[slot ^ along], along, size)
@@ -196,7 +217,7 @@
         whole = jnp.concatenate([value for value, _ in pieces])
         slots = [slot for _, held in pieces for slot in held]
         pieces = [(whole, slots), (swap(whole, 1 << bit, size), [slot | 1 << bit for slot in slots])]
-    return pieces + [(swap(value, 1, size), [slot | 1 for slot in slots]) for value, slots in pieces]
+    return pieces
 
 
 def per_device(traces, sketch):
@@ -209,44 +230,49 @@
     bits = size.bit_length() - 1
     chunk = lambda slots: jax.ShapeDtypeStruct((slots, 2 * rows, share), traces.dtype)
 
-    stay, core, near, far, cross, peak = pl.pallas_call(
+    stay, near, far, cross, peak, *core = pl.pallas_call(
         functools.partial(chunk_kernel, share),
         out_shape=(
             chunk(zones),
-            chunk(zones + half),
             chunk(half),
             chunk(half),
             chunk(half),
             jax.ShapeDtypeStruct((1, sources), jnp.float32),
-        ),
+        )
+        + (chunk(zones // PARTS),) * (2 * PARTS),
         in_specs=[SMEM, VMEM],
-        out_specs=(VMEM,) * 6,
+        out_specs=(VMEM,) * (5 + 2 * PARTS),
         scratch_shapes=[pltpu.VMEM((GROUPS, zones, 2 * rows, share), traces.dtype)],
         compiler_params=PARAMS,
         name="source_chunks",
     )(me.astype(jnp.int32).reshape(1), traces)
+    core_in = [swap(value, 1, size) for value in core]
     pieces = gather_slots(sketch.reshape(1, 2 * count, share), size, stay)
     values = [value for value, _ in pieces]
     held = {slot: (which, at) for which, (_, slots) in enumerate(pieces) for at, slot in enumerate(slots)}
-    sketched, gram = pl.pallas_call(
+    partial = pl.pallas_call(
         functools.partial(sketch_kernel, held),
-        out_shape=(
-            jax.ShapeDtypeStruct((2, rows, count), jnp.float32),
-            jax.ShapeDtypeStruct((count, count + 1), jnp.float32),
-        ),
-        in_specs=[VMEM] * (6 + len(values)),
+        out_shape=jax.ShapeDtypeStruct((2, 2, rows, count + 1), jnp.float32),
+        in_specs=[VMEM] * (4 + 2 * PARTS + len(values)),
+        out_specs=VMEM,
+        compiler_params=PARAMS,
+        name="sketch_rows",
+    )(peak, stay, near, far, *core_in, *values)
+    packet = jax.ShapeDtypeStruct((count + 2 * rows, count + 1), jnp.float32)
+    own_packet, core_packet = pl.pallas_call(
+        gram_kernel,
+        out_shape=(packet, packet),
+        in_specs=[VMEM] * 2,
         out_specs=(VMEM, VMEM),
         compiler_params=PARAMS,
-        name="sketch_rows",
-    )(stay, core, near, far, cross, peak, *values)
-
-    core_in = swap(core, 1, size)
-    gram = gram + swap(gram, 1, size)
-    beside = swap(gram, 2, size)
-    known = [swap(sketched, group, size) for group in range(1, GROUPS)]
-    (far_out, cross_out), _ = tied([far, cross], [beside, *known])
+        name="chip_gram",
+    )(partial, swap(partial, 1, size))
+
+    beside = swap(own_packet, 2, size)
+    known = [own_packet, core_packet, beside, swap(beside, 1, size)]
+    (far_out, cross_out), _ = tied([far, cross], [own_packet])
     far_in, cross_in = swap(far_out, 2, size), swap(cross_out, 3, size)
-    gram = gram + beside
+    gram = own_packet[:count] + beside[:count]
     for bit in range(2, bits):
         gram = gram + swap(gram, 1 << bit, size)
 
@@ -257,8 +283,9 @@
         in_specs=[VMEM] * (1 + GROUPS),
         out_specs=(VMEM,) * (1 + GROUPS),
         compiler_params=PARAMS,
+        cost_estimate=pl.CostEstimate(flops=1_500_000_000, bytes_accessed=1_000_000, transcendentals=0),
         name="orthonormal_basis",
-    )(gram, sketched, *known)
+    )(*known, gram)
     bound = 1.01 * math.sqrt(2 * rows * size)
     own, side, *away = pl.pallas_call(
         functools.partial(project_kernel, bound),
@@ -267,19 +294,18 @@
             jax.ShapeDtypeStruct((half, 2 * count, share), jnp.float32),
         )
         + (jax.ShapeDtypeStruct((2 * count, share), jnp.float32),) * half,
-        in_specs=[VMEM] * (1 + GROUPS + 5),
+        in_specs=[VMEM] * (1 + GROUPS + 4 + 2 * PARTS),
         out_specs=(VMEM,) * (2 + half),
         compiler_params=PARAMS,
         name="project_rows",
-    )(gram, *weights, stay, core_in, near, far_in, cross_in)
+    )(gram, *weights, stay, near, far_in, cross_in, *core_in)
 
     send = lambda value, mask: swap(value.astype(jnp.float16), mask, size).astype(jnp.float32)
     if zones <= 4:
-        total = sum(send(value, GROUPS * (half + zone)) for zone, value in enumerate(away))
         side = send(side, 2)
-        for zone in range(1, half):
-            total = total + send(own[zone] + side[zone], GROUPS * zone)
-        total = total + (own[0] + side[0])
+        parts = [send(away[zone], GROUPS * (half + zone)) for zone in reversed(range(half))]
+        parts += [send(own[zone] + side[zone], GROUPS * zone) for zone in range(1, half)]
+        total = own[0] + side[0] + sum(parts)
     else:
         total = own + send(side, 2) + send(jnp.stack(away), GROUPS * half)
         while total.shape[0] > 1:

time: 72 us -> 69 us (0.958)
  starting transfers between devices: 29.2 us -> 22.7 us
  waiting for transfers between devices: 27.4 us -> 30.8 us
    ppermute x29 -> x26, starting transfers between devices: 29.2 us -> 22.7 us  [swap(): return lax.ppermute(value, 'rcv', [(i, i ^ mask) for i in range(size)])]
    ppermute x29 -> x26, waiting for transfers between devices: 27.4 us -> 30.8 us  [swap(): return lax.ppermute(value, 'rcv', [(i, i ^ mask) for i in range(size)])]
    pallas_call x1 -> x2, Pallas kernels: 1.78 us -> 1.92 us  [the longest x1 1.19 us: per_device(): pl.pallas_call(functools.partial(sketch_kernel, held), out_shape=jax.Shap...]
  transfers between devices with their start and end apart: 29 -> 26, of which waited for: 13 -> 12; matrix products, arithmetic and copies ran while one was open for 1% -> 1% of each run, Pallas kernels for 14% -> 12%
where the time goes in v5:
time: 69 us; the launch traced here: 68.9 us
  waiting for transfers between devices  30.8 us (45%)
  starting transfers between devices  22.7 us (33%)
  Pallas kernels  10.8 us (16%)
  local copies, waits for them, and re-layouts  2.16 us (3%)
  between operations  1.39 us (2%)
  other arithmetic  0.97 us (1%)
    ppermute x26, waiting for transfers between devices, swap(): return lax.ppermute(value, 'rcv', [(i, i ^ mask) for i in range(size)])  30.8 us
    ppermute x26, starting transfers between devices, swap(): return lax.ppermute(value, 'rcv', [(i, i ^ mask) for i in range(size)])  22.7 us
    pallas_call x1, Pallas kernels, per_device(): pl.pallas_call(functools.partial(basis_kernel, math.sqrt(rows * size)), o...  6.38 us
    unnamed x4, local copies, waits for them, and re-layouts  1.58 us
    pallas_call x1, Pallas kernels, per_device(): pl.pallas_call(functools.partial(chunk_kernel, share), out_shape=(chunk(z...  1.56 us
  transfers between devices with their start and end apart: 26, of which 12 were waited for; matrix products, arithmetic and copies ran while one was open for 1% of the time, Pallas kernels for 12%

profile of v5, /device:TPU:0, one launch (start us, length us, event | category | flops | bytes accessed | tf_op | source)
XLA Modules:
  0.0 68.9 jit_solution(5459422692293024396)
XLA Ops:
  0.6 4.1 %collective-permute-start.10 = (bf16[1,192,336]{2,1,0:T(8,128)(2,1)}, bf16[1,192,336]{2,1,0:T(8,128)(2,1)S(1)}, u32[]{:S(2)}, u32[]{:S(2)}) collective-permute-start(bf16[1,192,336]{2,1,0:T(8,128)(2,1)} %bitcast.12), channel_id=1, source_target_pairs={{0,8},{1,9},{2,10},{3,11},{4,12},{5,13},{6,14},{7,15},{8,0},{9,1},... | collective-permute-start | bytes 387080 | tf_op jit(solution)/shard_map/ppermute | solution.py:21
  4.7 1.6 %copy-done = bf16[2,96,5376]{2,1,0:T(8,128)(2,1)S(1)} copy-done((bf16[2,96,5376]{2,1,0:T(8,128)(2,1)S(1)}, bf16[2,96,5376]{2,1,0:T(8,128)(2,1)}, u32[]{:S(2)}) %copy-start) | copy-done | bytes 2064408
  6.3 1.6 %source_chunks.1 = (bf16[4,192,336]{2,1,0:T(8,128)(2,1)S(1)}, bf16[2,192,336]{2,1,0:T(8,128)(2,1)S(1)}, bf16[2,192,336]{2,1,0:T(8,128)(2,1)S(1)}, bf16[2,192,336...) custom-call(s32[1]{0:T(128)} %bitcast.me_ref, ...), custom_call_target="tpu_custom_call" | custom-call | tf_op jit(solution)/shard_map/source_chunks/pallas_call | solution.py:233
  9.0 3.0 %collective-permute-done.10.refs_11_ = bf16[1,192,336]{2,1,0:T(8,128)(2,1)S(1)} collective-permute-done((bf16[1,192,336]{2,1,0:T(8,128)(2,1)}, bf16[1,192,336]{2,1,0:T(8,128)(2,1)S(1)}, u32[]{:S(2)}, u32[]{:S(2)}) %collective-permute-start.10) | collective-permute-done | bytes 129056 | tf_op jit(solution)/shard_map/ppermute | solution.py:21
  12.5 1.5 %collective-permute-start.8 = (bf16[1,192,336]{2,1,0:T(8,128)(2,1)S(1)}, bf16[1,192,336]{2,1,0:T(8,128)(2,1)S(1)}, u32[]{:S(2)}, u32[]{:S(2)}) collective-permute-start(bf16[1,192,336]{2,1,0:T(8,128)(2,1)S(1)} %bitcast.13), channel_id=1, source_target_pairs={{0,2},{1,3},{2,0},{3,1},{4,6},{5,7},{6,4},{7,5},{8,10},{9,11},{10,... | collective-permute-start | bytes 387080 | tf_op jit(solution)/shard_map/ppermute | solution.py:21
  14.1 0.8 %collective-permute-start.13 = (bf16[1,192,336]{2,1,0:T(8,128)(2,1)S(1)}, bf16[1,192,336]{2,1,0:T(8,128)(2,1)S(1)}, u32[]{:S(2)}, u32[]{:S(2)}) collective-permute-start(bf16[1,192,336]{2,1,0:T(8,128)(2,1)S(1)} %collective-permute-done.10.refs_11_), channel_id=1, source_target_pairs={{0,4},{1,5},{2,6},{3,7},{4,0},{5,1},{6,2},{7,3},{8,12},{9,13},{10,... | collective-permute-start | bytes 387080 | tf_op jit(solution)/shard_map/ppermute | solution.py:21
  14.9 1.2 %collective-permute-start.9 = (bf16[1,192,336]{2,1,0:T(8,128)(2,1)S(1)}, bf16[1,192,336]{2,1,0:T(8,128)(2,1)S(1)}, u32[]{:S(2)}, u32[]{:S(2)}) collective-permute-start(bf16[1,192,336]{2,1,0:T(8,128)(2,1)S(1)} %bitcast.14), channel_id=1, source_target_pairs={{0,4},{1,5},{2,6},{3,7},{4,0},{5,1},{6,2},{7,3},{8,12},{9,13},{10,... | collective-permute-start | bytes 387080 | tf_op jit(solution)/shard_map/ppermute | solution.py:21
  16.7 2.1 %collective-permute-done.8.refs_9_ = bf16[1,192,336]{2,1,0:T(8,128)(2,1)S(1)} collective-permute-done((bf16[1,192,336]{2,1,0:T(8,128)(2,1)S(1)}, bf16[1,192,336]{2,1,0:T(8,128)(2,1)S(1)}, u32[]{:S(2)}, u32[]{:S(2)}) %collective-permute-start.8) | collective-permute-done | bytes 129056 | tf_op jit(solution)/shard_map/ppermute | solution.py:21
  18.8 0.8 %collective-permute-start.11 = (bf16[1,192,336]{2,1,0:T(8,128)(2,1)S(1)}, bf16[1,192,336]{2,1,0:T(8,128)(2,1)S(1)}, u32[]{:S(2)}, u32[]{:S(2)}) collective-permute-start(bf16[1,192,336]{2,1,0:T(8,128)(2,1)S(1)} %collective-permute-done.8.refs_9_), channel_id=1, source_target_pairs={{0,4},{1,5},{2,6},{3,7},{4,0},{5,1},{6,2},{7,3},{8,12},{9,13},{10,... | collective-permute-start | bytes 387080 | tf_op jit(solution)/shard_map/ppermute | solution.py:21
  19.6 1.2 %collective-permute-done.13.refs_14_ = bf16[1,192,336]{2,1,0:T(8,128)(2,1)S(1)} collective-permute-done((bf16[1,192,336]{2,1,0:T(8,128)(2,1)S(1)}, bf16[1,192,336]{2,1,0:T(8,128)(2,1)S(1)}, u32[]{:S(2)}, u32[]{:S(2)}) %collective-permute-start.13) | collective-permute-done | bytes 129056 | tf_op jit(solution)/shard_map/ppermute | solution.py:21
  20.8 0.7 %collective-permute-start.14 = (bf16[1,192,336]{2,1,0:T(8,128)(2,1)S(1)}, bf16[1,192,336]{2,1,0:T(8,128)(2,1)S(1)}, u32[]{:S(2)}, u32[]{:S(2)}) collective-permute-start(bf16[1,192,336]{2,1,0:T(8,128)(2,1)S(1)} %collective-permute-done.13.refs_14_), channel_id=1, source_target_pairs={{0,2},{1,3},{2,0},{3,1},{4,6},{5,7},{6,4},{7,5},{8,10},{9,11},{10,... | collective-permute-start | bytes 387080 | tf_op jit(solution)/shard_map/ppermute | solution.py:21
  21.5 2.4 %collective-permute-done.9.refs_10_ = bf16[1,192,336]{2,1,0:T(8,128)(2,1)S(1)} collective-permute-done((bf16[1,192,336]{2,1,0:T(8,128)(2,1)S(1)}, bf16[1,192,336]{2,1,0:T(8,128)(2,1)S(1)}, u32[]{:S(2)}, u32[]{:S(2)}) %collective-permute-start.9) | collective-permute-done | bytes 129056 | tf_op jit(solution)/shard_map/ppermute | solution.py:21
  24.0 2.4 %collective-permute-done.11.refs_12_ = bf16[1,192,336]{2,1,0:T(8,128)(2,1)S(1)} collective-permute-done((bf16[1,192,336]{2,1,0:T(8,128)(2,1)S(1)}, bf16[1,192,336]{2,1,0:T(8,128)(2,1)S(1)}, u32[]{:S(2)}, u32[]{:S(2)}) %collective-permute-start.11) | collective-permute-done | bytes 129056 | tf_op jit(solution)/shard_map/ppermute | solution.py:21
  26.3 1.2 %sketch_rows.1.part_ref = f32[2,2,96,97]{3,2,1,0:T(8,128)S(1)} custom-call(f32[1,5376]{1,0:T(1,128)S(1)} %get-tuple-element.29.peak_ref, bf16[4,192,336]{2,1,0:T(8,128)(2,1)S(1)} %get-tuple-element.30.stay_ref.refs_4_, bf16[2,192,336]{2,1,0:T(8,128)(2,1)S(1)} %get-tuple-element.31.near_ref.refs_5_, bf16[2,192,336]{2,1,0:T(8,128)(2,1)S(1)} %get-tuple-element.50.far_ref, ...), custom_call_target="tpu_custom_call" | custom-call | tf_op jit(solution)/shard_map/sketch_rows/pallas_call | solution.py:253
  27.6 1.4 %collective-permute-done.15.other_ref = f32[2,2,96,97]{3,2,1,0:T(8,128)S(1)} collective-permute-done((f32[2,2,96,97]{3,2,1,0:T(8,128)S(1)}, f32[2,2,96,97]{3,2,1,0:T(8,128)S(1)}, u32[]{:S(2)}, u32[]{:S(2)}) %collective-permute-start.15) | collective-permute-done | bytes 149024 | tf_op jit(solution)/shard_map/ppermute | solution.py:21
  29.0 0.7 %chip_gram.1 = (f32[288,97]{1,0:T(8,128)S(1)}, f32[288,97]{1,0:T(8,128)S(1)}) custom-call(f32[2,2,96,97]{3,2,1,0:T(8,128)S(1)} %sketch_rows.1.part_ref, f32[2,2,96,97]{3,2,1,0:T(8,128)S(1)} %collective-permute-done.15.other_ref), custom_call_target="tpu_custom_call" | custom-call | tf_op jit(solution)/shard_map/chip_gram/pallas_call | solution.py:262
  30.3 1.5 %collective-permute-start.20 = (bf16[2,192,336]{2,1,0:T(8,128)(2,1)S(1)}, bf16[2,192,336]{2,1,0:T(8,128)(2,1)S(1)}, u32[]{:S(2)}, u32[]{:S(2)}) collective-permute-start(bf16[2,192,336]{2,1,0:T(8,128)(2,1)S(1)} %get-tuple-element.50.far_ref), channel_id=1, source_target_pairs={{0,2},{1,3},{2,0},{3,1},{4,6},{5,7},{6,4},{7,5},{8,10},{9,11},{10,... | collective-permute-start | bytes 774152 | tf_op jit(solution)/shard_map/ppermute | solution.py:21
  31.9 4.7 %collective-permute-done.16.refs_2_ = f32[288,97]{1,0:T(8,128)S(1)} collective-permute-done((f32[288,97]{1,0:T(8,128)S(1)}, f32[288,97]{1,0:T(8,128)S(1)}, u32[]{:S(2)}, u32[]{:S(2)}) %collective-permute-start.16) | collective-permute-done | bytes 111776 | tf_op jit(solution)/shard_map/ppermute | solution.py:21
  36.6 0.8 %collective-permute-start.18 = (f32[96,97]{1,0:T(8,128)S(1)}, f32[96,97]{1,0:T(8,128)S(1)}, u32[]{:S(2)}, u32[]{:S(2)}) collective-permute-start(f32[96,97]{1,0:T(8,128)S(1)} %slice_add_fusion.2), channel_id=1, source_target_pairs={{0,4},{1,5},{2,6},{3,7},{4,0},{5,1},{6,2},{7,3},{8,12},{9,13},{10,... | collective-permute-start | bytes 111752 | tf_op jit(solution)/shard_map/ppermute | solution.py:21
  37.4 3.3 %collective-permute-done.18 = f32[96,97]{1,0:T(8,128)S(1)} collective-permute-done((f32[96,97]{1,0:T(8,128)S(1)}, f32[96,97]{1,0:T(8,128)S(1)}, u32[]{:S(2)}, u32[]{:S(2)}) %collective-permute-start.18) | collective-permute-done | bytes 37280 | tf_op jit(solution)/shard_map/ppermute | solution.py:21
  40.7 2.4 %collective-permute-start.19 = (f32[96,97]{1,0:T(8,128)S(1)}, f32[96,97]{1,0:T(8,128)S(1)}, u32[]{:S(2)}, u32[]{:S(2)}) collective-permute-start(f32[96,97]{1,0:T(8,128)S(1)} %add.29), channel_id=1, source_target_pairs={{0,8},{1,9},{2,10},{3,11},{4,12},{5,13},{6,14},{7,15},{8,0},{9,1},... | collective-permute-start | bytes 111752 | tf_op jit(solution)/shard_map/ppermute | solution.py:21
  43.1 2.7 %collective-permute-done.19 = f32[96,97]{1,0:T(8,128)S(1)} collective-permute-done((f32[96,97]{1,0:T(8,128)S(1)}, f32[96,97]{1,0:T(8,128)S(1)}, u32[]{:S(2)}, u32[]{:S(2)}) %collective-permute-start.19) | collective-permute-done | bytes 37280 | tf_op jit(solution)/shard_map/ppermute | solution.py:21
  45.8 6.4 %orthonormal_basis.1 = (f32[2,96,96]{2,1,0:T(8,128)}, bf16[192,192]{1,0:T(8,128)(2,1)S(1)}, bf16[192,192]{1,0:T(8,128)(2,1)S(1)}, bf16[192,192]{1,0:T(8,128)(2,1)S(1)}, bf16[192,192]{1,0:T(8,128)(2,1)S(1)}) custom-call(f32[288,97]{1,0:T(8,128)S(1)} %get-tuple-element.42.refs_0_, f32[288,97]{1,0:T(8,128)S(1)} %get-tuple-element.43.refs_1_, ...), custom_call_target="tpu_custom_call" | custom-call | flops 1500000000 | bytes 1000000 | tf_op jit(solution)/shard_map/orthonormal_basis/pallas_call | solution.py:279
  52.2 1.0 %project_rows.1 = (f32[2,192,336]{2,1,0:T(8,128)S(1)}, f32[2,192,336]{2,1,0:T(8,128)S(1)}, f32[192,336]{1,0:T(8,128)S(1)}, f32[192,336]{1,0:T(8,128)S(1)}) custom-call(f32[96,97]{1,0:T(8,128)S(1)} %add.30.refs_4_.gram_ref, bf16[192,192]{1,0:T(8,128)(2,1)S(1)} %get-tuple-element.45.refs_0_, bf16[192,192]{1,0:T(8,128)(2,1)S(1)} %get-tuple-element.46.refs_1_, ...), custom_call_target="tpu_custom_call" | custom-call | tf_op jit(solution)/shard_map/project_rows/pallas_call | solution.py:290
  53.2 0.7 %collective-permute-start.22 = (f16[2,192,336]{2,1,0:T(8,128)(2,1)S(1)}, f16[2,192,336]{2,1,0:T(8,128)(2,1)S(1)}, u32[]{:S(2)}, u32[]{:S(2)}) collective-permute-start(f16[2,192,336]{2,1,0:T(8,128)(2,1)S(1)} %convert_element_type.27), channel_id=1, source_target_pairs={{0,2},{1,3},{2,0},{3,1},{4,6},{5,7},{6,4},{7,5},{8,10},{9,11},{10,... | collective-permute-start | bytes 774152 | tf_op jit(solution)/shard_map/ppermute | solution.py:21
  54.0 3.0 %collective-permute-start.24 = (f16[192,336]{1,0:T(8,128)(2,1)S(1)}, f16[192,336]{1,0:T(8,128)(2,1)S(1)}, u32[]{:S(2)}, u32[]{:S(2)}) collective-permute-start(f16[192,336]{1,0:T(8,128)(2,1)S(1)} %convert_element_type.31), channel_id=1, source_target_pairs={{0,8},{1,9},{2,10},{3,11},{4,12},{5,13},{6,14},{7,15},{8,0},{9,1},... | collective-permute-start | bytes 387080 | tf_op jit(solution)/shard_map/ppermute | solution.py:21
  57.6 3.0 %collective-permute-done.22 = f16[2,192,336]{2,1,0:T(8,128)(2,1)S(1)} collective-permute-done((f16[2,192,336]{2,1,0:T(8,128)(2,1)S(1)}, f16[2,192,336]{2,1,0:T(8,128)(2,1)S(1)}, u32[]{:S(2)}, u32[]{:S(2)}) %collective-permute-start.22) | collective-permute-done | bytes 258080 | tf_op jit(solution)/shard_map/ppermute | solution.py:21
  60.7 1.5 %collective-permute-start.25 = (f16[192,336]{1,0:T(8,128)(2,1)S(1)}, f16[192,336]{1,0:T(8,128)(2,1)S(1)}, u32[]{:S(2)}, u32[]{:S(2)}) collective-permute-start(f16[192,336]{1,0:T(8,128)(2,1)S(1)} %fusion.4), channel_id=1, source_target_pairs={{0,4},{1,5},{2,6},{3,7},{4,0},{5,1},{6,2},{7,3},{8,12},{9,13},{10,... | collective-permute-start | bytes 387080 | tf_op jit(solution)/shard_map/ppermute | solution.py:21
  62.2 0.6 slice.31
  63.5 3.1 %collective-permute-done.24 = f16[192,336]{1,0:T(8,128)(2,1)S(1)} collective-permute-done((f16[192,336]{1,0:T(8,128)(2,1)S(1)}, f16[192,336]{1,0:T(8,128)(2,1)S(1)}, u32[]{:S(2)}, u32[]{:S(2)}) %collective-permute-start.24) | collective-permute-done | bytes 129056 | tf_op jit(solution)/shard_map/ppermute | solution.py:21
  66.6 1.5 %collective-permute-done.25 = f16[192,336]{1,0:T(8,128)(2,1)S(1)} collective-permute-done((f16[192,336]{1,0:T(8,128)(2,1)S(1)}, f16[192,336]{1,0:T(8,128)(2,1)S(1)}, u32[]{:S(2)}, u32[]{:S(2)}) %collective-permute-start.25) | collective-permute-done | bytes 129056 | tf_op jit(solution)/shard_map/ppermute | solution.py:21
  68.1 0.8 %fusion.3 = f32[192,336]{1,0:T(8,128)} fusion(f32[2,192,336]{2,1,0:T(8,128)S(1)} %convert_element_type.28, f16[192,336]{1,0:T(8,128)(2,1)S(1)} %collective-permute-done.25, f16[192,336]{1,0:T(8,128)(2,1)S(1)} %collective-permute-done.24, f16[192,336]{1,0:T(8,128)(2,1)S(1)} %collective-permute-done.23, f32[2,192,336]{2,1,0:T(8,128)S(1)} %get-tuple-element.52, ...), kind=kLoop, calls=%fused_computation.5 | loop fusion | flops 516096 | bytes 1161220 | tf_op jit(solution)/shard_map/mul | solution.py:316
  (39 shorter events, 3.6 us)
Async XLA Ops:
  0.6 11.3 %collective-permute-start.10 = (bf16[1,192,336]{2,1,0:T(8,128)(2,1)}, bf16[1,192,336]{2,1,0:T(8,128)(2,1)S(1)}, u32[]{:S(2)}, u32[]{:S(2)}) collective-permute-start(bf16[1,192,336]{2,1,0:T(8,128)(2,1)} %bitcast.12), channel_id=1, source_target_pairs={{0,8},{1,9},{2,10},{3,11},{4,12},{5,13},{6,14},{7,15},{8,0},{9,1},... | collective-permute-start | bytes 387080 | tf_op jit(solution)/shard_map/ppermute | solution.py:21
  4.7 1.6 %copy-start = (bf16[2,96,5376]{2,1,0:T(8,128)(2,1)S(1)}, bf16[2,96,5376]{2,1,0:T(8,128)(2,1)}, u32[]{:S(2)}) copy-start(bf16[2,96,5376]{2,1,0:T(8,128)(2,1)} %traces_ref.1) | copy-start | bytes 6193156
  6.3 6.2 %copy-start.1 = (bf16[2,96,336]{2,1,0:T(8,128)(2,1)S(1)}, bf16[2,96,336]{2,1,0:T(8,128)(2,1)}, u32[]{:S(2)}) copy-start(bf16[2,96,336]{2,1,0:T(8,128)(2,1)} %param.3) | copy-start | bytes 387076
  7.9 4.1 %collective-permute-start = (bf16[1,192,336]{2,1,0:T(8,128)(2,1)S(1)}, bf16[1,192,336]{2,1,0:T(8,128)(2,1)S(1)}, u32[]{:S(2)}, u32[]{:S(2)}) collective-permute-start(bf16[1,192,336]{2,1,0:T(8,128)(2,1)S(1)} %get-tuple-element.33), channel_id=1, source_target_pairs={{0,1},{1,0},{2,3},{3,2},{4,5},{5,4},{6,7},{7,6},{8,9},{9,8},{10,11... | collective-permute-start | bytes 387080 | tf_op jit(solution)/shard_map/ppermute | solution.py:21
  8.0 4.5 %collective-permute-start.1 = (bf16[1,192,336]{2,1,0:T(8,128)(2,1)S(1)}, bf16[1,192,336]{2,1,0:T(8,128)(2,1)S(1)}, u32[]{:S(2)}, u32[]{:S(2)}) collective-permute-start(bf16[1,192,336]{2,1,0:T(8,128)(2,1)S(1)} %get-tuple-element.34), channel_id=1, source_target_pairs={{0,1},{1,0},{2,3},{3,2},{4,5},{5,4},{6,7},{7,6},{8,9},{9,8},{10,11... | collective-permute-start | bytes 387080 | tf_op jit(solution)/shard_map/ppermute | solution.py:21
  8.5 4.1 %collective-permute-start.2 = (bf16[1,192,336]{2,1,0:T(8,128)(2,1)S(1)}, bf16[1,192,336]{2,1,0:T(8,128)(2,1)S(1)}, u32[]{:S(2)}, u32[]{:S(2)}) collective-permute-start(bf16[1,192,336]{2,1,0:T(8,128)(2,1)S(1)} %get-tuple-element.35), channel_id=1, source_target_pairs={{0,1},{1,0},{2,3},{3,2},{4,5},{5,4},{6,7},{7,6},{8,9},{9,8},{10,11... | collective-permute-start | bytes 387080 | tf_op jit(solution)/shard_map/ppermute | solution.py:21
  8.5 5.6 %collective-permute-start.3 = (bf16[1,192,336]{2,1,0:T(8,128)(2,1)S(1)}, bf16[1,192,336]{2,1,0:T(8,128)(2,1)S(1)}, u32[]{:S(2)}, u32[]{:S(2)}) collective-permute-start(bf16[1,192,336]{2,1,0:T(8,128)(2,1)S(1)} %get-tuple-element.36), channel_id=1, source_target_pairs={{0,1},{1,0},{2,3},{3,2},{4,5},{5,4},{6,7},{7,6},{8,9},{9,8},{10,11... | collective-permute-start | bytes 387080 | tf_op jit(solution)/shard_map/ppermute | solution.py:21
  11.9 2.9 %collective-permute-start.4 = (bf16[1,192,336]{2,1,0:T(8,128)(2,1)S(1)}, bf16[1,192,336]{2,1,0:T(8,128)(2,1)S(1)}, u32[]{:S(2)}, u32[]{:S(2)}) collective-permute-start(bf16[1,192,336]{2,1,0:T(8,128)(2,1)S(1)} %get-tuple-element.37), channel_id=1, source_target_pairs={{0,1},{1,0},{2,3},{3,2},{4,5},{5,4},{6,7},{7,6},{8,9},{9,8},{10,11... | collective-permute-start | bytes 387080 | tf_op jit(solution)/shard_map/ppermute | solution.py:21
  12.0 4.2 %collective-permute-start.5 = (bf16[1,192,336]{2,1,0:T(8,128)(2,1)S(1)}, bf16[1,192,336]{2,1,0:T(8,128)(2,1)S(1)}, u32[]{:S(2)}, u32[]{:S(2)}) collective-permute-start(bf16[1,192,336]{2,1,0:T(8,128)(2,1)S(1)} %get-tuple-element.38), channel_id=1, source_target_pairs={{0,1},{1,0},{2,3},{3,2},{4,5},{5,4},{6,7},{7,6},{8,9},{9,8},{10,11... | collective-permute-start | bytes 387080 | tf_op jit(solution)/shard_map/ppermute | solution.py:21
  12.5 3.7 %collective-permute-start.6 = (bf16[1,192,336]{2,1,0:T(8,128)(2,1)S(1)}, bf16[1,192,336]{2,1,0:T(8,128)(2,1)S(1)}, u32[]{:S(2)}, u32[]{:S(2)}) collective-permute-start(bf16[1,192,336]{2,1,0:T(8,128)(2,1)S(1)} %get-tuple-element.39), channel_id=1, source_target_pairs={{0,1},{1,0},{2,3},{3,2},{4,5},{5,4},{6,7},{7,6},{8,9},{9,8},{10,11... | collective-permute-start | bytes 387080 | tf_op jit(solution)/shard_map/ppermute | solution.py:21
  12.5 6.2 %collective-permute-start.8 = (bf16[1,192,336]{2,1,0:T(8,128)(2,1)S(1)}, bf16[1,192,336]{2,1,0:T(8,128)(2,1)S(1)}, u32[]{:S(2)}, u32[]{:S(2)}) collective-permute-start(bf16[1,192,336]{2,1,0:T(8,128)(2,1)S(1)} %bitcast.13), channel_id=1, source_target_pairs={{0,2},{1,3},{2,0},{3,1},{4,6},{5,7},{6,4},{7,5},{8,10},{9,11},{10,... | collective-permute-start | bytes 387080 | tf_op jit(solution)/shard_map/ppermute | solution.py:21
  14.1 6.7 %collective-permute-start.13 = (bf16[1,192,336]{2,1,0:T(8,128)(2,1)S(1)}, bf16[1,192,336]{2,1,0:T(8,128)(2,1)S(1)}, u32[]{:S(2)}, u32[]{:S(2)}) collective-permute-start(bf16[1,192,336]{2,1,0:T(8,128)(2,1)S(1)} %collective-permute-done.10.refs_11_), channel_id=1, source_target_pairs={{0,4},{1,5},{2,6},{3,7},{4,0},{5,1},{6,2},{7,3},{8,12},{9,13},{10,... | collective-permute-start | bytes 387080 | tf_op jit(solution)/shard_map/ppermute | solution.py:21
  14.9 9.1 %collective-permute-start.9 = (bf16[1,192,336]{2,1,0:T(8,128)(2,1)S(1)}, bf16[1,192,336]{2,1,0:T(8,128)(2,1)S(1)}, u32[]{:S(2)}, u32[]{:S(2)}) collective-permute-start(bf16[1,192,336]{2,1,0:T(8,128)(2,1)S(1)} %bitcast.14), channel_id=1, source_target_pairs={{0,4},{1,5},{2,6},{3,7},{4,0},{5,1},{6,2},{7,3},{8,12},{9,13},{10,... | collective-permute-start | bytes 387080 | tf_op jit(solution)/shard_map/ppermute | solution.py:21
  16.1 5.4 %collective-permute-start.7 = (bf16[1,192,336]{2,1,0:T(8,128)(2,1)S(1)}, bf16[1,192,336]{2,1,0:T(8,128)(2,1)S(1)}, u32[]{:S(2)}, u32[]{:S(2)}) collective-permute-start(bf16[1,192,336]{2,1,0:T(8,128)(2,1)S(1)} %get-tuple-element.40), channel_id=1, source_target_pairs={{0,1},{1,0},{2,3},{3,2},{4,5},{5,4},{6,7},{7,6},{8,9},{9,8},{10,11... | collective-permute-start | bytes 387080 | tf_op jit(solution)/shard_map/ppermute | solution.py:21
  16.1 10.2 %collective-permute-start.12 = (bf16[1,192,336]{2,1,0:T(8,128)(2,1)S(1)}, bf16[1,192,336]{2,1,0:T(8,128)(2,1)S(1)}, u32[]{:S(2)}, u32[]{:S(2)}) collective-permute-start(bf16[1,192,336]{2,1,0:T(8,128)(2,1)S(1)} %collective-permute-done.10.refs_11_), channel_id=1, source_target_pairs={{0,2},{1,3},{2,0},{3,1},{4,6},{5,7},{6,4},{7,5},{8,10},{9,11},{10,... | collective-permute-start | bytes 387080 | tf_op jit(solution)/shard_map/ppermute | solution.py:21
  18.8 7.6 %collective-permute-start.11 = (bf16[1,192,336]{2,1,0:T(8,128)(2,1)S(1)}, bf16[1,192,336]{2,1,0:T(8,128)(2,1)S(1)}, u32[]{:S(2)}, u32[]{:S(2)}) collective-permute-start(bf16[1,192,336]{2,1,0:T(8,128)(2,1)S(1)} %collective-permute-done.8.refs_9_), channel_id=1, source_target_pairs={{0,4},{1,5},{2,6},{3,7},{4,0},{5,1},{6,2},{7,3},{8,12},{9,13},{10,... | collective-permute-start | bytes 387080 | tf_op jit(solution)/shard_map/ppermute | solution.py:21
  20.8 5.6 %collective-permute-start.14 = (bf16[1,192,336]{2,1,0:T(8,128)(2,1)S(1)}, bf16[1,192,336]{2,1,0:T(8,128)(2,1)S(1)}, u32[]{:S(2)}, u32[]{:S(2)}) collective-permute-start(bf16[1,192,336]{2,1,0:T(8,128)(2,1)S(1)} %collective-permute-done.13.refs_14_), channel_id=1, source_target_pairs={{0,2},{1,3},{2,0},{3,1},{4,6},{5,7},{6,4},{7,5},{8,10},{9,11},{10,... | collective-permute-start | bytes 387080 | tf_op jit(solution)/shard_map/ppermute | solution.py:21
  27.5 1.5 %collective-permute-start.15 = (f32[2,2,96,97]{3,2,1,0:T(8,128)S(1)}, f32[2,2,96,97]{3,2,1,0:T(8,128)S(1)}, u32[]{:S(2)}, u32[]{:S(2)}) collective-permute-start(f32[2,2,96,97]{3,2,1,0:T(8,128)S(1)} %sketch_rows.1.part_ref), channel_id=1, source_target_pairs={{0,1},{1,0},{2,3},{3,2},{4,5},{5,4},{6,7},{7,6},{8,9},{9,8},{10,11... | collective-permute-start | bytes 446984 | tf_op jit(solution)/shard_map/ppermute | solution.py:21
  29.8 6.8 %collective-permute-start.16 = (f32[288,97]{1,0:T(8,128)S(1)}, f32[288,97]{1,0:T(8,128)S(1)}, u32[]{:S(2)}, u32[]{:S(2)}) collective-permute-start(f32[288,97]{1,0:T(8,128)S(1)} %get-tuple-element.42.refs_0_), channel_id=1, source_target_pairs={{0,2},{1,3},{2,0},{3,1},{4,6},{5,7},{6,4},{7,5},{8,10},{9,11},{10,... | collective-permute-start | bytes 335240 | tf_op jit(solution)/shard_map/ppermute | solution.py:21
  30.3 21.9 %collective-permute-start.20 = (bf16[2,192,336]{2,1,0:T(8,128)(2,1)S(1)}, bf16[2,192,336]{2,1,0:T(8,128)(2,1)S(1)}, u32[]{:S(2)}, u32[]{:S(2)}) collective-permute-start(bf16[2,192,336]{2,1,0:T(8,128)(2,1)S(1)} %get-tuple-element.50.far_ref), channel_id=1, source_target_pairs={{0,2},{1,3},{2,0},{3,1},{4,6},{5,7},{6,4},{7,5},{8,10},{9,11},{10,... | collective-permute-start | bytes 774152 | tf_op jit(solution)/shard_map/ppermute | solution.py:21
  31.9 20.3 %collective-permute-start.21 = (bf16[2,192,336]{2,1,0:T(8,128)(2,1)S(1)}, bf16[2,192,336]{2,1,0:T(8,128)(2,1)S(1)}, u32[]{:S(2)}, u32[]{:S(2)}) collective-permute-start(bf16[2,192,336]{2,1,0:T(8,128)(2,1)S(1)} %get-tuple-element.51), channel_id=1, source_target_pairs={{0,3},{1,2},{2,1},{3,0},{4,7},{5,6},{6,5},{7,4},{8,11},{9,10},{10,... | collective-permute-start | bytes 774152 | tf_op jit(solution)/shard_map/ppermute | solution.py:21
  36.5 9.3 %collective-permute-start.17 = (f32[288,97]{1,0:T(8,128)S(1)}, f32[288,97]{1,0:T(8,128)S(1)}, u32[]{:S(2)}, u32[]{:S(2)}) collective-permute-start(f32[288,97]{1,0:T(8,128)S(1)} %collective-permute-done.16.refs_2_), channel_id=1, source_target_pairs={{0,1},{1,0},{2,3},{3,2},{4,5},{5,4},{6,7},{7,6},{8,9},{9,8},{10,11... | collective-permute-start | bytes 335240 | tf_op jit(solution)/shard_map/ppermute | solution.py:21
  36.6 4.2 %collective-permute-start.18 = (f32[96,97]{1,0:T(8,128)S(1)}, f32[96,97]{1,0:T(8,128)S(1)}, u32[]{:S(2)}, u32[]{:S(2)}) collective-permute-start(f32[96,97]{1,0:T(8,128)S(1)} %slice_add_fusion.2), channel_id=1, source_target_pairs={{0,4},{1,5},{2,6},{3,7},{4,0},{5,1},{6,2},{7,3},{8,12},{9,13},{10,... | collective-permute-start | bytes 111752 | tf_op jit(solution)/shard_map/ppermute | solution.py:21
  40.7 5.1 %collective-permute-start.19 = (f32[96,97]{1,0:T(8,128)S(1)}, f32[96,97]{1,0:T(8,128)S(1)}, u32[]{:S(2)}, u32[]{:S(2)}) collective-permute-start(f32[96,97]{1,0:T(8,128)S(1)} %add.29), channel_id=1, source_target_pairs={{0,8},{1,9},{2,10},{3,11},{4,12},{5,13},{6,14},{7,15},{8,0},{9,1},... | collective-permute-start | bytes 111752 | tf_op jit(solution)/shard_map/ppermute | solution.py:21
  53.2 7.4 %collective-permute-start.22 = (f16[2,192,336]{2,1,0:T(8,128)(2,1)S(1)}, f16[2,192,336]{2,1,0:T(8,128)(2,1)S(1)}, u32[]{:S(2)}, u32[]{:S(2)}) collective-permute-start(f16[2,192,336]{2,1,0:T(8,128)(2,1)S(1)} %convert_element_type.27), channel_id=1, source_target_pairs={{0,2},{1,3},{2,0},{3,1},{4,6},{5,7},{6,4},{7,5},{8,10},{9,11},{10,... | collective-permute-start | bytes 774152 | tf_op jit(solution)/shard_map/ppermute | solution.py:21
  54.0 12.6 %collective-permute-start.24 = (f16[192,336]{1,0:T(8,128)(2,1)S(1)}, f16[192,336]{1,0:T(8,128)(2,1)S(1)}, u32[]{:S(2)}, u32[]{:S(2)}) collective-permute-start(f16[192,336]{1,0:T(8,128)(2,1)S(1)} %convert_element_type.31), channel_id=1, source_target_pairs={{0,8},{1,9},{2,10},{3,11},{4,12},{5,13},{6,14},{7,15},{8,0},{9,1},... | collective-permute-start | bytes 387080 | tf_op jit(solution)/shard_map/ppermute | solution.py:21
  57.0 9.5 %collective-permute-start.23 = (f16[192,336]{1,0:T(8,128)(2,1)S(1)}, f16[192,336]{1,0:T(8,128)(2,1)S(1)}, u32[]{:S(2)}, u32[]{:S(2)}) collective-permute-start(f16[192,336]{1,0:T(8,128)(2,1)S(1)} %convert_element_type.29), channel_id=1, source_target_pairs={{0,12},{1,13},{2,14},{3,15},{4,8},{5,9},{6,10},{7,11},{8,4},{9,5},... | collective-permute-start | bytes 387080 | tf_op jit(solution)/shard_map/ppermute | solution.py:21
  60.7 7.4 %collective-permute-start.25 = (f16[192,336]{1,0:T(8,128)(2,1)S(1)}, f16[192,336]{1,0:T(8,128)(2,1)S(1)}, u32[]{:S(2)}, u32[]{:S(2)}) collective-permute-start(f16[192,336]{1,0:T(8,128)(2,1)S(1)} %fusion.4), channel_id=1, source_target_pairs={{0,4},{1,5},{2,6},{3,7},{4,0},{5,1},{6,2},{7,3},{8,12},{9,13},{10,... | collective-permute-start | bytes 387080 | tf_op jit(solution)/shard_map/ppermute | solution.py:21

commit v6 on v5

--- a/solution.py
+++ b/solution.py
@@ -207,7 +207,9 @@
     have = {0: piece}
     for level in range(1, direct):
         if level == 2:
-            (have[1 << direct - 1],), _ = tied([have[1 << direct - 1]], [ahead])
+            first = [1 << bit for bit in reversed(range(1, direct))]
+            values, _ = tied([have[slot] for slot in first], [ahead])
+            have.update(zip(first, values))
         for slot in range(0, 1 << direct, 2):
             if slot.bit_count() == level:
                 along = slot & -slot if slot >> direct - 1 else 1 << slot.bit_length() - 1

time: 69 us -> 67.5 us (0.978)
  waiting for transfers between devices: 30.8 us -> 22.1 us
  starting transfers between devices: 22.7 us -> 29.9 us
    ppermute x26, waiting for transfers between devices: 30.8 us -> 22.1 us  [swap(): return lax.ppermute(value, 'rcv', [(i, i ^ mask) for i in range(size)])]
    ppermute x26, starting transfers between devices: 22.7 us -> 29.9 us  [swap(): return lax.ppermute(value, 'rcv', [(i, i ^ mask) for i in range(size)])]
where the time goes in v6:
time: 67.5 us; the launch traced here: 67.4 us
  starting transfers between devices  29.9 us (44%)
  waiting for transfers between devices  22.1 us (33%)
  Pallas kernels  10.8 us (16%)
  local copies, waits for them, and re-layouts  2.16 us (3%)
  between operations  1.38 us (2%)
  other arithmetic  0.97 us (1%)
    ppermute x26, starting transfers between devices, swap(): return lax.ppermute(value, 'rcv', [(i, i ^ mask) for i in range(size)])  29.9 us
    ppermute x26, waiting for transfers between devices, swap(): return lax.ppermute(value, 'rcv', [(i, i ^ mask) for i in range(size)])  22.1 us
    pallas_call x1, Pallas kernels, per_device(): pl.pallas_call(functools.partial(basis_kernel, math.sqrt(rows * size)), o...  6.38 us
    unnamed x4, local copies, waits for them, and re-layouts  1.58 us
    pallas_call x1, Pallas kernels, per_device(): pl.pallas_call(functools.partial(chunk_kernel, share), out_shape=(chunk(z...  1.56 us
  transfers between devices with their start and end apart: 26, of which 12 were waited for; matrix products, arithmetic and copies ran while one was open for 1% of the time, Pallas kernels for 12%

profile of v6, /device:TPU:0, one launch (start us, length us, event | category | flops | bytes accessed | tf_op | source)
XLA Modules:
  0.0 67.4 jit_solution(3214689876606647603)
XLA Ops:
  0.6 4.1 %collective-permute-start.8 = (bf16[1,192,336]{2,1,0:T(8,128)(2,1)}, bf16[1,192,336]{2,1,0:T(8,128)(2,1)S(1)}, u32[]{:S(2)}, u32[]{:S(2)}) collective-permute-start(bf16[1,192,336]{2,1,0:T(8,128)(2,1)} %bitcast.12), channel_id=1, source_target_pairs={{0,8},{1,9},{2,10},{3,11},{4,12},{5,13},{6,14},{7,15},{8,0},{9,1},... | collective-permute-start | bytes 387080 | tf_op jit(solution)/shard_map/ppermute | solution.py:21
  4.7 1.6 %collective-permute-start.9 = (bf16[1,192,336]{2,1,0:T(8,128)(2,1)}, bf16[1,192,336]{2,1,0:T(8,128)(2,1)S(1)}, u32[]{:S(2)}, u32[]{:S(2)}) collective-permute-start(bf16[1,192,336]{2,1,0:T(8,128)(2,1)} %bitcast.13), channel_id=1, source_target_pairs={{0,4},{1,5},{2,6},{3,7},{4,0},{5,1},{6,2},{7,3},{8,12},{9,13},{10,... | collective-permute-start | bytes 387080 | tf_op jit(solution)/shard_map/ppermute | solution.py:21
  6.3 1.5 %collective-permute-start.10 = (bf16[1,192,336]{2,1,0:T(8,128)(2,1)}, bf16[1,192,336]{2,1,0:T(8,128)(2,1)S(1)}, u32[]{:S(2)}, u32[]{:S(2)}) collective-permute-start(bf16[1,192,336]{2,1,0:T(8,128)(2,1)} %bitcast.14), channel_id=1, source_target_pairs={{0,2},{1,3},{2,0},{3,1},{4,6},{5,7},{6,4},{7,5},{8,10},{9,11},{10,... | collective-permute-start | bytes 387080 | tf_op jit(solution)/shard_map/ppermute | solution.py:21
  7.8 1.6 %copy-done = bf16[2,96,5376]{2,1,0:T(8,128)(2,1)S(1)} copy-done((bf16[2,96,5376]{2,1,0:T(8,128)(2,1)S(1)}, bf16[2,96,5376]{2,1,0:T(8,128)(2,1)}, u32[]{:S(2)}) %copy-start) | copy-done | bytes 2064408
  9.4 1.6 %source_chunks.1 = (bf16[4,192,336]{2,1,0:T(8,128)(2,1)S(1)}, bf16[2,192,336]{2,1,0:T(8,128)(2,1)S(1)}, bf16[2,192,336]{2,1,0:T(8,128)(2,1)S(1)}, bf16[2,192,336...) custom-call(s32[1]{0:T(128)} %bitcast.me_ref, ...), custom_call_target="tpu_custom_call" | custom-call | tf_op jit(solution)/shard_map/source_chunks/pallas_call | solution.py:235
  13.1 1.2 %collective-permute-start.13 = (bf16[1,192,336]{2,1,0:T(8,128)(2,1)S(1)}, bf16[1,192,336]{2,1,0:T(8,128)(2,1)S(1)}, u32[]{:S(2)}, u32[]{:S(2)}) collective-permute-start(bf16[1,192,336]{2,1,0:T(8,128)(2,1)S(1)} %collective-permute-done.8.refs_11_), channel_id=1, source_target_pairs={{0,4},{1,5},{2,6},{3,7},{4,0},{5,1},{6,2},{7,3},{8,12},{9,13},{10,... | collective-permute-start | bytes 387080 | tf_op jit(solution)/shard_map/ppermute | solution.py:21
  14.8 1.5 %collective-permute-start.12 = (bf16[1,192,336]{2,1,0:T(8,128)(2,1)S(1)}, bf16[1,192,336]{2,1,0:T(8,128)(2,1)S(1)}, u32[]{:S(2)}, u32[]{:S(2)}) collective-permute-start(bf16[1,192,336]{2,1,0:T(8,128)(2,1)S(1)} %collective-permute-done.8.refs_11_), channel_id=1, source_target_pairs={{0,2},{1,3},{2,0},{3,1},{4,6},{5,7},{6,4},{7,5},{8,10},{9,11},{10,... | collective-permute-start | bytes 387080 | tf_op jit(solution)/shard_map/ppermute | solution.py:21
  16.3 0.8 %collective-permute-start.11 = (bf16[1,192,336]{2,1,0:T(8,128)(2,1)S(1)}, bf16[1,192,336]{2,1,0:T(8,128)(2,1)S(1)}, u32[]{:S(2)}, u32[]{:S(2)}) collective-permute-start(bf16[1,192,336]{2,1,0:T(8,128)(2,1)S(1)} %collective-permute-done.10.refs_9_), channel_id=1, source_target_pairs={{0,4},{1,5},{2,6},{3,7},{4,0},{5,1},{6,2},{7,3},{8,12},{9,13},{10,... | collective-permute-start | bytes 387080 | tf_op jit(solution)/shard_map/ppermute | solution.py:21
  17.2 2.0 %collective-permute-done.13.refs_14_ = bf16[1,192,336]{2,1,0:T(8,128)(2,1)S(1)} collective-permute-done((bf16[1,192,336]{2,1,0:T(8,128)(2,1)S(1)}, bf16[1,192,336]{2,1,0:T(8,128)(2,1)S(1)}, u32[]{:S(2)}, u32[]{:S(2)}) %collective-permute-start.13) | collective-permute-done | bytes 129056 | tf_op jit(solution)/shard_map/ppermute | solution.py:21
  19.2 2.1 %collective-permute-start.14 = (bf16[1,192,336]{2,1,0:T(8,128)(2,1)S(1)}, bf16[1,192,336]{2,1,0:T(8,128)(2,1)S(1)}, u32[]{:S(2)}, u32[]{:S(2)}) collective-permute-start(bf16[1,192,336]{2,1,0:T(8,128)(2,1)S(1)} %collective-permute-done.13.refs_14_), channel_id=1, source_target_pairs={{0,2},{1,3},{2,0},{3,1},{4,6},{5,7},{6,4},{7,5},{8,10},{9,11},{10,... | collective-permute-start | bytes 387080 | tf_op jit(solution)/shard_map/ppermute | solution.py:21
  21.3 0.9 %collective-permute-done.11.refs_12_ = bf16[1,192,336]{2,1,0:T(8,128)(2,1)S(1)} collective-permute-done((bf16[1,192,336]{2,1,0:T(8,128)(2,1)S(1)}, bf16[1,192,336]{2,1,0:T(8,128)(2,1)S(1)}, u32[]{:S(2)}, u32[]{:S(2)}) %collective-permute-start.11) | collective-permute-done | bytes 129056 | tf_op jit(solution)/shard_map/ppermute | solution.py:21
  22.2 2.2 %collective-permute-done.14.refs_15_ = bf16[1,192,336]{2,1,0:T(8,128)(2,1)S(1)} collective-permute-done((bf16[1,192,336]{2,1,0:T(8,128)(2,1)S(1)}, bf16[1,192,336]{2,1,0:T(8,128)(2,1)S(1)}, u32[]{:S(2)}, u32[]{:S(2)}) %collective-permute-start.14) | collective-permute-done | bytes 129056 | tf_op jit(solution)/shard_map/ppermute | solution.py:21
  24.4 1.2 %sketch_rows.1.part_ref = f32[2,2,96,97]{3,2,1,0:T(8,128)S(1)} custom-call(f32[1,5376]{1,0:T(1,128)S(1)} %get-tuple-element.31.peak_ref, bf16[4,192,336]{2,1,0:T(8,128)(2,1)S(1)} %get-tuple-element.32.stay_ref.refs_4_, bf16[2,192,336]{2,1,0:T(8,128)(2,1)S(1)} %get-tuple-element.33.near_ref.refs_5_, bf16[2,192,336]{2,1,0:T(8,128)(2,1)S(1)} %get-tuple-element.54.far_ref, ...), custom_call_target="tpu_custom_call" | custom-call | tf_op jit(solution)/shard_map/sketch_rows/pallas_call | solution.py:255
  25.7 1.4 %collective-permute-done.15.other_ref = f32[2,2,96,97]{3,2,1,0:T(8,128)S(1)} collective-permute-done((f32[2,2,96,97]{3,2,1,0:T(8,128)S(1)}, f32[2,2,96,97]{3,2,1,0:T(8,128)S(1)}, u32[]{:S(2)}, u32[]{:S(2)}) %collective-permute-start.15) | collective-permute-done | bytes 149024 | tf_op jit(solution)/shard_map/ppermute | solution.py:21
  27.1 0.7 %chip_gram.1 = (f32[288,97]{1,0:T(8,128)S(1)}, f32[288,97]{1,0:T(8,128)S(1)}) custom-call(f32[2,2,96,97]{3,2,1,0:T(8,128)S(1)} %sketch_rows.1.part_ref, f32[2,2,96,97]{3,2,1,0:T(8,128)S(1)} %collective-permute-done.15.other_ref), custom_call_target="tpu_custom_call" | custom-call | tf_op jit(solution)/shard_map/chip_gram/pallas_call | solution.py:264
  27.9 2.1 %collective-permute-start.16 = (f32[288,97]{1,0:T(8,128)S(1)}, f32[288,97]{1,0:T(8,128)S(1)}, u32[]{:S(2)}, u32[]{:S(2)}) collective-permute-start(f32[288,97]{1,0:T(8,128)S(1)} %get-tuple-element.46.refs_0_), channel_id=1, source_target_pairs={{0,2},{1,3},{2,0},{3,1},{4,6},{5,7},{6,4},{7,5},{8,10},{9,11},{10,... | collective-permute-start | bytes 335240 | tf_op jit(solution)/shard_map/ppermute | solution.py:21
  30.0 1.1 %collective-permute-start.21 = (bf16[2,192,336]{2,1,0:T(8,128)(2,1)S(1)}, bf16[2,192,336]{2,1,0:T(8,128)(2,1)S(1)}, u32[]{:S(2)}, u32[]{:S(2)}) collective-permute-start(bf16[2,192,336]{2,1,0:T(8,128)(2,1)S(1)} %get-tuple-element.55), channel_id=1, source_target_pairs={{0,3},{1,2},{2,1},{3,0},{4,7},{5,6},{6,5},{7,4},{8,11},{9,10},{10,... | collective-permute-start | bytes 774152 | tf_op jit(solution)/shard_map/ppermute | solution.py:21
  31.2 3.4 %collective-permute-done.16.refs_2_ = f32[288,97]{1,0:T(8,128)S(1)} collective-permute-done((f32[288,97]{1,0:T(8,128)S(1)}, f32[288,97]{1,0:T(8,128)S(1)}, u32[]{:S(2)}, u32[]{:S(2)}) %collective-permute-start.16) | collective-permute-done | bytes 111776 | tf_op jit(solution)/shard_map/ppermute | solution.py:21
  34.6 1.8 %collective-permute-start.18 = (f32[96,97]{1,0:T(8,128)S(1)}, f32[96,97]{1,0:T(8,128)S(1)}, u32[]{:S(2)}, u32[]{:S(2)}) collective-permute-start(f32[96,97]{1,0:T(8,128)S(1)} %slice_add_fusion.2), channel_id=1, source_target_pairs={{0,4},{1,5},{2,6},{3,7},{4,0},{5,1},{6,2},{7,3},{8,12},{9,13},{10,... | collective-permute-start | bytes 111752 | tf_op jit(solution)/shard_map/ppermute | solution.py:21
  36.4 2.4 %collective-permute-done.18 = f32[96,97]{1,0:T(8,128)S(1)} collective-permute-done((f32[96,97]{1,0:T(8,128)S(1)}, f32[96,97]{1,0:T(8,128)S(1)}, u32[]{:S(2)}, u32[]{:S(2)}) %collective-permute-start.18) | collective-permute-done | bytes 37280 | tf_op jit(solution)/shard_map/ppermute | solution.py:21
  38.8 2.9 %collective-permute-start.19 = (f32[96,97]{1,0:T(8,128)S(1)}, f32[96,97]{1,0:T(8,128)S(1)}, u32[]{:S(2)}, u32[]{:S(2)}) collective-permute-start(f32[96,97]{1,0:T(8,128)S(1)} %add.29), channel_id=1, source_target_pairs={{0,8},{1,9},{2,10},{3,11},{4,12},{5,13},{6,14},{7,15},{8,0},{9,1},... | collective-permute-start | bytes 111752 | tf_op jit(solution)/shard_map/ppermute | solution.py:21
  41.6 2.7 %collective-permute-done.19 = f32[96,97]{1,0:T(8,128)S(1)} collective-permute-done((f32[96,97]{1,0:T(8,128)S(1)}, f32[96,97]{1,0:T(8,128)S(1)}, u32[]{:S(2)}, u32[]{:S(2)}) %collective-permute-start.19) | collective-permute-done | bytes 37280 | tf_op jit(solution)/shard_map/ppermute | solution.py:21
  44.3 6.4 %orthonormal_basis.1 = (f32[2,96,96]{2,1,0:T(8,128)}, bf16[192,192]{1,0:T(8,128)(2,1)S(1)}, bf16[192,192]{1,0:T(8,128)(2,1)S(1)}, bf16[192,192]{1,0:T(8,128)(2,1)S(1)}, bf16[192,192]{1,0:T(8,128)(2,1)S(1)}) custom-call(f32[288,97]{1,0:T(8,128)S(1)} %get-tuple-element.46.refs_0_, f32[288,97]{1,0:T(8,128)S(1)} %get-tuple-element.47.refs_1_, ...), custom_call_target="tpu_custom_call" | custom-call | flops 1500000000 | bytes 1000000 | tf_op jit(solution)/shard_map/orthonormal_basis/pallas_call | solution.py:281
  50.7 1.0 %project_rows.1 = (f32[2,192,336]{2,1,0:T(8,128)S(1)}, f32[2,192,336]{2,1,0:T(8,128)S(1)}, f32[192,336]{1,0:T(8,128)S(1)}, f32[192,336]{1,0:T(8,128)S(1)}) custom-call(f32[96,97]{1,0:T(8,128)S(1)} %add.30.refs_4_.gram_ref, bf16[192,192]{1,0:T(8,128)(2,1)S(1)} %get-tuple-element.49.refs_0_, bf16[192,192]{1,0:T(8,128)(2,1)S(1)} %get-tuple-element.50.refs_1_, ...), custom_call_target="tpu_custom_call" | custom-call | tf_op jit(solution)/shard_map/project_rows/pallas_call | solution.py:292
  51.7 1.6 %collective-permute-start.22 = (f16[2,192,336]{2,1,0:T(8,128)(2,1)S(1)}, f16[2,192,336]{2,1,0:T(8,128)(2,1)S(1)}, u32[]{:S(2)}, u32[]{:S(2)}) collective-permute-start(f16[2,192,336]{2,1,0:T(8,128)(2,1)S(1)} %convert_element_type.27), channel_id=1, source_target_pairs={{0,2},{1,3},{2,0},{3,1},{4,6},{5,7},{6,4},{7,5},{8,10},{9,11},{10,... | collective-permute-start | bytes 774152 | tf_op jit(solution)/shard_map/ppermute | solution.py:21
  53.4 2.3 %collective-permute-start.24 = (f16[192,336]{1,0:T(8,128)(2,1)S(1)}, f16[192,336]{1,0:T(8,128)(2,1)S(1)}, u32[]{:S(2)}, u32[]{:S(2)}) collective-permute-start(f16[192,336]{1,0:T(8,128)(2,1)S(1)} %convert_element_type.31), channel_id=1, source_target_pairs={{0,8},{1,9},{2,10},{3,11},{4,12},{5,13},{6,14},{7,15},{8,0},{9,1},... | collective-permute-start | bytes 387080 | tf_op jit(solution)/shard_map/ppermute | solution.py:21
  55.8 1.5 %collective-permute-start.23 = (f16[192,336]{1,0:T(8,128)(2,1)S(1)}, f16[192,336]{1,0:T(8,128)(2,1)S(1)}, u32[]{:S(2)}, u32[]{:S(2)}) collective-permute-start(f16[192,336]{1,0:T(8,128)(2,1)S(1)} %convert_element_type.29), channel_id=1, source_target_pairs={{0,12},{1,13},{2,14},{3,15},{4,8},{5,9},{6,10},{7,11},{8,4},{9,5},... | collective-permute-start | bytes 387080 | tf_op jit(solution)/shard_map/ppermute | solution.py:21
  57.3 1.8 %collective-permute-done.22 = f16[2,192,336]{2,1,0:T(8,128)(2,1)S(1)} collective-permute-done((f16[2,192,336]{2,1,0:T(8,128)(2,1)S(1)}, f16[2,192,336]{2,1,0:T(8,128)(2,1)S(1)}, u32[]{:S(2)}, u32[]{:S(2)}) %collective-permute-start.22) | collective-permute-done | bytes 258080 | tf_op jit(solution)/shard_map/ppermute | solution.py:21
  59.2 1.6 %collective-permute-start.25 = (f16[192,336]{1,0:T(8,128)(2,1)S(1)}, f16[192,336]{1,0:T(8,128)(2,1)S(1)}, u32[]{:S(2)}, u32[]{:S(2)}) collective-permute-start(f16[192,336]{1,0:T(8,128)(2,1)S(1)} %fusion.4), channel_id=1, source_target_pairs={{0,4},{1,5},{2,6},{3,7},{4,0},{5,1},{6,2},{7,3},{8,12},{9,13},{10,... | collective-permute-start | bytes 387080 | tf_op jit(solution)/shard_map/ppermute | solution.py:21
  60.8 0.6 slice.31
  62.0 4.0 %collective-permute-done.24 = f16[192,336]{1,0:T(8,128)(2,1)S(1)} collective-permute-done((f16[192,336]{1,0:T(8,128)(2,1)S(1)}, f16[192,336]{1,0:T(8,128)(2,1)S(1)}, u32[]{:S(2)}, u32[]{:S(2)}) %collective-permute-start.24) | collective-permute-done | bytes 129056 | tf_op jit(solution)/shard_map/ppermute | solution.py:21
  66.6 0.8 %fusion.3 = f32[192,336]{1,0:T(8,128)} fusion(f32[2,192,336]{2,1,0:T(8,128)S(1)} %convert_element_type.28, f16[192,336]{1,0:T(8,128)(2,1)S(1)} %collective-permute-done.25, f16[192,336]{1,0:T(8,128)(2,1)S(1)} %collective-permute-done.24, f16[192,336]{1,0:T(8,128)(2,1)S(1)} %collective-permute-done.23, f32[2,192,336]{2,1,0:T(8,128)S(1)} %get-tuple-element.56, ...), kind=kLoop, calls=%fused_computation.5 | loop fusion | flops 516096 | bytes 1161220 | tf_op jit(solution)/shard_map/mul | solution.py:318
  (39 shorter events, 3.5 us)
Async XLA Ops:
  0.6 11.4 %collective-permute-start.8 = (bf16[1,192,336]{2,1,0:T(8,128)(2,1)}, bf16[1,192,336]{2,1,0:T(8,128)(2,1)S(1)}, u32[]{:S(2)}, u32[]{:S(2)}) collective-permute-start(bf16[1,192,336]{2,1,0:T(8,128)(2,1)} %bitcast.12), channel_id=1, source_target_pairs={{0,8},{1,9},{2,10},{3,11},{4,12},{5,13},{6,14},{7,15},{8,0},{9,1},... | collective-permute-start | bytes 387080 | tf_op jit(solution)/shard_map/ppermute | solution.py:21
  4.7 7.5 %collective-permute-start.9 = (bf16[1,192,336]{2,1,0:T(8,128)(2,1)}, bf16[1,192,336]{2,1,0:T(8,128)(2,1)S(1)}, u32[]{:S(2)}, u32[]{:S(2)}) collective-permute-start(bf16[1,192,336]{2,1,0:T(8,128)(2,1)} %bitcast.13), channel_id=1, source_target_pairs={{0,4},{1,5},{2,6},{3,7},{4,0},{5,1},{6,2},{7,3},{8,12},{9,13},{10,... | collective-permute-start | bytes 387080 | tf_op jit(solution)/shard_map/ppermute | solution.py:21
  6.3 6.3 %collective-permute-start.10 = (bf16[1,192,336]{2,1,0:T(8,128)(2,1)}, bf16[1,192,336]{2,1,0:T(8,128)(2,1)S(1)}, u32[]{:S(2)}, u32[]{:S(2)}) collective-permute-start(bf16[1,192,336]{2,1,0:T(8,128)(2,1)} %bitcast.14), channel_id=1, source_target_pairs={{0,2},{1,3},{2,0},{3,1},{4,6},{5,7},{6,4},{7,5},{8,10},{9,11},{10,... | collective-permute-start | bytes 387080 | tf_op jit(solution)/shard_map/ppermute | solution.py:21
  7.8 1.6 %copy-start = (bf16[2,96,5376]{2,1,0:T(8,128)(2,1)S(1)}, bf16[2,96,5376]{2,1,0:T(8,128)(2,1)}, u32[]{:S(2)}) copy-start(bf16[2,96,5376]{2,1,0:T(8,128)(2,1)} %traces_ref.1) | copy-start | bytes 6193156
  9.4 15.1 %copy-start.1 = (bf16[2,96,336]{2,1,0:T(8,128)(2,1)S(1)}, bf16[2,96,336]{2,1,0:T(8,128)(2,1)}, u32[]{:S(2)}) copy-start(bf16[2,96,336]{2,1,0:T(8,128)(2,1)} %param.3) | copy-start | bytes 387076
  10.9 1.8 %collective-permute-start = (bf16[1,192,336]{2,1,0:T(8,128)(2,1)S(1)}, bf16[1,192,336]{2,1,0:T(8,128)(2,1)S(1)}, u32[]{:S(2)}, u32[]{:S(2)}) collective-permute-start(bf16[1,192,336]{2,1,0:T(8,128)(2,1)S(1)} %get-tuple-element.35), channel_id=1, source_target_pairs={{0,1},{1,0},{2,3},{3,2},{4,5},{5,4},{6,7},{7,6},{8,9},{9,8},{10,11... | collective-permute-start | bytes 387080 | tf_op jit(solution)/shard_map/ppermute | solution.py:21
  11.0 2.1 %collective-permute-start.1 = (bf16[1,192,336]{2,1,0:T(8,128)(2,1)S(1)}, bf16[1,192,336]{2,1,0:T(8,128)(2,1)S(1)}, u32[]{:S(2)}, u32[]{:S(2)}) collective-permute-start(bf16[1,192,336]{2,1,0:T(8,128)(2,1)S(1)} %get-tuple-element.36), channel_id=1, source_target_pairs={{0,1},{1,0},{2,3},{3,2},{4,5},{5,4},{6,7},{7,6},{8,9},{9,8},{10,11... | collective-permute-start | bytes 387080 | tf_op jit(solution)/shard_map/ppermute | solution.py:21
  12.1 2.3 %collective-permute-start.2 = (bf16[1,192,336]{2,1,0:T(8,128)(2,1)S(1)}, bf16[1,192,336]{2,1,0:T(8,128)(2,1)S(1)}, u32[]{:S(2)}, u32[]{:S(2)}) collective-permute-start(bf16[1,192,336]{2,1,0:T(8,128)(2,1)S(1)} %get-tuple-element.37), channel_id=1, source_target_pairs={{0,1},{1,0},{2,3},{3,2},{4,5},{5,4},{6,7},{7,6},{8,9},{9,8},{10,11... | collective-permute-start | bytes 387080 | tf_op jit(solution)/shard_map/ppermute | solution.py:21
  12.2 2.2 %collective-permute-start.3 = (bf16[1,192,336]{2,1,0:T(8,128)(2,1)S(1)}, bf16[1,192,336]{2,1,0:T(8,128)(2,1)S(1)}, u32[]{:S(2)}, u32[]{:S(2)}) collective-permute-start(bf16[1,192,336]{2,1,0:T(8,128)(2,1)S(1)} %get-tuple-element.38), channel_id=1, source_target_pairs={{0,1},{1,0},{2,3},{3,2},{4,5},{5,4},{6,7},{7,6},{8,9},{9,8},{10,11... | collective-permute-start | bytes 387080 | tf_op jit(solution)/shard_map/ppermute | solution.py:21
  12.6 2.3 %collective-permute-start.4 = (bf16[1,192,336]{2,1,0:T(8,128)(2,1)S(1)}, bf16[1,192,336]{2,1,0:T(8,128)(2,1)S(1)}, u32[]{:S(2)}, u32[]{:S(2)}) collective-permute-start(bf16[1,192,336]{2,1,0:T(8,128)(2,1)S(1)} %get-tuple-element.39), channel_id=1, source_target_pairs={{0,1},{1,0},{2,3},{3,2},{4,5},{5,4},{6,7},{7,6},{8,9},{9,8},{10,11... | collective-permute-start | bytes 387080 | tf_op jit(solution)/shard_map/ppermute | solution.py:21
  12.8 3.6 %collective-permute-start.5 = (bf16[1,192,336]{2,1,0:T(8,128)(2,1)S(1)}, bf16[1,192,336]{2,1,0:T(8,128)(2,1)S(1)}, u32[]{:S(2)}, u32[]{:S(2)}) collective-permute-start(bf16[1,192,336]{2,1,0:T(8,128)(2,1)S(1)} %get-tuple-element.40), channel_id=1, source_target_pairs={{0,1},{1,0},{2,3},{3,2},{4,5},{5,4},{6,7},{7,6},{8,9},{9,8},{10,11... | collective-permute-start | bytes 387080 | tf_op jit(solution)/shard_map/ppermute | solution.py:21
  13.1 6.1 %collective-permute-start.13 = (bf16[1,192,336]{2,1,0:T(8,128)(2,1)S(1)}, bf16[1,192,336]{2,1,0:T(8,128)(2,1)S(1)}, u32[]{:S(2)}, u32[]{:S(2)}) collective-permute-start(bf16[1,192,336]{2,1,0:T(8,128)(2,1)S(1)} %collective-permute-done.8.refs_11_), channel_id=1, source_target_pairs={{0,4},{1,5},{2,6},{3,7},{4,0},{5,1},{6,2},{7,3},{8,12},{9,13},{10,... | collective-permute-start | bytes 387080 | tf_op jit(solution)/shard_map/ppermute | solution.py:21
  14.3 7.0 %collective-permute-start.6 = (bf16[1,192,336]{2,1,0:T(8,128)(2,1)S(1)}, bf16[1,192,336]{2,1,0:T(8,128)(2,1)S(1)}, u32[]{:S(2)}, u32[]{:S(2)}) collective-permute-start(bf16[1,192,336]{2,1,0:T(8,128)(2,1)S(1)} %get-tuple-element.41), channel_id=1, source_target_pairs={{0,1},{1,0},{2,3},{3,2},{4,5},{5,4},{6,7},{7,6},{8,9},{9,8},{10,11... | collective-permute-start | bytes 387080 | tf_op jit(solution)/shard_map/ppermute | solution.py:21
  14.5 6.8 %collective-permute-start.7 = (bf16[1,192,336]{2,1,0:T(8,128)(2,1)S(1)}, bf16[1,192,336]{2,1,0:T(8,128)(2,1)S(1)}, u32[]{:S(2)}, u32[]{:S(2)}) collective-permute-start(bf16[1,192,336]{2,1,0:T(8,128)(2,1)S(1)} %get-tuple-element.42), channel_id=1, source_target_pairs={{0,1},{1,0},{2,3},{3,2},{4,5},{5,4},{6,7},{7,6},{8,9},{9,8},{10,11... | collective-permute-start | bytes 387080 | tf_op jit(solution)/shard_map/ppermute | solution.py:21
  14.8 7.3 %collective-permute-start.12 = (bf16[1,192,336]{2,1,0:T(8,128)(2,1)S(1)}, bf16[1,192,336]{2,1,0:T(8,128)(2,1)S(1)}, u32[]{:S(2)}, u32[]{:S(2)}) collective-permute-start(bf16[1,192,336]{2,1,0:T(8,128)(2,1)S(1)} %collective-permute-done.8.refs_11_), channel_id=1, source_target_pairs={{0,2},{1,3},{2,0},{3,1},{4,6},{5,7},{6,4},{7,5},{8,10},{9,11},{10,... | collective-permute-start | bytes 387080 | tf_op jit(solution)/shard_map/ppermute | solution.py:21
  16.3 5.9 %collective-permute-start.11 = (bf16[1,192,336]{2,1,0:T(8,128)(2,1)S(1)}, bf16[1,192,336]{2,1,0:T(8,128)(2,1)S(1)}, u32[]{:S(2)}, u32[]{:S(2)}) collective-permute-start(bf16[1,192,336]{2,1,0:T(8,128)(2,1)S(1)} %collective-permute-done.10.refs_9_), channel_id=1, source_target_pairs={{0,4},{1,5},{2,6},{3,7},{4,0},{5,1},{6,2},{7,3},{8,12},{9,13},{10,... | collective-permute-start | bytes 387080 | tf_op jit(solution)/shard_map/ppermute | solution.py:21
  19.2 5.3 %collective-permute-start.14 = (bf16[1,192,336]{2,1,0:T(8,128)(2,1)S(1)}, bf16[1,192,336]{2,1,0:T(8,128)(2,1)S(1)}, u32[]{:S(2)}, u32[]{:S(2)}) collective-permute-start(bf16[1,192,336]{2,1,0:T(8,128)(2,1)S(1)} %collective-permute-done.13.refs_14_), channel_id=1, source_target_pairs={{0,2},{1,3},{2,0},{3,1},{4,6},{5,7},{6,4},{7,5},{8,10},{9,11},{10,... | collective-permute-start | bytes 387080 | tf_op jit(solution)/shard_map/ppermute | solution.py:21
  25.6 1.5 %collective-permute-start.15 = (f32[2,2,96,97]{3,2,1,0:T(8,128)S(1)}, f32[2,2,96,97]{3,2,1,0:T(8,128)S(1)}, u32[]{:S(2)}, u32[]{:S(2)}) collective-permute-start(f32[2,2,96,97]{3,2,1,0:T(8,128)S(1)} %sketch_rows.1.part_ref), channel_id=1, source_target_pairs={{0,1},{1,0},{2,3},{3,2},{4,5},{5,4},{6,7},{7,6},{8,9},{9,8},{10,11... | collective-permute-start | bytes 446984 | tf_op jit(solution)/shard_map/ppermute | solution.py:21
  27.9 6.7 %collective-permute-start.16 = (f32[288,97]{1,0:T(8,128)S(1)}, f32[288,97]{1,0:T(8,128)S(1)}, u32[]{:S(2)}, u32[]{:S(2)}) collective-permute-start(f32[288,97]{1,0:T(8,128)S(1)} %get-tuple-element.46.refs_0_), channel_id=1, source_target_pairs={{0,2},{1,3},{2,0},{3,1},{4,6},{5,7},{6,4},{7,5},{8,10},{9,11},{10,... | collective-permute-start | bytes 335240 | tf_op jit(solution)/shard_map/ppermute | solution.py:21
  30.0 20.7 %collective-permute-start.20 = (bf16[2,192,336]{2,1,0:T(8,128)(2,1)S(1)}, bf16[2,192,336]{2,1,0:T(8,128)(2,1)S(1)}, u32[]{:S(2)}, u32[]{:S(2)}) collective-permute-start(bf16[2,192,336]{2,1,0:T(8,128)(2,1)S(1)} %get-tuple-element.54.far_ref), channel_id=1, source_target_pairs={{0,2},{1,3},{2,0},{3,1},{4,6},{5,7},{6,4},{7,5},{8,10},{9,11},{10,... | collective-permute-start | bytes 774152 | tf_op jit(solution)/shard_map/ppermute | solution.py:21
  30.0 20.7 %collective-permute-start.21 = (bf16[2,192,336]{2,1,0:T(8,128)(2,1)S(1)}, bf16[2,192,336]{2,1,0:T(8,128)(2,1)S(1)}, u32[]{:S(2)}, u32[]{:S(2)}) collective-permute-start(bf16[2,192,336]{2,1,0:T(8,128)(2,1)S(1)} %get-tuple-element.55), channel_id=1, source_target_pairs={{0,3},{1,2},{2,1},{3,0},{4,7},{5,6},{6,5},{7,4},{8,11},{9,10},{10,... | collective-permute-start | bytes 774152 | tf_op jit(solution)/shard_map/ppermute | solution.py:21
  34.6 9.7 %collective-permute-start.17 = (f32[288,97]{1,0:T(8,128)S(1)}, f32[288,97]{1,0:T(8,128)S(1)}, u32[]{:S(2)}, u32[]{:S(2)}) collective-permute-start(f32[288,97]{1,0:T(8,128)S(1)} %collective-permute-done.16.refs_2_), channel_id=1, source_target_pairs={{0,1},{1,0},{2,3},{3,2},{4,5},{5,4},{6,7},{7,6},{8,9},{9,8},{10,11... | collective-permute-start | bytes 335240 | tf_op jit(solution)/shard_map/ppermute | solution.py:21
  34.6 4.2 %collective-permute-start.18 = (f32[96,97]{1,0:T(8,128)S(1)}, f32[96,97]{1,0:T(8,128)S(1)}, u32[]{:S(2)}, u32[]{:S(2)}) collective-permute-start(f32[96,97]{1,0:T(8,128)S(1)} %slice_add_fusion.2), channel_id=1, source_target_pairs={{0,4},{1,5},{2,6},{3,7},{4,0},{5,1},{6,2},{7,3},{8,12},{9,13},{10,... | collective-permute-start | bytes 111752 | tf_op jit(solution)/shard_map/ppermute | solution.py:21
  38.8 5.5 %collective-permute-start.19 = (f32[96,97]{1,0:T(8,128)S(1)}, f32[96,97]{1,0:T(8,128)S(1)}, u32[]{:S(2)}, u32[]{:S(2)}) collective-permute-start(f32[96,97]{1,0:T(8,128)S(1)} %add.29), channel_id=1, source_target_pairs={{0,8},{1,9},{2,10},{3,11},{4,12},{5,13},{6,14},{7,15},{8,0},{9,1},... | collective-permute-start | bytes 111752 | tf_op jit(solution)/shard_map/ppermute | solution.py:21
  51.7 7.4 %collective-permute-start.22 = (f16[2,192,336]{2,1,0:T(8,128)(2,1)S(1)}, f16[2,192,336]{2,1,0:T(8,128)(2,1)S(1)}, u32[]{:S(2)}, u32[]{:S(2)}) collective-permute-start(f16[2,192,336]{2,1,0:T(8,128)(2,1)S(1)} %convert_element_type.27), channel_id=1, source_target_pairs={{0,2},{1,3},{2,0},{3,1},{4,6},{5,7},{6,4},{7,5},{8,10},{9,11},{10,... | collective-permute-start | bytes 774152 | tf_op jit(solution)/shard_map/ppermute | solution.py:21
  53.4 12.7 %collective-permute-start.24 = (f16[192,336]{1,0:T(8,128)(2,1)S(1)}, f16[192,336]{1,0:T(8,128)(2,1)S(1)}, u32[]{:S(2)}, u32[]{:S(2)}) collective-permute-start(f16[192,336]{1,0:T(8,128)(2,1)S(1)} %convert_element_type.31), channel_id=1, source_target_pairs={{0,8},{1,9},{2,10},{3,11},{4,12},{5,13},{6,14},{7,15},{8,0},{9,1},... | collective-permute-start | bytes 387080 | tf_op jit(solution)/shard_map/ppermute | solution.py:21
  55.8 10.3 %collective-permute-start.23 = (f16[192,336]{1,0:T(8,128)(2,1)S(1)}, f16[192,336]{1,0:T(8,128)(2,1)S(1)}, u32[]{:S(2)}, u32[]{:S(2)}) collective-permute-start(f16[192,336]{1,0:T(8,128)(2,1)S(1)} %convert_element_type.29), channel_id=1, source_target_pairs={{0,12},{1,13},{2,14},{3,15},{4,8},{5,9},{6,10},{7,11},{8,4},{9,5},... | collective-permute-start | bytes 387080 | tf_op jit(solution)/shard_map/ppermute | solution.py:21
  59.2 7.4 %collective-permute-start.25 = (f16[192,336]{1,0:T(8,128)(2,1)S(1)}, f16[192,336]{1,0:T(8,128)(2,1)S(1)}, u32[]{:S(2)}, u32[]{:S(2)}) collective-permute-start(f16[192,336]{1,0:T(8,128)(2,1)S(1)} %fusion.4), channel_id=1, source_target_pairs={{0,4},{1,5},{2,6},{3,7},{4,0},{5,1},{6,2},{7,3},{8,12},{9,13},{10,... | collective-permute-start | bytes 387080 | tf_op jit(solution)/shard_map/ppermute | solution.py:21

commit v7 on v6

--- a/solution.py
+++ b/solution.py
@@ -114,32 +114,95 @@
     blocks = count // ROWS
     re = [real[ROWS * i : ROWS * (i + 1)] for i in range(blocks)]
     im = [imag[ROWS * i : ROWS * (i + 1)] for i in range(blocks)]
+    out_re, out_im = [], []
+    spread = lambda value: jnp.broadcast_to(value, (ROWS, width))
+    pick = lambda value, at: spread(value[at : at + 1])
+    solved = None
     for b in range(blocks):
-        col_re, col_im = [], []
-        for o in range(ROWS):
-            k = ROWS * b + o
-            col_re.append([jnp.broadcast_to(re[i][:, k : k + 1], (ROWS, width)) for i in range(b, blocks)])
-            col_im.append([jnp.broadcast_to(im[i][:, k : k + 1], (ROWS, width)) for i in range(b, blocks)])
-        for o in range(ROWS):
-            hit = lane == ROWS * b + o
-            scale = lax.rsqrt(col_re[o][0][o : o + 1])
-            pivot_re = jnp.where(hit[:1], scale, re[b][o : o + 1] * scale)
-            pivot_im = jnp.where(hit[:1], 0.0, im[b][o : o + 1] * scale)
-            by_re = [v * scale for v in col_re[o]]
-            by_im = [v * scale for v in col_im[o]]
-            for j in range(o + 1, ROWS):
-                x_re, x_im = by_re[0][j : j + 1], by_im[0][j : j + 1]
-                for q in range(blocks - b):
-                    col_re[j][q] = col_re[j][q] - (by_re[q] * x_re + by_im[q] * x_im)
-                    col_im[j][q] = col_im[j][q] - (by_im[q] * x_re - by_re[q] * x_im)
-            for q, i in enumerate(range(b, blocks)):
-                new_re = jnp.where(hit, 0.0, re[i]) - (by_re[q] * pivot_re - by_im[q] * pivot_im)
-                new_im = jnp.where(hit, 0.0, im[i]) - (by_re[q] * pivot_im + by_im[q] * pivot_re)
-                if i == b:
-                    new_re = jnp.where(row > o, new_re, jnp.where(row == o, pivot_re, re[i]))
-                    new_im = jnp.where(row > o, new_im, jnp.where(row == o, pivot_im, im[i]))
-                re[i], im[i] = new_re, new_im
-    return jnp.concatenate(re, axis=0), jnp.concatenate(im, axis=0)
+        first = ROWS * b
+        if b:
+            old = first - ROWS
+            cleared = (lane >= old) & (lane < first)
+            next_re, next_im = jnp.where(cleared, 0.0, re[b]), jnp.where(cleared, 0.0, im[b])
+            parts_re, parts_im = [], []
+            for o in range(ROWS):
+                c_re, c_im = spread(re[b][:, old + o : old + o + 1]), spread(im[b][:, old + o : old + o + 1])
+                s_re, s_im = pick(solved[0], o), pick(solved[1], o)
+                parts_re.append(c_re * s_re - c_im * s_im)
+                parts_im.append(c_re * s_im + c_im * s_re)
+            while len(parts_re) > 1:
+                parts_re = [left + right for left, right in zip(parts_re[0::2], parts_re[1::2])]
+                parts_im = [left + right for left, right in zip(parts_im[0::2], parts_im[1::2])]
+            re[b], im[b] = next_re - parts_re[0], next_im - parts_im[0]
+            if b + 1 < blocks:
+                rest_re, rest_im = jnp.concatenate(re[b + 1 :]), jnp.concatenate(im[b + 1 :])
+                columns = jnp.concatenate([rest_re[:, old:first], rest_im[:, old:first]], axis=1)
+                weights = jnp.concatenate(
+                    [
+                        jnp.concatenate([solved[0], solved[1]], axis=1),
+                        jnp.concatenate([-solved[1], solved[0]], axis=1),
+                    ]
+                )
+                taken = exact(columns, weights, ((1,), (0,)))
+                for at, i in enumerate(range(b + 1, blocks)):
+                    some = slice(ROWS * at, ROWS * (at + 1))
+                    re[i] = jnp.where(cleared, 0.0, re[i]) - taken[some, :width]
+                    im[i] = jnp.where(cleared, 0.0, im[i]) - taken[some, width:]
+        x_re, x_im = re[b], im[b]
+        done_re, done_im = x_re, x_im
+        col_re = [spread(x_re[:, first + o : first + o + 1]) for o in range(ROWS)]
+        col_im = [spread(x_im[:, first + o : first + o + 1]) for o in range(ROWS)]
+        live_re, live_im = list(col_re), list(col_im)
+        for o in range(0, ROWS, 2):
+            hit0, hit1 = lane == first + o, lane == first + o + 1
+            hit = hit0 | hit1
+            row0 = row == o
+            pair = row0 | (row == o + 1)
+            a, c = pick(live_re[o], o), pick(live_re[o + 1], o + 1)
+            f_re, f_im = pick(live_re[o], o + 1), pick(live_im[o], o + 1)
+            root = lax.rsqrt(a * c - (f_re * f_re + f_im * f_im))
+            inverse = root * root
+
+            def solve(re0, im0, re1, im1):
+                return (
+                    c * re0 - (f_re * re1 + f_im * im1),
+                    c * im0 - (f_re * im1 - f_im * re1),
+                    a * re1 - (f_re * re0 - f_im * im0),
+                    a * im1 - (f_re * im0 + f_im * re0),
+                )
+
+            def less(z0_re, z0_im, z1_re, z1_im):
+                return (
+                    (col_re[o] * z0_re - col_im[o] * z0_im) + (col_re[o + 1] * z1_re - col_im[o + 1] * z1_im),
+                    (col_re[o] * z0_im + col_im[o] * z0_re) + (col_re[o + 1] * z1_im + col_im[o + 1] * z1_re),
+                )
+
+            for j in range(o + 2, ROWS):
+                z = solve(pick(live_re[j], o), pick(live_im[j], o), pick(live_re[j], o + 1), pick(live_im[j], o + 1))
+                off_re, off_im = less(*z)
+                live_re[j] = col_re[j] - off_re * inverse
+                live_im[j] = col_im[j] - off_im * inverse
+                col_re[j] = jnp.where(pair, jnp.where(row0, z[0], z[2]) * inverse, live_re[j])
+                col_im[j] = jnp.where(pair, jnp.where(row0, z[1], z[3]) * inverse, live_im[j])
+            re0 = jnp.where(hit0, 1.0, jnp.where(hit1, 0.0, pick(x_re, o)))
+            re1 = jnp.where(hit1, 1.0, jnp.where(hit0, 0.0, pick(x_re, o + 1)))
+            im0, im1 = jnp.where(hit, 0.0, pick(x_im, o)), jnp.where(hit, 0.0, pick(x_im, o + 1))
+            z = solve(re0, im0, re1, im1)
+            scale0 = lax.rsqrt(a)
+            scale1 = root * scale0
+            done_re = jnp.where(row0, re0 * scale0, jnp.where(pair, z[2] * scale1, done_re))
+            done_im = jnp.where(row0, im0 * scale0, jnp.where(pair, z[3] * scale1, done_im))
+            off_re, off_im = less(*z)
+            x_re = jnp.where(
+                pair, jnp.where(row0, z[0], z[2]) * inverse, jnp.where(hit, 0.0, x_re) - off_re * inverse
+            )
+            x_im = jnp.where(
+                pair, jnp.where(row0, z[1], z[3]) * inverse, jnp.where(hit, 0.0, x_im) - off_im * inverse
+            )
+        out_re.append(done_re)
+        out_im.append(done_im)
+        solved = (x_re, x_im)
+    return jnp.concatenate(out_re), jnp.concatenate(out_im)
 
 
 def basis_kernel(scale, *refs):
@@ -152,9 +215,15 @@
     column = lax.broadcasted_iota(jnp.int32, packed.shape, 1)
     gram_re = jnp.where(row <= column, packed, flipped)
     gram_im = jnp.where(row > column, packed, jnp.where(row < column, -flipped, 0.0))
-    low_re, low_im = eliminate(gram_re, gram_im)
-    low_re = jnp.where(row >= column, low_re, 0.0)
-    low_im = jnp.where(row >= column, low_im, 0.0)
+    diagonal = jnp.where(row == column, gram_re, 0.0)
+    across = lax.rsqrt(jnp.sum(diagonal, axis=0, keepdims=True))
+    down = lax.rsqrt(jnp.sum(diagonal, axis=1, keepdims=True))
+    padding = [(0, 0), (0, -count % 128)]
+    low_re, low_im = eliminate(
+        jnp.pad(gram_re * down * across, padding), jnp.pad(gram_im * down * across, padding)
+    )
+    low_re = jnp.where(row >= column, low_re[:, :count] * across, 0.0)
+    low_im = jnp.where(row >= column, low_im[:, :count] * across, 0.0)
     stacked = jnp.concatenate([ref[count:, :count] for ref in sketched], axis=0)
     by_re = exact(stacked, low_re, ((1,), (1,)))
     by_im = exact(stacked, low_im, ((1,), (1,)))

time: 67.5 us -> 66.4 us (0.984)
  Pallas kernels: 10.8 us -> 9.71 us
    pallas_call x1, Pallas kernels: 6.38 us -> 5.24 us  [per_device(): pl.pallas_call(functools.partial(basis_kernel, math.sqrt(rows * size)), o...]
  transfers between devices with their start and end apart: 26 -> 26, of which waited for: 12 -> 12; matrix products, arithmetic and copies ran while one was open for 1% -> 1% of each run, Pallas kernels for 12% -> 10%
where the time goes in v7:
time: 66.4 us; the launch traced here: 66.2 us
  starting transfers between devices  29.9 us (45%)
  waiting for transfers between devices  22.1 us (33%)
  Pallas kernels  9.71 us (15%)
  local copies, waits for them, and re-layouts  2.16 us (3%)
  between operations  1.38 us (2%)
  other arithmetic  0.97 us (1%)
    ppermute x26, starting transfers between devices, swap(): return lax.ppermute(value, 'rcv', [(i, i ^ mask) for i in range(size)])  29.9 us
    ppermute x26, waiting for transfers between devices, swap(): return lax.ppermute(value, 'rcv', [(i, i ^ mask) for i in range(size)])  22.1 us
    pallas_call x1, Pallas kernels, per_device(): pl.pallas_call(functools.partial(basis_kernel, math.sqrt(rows * size)), o...  5.24 us
    unnamed x4, local copies, waits for them, and re-layouts  1.58 us
    pallas_call x1, Pallas kernels, per_device(): pl.pallas_call(functools.partial(chunk_kernel, share), out_shape=(chunk(z...  1.56 us
  transfers between devices with their start and end apart: 26, of which 12 were waited for; matrix products, arithmetic and copies ran while one was open for 1% of the time, Pallas kernels for 10%

profile of v7, /device:TPU:0, one launch (start us, length us, event | category | flops | bytes accessed | tf_op | source)
XLA Modules:
  0.0 66.2 jit_solution(5599764966461808460)
XLA Ops:
  0.6 4.1 %collective-permute-start.8 = (bf16[1,192,336]{2,1,0:T(8,128)(2,1)}, bf16[1,192,336]{2,1,0:T(8,128)(2,1)S(1)}, u32[]{:S(2)}, u32[]{:S(2)}) collective-permute-start(bf16[1,192,336]{2,1,0:T(8,128)(2,1)} %bitcast.12), channel_id=1, source_target_pairs={{0,8},{1,9},{2,10},{3,11},{4,12},{5,13},{6,14},{7,15},{8,0},{9,1},... | collective-permute-start | bytes 387080 | tf_op jit(solution)/shard_map/ppermute | solution.py:21
  4.7 1.6 %collective-permute-start.9 = (bf16[1,192,336]{2,1,0:T(8,128)(2,1)}, bf16[1,192,336]{2,1,0:T(8,128)(2,1)S(1)}, u32[]{:S(2)}, u32[]{:S(2)}) collective-permute-start(bf16[1,192,336]{2,1,0:T(8,128)(2,1)} %bitcast.13), channel_id=1, source_target_pairs={{0,4},{1,5},{2,6},{3,7},{4,0},{5,1},{6,2},{7,3},{8,12},{9,13},{10,... | collective-permute-start | bytes 387080 | tf_op jit(solution)/shard_map/ppermute | solution.py:21
  6.3 1.5 %collective-permute-start.10 = (bf16[1,192,336]{2,1,0:T(8,128)(2,1)}, bf16[1,192,336]{2,1,0:T(8,128)(2,1)S(1)}, u32[]{:S(2)}, u32[]{:S(2)}) collective-permute-start(bf16[1,192,336]{2,1,0:T(8,128)(2,1)} %bitcast.14), channel_id=1, source_target_pairs={{0,2},{1,3},{2,0},{3,1},{4,6},{5,7},{6,4},{7,5},{8,10},{9,11},{10,... | collective-permute-start | bytes 387080 | tf_op jit(solution)/shard_map/ppermute | solution.py:21
  7.8 1.6 %copy-done = bf16[2,96,5376]{2,1,0:T(8,128)(2,1)S(1)} copy-done((bf16[2,96,5376]{2,1,0:T(8,128)(2,1)S(1)}, bf16[2,96,5376]{2,1,0:T(8,128)(2,1)}, u32[]{:S(2)}) %copy-start) | copy-done | bytes 2064408
  9.4 1.6 %source_chunks.1 = (bf16[4,192,336]{2,1,0:T(8,128)(2,1)S(1)}, bf16[2,192,336]{2,1,0:T(8,128)(2,1)S(1)}, bf16[2,192,336]{2,1,0:T(8,128)(2,1)S(1)}, bf16[2,192,336...) custom-call(s32[1]{0:T(128)} %bitcast.me_ref, ...), custom_call_target="tpu_custom_call" | custom-call | tf_op jit(solution)/shard_map/source_chunks/pallas_call | solution.py:304
  13.1 1.2 %collective-permute-start.13 = (bf16[1,192,336]{2,1,0:T(8,128)(2,1)S(1)}, bf16[1,192,336]{2,1,0:T(8,128)(2,1)S(1)}, u32[]{:S(2)}, u32[]{:S(2)}) collective-permute-start(bf16[1,192,336]{2,1,0:T(8,128)(2,1)S(1)} %collective-permute-done.8.refs_11_), channel_id=1, source_target_pairs={{0,4},{1,5},{2,6},{3,7},{4,0},{5,1},{6,2},{7,3},{8,12},{9,13},{10,... | collective-permute-start | bytes 387080 | tf_op jit(solution)/shard_map/ppermute | solution.py:21
  14.8 1.5 %collective-permute-start.12 = (bf16[1,192,336]{2,1,0:T(8,128)(2,1)S(1)}, bf16[1,192,336]{2,1,0:T(8,128)(2,1)S(1)}, u32[]{:S(2)}, u32[]{:S(2)}) collective-permute-start(bf16[1,192,336]{2,1,0:T(8,128)(2,1)S(1)} %collective-permute-done.8.refs_11_), channel_id=1, source_target_pairs={{0,2},{1,3},{2,0},{3,1},{4,6},{5,7},{6,4},{7,5},{8,10},{9,11},{10,... | collective-permute-start | bytes 387080 | tf_op jit(solution)/shard_map/ppermute | solution.py:21
  16.3 0.8 %collective-permute-start.11 = (bf16[1,192,336]{2,1,0:T(8,128)(2,1)S(1)}, bf16[1,192,336]{2,1,0:T(8,128)(2,1)S(1)}, u32[]{:S(2)}, u32[]{:S(2)}) collective-permute-start(bf16[1,192,336]{2,1,0:T(8,128)(2,1)S(1)} %collective-permute-done.10.refs_9_), channel_id=1, source_target_pairs={{0,4},{1,5},{2,6},{3,7},{4,0},{5,1},{6,2},{7,3},{8,12},{9,13},{10,... | collective-permute-start | bytes 387080 | tf_op jit(solution)/shard_map/ppermute | solution.py:21
  17.2 2.0 %collective-permute-done.13.refs_14_ = bf16[1,192,336]{2,1,0:T(8,128)(2,1)S(1)} collective-permute-done((bf16[1,192,336]{2,1,0:T(8,128)(2,1)S(1)}, bf16[1,192,336]{2,1,0:T(8,128)(2,1)S(1)}, u32[]{:S(2)}, u32[]{:S(2)}) %collective-permute-start.13) | collective-permute-done | bytes 129056 | tf_op jit(solution)/shard_map/ppermute | solution.py:21
  19.2 2.1 %collective-permute-start.14 = (bf16[1,192,336]{2,1,0:T(8,128)(2,1)S(1)}, bf16[1,192,336]{2,1,0:T(8,128)(2,1)S(1)}, u32[]{:S(2)}, u32[]{:S(2)}) collective-permute-start(bf16[1,192,336]{2,1,0:T(8,128)(2,1)S(1)} %collective-permute-done.13.refs_14_), channel_id=1, source_target_pairs={{0,2},{1,3},{2,0},{3,1},{4,6},{5,7},{6,4},{7,5},{8,10},{9,11},{10,... | collective-permute-start | bytes 387080 | tf_op jit(solution)/shard_map/ppermute | solution.py:21
  21.3 0.9 %collective-permute-done.11.refs_12_ = bf16[1,192,336]{2,1,0:T(8,128)(2,1)S(1)} collective-permute-done((bf16[1,192,336]{2,1,0:T(8,128)(2,1)S(1)}, bf16[1,192,336]{2,1,0:T(8,128)(2,1)S(1)}, u32[]{:S(2)}, u32[]{:S(2)}) %collective-permute-start.11) | collective-permute-done | bytes 129056 | tf_op jit(solution)/shard_map/ppermute | solution.py:21
  22.2 2.2 %collective-permute-done.14.refs_15_ = bf16[1,192,336]{2,1,0:T(8,128)(2,1)S(1)} collective-permute-done((bf16[1,192,336]{2,1,0:T(8,128)(2,1)S(1)}, bf16[1,192,336]{2,1,0:T(8,128)(2,1)S(1)}, u32[]{:S(2)}, u32[]{:S(2)}) %collective-permute-start.14) | collective-permute-done | bytes 129056 | tf_op jit(solution)/shard_map/ppermute | solution.py:21
  24.4 1.2 %sketch_rows.1.part_ref = f32[2,2,96,97]{3,2,1,0:T(8,128)S(1)} custom-call(f32[1,5376]{1,0:T(1,128)S(1)} %get-tuple-element.31.peak_ref, bf16[4,192,336]{2,1,0:T(8,128)(2,1)S(1)} %get-tuple-element.32.stay_ref.refs_4_, bf16[2,192,336]{2,1,0:T(8,128)(2,1)S(1)} %get-tuple-element.33.near_ref.refs_5_, bf16[2,192,336]{2,1,0:T(8,128)(2,1)S(1)} %get-tuple-element.54.far_ref, ...), custom_call_target="tpu_custom_call" | custom-call | tf_op jit(solution)/shard_map/sketch_rows/pallas_call | solution.py:324
  25.7 1.4 %collective-permute-done.15.other_ref = f32[2,2,96,97]{3,2,1,0:T(8,128)S(1)} collective-permute-done((f32[2,2,96,97]{3,2,1,0:T(8,128)S(1)}, f32[2,2,96,97]{3,2,1,0:T(8,128)S(1)}, u32[]{:S(2)}, u32[]{:S(2)}) %collective-permute-start.15) | collective-permute-done | bytes 149024 | tf_op jit(solution)/shard_map/ppermute | solution.py:21
  27.1 0.7 %chip_gram.1 = (f32[288,97]{1,0:T(8,128)S(1)}, f32[288,97]{1,0:T(8,128)S(1)}) custom-call(f32[2,2,96,97]{3,2,1,0:T(8,128)S(1)} %sketch_rows.1.part_ref, f32[2,2,96,97]{3,2,1,0:T(8,128)S(1)} %collective-permute-done.15.other_ref), custom_call_target="tpu_custom_call" | custom-call | tf_op jit(solution)/shard_map/chip_gram/pallas_call | solution.py:333
  27.9 2.1 %collective-permute-start.16 = (f32[288,97]{1,0:T(8,128)S(1)}, f32[288,97]{1,0:T(8,128)S(1)}, u32[]{:S(2)}, u32[]{:S(2)}) collective-permute-start(f32[288,97]{1,0:T(8,128)S(1)} %get-tuple-element.46.refs_0_), channel_id=1, source_target_pairs={{0,2},{1,3},{2,0},{3,1},{4,6},{5,7},{6,4},{7,5},{8,10},{9,11},{10,... | collective-permute-start | bytes 335240 | tf_op jit(solution)/shard_map/ppermute | solution.py:21
  30.0 1.1 %collective-permute-start.21 = (bf16[2,192,336]{2,1,0:T(8,128)(2,1)S(1)}, bf16[2,192,336]{2,1,0:T(8,128)(2,1)S(1)}, u32[]{:S(2)}, u32[]{:S(2)}) collective-permute-start(bf16[2,192,336]{2,1,0:T(8,128)(2,1)S(1)} %get-tuple-element.55), channel_id=1, source_target_pairs={{0,3},{1,2},{2,1},{3,0},{4,7},{5,6},{6,5},{7,4},{8,11},{9,10},{10,... | collective-permute-start | bytes 774152 | tf_op jit(solution)/shard_map/ppermute | solution.py:21
  31.2 3.4 %collective-permute-done.16.refs_2_ = f32[288,97]{1,0:T(8,128)S(1)} collective-permute-done((f32[288,97]{1,0:T(8,128)S(1)}, f32[288,97]{1,0:T(8,128)S(1)}, u32[]{:S(2)}, u32[]{:S(2)}) %collective-permute-start.16) | collective-permute-done | bytes 111776 | tf_op jit(solution)/shard_map/ppermute | solution.py:21
  34.6 1.8 %collective-permute-start.18 = (f32[96,97]{1,0:T(8,128)S(1)}, f32[96,97]{1,0:T(8,128)S(1)}, u32[]{:S(2)}, u32[]{:S(2)}) collective-permute-start(f32[96,97]{1,0:T(8,128)S(1)} %slice_add_fusion.2), channel_id=1, source_target_pairs={{0,4},{1,5},{2,6},{3,7},{4,0},{5,1},{6,2},{7,3},{8,12},{9,13},{10,... | collective-permute-start | bytes 111752 | tf_op jit(solution)/shard_map/ppermute | solution.py:21
  36.4 2.4 %collective-permute-done.18 = f32[96,97]{1,0:T(8,128)S(1)} collective-permute-done((f32[96,97]{1,0:T(8,128)S(1)}, f32[96,97]{1,0:T(8,128)S(1)}, u32[]{:S(2)}, u32[]{:S(2)}) %collective-permute-start.18) | collective-permute-done | bytes 37280 | tf_op jit(solution)/shard_map/ppermute | solution.py:21
  38.8 2.9 %collective-permute-start.19 = (f32[96,97]{1,0:T(8,128)S(1)}, f32[96,97]{1,0:T(8,128)S(1)}, u32[]{:S(2)}, u32[]{:S(2)}) collective-permute-start(f32[96,97]{1,0:T(8,128)S(1)} %add.29), channel_id=1, source_target_pairs={{0,8},{1,9},{2,10},{3,11},{4,12},{5,13},{6,14},{7,15},{8,0},{9,1},... | collective-permute-start | bytes 111752 | tf_op jit(solution)/shard_map/ppermute | solution.py:21
  41.6 2.7 %collective-permute-done.19 = f32[96,97]{1,0:T(8,128)S(1)} collective-permute-done((f32[96,97]{1,0:T(8,128)S(1)}, f32[96,97]{1,0:T(8,128)S(1)}, u32[]{:S(2)}, u32[]{:S(2)}) %collective-permute-start.19) | collective-permute-done | bytes 37280 | tf_op jit(solution)/shard_map/ppermute | solution.py:21
  44.3 5.2 %orthonormal_basis.1 = (f32[2,96,96]{2,1,0:T(8,128)}, bf16[192,192]{1,0:T(8,128)(2,1)S(1)}, bf16[192,192]{1,0:T(8,128)(2,1)S(1)}, bf16[192,192]{1,0:T(8,128)(2,1)S(1)}, bf16[192,192]{1,0:T(8,128)(2,1)S(1)}) custom-call(f32[288,97]{1,0:T(8,128)S(1)} %get-tuple-element.46.refs_0_, f32[288,97]{1,0:T(8,128)S(1)} %get-tuple-element.47.refs_1_, ...), custom_call_target="tpu_custom_call" | custom-call | flops 1500000000 | bytes 1000000 | tf_op jit(solution)/shard_map/orthonormal_basis/pallas_call | solution.py:350
  49.6 1.0 %project_rows.1 = (f32[2,192,336]{2,1,0:T(8,128)S(1)}, f32[2,192,336]{2,1,0:T(8,128)S(1)}, f32[192,336]{1,0:T(8,128)S(1)}, f32[192,336]{1,0:T(8,128)S(1)}) custom-call(f32[96,97]{1,0:T(8,128)S(1)} %add.30.refs_4_.gram_ref, bf16[192,192]{1,0:T(8,128)(2,1)S(1)} %get-tuple-element.49.refs_0_, bf16[192,192]{1,0:T(8,128)(2,1)S(1)} %get-tuple-element.50.refs_1_, ...), custom_call_target="tpu_custom_call" | custom-call | tf_op jit(solution)/shard_map/project_rows/pallas_call | solution.py:361
  50.6 1.6 %collective-permute-start.22 = (f16[2,192,336]{2,1,0:T(8,128)(2,1)S(1)}, f16[2,192,336]{2,1,0:T(8,128)(2,1)S(1)}, u32[]{:S(2)}, u32[]{:S(2)}) collective-permute-start(f16[2,192,336]{2,1,0:T(8,128)(2,1)S(1)} %convert_element_type.27), channel_id=1, source_target_pairs={{0,2},{1,3},{2,0},{3,1},{4,6},{5,7},{6,4},{7,5},{8,10},{9,11},{10,... | collective-permute-start | bytes 774152 | tf_op jit(solution)/shard_map/ppermute | solution.py:21
  52.3 2.3 %collective-permute-start.24 = (f16[192,336]{1,0:T(8,128)(2,1)S(1)}, f16[192,336]{1,0:T(8,128)(2,1)S(1)}, u32[]{:S(2)}, u32[]{:S(2)}) collective-permute-start(f16[192,336]{1,0:T(8,128)(2,1)S(1)} %convert_element_type.31), channel_id=1, source_target_pairs={{0,8},{1,9},{2,10},{3,11},{4,12},{5,13},{6,14},{7,15},{8,0},{9,1},... | collective-permute-start | bytes 387080 | tf_op jit(solution)/shard_map/ppermute | solution.py:21
  54.6 1.5 %collective-permute-start.23 = (f16[192,336]{1,0:T(8,128)(2,1)S(1)}, f16[192,336]{1,0:T(8,128)(2,1)S(1)}, u32[]{:S(2)}, u32[]{:S(2)}) collective-permute-start(f16[192,336]{1,0:T(8,128)(2,1)S(1)} %convert_element_type.29), channel_id=1, source_target_pairs={{0,12},{1,13},{2,14},{3,15},{4,8},{5,9},{6,10},{7,11},{8,4},{9,5},... | collective-permute-start | bytes 387080 | tf_op jit(solution)/shard_map/ppermute | solution.py:21
  56.1 1.8 %collective-permute-done.22 = f16[2,192,336]{2,1,0:T(8,128)(2,1)S(1)} collective-permute-done((f16[2,192,336]{2,1,0:T(8,128)(2,1)S(1)}, f16[2,192,336]{2,1,0:T(8,128)(2,1)S(1)}, u32[]{:S(2)}, u32[]{:S(2)}) %collective-permute-start.22) | collective-permute-done | bytes 258080 | tf_op jit(solution)/shard_map/ppermute | solution.py:21
  58.1 1.6 %collective-permute-start.25 = (f16[192,336]{1,0:T(8,128)(2,1)S(1)}, f16[192,336]{1,0:T(8,128)(2,1)S(1)}, u32[]{:S(2)}, u32[]{:S(2)}) collective-permute-start(f16[192,336]{1,0:T(8,128)(2,1)S(1)} %fusion.4), channel_id=1, source_target_pairs={{0,4},{1,5},{2,6},{3,7},{4,0},{5,1},{6,2},{7,3},{8,12},{9,13},{10,... | collective-permute-start | bytes 387080 | tf_op jit(solution)/shard_map/ppermute | solution.py:21
  59.7 0.6 slice.31
  60.9 4.1 %collective-permute-done.24 = f16[192,336]{1,0:T(8,128)(2,1)S(1)} collective-permute-done((f16[192,336]{1,0:T(8,128)(2,1)S(1)}, f16[192,336]{1,0:T(8,128)(2,1)S(1)}, u32[]{:S(2)}, u32[]{:S(2)}) %collective-permute-start.24) | collective-permute-done | bytes 129056 | tf_op jit(solution)/shard_map/ppermute | solution.py:21
  65.4 0.8 %fusion.3 = f32[192,336]{1,0:T(8,128)} fusion(f32[2,192,336]{2,1,0:T(8,128)S(1)} %convert_element_type.28, f16[192,336]{1,0:T(8,128)(2,1)S(1)} %collective-permute-done.25, f16[192,336]{1,0:T(8,128)(2,1)S(1)} %collective-permute-done.24, f16[192,336]{1,0:T(8,128)(2,1)S(1)} %collective-permute-done.23, f32[2,192,336]{2,1,0:T(8,128)S(1)} %get-tuple-element.56, ...), kind=kLoop, calls=%fused_computation.5 | loop fusion | flops 516096 | bytes 1161220 | tf_op jit(solution)/shard_map/mul | solution.py:387
  (39 shorter events, 3.5 us)
Async XLA Ops:
  0.6 11.4 %collective-permute-start.8 = (bf16[1,192,336]{2,1,0:T(8,128)(2,1)}, bf16[1,192,336]{2,1,0:T(8,128)(2,1)S(1)}, u32[]{:S(2)}, u32[]{:S(2)}) collective-permute-start(bf16[1,192,336]{2,1,0:T(8,128)(2,1)} %bitcast.12), channel_id=1, source_target_pairs={{0,8},{1,9},{2,10},{3,11},{4,12},{5,13},{6,14},{7,15},{8,0},{9,1},... | collective-permute-start | bytes 387080 | tf_op jit(solution)/shard_map/ppermute | solution.py:21
  4.7 7.5 %collective-permute-start.9 = (bf16[1,192,336]{2,1,0:T(8,128)(2,1)}, bf16[1,192,336]{2,1,0:T(8,128)(2,1)S(1)}, u32[]{:S(2)}, u32[]{:S(2)}) collective-permute-start(bf16[1,192,336]{2,1,0:T(8,128)(2,1)} %bitcast.13), channel_id=1, source_target_pairs={{0,4},{1,5},{2,6},{3,7},{4,0},{5,1},{6,2},{7,3},{8,12},{9,13},{10,... | collective-permute-start | bytes 387080 | tf_op jit(solution)/shard_map/ppermute | solution.py:21
  6.3 6.3 %collective-permute-start.10 = (bf16[1,192,336]{2,1,0:T(8,128)(2,1)}, bf16[1,192,336]{2,1,0:T(8,128)(2,1)S(1)}, u32[]{:S(2)}, u32[]{:S(2)}) collective-permute-start(bf16[1,192,336]{2,1,0:T(8,128)(2,1)} %bitcast.14), channel_id=1, source_target_pairs={{0,2},{1,3},{2,0},{3,1},{4,6},{5,7},{6,4},{7,5},{8,10},{9,11},{10,... | collective-permute-start | bytes 387080 | tf_op jit(solution)/shard_map/ppermute | solution.py:21
  7.8 1.6 %copy-start = (bf16[2,96,5376]{2,1,0:T(8,128)(2,1)S(1)}, bf16[2,96,5376]{2,1,0:T(8,128)(2,1)}, u32[]{:S(2)}) copy-start(bf16[2,96,5376]{2,1,0:T(8,128)(2,1)} %traces_ref.1) | copy-start | bytes 6193156
  9.4 15.1 %copy-start.1 = (bf16[2,96,336]{2,1,0:T(8,128)(2,1)S(1)}, bf16[2,96,336]{2,1,0:T(8,128)(2,1)}, u32[]{:S(2)}) copy-start(bf16[2,96,336]{2,1,0:T(8,128)(2,1)} %param.3) | copy-start | bytes 387076
  10.9 1.8 %collective-permute-start = (bf16[1,192,336]{2,1,0:T(8,128)(2,1)S(1)}, bf16[1,192,336]{2,1,0:T(8,128)(2,1)S(1)}, u32[]{:S(2)}, u32[]{:S(2)}) collective-permute-start(bf16[1,192,336]{2,1,0:T(8,128)(2,1)S(1)} %get-tuple-element.35), channel_id=1, source_target_pairs={{0,1},{1,0},{2,3},{3,2},{4,5},{5,4},{6,7},{7,6},{8,9},{9,8},{10,11... | collective-permute-start | bytes 387080 | tf_op jit(solution)/shard_map/ppermute | solution.py:21
  11.0 2.1 %collective-permute-start.1 = (bf16[1,192,336]{2,1,0:T(8,128)(2,1)S(1)}, bf16[1,192,336]{2,1,0:T(8,128)(2,1)S(1)}, u32[]{:S(2)}, u32[]{:S(2)}) collective-permute-start(bf16[1,192,336]{2,1,0:T(8,128)(2,1)S(1)} %get-tuple-element.36), channel_id=1, source_target_pairs={{0,1},{1,0},{2,3},{3,2},{4,5},{5,4},{6,7},{7,6},{8,9},{9,8},{10,11... | collective-permute-start | bytes 387080 | tf_op jit(solution)/shard_map/ppermute | solution.py:21
  12.1 2.3 %collective-permute-start.2 = (bf16[1,192,336]{2,1,0:T(8,128)(2,1)S(1)}, bf16[1,192,336]{2,1,0:T(8,128)(2,1)S(1)}, u32[]{:S(2)}, u32[]{:S(2)}) collective-permute-start(bf16[1,192,336]{2,1,0:T(8,128)(2,1)S(1)} %get-tuple-element.37), channel_id=1, source_target_pairs={{0,1},{1,0},{2,3},{3,2},{4,5},{5,4},{6,7},{7,6},{8,9},{9,8},{10,11... | collective-permute-start | bytes 387080 | tf_op jit(solution)/shard_map/ppermute | solution.py:21
  12.2 2.2 %collective-permute-start.3 = (bf16[1,192,336]{2,1,0:T(8,128)(2,1)S(1)}, bf16[1,192,336]{2,1,0:T(8,128)(2,1)S(1)}, u32[]{:S(2)}, u32[]{:S(2)}) collective-permute-start(bf16[1,192,336]{2,1,0:T(8,128)(2,1)S(1)} %get-tuple-element.38), channel_id=1, source_target_pairs={{0,1},{1,0},{2,3},{3,2},{4,5},{5,4},{6,7},{7,6},{8,9},{9,8},{10,11... | collective-permute-start | bytes 387080 | tf_op jit(solution)/shard_map/ppermute | solution.py:21
  12.6 2.3 %collective-permute-start.4 = (bf16[1,192,336]{2,1,0:T(8,128)(2,1)S(1)}, bf16[1,192,336]{2,1,0:T(8,128)(2,1)S(1)}, u32[]{:S(2)}, u32[]{:S(2)}) collective-permute-start(bf16[1,192,336]{2,1,0:T(8,128)(2,1)S(1)} %get-tuple-element.39), channel_id=1, source_target_pairs={{0,1},{1,0},{2,3},{3,2},{4,5},{5,4},{6,7},{7,6},{8,9},{9,8},{10,11... | collective-permute-start | bytes 387080 | tf_op jit(solution)/shard_map/ppermute | solution.py:21
  12.8 3.6 %collective-permute-start.5 = (bf16[1,192,336]{2,1,0:T(8,128)(2,1)S(1)}, bf16[1,192,336]{2,1,0:T(8,128)(2,1)S(1)}, u32[]{:S(2)}, u32[]{:S(2)}) collective-permute-start(bf16[1,192,336]{2,1,0:T(8,128)(2,1)S(1)} %get-tuple-element.40), channel_id=1, source_target_pairs={{0,1},{1,0},{2,3},{3,2},{4,5},{5,4},{6,7},{7,6},{8,9},{9,8},{10,11... | collective-permute-start | bytes 387080 | tf_op jit(solution)/shard_map/ppermute | solution.py:21
  13.1 6.1 %collective-permute-start.13 = (bf16[1,192,336]{2,1,0:T(8,128)(2,1)S(1)}, bf16[1,192,336]{2,1,0:T(8,128)(2,1)S(1)}, u32[]{:S(2)}, u32[]{:S(2)}) collective-permute-start(bf16[1,192,336]{2,1,0:T(8,128)(2,1)S(1)} %collective-permute-done.8.refs_11_), channel_id=1, source_target_pairs={{0,4},{1,5},{2,6},{3,7},{4,0},{5,1},{6,2},{7,3},{8,12},{9,13},{10,... | collective-permute-start | bytes 387080 | tf_op jit(solution)/shard_map/ppermute | solution.py:21
  14.3 7.0 %collective-permute-start.6 = (bf16[1,192,336]{2,1,0:T(8,128)(2,1)S(1)}, bf16[1,192,336]{2,1,0:T(8,128)(2,1)S(1)}, u32[]{:S(2)}, u32[]{:S(2)}) collective-permute-start(bf16[1,192,336]{2,1,0:T(8,128)(2,1)S(1)} %get-tuple-element.41), channel_id=1, source_target_pairs={{0,1},{1,0},{2,3},{3,2},{4,5},{5,4},{6,7},{7,6},{8,9},{9,8},{10,11... | collective-permute-start | bytes 387080 | tf_op jit(solution)/shard_map/ppermute | solution.py:21
  14.5 6.8 %collective-permute-start.7 = (bf16[1,192,336]{2,1,0:T(8,128)(2,1)S(1)}, bf16[1,192,336]{2,1,0:T(8,128)(2,1)S(1)}, u32[]{:S(2)}, u32[]{:S(2)}) collective-permute-start(bf16[1,192,336]{2,1,0:T(8,128)(2,1)S(1)} %get-tuple-element.42), channel_id=1, source_target_pairs={{0,1},{1,0},{2,3},{3,2},{4,5},{5,4},{6,7},{7,6},{8,9},{9,8},{10,11... | collective-permute-start | bytes 387080 | tf_op jit(solution)/shard_map/ppermute | solution.py:21
  14.8 7.3 %collective-permute-start.12 = (bf16[1,192,336]{2,1,0:T(8,128)(2,1)S(1)}, bf16[1,192,336]{2,1,0:T(8,128)(2,1)S(1)}, u32[]{:S(2)}, u32[]{:S(2)}) collective-permute-start(bf16[1,192,336]{2,1,0:T(8,128)(2,1)S(1)} %collective-permute-done.8.refs_11_), channel_id=1, source_target_pairs={{0,2},{1,3},{2,0},{3,1},{4,6},{5,7},{6,4},{7,5},{8,10},{9,11},{10,... | collective-permute-start | bytes 387080 | tf_op jit(solution)/shard_map/ppermute | solution.py:21
  16.3 5.9 %collective-permute-start.11 = (bf16[1,192,336]{2,1,0:T(8,128)(2,1)S(1)}, bf16[1,192,336]{2,1,0:T(8,128)(2,1)S(1)}, u32[]{:S(2)}, u32[]{:S(2)}) collective-permute-start(bf16[1,192,336]{2,1,0:T(8,128)(2,1)S(1)} %collective-permute-done.10.refs_9_), channel_id=1, source_target_pairs={{0,4},{1,5},{2,6},{3,7},{4,0},{5,1},{6,2},{7,3},{8,12},{9,13},{10,... | collective-permute-start | bytes 387080 | tf_op jit(solution)/shard_map/ppermute | solution.py:21
  19.2 5.3 %collective-permute-start.14 = (bf16[1,192,336]{2,1,0:T(8,128)(2,1)S(1)}, bf16[1,192,336]{2,1,0:T(8,128)(2,1)S(1)}, u32[]{:S(2)}, u32[]{:S(2)}) collective-permute-start(bf16[1,192,336]{2,1,0:T(8,128)(2,1)S(1)} %collective-permute-done.13.refs_14_), channel_id=1, source_target_pairs={{0,2},{1,3},{2,0},{3,1},{4,6},{5,7},{6,4},{7,5},{8,10},{9,11},{10,... | collective-permute-start | bytes 387080 | tf_op jit(solution)/shard_map/ppermute | solution.py:21
  25.6 1.5 %collective-permute-start.15 = (f32[2,2,96,97]{3,2,1,0:T(8,128)S(1)}, f32[2,2,96,97]{3,2,1,0:T(8,128)S(1)}, u32[]{:S(2)}, u32[]{:S(2)}) collective-permute-start(f32[2,2,96,97]{3,2,1,0:T(8,128)S(1)} %sketch_rows.1.part_ref), channel_id=1, source_target_pairs={{0,1},{1,0},{2,3},{3,2},{4,5},{5,4},{6,7},{7,6},{8,9},{9,8},{10,11... | collective-permute-start | bytes 446984 | tf_op jit(solution)/shard_map/ppermute | solution.py:21
  27.9 6.7 %collective-permute-start.16 = (f32[288,97]{1,0:T(8,128)S(1)}, f32[288,97]{1,0:T(8,128)S(1)}, u32[]{:S(2)}, u32[]{:S(2)}) collective-permute-start(f32[288,97]{1,0:T(8,128)S(1)} %get-tuple-element.46.refs_0_), channel_id=1, source_target_pairs={{0,2},{1,3},{2,0},{3,1},{4,6},{5,7},{6,4},{7,5},{8,10},{9,11},{10,... | collective-permute-start | bytes 335240 | tf_op jit(solution)/shard_map/ppermute | solution.py:21
  30.0 19.6 %collective-permute-start.20 = (bf16[2,192,336]{2,1,0:T(8,128)(2,1)S(1)}, bf16[2,192,336]{2,1,0:T(8,128)(2,1)S(1)}, u32[]{:S(2)}, u32[]{:S(2)}) collective-permute-start(bf16[2,192,336]{2,1,0:T(8,128)(2,1)S(1)} %get-tuple-element.54.far_ref), channel_id=1, source_target_pairs={{0,2},{1,3},{2,0},{3,1},{4,6},{5,7},{6,4},{7,5},{8,10},{9,11},{10,... | collective-permute-start | bytes 774152 | tf_op jit(solution)/shard_map/ppermute | solution.py:21
  30.0 19.5 %collective-permute-start.21 = (bf16[2,192,336]{2,1,0:T(8,128)(2,1)S(1)}, bf16[2,192,336]{2,1,0:T(8,128)(2,1)S(1)}, u32[]{:S(2)}, u32[]{:S(2)}) collective-permute-start(bf16[2,192,336]{2,1,0:T(8,128)(2,1)S(1)} %get-tuple-element.55), channel_id=1, source_target_pairs={{0,3},{1,2},{2,1},{3,0},{4,7},{5,6},{6,5},{7,4},{8,11},{9,10},{10,... | collective-permute-start | bytes 774152 | tf_op jit(solution)/shard_map/ppermute | solution.py:21
  34.6 9.7 %collective-permute-start.17 = (f32[288,97]{1,0:T(8,128)S(1)}, f32[288,97]{1,0:T(8,128)S(1)}, u32[]{:S(2)}, u32[]{:S(2)}) collective-permute-start(f32[288,97]{1,0:T(8,128)S(1)} %collective-permute-done.16.refs_2_), channel_id=1, source_target_pairs={{0,1},{1,0},{2,3},{3,2},{4,5},{5,4},{6,7},{7,6},{8,9},{9,8},{10,11... | collective-permute-start | bytes 335240 | tf_op jit(solution)/shard_map/ppermute | solution.py:21
  34.6 4.2 %collective-permute-start.18 = (f32[96,97]{1,0:T(8,128)S(1)}, f32[96,97]{1,0:T(8,128)S(1)}, u32[]{:S(2)}, u32[]{:S(2)}) collective-permute-start(f32[96,97]{1,0:T(8,128)S(1)} %slice_add_fusion.2), channel_id=1, source_target_pairs={{0,4},{1,5},{2,6},{3,7},{4,0},{5,1},{6,2},{7,3},{8,12},{9,13},{10,... | collective-permute-start | bytes 111752 | tf_op jit(solution)/shard_map/ppermute | solution.py:21
  38.8 5.5 %collective-permute-start.19 = (f32[96,97]{1,0:T(8,128)S(1)}, f32[96,97]{1,0:T(8,128)S(1)}, u32[]{:S(2)}, u32[]{:S(2)}) collective-permute-start(f32[96,97]{1,0:T(8,128)S(1)} %add.29), channel_id=1, source_target_pairs={{0,8},{1,9},{2,10},{3,11},{4,12},{5,13},{6,14},{7,15},{8,0},{9,1},... | collective-permute-start | bytes 111752 | tf_op jit(solution)/shard_map/ppermute | solution.py:21
  50.6 7.4 %collective-permute-start.22 = (f16[2,192,336]{2,1,0:T(8,128)(2,1)S(1)}, f16[2,192,336]{2,1,0:T(8,128)(2,1)S(1)}, u32[]{:S(2)}, u32[]{:S(2)}) collective-permute-start(f16[2,192,336]{2,1,0:T(8,128)(2,1)S(1)} %convert_element_type.27), channel_id=1, source_target_pairs={{0,2},{1,3},{2,0},{3,1},{4,6},{5,7},{6,4},{7,5},{8,10},{9,11},{10,... | collective-permute-start | bytes 774152 | tf_op jit(solution)/shard_map/ppermute | solution.py:21
  52.3 12.7 %collective-permute-start.24 = (f16[192,336]{1,0:T(8,128)(2,1)S(1)}, f16[192,336]{1,0:T(8,128)(2,1)S(1)}, u32[]{:S(2)}, u32[]{:S(2)}) collective-permute-start(f16[192,336]{1,0:T(8,128)(2,1)S(1)} %convert_element_type.31), channel_id=1, source_target_pairs={{0,8},{1,9},{2,10},{3,11},{4,12},{5,13},{6,14},{7,15},{8,0},{9,1},... | collective-permute-start | bytes 387080 | tf_op jit(solution)/shard_map/ppermute | solution.py:21
  54.6 10.3 %collective-permute-start.23 = (f16[192,336]{1,0:T(8,128)(2,1)S(1)}, f16[192,336]{1,0:T(8,128)(2,1)S(1)}, u32[]{:S(2)}, u32[]{:S(2)}) collective-permute-start(f16[192,336]{1,0:T(8,128)(2,1)S(1)} %convert_element_type.29), channel_id=1, source_target_pairs={{0,12},{1,13},{2,14},{3,15},{4,8},{5,9},{6,10},{7,11},{8,4},{9,5},... | collective-permute-start | bytes 387080 | tf_op jit(solution)/shard_map/ppermute | solution.py:21
  58.1 7.4 %collective-permute-start.25 = (f16[192,336]{1,0:T(8,128)(2,1)S(1)}, f16[192,336]{1,0:T(8,128)(2,1)S(1)}, u32[]{:S(2)}, u32[]{:S(2)}) collective-permute-start(f16[192,336]{1,0:T(8,128)(2,1)S(1)} %fusion.4), channel_id=1, source_target_pairs={{0,4},{1,5},{2,6},{3,7},{4,0},{5,1},{6,2},{7,3},{8,12},{9,13},{10,... | collective-permute-start | bytes 387080 | tf_op jit(solution)/shard_map/ppermute | solution.py:21

commit v8 on v7

--- a/solution.py
+++ b/solution.py
@@ -10,7 +10,7 @@
 
 ROWS = 8
 GROUPS = 4
-PARTS = 4
+PARTS = 2
 TOP = 32768.0
 VMEM = pl.BlockSpec(memory_space=pltpu.VMEM)
 SMEM = pl.BlockSpec(memory_space=pltpu.SMEM)
@@ -241,6 +241,44 @@
         weights[group][...] = jnp.concatenate([top, low], axis=0).astype(jnp.bfloat16)
 
 
+def folds(rows, share):
+    whole = share // 128 * 128
+    rest = share - whole
+    count = whole // rest if rest else 0
+    return count if count and rows % (16 * count) == 0 else 0
+
+
+def folded_shape(rows, share):
+    count = folds(rows, share)
+    return (rows + rows // count, share // 128 * 128) if count else (rows, share)
+
+
+def fold(value):
+    rows, share = value.shape
+    count = folds(rows, share)
+    if not count:
+        return value
+    whole, each = share // 128 * 128, rows // count
+    rest = [value[each * i : each * (i + 1), whole:] for i in range(count)]
+    spare = whole - count * (share - whole)
+    if spare:
+        rest.append(jnp.zeros((each, spare), value.dtype))
+    return jnp.concatenate([value[:, :whole], jnp.concatenate(rest, axis=1)], axis=0)
+
+
+def unfold_kernel(folded_ref, out_ref):
+    rows, share = out_ref.shape
+    count = folds(rows, share)
+    if not count:
+        out_ref[...] = folded_ref[...]
+        return
+    whole, each = share // 128 * 128, rows // count
+    wide = share - whole
+    out_ref[:, :whole] = folded_ref[:rows, :]
+    for i in range(count):
+        out_ref[each * i : each * (i + 1), whole:] = folded_ref[rows:, wide * i : wide * (i + 1)]
+
+
 def project_kernel(bound, gram_ref, *refs):
     weights, (stay_ref, near_ref, far_ref, cross_ref) = refs[:GROUPS], refs[GROUPS : GROUPS + 4]
     core, (own_ref, side_ref, *far_outs) = refs[GROUPS + 4 : GROUPS + 4 + 2 * PARTS], refs[GROUPS + 4 + 2 * PARTS :]
@@ -253,7 +291,7 @@
         for weight_ref, block in zip(weights, data):
             term = jnp.dot(weight_ref[...], block, preferred_element_type=jnp.float32)
             total = term if total is None else total + term
-        return total * factor
+        return fold(total * factor)
 
     for zone in range(half):
         far_outs[zone][...] = project(
@@ -357,14 +395,15 @@
         cost_estimate=pl.CostEstimate(flops=1_500_000_000, bytes_accessed=1_000_000, transcendentals=0),
         name="orthonormal_basis",
     )(*known, gram)
+    folded = folded_shape(2 * count, share)
     bound = 1.01 * math.sqrt(2 * rows * size)
     own, side, *away = pl.pallas_call(
         functools.partial(project_kernel, bound),
         out_shape=(
-            jax.ShapeDtypeStruct((half, 2 * count, share), jnp.float32),
-            jax.ShapeDtypeStruct((half, 2 * count, share), jnp.float32),
+            jax.ShapeDtypeStruct((half, *folded), jnp.float32),
+            jax.ShapeDtypeStruct((half, *folded), jnp.float32),
         )
-        + (jax.ShapeDtypeStruct((2 * count, share), jnp.float32),) * half,
+        + (jax.ShapeDtypeStruct(folded, jnp.float32),) * half,
         in_specs=[VMEM] * (1 + GROUPS + 4 + 2 * PARTS),
         out_specs=(VMEM,) * (2 + half),
         compiler_params=PARAMS,
@@ -384,7 +423,12 @@
             total = low + send(high, GROUPS * low.shape[0])
         total = total[0]
     level = gram[0, count] * bound
-    return basis, (total * (level / TOP)).reshape(2, count, share)
+    total = total * (level / TOP)
+    groups = folds(2 * count, share)
+    if groups:
+        rest = [total[2 * count :, i * (share - folded[1]) : (i + 1) * (share - folded[1])] for i in range(groups)]
+        total = jnp.concatenate([total[: 2 * count], jnp.concatenate(rest)], axis=1)
+    return basis, total.reshape(2, count, share)
 
 
 def solution(mesh):

time: 66.4 us -> 64.9 us (0.977)
  starting transfers between devices: 29.9 us -> 27 us
  waiting for transfers between devices: 22.1 us -> 23.4 us
    ppermute x26 -> x22, starting transfers between devices: 29.9 us -> 27 us  [swap(): return lax.ppermute(value, 'rcv', [(i, i ^ mask) for i in range(size)])]
    ppermute x26 -> x22, waiting for transfers between devices: 22.1 us -> 23.4 us  [swap(): return lax.ppermute(value, 'rcv', [(i, i ^ mask) for i in range(size)])]
    concatenate x0 -> x1, other arithmetic: none -> 0.74 us  [per_device(): total = jnp.concatenate([total[:2 * count], jnp.concatenate(rest)], axis=1)]
    mul x1, other arithmetic: 0.79 us -> 0.08 us  [per_device(): total = total * (level / TOP)]
  transfers between devices with their start and end apart: 26 -> 22, of which waited for: 12 -> 12; matrix products, arithmetic and copies ran while one was open for 1% -> 1% of each run, Pallas kernels for 10% -> 10%
where the time goes in v8:
time: 64.9 us; the launch traced here: 64.8 us
  starting transfers between devices  27 us (42%)
  waiting for transfers between devices  23.4 us (36%)
  Pallas kernels  9.79 us (15%)
  local copies, waits for them, and re-layouts  2.26 us (3%)
  between operations  1.39 us (2%)
  other arithmetic  0.99 us (2%)
    ppermute x22, starting transfers between devices, swap(): return lax.ppermute(value, 'rcv', [(i, i ^ mask) for i in range(size)])  27 us
    ppermute x22, waiting for transfers between devices, swap(): return lax.ppermute(value, 'rcv', [(i, i ^ mask) for i in range(size)])  23.4 us
    pallas_call x1, Pallas kernels, per_device(): pl.pallas_call(functools.partial(basis_kernel, math.sqrt(rows * size)), o...  5.24 us
    unnamed x4, local copies, waits for them, and re-layouts  1.58 us
    pallas_call x1, Pallas kernels, per_device(): pl.pallas_call(functools.partial(chunk_kernel, share), out_shape=(chunk(z...  1.56 us
  transfers between devices with their start and end apart: 22, of which 12 were waited for; matrix products, arithmetic and copies ran while one was open for 1% of the time, Pallas kernels for 10%

profile of v8, /device:TPU:0, one launch (start us, length us, event | category | flops | bytes accessed | tf_op | source)
XLA Modules:
  0.0 64.8 jit_solution(16562619982729392085)
XLA Ops:
  0.6 4.1 %collective-permute-start.4 = (bf16[1,192,336]{2,1,0:T(8,128)(2,1)}, bf16[1,192,336]{2,1,0:T(8,128)(2,1)S(1)}, u32[]{:S(2)}, u32[]{:S(2)}) collective-permute-start(bf16[1,192,336]{2,1,0:T(8,128)(2,1)} %bitcast.12), channel_id=1, source_target_pairs={{0,8},{1,9},{2,10},{3,11},{4,12},{5,13},{6,14},{7,15},{8,0},{9,1},... | collective-permute-start | bytes 387080 | tf_op jit(solution)/shard_map/ppermute | solution.py:21
  4.7 1.6 %collective-permute-start.5 = (bf16[1,192,336]{2,1,0:T(8,128)(2,1)}, bf16[1,192,336]{2,1,0:T(8,128)(2,1)S(1)}, u32[]{:S(2)}, u32[]{:S(2)}) collective-permute-start(bf16[1,192,336]{2,1,0:T(8,128)(2,1)} %bitcast.13), channel_id=1, source_target_pairs={{0,4},{1,5},{2,6},{3,7},{4,0},{5,1},{6,2},{7,3},{8,12},{9,13},{10,... | collective-permute-start | bytes 387080 | tf_op jit(solution)/shard_map/ppermute | solution.py:21
  6.3 1.5 %collective-permute-start.6 = (bf16[1,192,336]{2,1,0:T(8,128)(2,1)}, bf16[1,192,336]{2,1,0:T(8,128)(2,1)S(1)}, u32[]{:S(2)}, u32[]{:S(2)}) collective-permute-start(bf16[1,192,336]{2,1,0:T(8,128)(2,1)} %bitcast.14), channel_id=1, source_target_pairs={{0,2},{1,3},{2,0},{3,1},{4,6},{5,7},{6,4},{7,5},{8,10},{9,11},{10,... | collective-permute-start | bytes 387080 | tf_op jit(solution)/shard_map/ppermute | solution.py:21
  7.8 1.6 %copy-done = bf16[2,96,5376]{2,1,0:T(8,128)(2,1)S(1)} copy-done((bf16[2,96,5376]{2,1,0:T(8,128)(2,1)S(1)}, bf16[2,96,5376]{2,1,0:T(8,128)(2,1)}, u32[]{:S(2)}) %copy-start) | copy-done | bytes 2064408
  9.4 1.6 %source_chunks.1 = (bf16[4,192,336]{2,1,0:T(8,128)(2,1)S(1)}, bf16[2,192,336]{2,1,0:T(8,128)(2,1)S(1)}, bf16[2,192,336]{2,1,0:T(8,128)(2,1)S(1)}, bf16[2,192,336...) custom-call(s32[1]{0:T(128)} %bitcast.me_ref, ...), custom_call_target="tpu_custom_call" | custom-call | tf_op jit(solution)/shard_map/source_chunks/pallas_call | solution.py:342
  12.6 1.2 %collective-permute-start.9 = (bf16[1,192,336]{2,1,0:T(8,128)(2,1)S(1)}, bf16[1,192,336]{2,1,0:T(8,128)(2,1)S(1)}, u32[]{:S(2)}, u32[]{:S(2)}) collective-permute-start(bf16[1,192,336]{2,1,0:T(8,128)(2,1)S(1)} %collective-permute-done.4.refs_7_), channel_id=1, source_target_pairs={{0,4},{1,5},{2,6},{3,7},{4,0},{5,1},{6,2},{7,3},{8,12},{9,13},{10,... | collective-permute-start | bytes 387080 | tf_op jit(solution)/shard_map/ppermute | solution.py:21
  13.7 1.5 %collective-permute-start.8 = (bf16[1,192,336]{2,1,0:T(8,128)(2,1)S(1)}, bf16[1,192,336]{2,1,0:T(8,128)(2,1)S(1)}, u32[]{:S(2)}, u32[]{:S(2)}) collective-permute-start(bf16[1,192,336]{2,1,0:T(8,128)(2,1)S(1)} %collective-permute-done.4.refs_7_), channel_id=1, source_target_pairs={{0,2},{1,3},{2,0},{3,1},{4,6},{5,7},{6,4},{7,5},{8,10},{9,11},{10,... | collective-permute-start | bytes 387080 | tf_op jit(solution)/shard_map/ppermute | solution.py:21
  15.2 0.9 %collective-permute-start.7 = (bf16[1,192,336]{2,1,0:T(8,128)(2,1)S(1)}, bf16[1,192,336]{2,1,0:T(8,128)(2,1)S(1)}, u32[]{:S(2)}, u32[]{:S(2)}) collective-permute-start(bf16[1,192,336]{2,1,0:T(8,128)(2,1)S(1)} %collective-permute-done.6.refs_5_), channel_id=1, source_target_pairs={{0,4},{1,5},{2,6},{3,7},{4,0},{5,1},{6,2},{7,3},{8,12},{9,13},{10,... | collective-permute-start | bytes 387080 | tf_op jit(solution)/shard_map/ppermute | solution.py:21
  16.1 3.0 %collective-permute-done.9.refs_10_ = bf16[1,192,336]{2,1,0:T(8,128)(2,1)S(1)} collective-permute-done((bf16[1,192,336]{2,1,0:T(8,128)(2,1)S(1)}, bf16[1,192,336]{2,1,0:T(8,128)(2,1)S(1)}, u32[]{:S(2)}, u32[]{:S(2)}) %collective-permute-start.9) | collective-permute-done | bytes 129056 | tf_op jit(solution)/shard_map/ppermute | solution.py:21
  19.2 1.6 %collective-permute-start.10 = (bf16[1,192,336]{2,1,0:T(8,128)(2,1)S(1)}, bf16[1,192,336]{2,1,0:T(8,128)(2,1)S(1)}, u32[]{:S(2)}, u32[]{:S(2)}) collective-permute-start(bf16[1,192,336]{2,1,0:T(8,128)(2,1)S(1)} %collective-permute-done.9.refs_10_), channel_id=1, source_target_pairs={{0,2},{1,3},{2,0},{3,1},{4,6},{5,7},{6,4},{7,5},{8,10},{9,11},{10,... | collective-permute-start | bytes 387080 | tf_op jit(solution)/shard_map/ppermute | solution.py:21
  20.8 0.9 %collective-permute-done.7.refs_8_ = bf16[1,192,336]{2,1,0:T(8,128)(2,1)S(1)} collective-permute-done((bf16[1,192,336]{2,1,0:T(8,128)(2,1)S(1)}, bf16[1,192,336]{2,1,0:T(8,128)(2,1)S(1)}, u32[]{:S(2)}, u32[]{:S(2)}) %collective-permute-start.7) | collective-permute-done | bytes 129056 | tf_op jit(solution)/shard_map/ppermute | solution.py:21
  21.7 2.6 %collective-permute-done.10.refs_11_ = bf16[1,192,336]{2,1,0:T(8,128)(2,1)S(1)} collective-permute-done((bf16[1,192,336]{2,1,0:T(8,128)(2,1)S(1)}, bf16[1,192,336]{2,1,0:T(8,128)(2,1)S(1)}, u32[]{:S(2)}, u32[]{:S(2)}) %collective-permute-start.10) | collective-permute-done | bytes 129056 | tf_op jit(solution)/shard_map/ppermute | solution.py:21
  24.3 1.2 %sketch_rows.1.part_ref = f32[2,2,96,97]{3,2,1,0:T(8,128)S(1)} custom-call(f32[1,5376]{1,0:T(1,128)S(1)} %get-tuple-element.27.peak_ref, bf16[4,192,336]{2,1,0:T(8,128)(2,1)S(1)} %get-tuple-element.28.stay_ref.refs_4_, bf16[2,192,336]{2,1,0:T(8,128)(2,1)S(1)} %get-tuple-element.29.near_ref.refs_5_, bf16[2,192,336]{2,1,0:T(8,128)(2,1)S(1)} %get-tuple-element.46.far_ref, ...), custom_call_target="tpu_custom_call" | custom-call | tf_op jit(solution)/shard_map/sketch_rows/pallas_call | solution.py:362
  25.6 1.4 %collective-permute-done.11.other_ref = f32[2,2,96,97]{3,2,1,0:T(8,128)S(1)} collective-permute-done((f32[2,2,96,97]{3,2,1,0:T(8,128)S(1)}, f32[2,2,96,97]{3,2,1,0:T(8,128)S(1)}, u32[]{:S(2)}, u32[]{:S(2)}) %collective-permute-start.11) | collective-permute-done | bytes 149024 | tf_op jit(solution)/shard_map/ppermute | solution.py:21
  27.0 0.7 %chip_gram.1 = (f32[288,97]{1,0:T(8,128)S(1)}, f32[288,97]{1,0:T(8,128)S(1)}) custom-call(f32[2,2,96,97]{3,2,1,0:T(8,128)S(1)} %sketch_rows.1.part_ref, f32[2,2,96,97]{3,2,1,0:T(8,128)S(1)} %collective-permute-done.11.other_ref), custom_call_target="tpu_custom_call" | custom-call | tf_op jit(solution)/shard_map/chip_gram/pallas_call | solution.py:371
  27.8 1.7 %collective-permute-start.12 = (f32[288,97]{1,0:T(8,128)S(1)}, f32[288,97]{1,0:T(8,128)S(1)}, u32[]{:S(2)}, u32[]{:S(2)}) collective-permute-start(f32[288,97]{1,0:T(8,128)S(1)} %get-tuple-element.38.refs_0_), channel_id=1, source_target_pairs={{0,2},{1,3},{2,0},{3,1},{4,6},{5,7},{6,4},{7,5},{8,10},{9,11},{10,... | collective-permute-start | bytes 335240 | tf_op jit(solution)/shard_map/ppermute | solution.py:21
  29.9 0.8 %collective-permute-start.17 = (bf16[2,192,336]{2,1,0:T(8,128)(2,1)S(1)}, bf16[2,192,336]{2,1,0:T(8,128)(2,1)S(1)}, u32[]{:S(2)}, u32[]{:S(2)}) collective-permute-start(bf16[2,192,336]{2,1,0:T(8,128)(2,1)S(1)} %get-tuple-element.47), channel_id=1, source_target_pairs={{0,3},{1,2},{2,1},{3,0},{4,7},{5,6},{6,5},{7,4},{8,11},{9,10},{10,... | collective-permute-start | bytes 774152 | tf_op jit(solution)/shard_map/ppermute | solution.py:21
  30.7 3.9 %collective-permute-done.12.refs_2_ = f32[288,97]{1,0:T(8,128)S(1)} collective-permute-done((f32[288,97]{1,0:T(8,128)S(1)}, f32[288,97]{1,0:T(8,128)S(1)}, u32[]{:S(2)}, u32[]{:S(2)}) %collective-permute-start.12) | collective-permute-done | bytes 111776 | tf_op jit(solution)/shard_map/ppermute | solution.py:21
  34.5 1.3 %collective-permute-start.14 = (f32[96,97]{1,0:T(8,128)S(1)}, f32[96,97]{1,0:T(8,128)S(1)}, u32[]{:S(2)}, u32[]{:S(2)}) collective-permute-start(f32[96,97]{1,0:T(8,128)S(1)} %slice_add_fusion.2), channel_id=1, source_target_pairs={{0,4},{1,5},{2,6},{3,7},{4,0},{5,1},{6,2},{7,3},{8,12},{9,13},{10,... | collective-permute-start | bytes 111752 | tf_op jit(solution)/shard_map/ppermute | solution.py:21
  35.8 2.9 %collective-permute-done.14 = f32[96,97]{1,0:T(8,128)S(1)} collective-permute-done((f32[96,97]{1,0:T(8,128)S(1)}, f32[96,97]{1,0:T(8,128)S(1)}, u32[]{:S(2)}, u32[]{:S(2)}) %collective-permute-start.14) | collective-permute-done | bytes 37280 | tf_op jit(solution)/shard_map/ppermute | solution.py:21
  38.7 2.4 %collective-permute-start.15 = (f32[96,97]{1,0:T(8,128)S(1)}, f32[96,97]{1,0:T(8,128)S(1)}, u32[]{:S(2)}, u32[]{:S(2)}) collective-permute-start(f32[96,97]{1,0:T(8,128)S(1)} %add.29), channel_id=1, source_target_pairs={{0,8},{1,9},{2,10},{3,11},{4,12},{5,13},{6,14},{7,15},{8,0},{9,1},... | collective-permute-start | bytes 111752 | tf_op jit(solution)/shard_map/ppermute | solution.py:21
  41.1 2.7 %collective-permute-done.15 = f32[96,97]{1,0:T(8,128)S(1)} collective-permute-done((f32[96,97]{1,0:T(8,128)S(1)}, f32[96,97]{1,0:T(8,128)S(1)}, u32[]{:S(2)}, u32[]{:S(2)}) %collective-permute-start.15) | collective-permute-done | bytes 37280 | tf_op jit(solution)/shard_map/ppermute | solution.py:21
  43.8 5.2 %orthonormal_basis.1 = (f32[2,96,96]{2,1,0:T(8,128)}, bf16[192,192]{1,0:T(8,128)(2,1)S(1)}, bf16[192,192]{1,0:T(8,128)(2,1)S(1)}, bf16[192,192]{1,0:T(8,128)(2,1)S(1)}, bf16[192,192]{1,0:T(8,128)(2,1)S(1)}) custom-call(f32[288,97]{1,0:T(8,128)S(1)} %get-tuple-element.38.refs_0_, f32[288,97]{1,0:T(8,128)S(1)} %get-tuple-element.39.refs_1_, ...), custom_call_target="tpu_custom_call" | custom-call | flops 1500000000 | bytes 1000000 | tf_op jit(solution)/shard_map/orthonormal_basis/pallas_call | solution.py:388
  49.0 1.1 %project_rows.1 = (f32[2,256,256]{2,1,0:T(8,128)S(1)}, f32[2,256,256]{2,1,0:T(8,128)S(1)}, f32[256,256]{1,0:T(8,128)S(1)}, f32[256,256]{1,0:T(8,128)S(1)}) custom-call(f32[96,97]{1,0:T(8,128)S(1)} %add.30.refs_4_.gram_ref, bf16[192,192]{1,0:T(8,128)(2,1)S(1)} %get-tuple-element.41.refs_0_, bf16[192,192]{1,0:T(8,128)(2,1)S(1)} %get-tuple-element.42.refs_1_, ...), custom_call_target="tpu_custom_call" | custom-call | tf_op jit(solution)/shard_map/project_rows/pallas_call | solution.py:400
  50.2 1.7 %collective-permute-start.18 = (f16[2,256,256]{2,1,0:T(8,128)(2,1)S(1)}, f16[2,256,256]{2,1,0:T(8,128)(2,1)S(1)}, u32[]{:S(2)}, u32[]{:S(2)}) collective-permute-start(f16[2,256,256]{2,1,0:T(8,128)(2,1)S(1)} %convert_element_type.27), channel_id=1, source_target_pairs={{0,2},{1,3},{2,0},{3,1},{4,6},{5,7},{6,4},{7,5},{8,10},{9,11},{10,... | collective-permute-start | bytes 786440 | tf_op jit(solution)/shard_map/ppermute | solution.py:21
  51.8 2.3 %collective-permute-start.20 = (f16[256,256]{1,0:T(8,128)(2,1)S(1)}, f16[256,256]{1,0:T(8,128)(2,1)S(1)}, u32[]{:S(2)}, u32[]{:S(2)}) collective-permute-start(f16[256,256]{1,0:T(8,128)(2,1)S(1)} %convert_element_type.31), channel_id=1, source_target_pairs={{0,8},{1,9},{2,10},{3,11},{4,12},{5,13},{6,14},{7,15},{8,0},{9,1},... | collective-permute-start | bytes 393224 | tf_op jit(solution)/shard_map/ppermute | solution.py:21
  54.2 1.5 %collective-permute-start.19 = (f16[256,256]{1,0:T(8,128)(2,1)S(1)}, f16[256,256]{1,0:T(8,128)(2,1)S(1)}, u32[]{:S(2)}, u32[]{:S(2)}) collective-permute-start(f16[256,256]{1,0:T(8,128)(2,1)S(1)} %convert_element_type.29), channel_id=1, source_target_pairs={{0,12},{1,13},{2,14},{3,15},{4,8},{5,9},{6,10},{7,11},{8,4},{9,5},... | collective-permute-start | bytes 393224 | tf_op jit(solution)/shard_map/ppermute | solution.py:21
  55.7 1.2 %collective-permute-done.18 = f16[2,256,256]{2,1,0:T(8,128)(2,1)S(1)} collective-permute-done((f16[2,256,256]{2,1,0:T(8,128)(2,1)S(1)}, f16[2,256,256]{2,1,0:T(8,128)(2,1)S(1)}, u32[]{:S(2)}, u32[]{:S(2)}) %collective-permute-start.18) | collective-permute-done | bytes 262176 | tf_op jit(solution)/shard_map/ppermute | solution.py:21
  56.9 1.6 %collective-permute-start.21 = (f16[256,256]{1,0:T(8,128)(2,1)S(1)}, f16[256,256]{1,0:T(8,128)(2,1)S(1)}, u32[]{:S(2)}, u32[]{:S(2)}) collective-permute-start(f16[256,256]{1,0:T(8,128)(2,1)S(1)} %fusion.4), channel_id=1, source_target_pairs={{0,4},{1,5},{2,6},{3,7},{4,0},{5,1},{6,2},{7,3},{8,12},{9,13},{10,... | collective-permute-start | bytes 393224 | tf_op jit(solution)/shard_map/ppermute | solution.py:21
  58.5 0.6 slice.47
  59.8 3.6 %collective-permute-done.20 = f16[256,256]{1,0:T(8,128)(2,1)S(1)} collective-permute-done((f16[256,256]{1,0:T(8,128)(2,1)S(1)}, f16[256,256]{1,0:T(8,128)(2,1)S(1)}, u32[]{:S(2)}, u32[]{:S(2)}) %collective-permute-start.20) | collective-permute-done | bytes 131104 | tf_op jit(solution)/shard_map/ppermute | solution.py:21
  64.0 0.7 %maximum_maximum_fusion = f32[192,336]{1,0:T(8,128)} fusion(f32[64,80]{1,0:T(8,128)S(1)} %get-tuple-element.53, f32[64,80]{1,0:T(8,128)S(1)} %get-tuple-element.54, f32[64,80]{1,0:T(8,128)S(1)} %get-tuple-element.52, f32[192,256]{1,0:T(8,128)S(1)} %slice.48), kind=kLoop, calls=%fused_computation | loop fusion | flops 193536 | bytes 516096 | tf_op jit(solution)/shard_map/concatenate | solution.py:430
  (34 shorter events, 2.9 us)
Async XLA Ops:
  0.6 11.4 %collective-permute-start.4 = (bf16[1,192,336]{2,1,0:T(8,128)(2,1)}, bf16[1,192,336]{2,1,0:T(8,128)(2,1)S(1)}, u32[]{:S(2)}, u32[]{:S(2)}) collective-permute-start(bf16[1,192,336]{2,1,0:T(8,128)(2,1)} %bitcast.12), channel_id=1, source_target_pairs={{0,8},{1,9},{2,10},{3,11},{4,12},{5,13},{6,14},{7,15},{8,0},{9,1},... | collective-permute-start | bytes 387080 | tf_op jit(solution)/shard_map/ppermute | solution.py:21
  4.7 7.5 %collective-permute-start.5 = (bf16[1,192,336]{2,1,0:T(8,128)(2,1)}, bf16[1,192,336]{2,1,0:T(8,128)(2,1)S(1)}, u32[]{:S(2)}, u32[]{:S(2)}) collective-permute-start(bf16[1,192,336]{2,1,0:T(8,128)(2,1)} %bitcast.13), channel_id=1, source_target_pairs={{0,4},{1,5},{2,6},{3,7},{4,0},{5,1},{6,2},{7,3},{8,12},{9,13},{10,... | collective-permute-start | bytes 387080 | tf_op jit(solution)/shard_map/ppermute | solution.py:21
  6.3 6.3 %collective-permute-start.6 = (bf16[1,192,336]{2,1,0:T(8,128)(2,1)}, bf16[1,192,336]{2,1,0:T(8,128)(2,1)S(1)}, u32[]{:S(2)}, u32[]{:S(2)}) collective-permute-start(bf16[1,192,336]{2,1,0:T(8,128)(2,1)} %bitcast.14), channel_id=1, source_target_pairs={{0,2},{1,3},{2,0},{3,1},{4,6},{5,7},{6,4},{7,5},{8,10},{9,11},{10,... | collective-permute-start | bytes 387080 | tf_op jit(solution)/shard_map/ppermute | solution.py:21
  7.8 1.6 %copy-start = (bf16[2,96,5376]{2,1,0:T(8,128)(2,1)S(1)}, bf16[2,96,5376]{2,1,0:T(8,128)(2,1)}, u32[]{:S(2)}) copy-start(bf16[2,96,5376]{2,1,0:T(8,128)(2,1)} %traces_ref.1) | copy-start | bytes 6193156
  9.4 15.0 %copy-start.1 = (bf16[2,96,336]{2,1,0:T(8,128)(2,1)S(1)}, bf16[2,96,336]{2,1,0:T(8,128)(2,1)}, u32[]{:S(2)}) copy-start(bf16[2,96,336]{2,1,0:T(8,128)(2,1)} %param.3) | copy-start | bytes 387076
  10.9 2.8 %collective-permute-start = (bf16[2,192,336]{2,1,0:T(8,128)(2,1)S(1)}, bf16[2,192,336]{2,1,0:T(8,128)(2,1)S(1)}, u32[]{:S(2)}, u32[]{:S(2)}) collective-permute-start(bf16[2,192,336]{2,1,0:T(8,128)(2,1)S(1)} %get-tuple-element.31), channel_id=1, source_target_pairs={{0,1},{1,0},{2,3},{3,2},{4,5},{5,4},{6,7},{7,6},{8,9},{9,8},{10,11... | collective-permute-start | bytes 774152 | tf_op jit(solution)/shard_map/ppermute | solution.py:21
  11.0 4.2 %collective-permute-start.1 = (bf16[2,192,336]{2,1,0:T(8,128)(2,1)S(1)}, bf16[2,192,336]{2,1,0:T(8,128)(2,1)S(1)}, u32[]{:S(2)}, u32[]{:S(2)}) collective-permute-start(bf16[2,192,336]{2,1,0:T(8,128)(2,1)S(1)} %get-tuple-element.32), channel_id=1, source_target_pairs={{0,1},{1,0},{2,3},{3,2},{4,5},{5,4},{6,7},{7,6},{8,9},{9,8},{10,11... | collective-permute-start | bytes 774152 | tf_op jit(solution)/shard_map/ppermute | solution.py:21
  12.1 8.7 %collective-permute-start.2 = (bf16[2,192,336]{2,1,0:T(8,128)(2,1)S(1)}, bf16[2,192,336]{2,1,0:T(8,128)(2,1)S(1)}, u32[]{:S(2)}, u32[]{:S(2)}) collective-permute-start(bf16[2,192,336]{2,1,0:T(8,128)(2,1)S(1)} %get-tuple-element.33), channel_id=1, source_target_pairs={{0,1},{1,0},{2,3},{3,2},{4,5},{5,4},{6,7},{7,6},{8,9},{9,8},{10,11... | collective-permute-start | bytes 774152 | tf_op jit(solution)/shard_map/ppermute | solution.py:21
  12.2 8.6 %collective-permute-start.3 = (bf16[2,192,336]{2,1,0:T(8,128)(2,1)S(1)}, bf16[2,192,336]{2,1,0:T(8,128)(2,1)S(1)}, u32[]{:S(2)}, u32[]{:S(2)}) collective-permute-start(bf16[2,192,336]{2,1,0:T(8,128)(2,1)S(1)} %get-tuple-element.34), channel_id=1, source_target_pairs={{0,1},{1,0},{2,3},{3,2},{4,5},{5,4},{6,7},{7,6},{8,9},{9,8},{10,11... | collective-permute-start | bytes 774152 | tf_op jit(solution)/shard_map/ppermute | solution.py:21
  12.6 6.6 %collective-permute-start.9 = (bf16[1,192,336]{2,1,0:T(8,128)(2,1)S(1)}, bf16[1,192,336]{2,1,0:T(8,128)(2,1)S(1)}, u32[]{:S(2)}, u32[]{:S(2)}) collective-permute-start(bf16[1,192,336]{2,1,0:T(8,128)(2,1)S(1)} %collective-permute-done.4.refs_7_), channel_id=1, source_target_pairs={{0,4},{1,5},{2,6},{3,7},{4,0},{5,1},{6,2},{7,3},{8,12},{9,13},{10,... | collective-permute-start | bytes 387080 | tf_op jit(solution)/shard_map/ppermute | solution.py:21
  13.7 7.9 %collective-permute-start.8 = (bf16[1,192,336]{2,1,0:T(8,128)(2,1)S(1)}, bf16[1,192,336]{2,1,0:T(8,128)(2,1)S(1)}, u32[]{:S(2)}, u32[]{:S(2)}) collective-permute-start(bf16[1,192,336]{2,1,0:T(8,128)(2,1)S(1)} %collective-permute-done.4.refs_7_), channel_id=1, source_target_pairs={{0,2},{1,3},{2,0},{3,1},{4,6},{5,7},{6,4},{7,5},{8,10},{9,11},{10,... | collective-permute-start | bytes 387080 | tf_op jit(solution)/shard_map/ppermute | solution.py:21
  15.2 6.4 %collective-permute-start.7 = (bf16[1,192,336]{2,1,0:T(8,128)(2,1)S(1)}, bf16[1,192,336]{2,1,0:T(8,128)(2,1)S(1)}, u32[]{:S(2)}, u32[]{:S(2)}) collective-permute-start(bf16[1,192,336]{2,1,0:T(8,128)(2,1)S(1)} %collective-permute-done.6.refs_5_), channel_id=1, source_target_pairs={{0,4},{1,5},{2,6},{3,7},{4,0},{5,1},{6,2},{7,3},{8,12},{9,13},{10,... | collective-permute-start | bytes 387080 | tf_op jit(solution)/shard_map/ppermute | solution.py:21
  19.2 5.1 %collective-permute-start.10 = (bf16[1,192,336]{2,1,0:T(8,128)(2,1)S(1)}, bf16[1,192,336]{2,1,0:T(8,128)(2,1)S(1)}, u32[]{:S(2)}, u32[]{:S(2)}) collective-permute-start(bf16[1,192,336]{2,1,0:T(8,128)(2,1)S(1)} %collective-permute-done.9.refs_10_), channel_id=1, source_target_pairs={{0,2},{1,3},{2,0},{3,1},{4,6},{5,7},{6,4},{7,5},{8,10},{9,11},{10,... | collective-permute-start | bytes 387080 | tf_op jit(solution)/shard_map/ppermute | solution.py:21
  25.5 1.5 %collective-permute-start.11 = (f32[2,2,96,97]{3,2,1,0:T(8,128)S(1)}, f32[2,2,96,97]{3,2,1,0:T(8,128)S(1)}, u32[]{:S(2)}, u32[]{:S(2)}) collective-permute-start(f32[2,2,96,97]{3,2,1,0:T(8,128)S(1)} %sketch_rows.1.part_ref), channel_id=1, source_target_pairs={{0,1},{1,0},{2,3},{3,2},{4,5},{5,4},{6,7},{7,6},{8,9},{9,8},{10,11... | collective-permute-start | bytes 446984 | tf_op jit(solution)/shard_map/ppermute | solution.py:21
  27.8 6.8 %collective-permute-start.12 = (f32[288,97]{1,0:T(8,128)S(1)}, f32[288,97]{1,0:T(8,128)S(1)}, u32[]{:S(2)}, u32[]{:S(2)}) collective-permute-start(f32[288,97]{1,0:T(8,128)S(1)} %get-tuple-element.38.refs_0_), channel_id=1, source_target_pairs={{0,2},{1,3},{2,0},{3,1},{4,6},{5,7},{6,4},{7,5},{8,10},{9,11},{10,... | collective-permute-start | bytes 335240 | tf_op jit(solution)/shard_map/ppermute | solution.py:21
  29.5 19.6 %collective-permute-start.16 = (bf16[2,192,336]{2,1,0:T(8,128)(2,1)S(1)}, bf16[2,192,336]{2,1,0:T(8,128)(2,1)S(1)}, u32[]{:S(2)}, u32[]{:S(2)}) collective-permute-start(bf16[2,192,336]{2,1,0:T(8,128)(2,1)S(1)} %get-tuple-element.46.far_ref), channel_id=1, source_target_pairs={{0,2},{1,3},{2,0},{3,1},{4,6},{5,7},{6,4},{7,5},{8,10},{9,11},{10,... | collective-permute-start | bytes 774152 | tf_op jit(solution)/shard_map/ppermute | solution.py:21
  29.9 19.2 %collective-permute-start.17 = (bf16[2,192,336]{2,1,0:T(8,128)(2,1)S(1)}, bf16[2,192,336]{2,1,0:T(8,128)(2,1)S(1)}, u32[]{:S(2)}, u32[]{:S(2)}) collective-permute-start(bf16[2,192,336]{2,1,0:T(8,128)(2,1)S(1)} %get-tuple-element.47), channel_id=1, source_target_pairs={{0,3},{1,2},{2,1},{3,0},{4,7},{5,6},{6,5},{7,4},{8,11},{9,10},{10,... | collective-permute-start | bytes 774152 | tf_op jit(solution)/shard_map/ppermute | solution.py:21
  34.5 9.3 %collective-permute-start.13 = (f32[288,97]{1,0:T(8,128)S(1)}, f32[288,97]{1,0:T(8,128)S(1)}, u32[]{:S(2)}, u32[]{:S(2)}) collective-permute-start(f32[288,97]{1,0:T(8,128)S(1)} %collective-permute-done.12.refs_2_), channel_id=1, source_target_pairs={{0,1},{1,0},{2,3},{3,2},{4,5},{5,4},{6,7},{7,6},{8,9},{9,8},{10,11... | collective-permute-start | bytes 335240 | tf_op jit(solution)/shard_map/ppermute | solution.py:21
  34.5 4.2 %collective-permute-start.14 = (f32[96,97]{1,0:T(8,128)S(1)}, f32[96,97]{1,0:T(8,128)S(1)}, u32[]{:S(2)}, u32[]{:S(2)}) collective-permute-start(f32[96,97]{1,0:T(8,128)S(1)} %slice_add_fusion.2), channel_id=1, source_target_pairs={{0,4},{1,5},{2,6},{3,7},{4,0},{5,1},{6,2},{7,3},{8,12},{9,13},{10,... | collective-permute-start | bytes 111752 | tf_op jit(solution)/shard_map/ppermute | solution.py:21
  38.7 5.1 %collective-permute-start.15 = (f32[96,97]{1,0:T(8,128)S(1)}, f32[96,97]{1,0:T(8,128)S(1)}, u32[]{:S(2)}, u32[]{:S(2)}) collective-permute-start(f32[96,97]{1,0:T(8,128)S(1)} %add.29), channel_id=1, source_target_pairs={{0,8},{1,9},{2,10},{3,11},{4,12},{5,13},{6,14},{7,15},{8,0},{9,1},... | collective-permute-start | bytes 111752 | tf_op jit(solution)/shard_map/ppermute | solution.py:21
  50.2 6.7 %collective-permute-start.18 = (f16[2,256,256]{2,1,0:T(8,128)(2,1)S(1)}, f16[2,256,256]{2,1,0:T(8,128)(2,1)S(1)}, u32[]{:S(2)}, u32[]{:S(2)}) collective-permute-start(f16[2,256,256]{2,1,0:T(8,128)(2,1)S(1)} %convert_element_type.27), channel_id=1, source_target_pairs={{0,2},{1,3},{2,0},{3,1},{4,6},{5,7},{6,4},{7,5},{8,10},{9,11},{10,... | collective-permute-start | bytes 786440 | tf_op jit(solution)/shard_map/ppermute | solution.py:21
  51.8 11.5 %collective-permute-start.20 = (f16[256,256]{1,0:T(8,128)(2,1)S(1)}, f16[256,256]{1,0:T(8,128)(2,1)S(1)}, u32[]{:S(2)}, u32[]{:S(2)}) collective-permute-start(f16[256,256]{1,0:T(8,128)(2,1)S(1)} %convert_element_type.31), channel_id=1, source_target_pairs={{0,8},{1,9},{2,10},{3,11},{4,12},{5,13},{6,14},{7,15},{8,0},{9,1},... | collective-permute-start | bytes 393224 | tf_op jit(solution)/shard_map/ppermute | solution.py:21
  54.2 9.2 %collective-permute-start.19 = (f16[256,256]{1,0:T(8,128)(2,1)S(1)}, f16[256,256]{1,0:T(8,128)(2,1)S(1)}, u32[]{:S(2)}, u32[]{:S(2)}) collective-permute-start(f16[256,256]{1,0:T(8,128)(2,1)S(1)} %convert_element_type.29), channel_id=1, source_target_pairs={{0,12},{1,13},{2,14},{3,15},{4,8},{5,9},{6,10},{7,11},{8,4},{9,5},... | collective-permute-start | bytes 393224 | tf_op jit(solution)/shard_map/ppermute | solution.py:21
  56.9 6.9 %collective-permute-start.21 = (f16[256,256]{1,0:T(8,128)(2,1)S(1)}, f16[256,256]{1,0:T(8,128)(2,1)S(1)}, u32[]{:S(2)}, u32[]{:S(2)}) collective-permute-start(f16[256,256]{1,0:T(8,128)(2,1)S(1)} %fusion.4), channel_id=1, source_target_pairs={{0,4},{1,5},{2,6},{3,7},{4,0},{5,1},{6,2},{7,3},{8,12},{9,13},{10,... | collective-permute-start | bytes 393224 | tf_op jit(solution)/shard_map/ppermute | solution.py:21

commit v9 on v8

--- a/solution.py
+++ b/solution.py
@@ -73,10 +73,9 @@
         else:
             own = stay_ref[zone]
         which, at = held[slot]
+        block = unfold(pieces[which][at], 2 * count, own.shape[1])
         for rows, data in enumerate((own, of_core(core, beside, zone))):
-            term = lax.dot_general(
-                data, pieces[which][at], (((1,), (1,)), ((), ())), preferred_element_type=jnp.float32
-            )
+            term = lax.dot_general(data, block, (((1,), (1,)), ((), ())), preferred_element_type=jnp.float32)
             totals[rows] = term if totals[rows] is None else totals[rows] + term
     for part, total in enumerate(totals):
         rows = total.shape[0] // 2
@@ -266,17 +265,17 @@
     return jnp.concatenate([value[:, :whole], jnp.concatenate(rest, axis=1)], axis=0)
 
 
-def unfold_kernel(folded_ref, out_ref):
-    rows, share = out_ref.shape
+def fold_kernel(sketch_ref, out_ref):
+    out_ref[0] = fold(jnp.concatenate([sketch_ref[0], sketch_ref[1]], axis=0))
+
+
+def unfold(value, rows, share):
     count = folds(rows, share)
     if not count:
-        out_ref[...] = folded_ref[...]
-        return
-    whole, each = share // 128 * 128, rows // count
-    wide = share - whole
-    out_ref[:, :whole] = folded_ref[:rows, :]
-    for i in range(count):
-        out_ref[each * i : each * (i + 1), whole:] = folded_ref[rows:, wide * i : wide * (i + 1)]
+        return value
+    wide = share - value.shape[1]
+    rest = [value[rows:, wide * i : wide * (i + 1)] for i in range(count)]
+    return jnp.concatenate([value[:rows], jnp.concatenate(rest, axis=0)], axis=1)
 
 
 def project_kernel(bound, gram_ref, *refs):
@@ -315,7 +314,7 @@
     for level in range(1, direct):
         if level == 2:
             first = [1 << bit for bit in reversed(range(1, direct))]
-            values, _ = tied([have[slot] for slot in first], [ahead])
+            values = lax.optimization_barrier(tuple(have[slot] for slot in first))
             have.update(zip(first, values))
         for slot in range(0, 1 << direct, 2):
             if slot.bit_count() == level:
@@ -356,7 +355,15 @@
         name="source_chunks",
     )(me.astype(jnp.int32).reshape(1), traces)
     core_in = [swap(value, 1, size) for value in core]
-    pieces = gather_slots(sketch.reshape(1, 2 * count, share), size, stay)
+    piece = pl.pallas_call(
+        fold_kernel,
+        out_shape=jax.ShapeDtypeStruct((1, *folded_shape(2 * count, share)), sketch.dtype),
+        in_specs=[VMEM],
+        out_specs=VMEM,
+        compiler_params=PARAMS,
+        name="fold_columns",
+    )(sketch)
+    pieces = gather_slots(piece, size, stay)
     values = [value for value, _ in pieces]
     held = {slot: (which, at) for which, (_, slots) in enumerate(pieces) for at, slot in enumerate(slots)}
     partial = pl.pallas_call(
@@ -422,12 +429,9 @@
             low, high = jnp.split(total, 2)
             total = low + send(high, GROUPS * low.shape[0])
         total = total[0]
-    level = gram[0, count] * bound
+    level = gram[:1, count:] * bound
     total = total * (level / TOP)
-    groups = folds(2 * count, share)
-    if groups:
-        rest = [total[2 * count :, i * (share - folded[1]) : (i + 1) * (share - folded[1])] for i in range(groups)]
-        total = jnp.concatenate([total[: 2 * count], jnp.concatenate(rest)], axis=1)
+    total = unfold(total, 2 * count, share)
     return basis, total.reshape(2, count, share)
 
 

time: 64.9 us -> 63.8 us (0.983)
  starting transfers between devices: 27 us -> 25.6 us
  local copies, waits for them, and re-layouts: 2.26 us -> 3.16 us
  waiting for transfers between devices: 23.4 us -> 22.6 us
    ppermute x22, starting transfers between devices: 27 us -> 25.6 us  [swap(): return lax.ppermute(value, 'rcv', [(i, i ^ mask) for i in range(size)])]
    unnamed x4, local copies, waits for them, and re-layouts: 1.58 us -> 2.48 us
    ppermute x22, waiting for transfers between devices: 23.4 us -> 22.6 us  [swap(): return lax.ppermute(value, 'rcv', [(i, i ^ mask) for i in range(size)])]
  transfers between devices with their start and end apart: 22 -> 22, of which waited for: 12 -> 10; matrix products, arithmetic and copies ran while one was open for 1% -> 1% of each run, Pallas kernels for 10% -> 11%
where the time goes in v9:
time: 63.8 us; the launch traced here: 63.6 us
  starting transfers between devices  25.6 us (40%)
  waiting for transfers between devices  22.6 us (35%)
  Pallas kernels  9.86 us (15%)
  local copies, waits for them, and re-layouts  3.16 us (5%)
  between operations  1.4 us (2%)
  other arithmetic  0.98 us (2%)
    ppermute x22, starting transfers between devices, swap(): return lax.ppermute(value, 'rcv', [(i, i ^ mask) for i in range(size)])  25.6 us
    ppermute x22, waiting for transfers between devices, swap(): return lax.ppermute(value, 'rcv', [(i, i ^ mask) for i in range(size)])  22.6 us
    pallas_call x1, Pallas kernels, per_device(): pl.pallas_call(functools.partial(basis_kernel, math.sqrt(rows * size)), o...  5.24 us
    unnamed x4, local copies, waits for them, and re-layouts  2.48 us
    pallas_call x1, Pallas kernels, per_device(): pl.pallas_call(functools.partial(chunk_kernel, share), out_shape=(chunk(z...  1.56 us
  transfers between devices with their start and end apart: 22, of which 10 were waited for; matrix products, arithmetic and copies ran while one was open for 1% of the time, Pallas kernels for 11%

profile of v9, /device:TPU:0, one launch (start us, length us, event | category | flops | bytes accessed | tf_op | source)
XLA Modules:
  0.0 63.6 jit_solution(6599048547283620644)
XLA Ops:
  0.6 0.9 %copy-done.1 = bf16[2,96,336]{2,1,0:T(8,128)(2,1)S(1)} copy-done((bf16[2,96,336]{2,1,0:T(8,128)(2,1)S(1)}, bf16[2,96,336]{2,1,0:T(8,128)(2,1)}, u32[]{:S(2)}) %copy-start.1) | copy-done | bytes 129048
  1.6 4.0 %collective-permute-start.4 = (bf16[1,256,256]{2,1,0:T(8,128)(2,1)S(1)}, bf16[1,256,256]{2,1,0:T(8,128)(2,1)S(1)}, u32[]{:S(2)}, u32[]{:S(2)}) collective-permute-start(bf16[1,256,256]{2,1,0:T(8,128)(2,1)S(1)} %fold_columns.1.refs_4_), channel_id=1, source_target_pairs={{0,8},{1,9},{2,10},{3,11},{4,12},{5,13},{6,14},{7,15},{8,0},{9,1},... | collective-permute-start | bytes 393224 | tf_op jit(solution)/shard_map/ppermute | solution.py:21
  5.7 1.6 %collective-permute-start.5 = (bf16[1,256,256]{2,1,0:T(8,128)(2,1)S(1)}, bf16[1,256,256]{2,1,0:T(8,128)(2,1)S(1)}, u32[]{:S(2)}, u32[]{:S(2)}) collective-permute-start(bf16[1,256,256]{2,1,0:T(8,128)(2,1)S(1)} %fold_columns.1.refs_4_), channel_id=1, source_target_pairs={{0,4},{1,5},{2,6},{3,7},{4,0},{5,1},{6,2},{7,3},{8,12},{9,13},{10,... | collective-permute-start | bytes 393224 | tf_op jit(solution)/shard_map/ppermute | solution.py:21
  7.2 1.5 %collective-permute-start.6 = (bf16[1,256,256]{2,1,0:T(8,128)(2,1)S(1)}, bf16[1,256,256]{2,1,0:T(8,128)(2,1)S(1)}, u32[]{:S(2)}, u32[]{:S(2)}) collective-permute-start(bf16[1,256,256]{2,1,0:T(8,128)(2,1)S(1)} %fold_columns.1.refs_4_), channel_id=1, source_target_pairs={{0,2},{1,3},{2,0},{3,1},{4,6},{5,7},{6,4},{7,5},{8,10},{9,11},{10,... | collective-permute-start | bytes 393224 | tf_op jit(solution)/shard_map/ppermute | solution.py:21
  8.7 1.6 %copy-done = bf16[2,96,5376]{2,1,0:T(8,128)(2,1)S(1)} copy-done((bf16[2,96,5376]{2,1,0:T(8,128)(2,1)S(1)}, bf16[2,96,5376]{2,1,0:T(8,128)(2,1)}, u32[]{:S(2)}) %copy-start) | copy-done | bytes 2064408
  10.3 1.6 %source_chunks.1 = (bf16[4,192,336]{2,1,0:T(8,128)(2,1)S(1)}, bf16[2,192,336]{2,1,0:T(8,128)(2,1)S(1)}, bf16[2,192,336]{2,1,0:T(8,128)(2,1)S(1)}, bf16[2,192,336...) custom-call(s32[1]{0:T(128)} %bitcast.me_ref, ...), custom_call_target="tpu_custom_call" | custom-call | tf_op jit(solution)/shard_map/source_chunks/pallas_call | solution.py:341
  12.5 1.3 %collective-permute-start.9 = (bf16[1,256,256]{2,1,0:T(8,128)(2,1)S(1)}, bf16[1,256,256]{2,1,0:T(8,128)(2,1)S(1)}, u32[]{:S(2)}, u32[]{:S(2)}) collective-permute-start(bf16[1,256,256]{2,1,0:T(8,128)(2,1)S(1)} %collective-permute-done.4.refs_7_), channel_id=1, source_target_pairs={{0,4},{1,5},{2,6},{3,7},{4,0},{5,1},{6,2},{7,3},{8,12},{9,13},{10,... | collective-permute-start | bytes 393224 | tf_op jit(solution)/shard_map/ppermute | solution.py:21
  14.2 1.5 %collective-permute-start.8 = (bf16[1,256,256]{2,1,0:T(8,128)(2,1)S(1)}, bf16[1,256,256]{2,1,0:T(8,128)(2,1)S(1)}, u32[]{:S(2)}, u32[]{:S(2)}) collective-permute-start(bf16[1,256,256]{2,1,0:T(8,128)(2,1)S(1)} %collective-permute-done.4.refs_7_), channel_id=1, source_target_pairs={{0,2},{1,3},{2,0},{3,1},{4,6},{5,7},{6,4},{7,5},{8,10},{9,11},{10,... | collective-permute-start | bytes 393224 | tf_op jit(solution)/shard_map/ppermute | solution.py:21
  15.7 0.6 %collective-permute-start.7 = (bf16[1,256,256]{2,1,0:T(8,128)(2,1)S(1)}, bf16[1,256,256]{2,1,0:T(8,128)(2,1)S(1)}, u32[]{:S(2)}, u32[]{:S(2)}) collective-permute-start(bf16[1,256,256]{2,1,0:T(8,128)(2,1)S(1)} %collective-permute-done.6.refs_5_), channel_id=1, source_target_pairs={{0,4},{1,5},{2,6},{3,7},{4,0},{5,1},{6,2},{7,3},{8,12},{9,13},{10,... | collective-permute-start | bytes 393224 | tf_op jit(solution)/shard_map/ppermute | solution.py:21
  16.4 1.6 %collective-permute-done.9.refs_10_ = bf16[1,256,256]{2,1,0:T(8,128)(2,1)S(1)} collective-permute-done((bf16[1,256,256]{2,1,0:T(8,128)(2,1)S(1)}, bf16[1,256,256]{2,1,0:T(8,128)(2,1)S(1)}, u32[]{:S(2)}, u32[]{:S(2)}) %collective-permute-start.9) | collective-permute-done | bytes 131104 | tf_op jit(solution)/shard_map/ppermute | solution.py:21
  18.0 1.0 %collective-permute-start.10 = (bf16[1,256,256]{2,1,0:T(8,128)(2,1)S(1)}, bf16[1,256,256]{2,1,0:T(8,128)(2,1)S(1)}, u32[]{:S(2)}, u32[]{:S(2)}) collective-permute-start(bf16[1,256,256]{2,1,0:T(8,128)(2,1)S(1)} %collective-permute-done.9.refs_10_), channel_id=1, source_target_pairs={{0,2},{1,3},{2,0},{3,1},{4,6},{5,7},{6,4},{7,5},{8,10},{9,11},{10,... | collective-permute-start | bytes 393224 | tf_op jit(solution)/shard_map/ppermute | solution.py:21
  19.0 1.9 %collective-permute-done.7.refs_8_ = bf16[1,256,256]{2,1,0:T(8,128)(2,1)S(1)} collective-permute-done((bf16[1,256,256]{2,1,0:T(8,128)(2,1)S(1)}, bf16[1,256,256]{2,1,0:T(8,128)(2,1)S(1)}, u32[]{:S(2)}, u32[]{:S(2)}) %collective-permute-start.7) | collective-permute-done | bytes 131104 | tf_op jit(solution)/shard_map/ppermute | solution.py:21
  20.9 2.1 %collective-permute-done.10.refs_11_ = bf16[1,256,256]{2,1,0:T(8,128)(2,1)S(1)} collective-permute-done((bf16[1,256,256]{2,1,0:T(8,128)(2,1)S(1)}, bf16[1,256,256]{2,1,0:T(8,128)(2,1)S(1)}, u32[]{:S(2)}, u32[]{:S(2)}) %collective-permute-start.10) | collective-permute-done | bytes 131104 | tf_op jit(solution)/shard_map/ppermute | solution.py:21
  23.0 1.2 %sketch_rows.1.part_ref = f32[2,2,96,97]{3,2,1,0:T(8,128)S(1)} custom-call(f32[1,5376]{1,0:T(1,128)S(1)} %get-tuple-element.27.peak_ref, bf16[4,192,336]{2,1,0:T(8,128)(2,1)S(1)} %get-tuple-element.28.stay_ref.refs_4_, bf16[2,192,336]{2,1,0:T(8,128)(2,1)S(1)} %get-tuple-element.29.near_ref.refs_5_, bf16[2,192,336]{2,1,0:T(8,128)(2,1)S(1)} %get-tuple-element.46.far_ref, ...), custom_call_target="tpu_custom_call" | custom-call | tf_op jit(solution)/shard_map/sketch_rows/pallas_call | solution.py:369
  24.2 1.4 %collective-permute-done.11.other_ref = f32[2,2,96,97]{3,2,1,0:T(8,128)S(1)} collective-permute-done((f32[2,2,96,97]{3,2,1,0:T(8,128)S(1)}, f32[2,2,96,97]{3,2,1,0:T(8,128)S(1)}, u32[]{:S(2)}, u32[]{:S(2)}) %collective-permute-start.11) | collective-permute-done | bytes 149024 | tf_op jit(solution)/shard_map/ppermute | solution.py:21
  25.7 0.7 %chip_gram.1 = (f32[288,97]{1,0:T(8,128)S(1)}, f32[288,97]{1,0:T(8,128)S(1)}) custom-call(f32[2,2,96,97]{3,2,1,0:T(8,128)S(1)} %sketch_rows.1.part_ref, f32[2,2,96,97]{3,2,1,0:T(8,128)S(1)} %collective-permute-done.11.other_ref), custom_call_target="tpu_custom_call" | custom-call | tf_op jit(solution)/shard_map/chip_gram/pallas_call | solution.py:378
  26.4 1.0 %collective-permute-start.12 = (f32[288,97]{1,0:T(8,128)S(1)}, f32[288,97]{1,0:T(8,128)S(1)}, u32[]{:S(2)}, u32[]{:S(2)}) collective-permute-start(f32[288,97]{1,0:T(8,128)S(1)} %get-tuple-element.38.refs_0_), channel_id=1, source_target_pairs={{0,2},{1,3},{2,0},{3,1},{4,6},{5,7},{6,4},{7,5},{8,10},{9,11},{10,... | collective-permute-start | bytes 335240 | tf_op jit(solution)/shard_map/ppermute | solution.py:21
  27.4 1.1 %collective-permute-start.16 = (bf16[2,192,336]{2,1,0:T(8,128)(2,1)S(1)}, bf16[2,192,336]{2,1,0:T(8,128)(2,1)S(1)}, u32[]{:S(2)}, u32[]{:S(2)}) collective-permute-start(bf16[2,192,336]{2,1,0:T(8,128)(2,1)S(1)} %get-tuple-element.46.far_ref), channel_id=1, source_target_pairs={{0,2},{1,3},{2,0},{3,1},{4,6},{5,7},{6,4},{7,5},{8,10},{9,11},{10,... | collective-permute-start | bytes 774152 | tf_op jit(solution)/shard_map/ppermute | solution.py:21
  28.6 4.5 %collective-permute-done.12.refs_2_ = f32[288,97]{1,0:T(8,128)S(1)} collective-permute-done((f32[288,97]{1,0:T(8,128)S(1)}, f32[288,97]{1,0:T(8,128)S(1)}, u32[]{:S(2)}, u32[]{:S(2)}) %collective-permute-start.12) | collective-permute-done | bytes 111776 | tf_op jit(solution)/shard_map/ppermute | solution.py:21
  33.2 1.0 %collective-permute-start.14 = (f32[96,97]{1,0:T(8,128)S(1)}, f32[96,97]{1,0:T(8,128)S(1)}, u32[]{:S(2)}, u32[]{:S(2)}) collective-permute-start(f32[96,97]{1,0:T(8,128)S(1)} %slice_add_fusion.2), channel_id=1, source_target_pairs={{0,4},{1,5},{2,6},{3,7},{4,0},{5,1},{6,2},{7,3},{8,12},{9,13},{10,... | collective-permute-start | bytes 111752 | tf_op jit(solution)/shard_map/ppermute | solution.py:21
  34.2 3.2 %collective-permute-done.14 = f32[96,97]{1,0:T(8,128)S(1)} collective-permute-done((f32[96,97]{1,0:T(8,128)S(1)}, f32[96,97]{1,0:T(8,128)S(1)}, u32[]{:S(2)}, u32[]{:S(2)}) %collective-permute-start.14) | collective-permute-done | bytes 37280 | tf_op jit(solution)/shard_map/ppermute | solution.py:21
  37.3 2.6 %collective-permute-start.15 = (f32[96,97]{1,0:T(8,128)S(1)}, f32[96,97]{1,0:T(8,128)S(1)}, u32[]{:S(2)}, u32[]{:S(2)}) collective-permute-start(f32[96,97]{1,0:T(8,128)S(1)} %add.29), channel_id=1, source_target_pairs={{0,8},{1,9},{2,10},{3,11},{4,12},{5,13},{6,14},{7,15},{8,0},{9,1},... | collective-permute-start | bytes 111752 | tf_op jit(solution)/shard_map/ppermute | solution.py:21
  39.9 2.7 %collective-permute-done.15 = f32[96,97]{1,0:T(8,128)S(1)} collective-permute-done((f32[96,97]{1,0:T(8,128)S(1)}, f32[96,97]{1,0:T(8,128)S(1)}, u32[]{:S(2)}, u32[]{:S(2)}) %collective-permute-start.15) | collective-permute-done | bytes 37280 | tf_op jit(solution)/shard_map/ppermute | solution.py:21
  42.6 5.2 %orthonormal_basis.1 = (f32[2,96,96]{2,1,0:T(8,128)}, bf16[192,192]{1,0:T(8,128)(2,1)S(1)}, bf16[192,192]{1,0:T(8,128)(2,1)S(1)}, bf16[192,192]{1,0:T(8,128)(2,1)S(1)}, bf16[192,192]{1,0:T(8,128)(2,1)S(1)}) custom-call(f32[288,97]{1,0:T(8,128)S(1)} %get-tuple-element.38.refs_0_, f32[288,97]{1,0:T(8,128)S(1)} %get-tuple-element.39.refs_1_, ...), custom_call_target="tpu_custom_call" | custom-call | flops 1500000000 | bytes 1000000 | tf_op jit(solution)/shard_map/orthonormal_basis/pallas_call | solution.py:395
  47.9 1.1 %project_rows.1 = (f32[2,256,256]{2,1,0:T(8,128)S(1)}, f32[2,256,256]{2,1,0:T(8,128)S(1)}, f32[256,256]{1,0:T(8,128)S(1)}, f32[256,256]{1,0:T(8,128)S(1)}) custom-call(f32[96,97]{1,0:T(8,128)S(1)} %add.30.refs_4_.gram_ref, bf16[192,192]{1,0:T(8,128)(2,1)S(1)} %get-tuple-element.41.refs_0_, bf16[192,192]{1,0:T(8,128)(2,1)S(1)} %get-tuple-element.42.refs_1_, ...), custom_call_target="tpu_custom_call" | custom-call | tf_op jit(solution)/shard_map/project_rows/pallas_call | solution.py:407
  49.0 1.6 %collective-permute-start.18 = (f16[2,256,256]{2,1,0:T(8,128)(2,1)S(1)}, f16[2,256,256]{2,1,0:T(8,128)(2,1)S(1)}, u32[]{:S(2)}, u32[]{:S(2)}) collective-permute-start(f16[2,256,256]{2,1,0:T(8,128)(2,1)S(1)} %convert_element_type.27), channel_id=1, source_target_pairs={{0,2},{1,3},{2,0},{3,1},{4,6},{5,7},{6,4},{7,5},{8,10},{9,11},{10,... | collective-permute-start | bytes 786440 | tf_op jit(solution)/shard_map/ppermute | solution.py:21
  50.6 2.5 %collective-permute-start.20 = (f16[256,256]{1,0:T(8,128)(2,1)S(1)}, f16[256,256]{1,0:T(8,128)(2,1)S(1)}, u32[]{:S(2)}, u32[]{:S(2)}) collective-permute-start(f16[256,256]{1,0:T(8,128)(2,1)S(1)} %convert_element_type.31), channel_id=1, source_target_pairs={{0,8},{1,9},{2,10},{3,11},{4,12},{5,13},{6,14},{7,15},{8,0},{9,1},... | collective-permute-start | bytes 393224 | tf_op jit(solution)/shard_map/ppermute | solution.py:21
  53.1 1.5 %collective-permute-start.19 = (f16[256,256]{1,0:T(8,128)(2,1)S(1)}, f16[256,256]{1,0:T(8,128)(2,1)S(1)}, u32[]{:S(2)}, u32[]{:S(2)}) collective-permute-start(f16[256,256]{1,0:T(8,128)(2,1)S(1)} %convert_element_type.29), channel_id=1, source_target_pairs={{0,12},{1,13},{2,14},{3,15},{4,8},{5,9},{6,10},{7,11},{8,4},{9,5},... | collective-permute-start | bytes 393224 | tf_op jit(solution)/shard_map/ppermute | solution.py:21
  54.6 1.0 %collective-permute-done.18 = f16[2,256,256]{2,1,0:T(8,128)(2,1)S(1)} collective-permute-done((f16[2,256,256]{2,1,0:T(8,128)(2,1)S(1)}, f16[2,256,256]{2,1,0:T(8,128)(2,1)S(1)}, u32[]{:S(2)}, u32[]{:S(2)}) %collective-permute-start.18) | collective-permute-done | bytes 262176 | tf_op jit(solution)/shard_map/ppermute | solution.py:21
  55.8 1.6 %collective-permute-start.21 = (f16[256,256]{1,0:T(8,128)(2,1)S(1)}, f16[256,256]{1,0:T(8,128)(2,1)S(1)}, u32[]{:S(2)}, u32[]{:S(2)}) collective-permute-start(f16[256,256]{1,0:T(8,128)(2,1)S(1)} %fusion.4), channel_id=1, source_target_pairs={{0,4},{1,5},{2,6},{3,7},{4,0},{5,1},{6,2},{7,3},{8,12},{9,13},{10,... | collective-permute-start | bytes 393224 | tf_op jit(solution)/shard_map/ppermute | solution.py:21
  58.6 3.6 %collective-permute-done.20 = f16[256,256]{1,0:T(8,128)(2,1)S(1)} collective-permute-done((f16[256,256]{1,0:T(8,128)(2,1)S(1)}, f16[256,256]{1,0:T(8,128)(2,1)S(1)}, u32[]{:S(2)}, u32[]{:S(2)}) %collective-permute-start.20) | collective-permute-done | bytes 131104 | tf_op jit(solution)/shard_map/ppermute | solution.py:21
  62.9 0.7 %maximum_maximum_fusion = f32[192,336]{1,0:T(8,128)} fusion(f32[64,80]{1,0:T(8,128)S(1)} %get-tuple-element.53, f32[64,80]{1,0:T(8,128)S(1)} %get-tuple-element.54, f32[64,80]{1,0:T(8,128)S(1)} %get-tuple-element.52, f32[192,256]{1,0:T(8,128)S(1)} %slice.48), kind=kLoop, calls=%fused_computation | loop fusion | flops 193536 | bytes 516096 | tf_op jit(solution)/shard_map/concatenate | solution.py:278
  (35 shorter events, 2.9 us)
Async XLA Ops:
  0.6 0.9 %copy-start.1 = (bf16[2,96,336]{2,1,0:T(8,128)(2,1)S(1)}, bf16[2,96,336]{2,1,0:T(8,128)(2,1)}, u32[]{:S(2)}) copy-start(bf16[2,96,336]{2,1,0:T(8,128)(2,1)} %sketch_ref.1) | copy-start | bytes 387076
  1.6 10.8 %collective-permute-start.4 = (bf16[1,256,256]{2,1,0:T(8,128)(2,1)S(1)}, bf16[1,256,256]{2,1,0:T(8,128)(2,1)S(1)}, u32[]{:S(2)}, u32[]{:S(2)}) collective-permute-start(bf16[1,256,256]{2,1,0:T(8,128)(2,1)S(1)} %fold_columns.1.refs_4_), channel_id=1, source_target_pairs={{0,8},{1,9},{2,10},{3,11},{4,12},{5,13},{6,14},{7,15},{8,0},{9,1},... | collective-permute-start | bytes 393224 | tf_op jit(solution)/shard_map/ppermute | solution.py:21
  5.7 6.8 %collective-permute-start.5 = (bf16[1,256,256]{2,1,0:T(8,128)(2,1)S(1)}, bf16[1,256,256]{2,1,0:T(8,128)(2,1)S(1)}, u32[]{:S(2)}, u32[]{:S(2)}) collective-permute-start(bf16[1,256,256]{2,1,0:T(8,128)(2,1)S(1)} %fold_columns.1.refs_4_), channel_id=1, source_target_pairs={{0,4},{1,5},{2,6},{3,7},{4,0},{5,1},{6,2},{7,3},{8,12},{9,13},{10,... | collective-permute-start | bytes 393224 | tf_op jit(solution)/shard_map/ppermute | solution.py:21
  7.2 5.2 %collective-permute-start.6 = (bf16[1,256,256]{2,1,0:T(8,128)(2,1)S(1)}, bf16[1,256,256]{2,1,0:T(8,128)(2,1)S(1)}, u32[]{:S(2)}, u32[]{:S(2)}) collective-permute-start(bf16[1,256,256]{2,1,0:T(8,128)(2,1)S(1)} %fold_columns.1.refs_4_), channel_id=1, source_target_pairs={{0,2},{1,3},{2,0},{3,1},{4,6},{5,7},{6,4},{7,5},{8,10},{9,11},{10,... | collective-permute-start | bytes 393224 | tf_op jit(solution)/shard_map/ppermute | solution.py:21
  8.7 1.6 %copy-start = (bf16[2,96,5376]{2,1,0:T(8,128)(2,1)S(1)}, bf16[2,96,5376]{2,1,0:T(8,128)(2,1)}, u32[]{:S(2)}) copy-start(bf16[2,96,5376]{2,1,0:T(8,128)(2,1)} %traces_ref.1) | copy-start | bytes 6193156
  11.9 2.4 %collective-permute-start = (bf16[2,192,336]{2,1,0:T(8,128)(2,1)S(1)}, bf16[2,192,336]{2,1,0:T(8,128)(2,1)S(1)}, u32[]{:S(2)}, u32[]{:S(2)}) collective-permute-start(bf16[2,192,336]{2,1,0:T(8,128)(2,1)S(1)} %get-tuple-element.31), channel_id=1, source_target_pairs={{0,1},{1,0},{2,3},{3,2},{4,5},{5,4},{6,7},{7,6},{8,9},{9,8},{10,11... | collective-permute-start | bytes 774152 | tf_op jit(solution)/shard_map/ppermute | solution.py:21
  12.0 3.8 %collective-permute-start.1 = (bf16[2,192,336]{2,1,0:T(8,128)(2,1)S(1)}, bf16[2,192,336]{2,1,0:T(8,128)(2,1)S(1)}, u32[]{:S(2)}, u32[]{:S(2)}) collective-permute-start(bf16[2,192,336]{2,1,0:T(8,128)(2,1)S(1)} %get-tuple-element.32), channel_id=1, source_target_pairs={{0,1},{1,0},{2,3},{3,2},{4,5},{5,4},{6,7},{7,6},{8,9},{9,8},{10,11... | collective-permute-start | bytes 774152 | tf_op jit(solution)/shard_map/ppermute | solution.py:21
  12.5 5.5 %collective-permute-start.9 = (bf16[1,256,256]{2,1,0:T(8,128)(2,1)S(1)}, bf16[1,256,256]{2,1,0:T(8,128)(2,1)S(1)}, u32[]{:S(2)}, u32[]{:S(2)}) collective-permute-start(bf16[1,256,256]{2,1,0:T(8,128)(2,1)S(1)} %collective-permute-done.4.refs_7_), channel_id=1, source_target_pairs={{0,4},{1,5},{2,6},{3,7},{4,0},{5,1},{6,2},{7,3},{8,12},{9,13},{10,... | collective-permute-start | bytes 393224 | tf_op jit(solution)/shard_map/ppermute | solution.py:21
  13.7 5.3 %collective-permute-start.2 = (bf16[2,192,336]{2,1,0:T(8,128)(2,1)S(1)}, bf16[2,192,336]{2,1,0:T(8,128)(2,1)S(1)}, u32[]{:S(2)}, u32[]{:S(2)}) collective-permute-start(bf16[2,192,336]{2,1,0:T(8,128)(2,1)S(1)} %get-tuple-element.33), channel_id=1, source_target_pairs={{0,1},{1,0},{2,3},{3,2},{4,5},{5,4},{6,7},{7,6},{8,9},{9,8},{10,11... | collective-permute-start | bytes 774152 | tf_op jit(solution)/shard_map/ppermute | solution.py:21
  13.7 5.3 %collective-permute-start.3 = (bf16[2,192,336]{2,1,0:T(8,128)(2,1)S(1)}, bf16[2,192,336]{2,1,0:T(8,128)(2,1)S(1)}, u32[]{:S(2)}, u32[]{:S(2)}) collective-permute-start(bf16[2,192,336]{2,1,0:T(8,128)(2,1)S(1)} %get-tuple-element.34), channel_id=1, source_target_pairs={{0,1},{1,0},{2,3},{3,2},{4,5},{5,4},{6,7},{7,6},{8,9},{9,8},{10,11... | collective-permute-start | bytes 774152 | tf_op jit(solution)/shard_map/ppermute | solution.py:21
  14.2 6.6 %collective-permute-start.8 = (bf16[1,256,256]{2,1,0:T(8,128)(2,1)S(1)}, bf16[1,256,256]{2,1,0:T(8,128)(2,1)S(1)}, u32[]{:S(2)}, u32[]{:S(2)}) collective-permute-start(bf16[1,256,256]{2,1,0:T(8,128)(2,1)S(1)} %collective-permute-done.4.refs_7_), channel_id=1, source_target_pairs={{0,2},{1,3},{2,0},{3,1},{4,6},{5,7},{6,4},{7,5},{8,10},{9,11},{10,... | collective-permute-start | bytes 393224 | tf_op jit(solution)/shard_map/ppermute | solution.py:21
  15.7 5.1 %collective-permute-start.7 = (bf16[1,256,256]{2,1,0:T(8,128)(2,1)S(1)}, bf16[1,256,256]{2,1,0:T(8,128)(2,1)S(1)}, u32[]{:S(2)}, u32[]{:S(2)}) collective-permute-start(bf16[1,256,256]{2,1,0:T(8,128)(2,1)S(1)} %collective-permute-done.6.refs_5_), channel_id=1, source_target_pairs={{0,4},{1,5},{2,6},{3,7},{4,0},{5,1},{6,2},{7,3},{8,12},{9,13},{10,... | collective-permute-start | bytes 393224 | tf_op jit(solution)/shard_map/ppermute | solution.py:21
  18.0 5.0 %collective-permute-start.10 = (bf16[1,256,256]{2,1,0:T(8,128)(2,1)S(1)}, bf16[1,256,256]{2,1,0:T(8,128)(2,1)S(1)}, u32[]{:S(2)}, u32[]{:S(2)}) collective-permute-start(bf16[1,256,256]{2,1,0:T(8,128)(2,1)S(1)} %collective-permute-done.9.refs_10_), channel_id=1, source_target_pairs={{0,2},{1,3},{2,0},{3,1},{4,6},{5,7},{6,4},{7,5},{8,10},{9,11},{10,... | collective-permute-start | bytes 393224 | tf_op jit(solution)/shard_map/ppermute | solution.py:21
  24.2 1.5 %collective-permute-start.11 = (f32[2,2,96,97]{3,2,1,0:T(8,128)S(1)}, f32[2,2,96,97]{3,2,1,0:T(8,128)S(1)}, u32[]{:S(2)}, u32[]{:S(2)}) collective-permute-start(f32[2,2,96,97]{3,2,1,0:T(8,128)S(1)} %sketch_rows.1.part_ref), channel_id=1, source_target_pairs={{0,1},{1,0},{2,3},{3,2},{4,5},{5,4},{6,7},{7,6},{8,9},{9,8},{10,11... | collective-permute-start | bytes 446984 | tf_op jit(solution)/shard_map/ppermute | solution.py:21
  26.4 6.8 %collective-permute-start.12 = (f32[288,97]{1,0:T(8,128)S(1)}, f32[288,97]{1,0:T(8,128)S(1)}, u32[]{:S(2)}, u32[]{:S(2)}) collective-permute-start(f32[288,97]{1,0:T(8,128)S(1)} %get-tuple-element.38.refs_0_), channel_id=1, source_target_pairs={{0,2},{1,3},{2,0},{3,1},{4,6},{5,7},{6,4},{7,5},{8,10},{9,11},{10,... | collective-permute-start | bytes 335240 | tf_op jit(solution)/shard_map/ppermute | solution.py:21
  27.4 20.4 %collective-permute-start.16 = (bf16[2,192,336]{2,1,0:T(8,128)(2,1)S(1)}, bf16[2,192,336]{2,1,0:T(8,128)(2,1)S(1)}, u32[]{:S(2)}, u32[]{:S(2)}) collective-permute-start(bf16[2,192,336]{2,1,0:T(8,128)(2,1)S(1)} %get-tuple-element.46.far_ref), channel_id=1, source_target_pairs={{0,2},{1,3},{2,0},{3,1},{4,6},{5,7},{6,4},{7,5},{8,10},{9,11},{10,... | collective-permute-start | bytes 774152 | tf_op jit(solution)/shard_map/ppermute | solution.py:21
  28.5 19.4 %collective-permute-start.17 = (bf16[2,192,336]{2,1,0:T(8,128)(2,1)S(1)}, bf16[2,192,336]{2,1,0:T(8,128)(2,1)S(1)}, u32[]{:S(2)}, u32[]{:S(2)}) collective-permute-start(bf16[2,192,336]{2,1,0:T(8,128)(2,1)S(1)} %get-tuple-element.47), channel_id=1, source_target_pairs={{0,3},{1,2},{2,1},{3,0},{4,7},{5,6},{6,5},{7,4},{8,11},{9,10},{10,... | collective-permute-start | bytes 774152 | tf_op jit(solution)/shard_map/ppermute | solution.py:21
  33.2 9.5 %collective-permute-start.13 = (f32[288,97]{1,0:T(8,128)S(1)}, f32[288,97]{1,0:T(8,128)S(1)}, u32[]{:S(2)}, u32[]{:S(2)}) collective-permute-start(f32[288,97]{1,0:T(8,128)S(1)} %collective-permute-done.12.refs_2_), channel_id=1, source_target_pairs={{0,1},{1,0},{2,3},{3,2},{4,5},{5,4},{6,7},{7,6},{8,9},{9,8},{10,11... | collective-permute-start | bytes 335240 | tf_op jit(solution)/shard_map/ppermute | solution.py:21
  33.2 4.2 %collective-permute-start.14 = (f32[96,97]{1,0:T(8,128)S(1)}, f32[96,97]{1,0:T(8,128)S(1)}, u32[]{:S(2)}, u32[]{:S(2)}) collective-permute-start(f32[96,97]{1,0:T(8,128)S(1)} %slice_add_fusion.2), channel_id=1, source_target_pairs={{0,4},{1,5},{2,6},{3,7},{4,0},{5,1},{6,2},{7,3},{8,12},{9,13},{10,... | collective-permute-start | bytes 111752 | tf_op jit(solution)/shard_map/ppermute | solution.py:21
  37.3 5.3 %collective-permute-start.15 = (f32[96,97]{1,0:T(8,128)S(1)}, f32[96,97]{1,0:T(8,128)S(1)}, u32[]{:S(2)}, u32[]{:S(2)}) collective-permute-start(f32[96,97]{1,0:T(8,128)S(1)} %add.29), channel_id=1, source_target_pairs={{0,8},{1,9},{2,10},{3,11},{4,12},{5,13},{6,14},{7,15},{8,0},{9,1},... | collective-permute-start | bytes 111752 | tf_op jit(solution)/shard_map/ppermute | solution.py:21
  49.0 6.7 %collective-permute-start.18 = (f16[2,256,256]{2,1,0:T(8,128)(2,1)S(1)}, f16[2,256,256]{2,1,0:T(8,128)(2,1)S(1)}, u32[]{:S(2)}, u32[]{:S(2)}) collective-permute-start(f16[2,256,256]{2,1,0:T(8,128)(2,1)S(1)} %convert_element_type.27), channel_id=1, source_target_pairs={{0,2},{1,3},{2,0},{3,1},{4,6},{5,7},{6,4},{7,5},{8,10},{9,11},{10,... | collective-permute-start | bytes 786440 | tf_op jit(solution)/shard_map/ppermute | solution.py:21
  50.6 11.5 %collective-permute-start.20 = (f16[256,256]{1,0:T(8,128)(2,1)S(1)}, f16[256,256]{1,0:T(8,128)(2,1)S(1)}, u32[]{:S(2)}, u32[]{:S(2)}) collective-permute-start(f16[256,256]{1,0:T(8,128)(2,1)S(1)} %convert_element_type.31), channel_id=1, source_target_pairs={{0,8},{1,9},{2,10},{3,11},{4,12},{5,13},{6,14},{7,15},{8,0},{9,1},... | collective-permute-start | bytes 393224 | tf_op jit(solution)/shard_map/ppermute | solution.py:21
  53.1 9.0 %collective-permute-start.19 = (f16[256,256]{1,0:T(8,128)(2,1)S(1)}, f16[256,256]{1,0:T(8,128)(2,1)S(1)}, u32[]{:S(2)}, u32[]{:S(2)}) collective-permute-start(f16[256,256]{1,0:T(8,128)(2,1)S(1)} %convert_element_type.29), channel_id=1, source_target_pairs={{0,12},{1,13},{2,14},{3,15},{4,8},{5,9},{6,10},{7,11},{8,4},{9,5},... | collective-permute-start | bytes 393224 | tf_op jit(solution)/shard_map/ppermute | solution.py:21
  55.8 7.0 %collective-permute-start.21 = (f16[256,256]{1,0:T(8,128)(2,1)S(1)}, f16[256,256]{1,0:T(8,128)(2,1)S(1)}, u32[]{:S(2)}, u32[]{:S(2)}) collective-permute-start(f16[256,256]{1,0:T(8,128)(2,1)S(1)} %fusion.4), channel_id=1, source_target_pairs={{0,4},{1,5},{2,6},{3,7},{4,0},{5,1},{6,2},{7,3},{8,12},{9,13},{10,... | collective-permute-start | bytes 393224 | tf_op jit(solution)/shard_map/ppermute | solution.py:21

commit v10 on v9

--- a/solution.py
+++ b/solution.py
@@ -31,7 +31,7 @@
     )
 
 
-def chunk_kernel(share, me_ref, traces_ref, stay_ref, near_ref, far_ref, cross_ref, peak_ref, *refs):
+def chunk_kernel(share, me_ref, traces_ref, stay_ref, near_ref, far_ref, cross_ref, *refs):
     core, held_ref = refs[:-1], refs[-1]
     rows, sources = traces_ref.shape[1:]
     me = me_ref[0]
@@ -49,11 +49,15 @@
     near_ref[...] = held_ref[2, :half]
     far_ref[...] = held_ref[2, half:]
     cross_ref[...] = held_ref[3, half:]
-    peak = jnp.maximum(
-        jnp.max(jnp.abs(traces_ref[0]), axis=0, keepdims=True),
-        jnp.max(jnp.abs(traces_ref[1]), axis=0, keepdims=True),
-    )
-    peak_ref[...] = peak.astype(jnp.float32)
+
+
+def peak_kernel(*refs):
+    peak = None
+    for ref in refs[:-1]:
+        for zone in range(ref.shape[0]):
+            largest = jnp.max(jnp.abs(ref[zone]), axis=0, keepdims=True)
+            peak = largest if peak is None else jnp.maximum(peak, largest)
+    refs[-1][...] = peak.astype(jnp.float32)
 
 
 def of_core(core, beside, zone):
@@ -224,8 +228,9 @@
     low_re = jnp.where(row >= column, low_re[:, :count] * across, 0.0)
     low_im = jnp.where(row >= column, low_im[:, :count] * across, 0.0)
     stacked = jnp.concatenate([ref[count:, :count] for ref in sketched], axis=0)
-    by_re = exact(stacked, low_re, ((1,), (1,)))
-    by_im = exact(stacked, low_im, ((1,), (1,)))
+    spare = jnp.zeros((-count % 128, count), jnp.float32)
+    both = exact(stacked, jnp.concatenate([low_re, spare, low_im], axis=0), ((1,), (1,)))
+    by_re, by_im = both[:, :count], both[:, count + spare.shape[0] :]
     for group in range(GROUPS):
         real = slice(2 * rows * group, 2 * rows * group + rows)
         imag = slice(2 * rows * group + rows, 2 * rows * (group + 1))
@@ -338,23 +343,30 @@
     bits = size.bit_length() - 1
     chunk = lambda slots: jax.ShapeDtypeStruct((slots, 2 * rows, share), traces.dtype)
 
-    stay, near, far, cross, peak, *core = pl.pallas_call(
+    stay, near, far, cross, *core = pl.pallas_call(
         functools.partial(chunk_kernel, share),
         out_shape=(
             chunk(zones),
             chunk(half),
             chunk(half),
             chunk(half),
-            jax.ShapeDtypeStruct((1, sources), jnp.float32),
         )
         + (chunk(zones // PARTS),) * (2 * PARTS),
         in_specs=[SMEM, VMEM],
-        out_specs=(VMEM,) * (5 + 2 * PARTS),
+        out_specs=(VMEM,) * (4 + 2 * PARTS),
         scratch_shapes=[pltpu.VMEM((GROUPS, zones, 2 * rows, share), traces.dtype)],
         compiler_params=PARAMS,
         name="source_chunks",
     )(me.astype(jnp.int32).reshape(1), traces)
     core_in = [swap(value, 1, size) for value in core]
+    peak = pl.pallas_call(
+        peak_kernel,
+        out_shape=jax.ShapeDtypeStruct((1, share), jnp.float32),
+        in_specs=[VMEM] * (4 + 2 * PARTS),
+        out_specs=VMEM,
+        compiler_params=PARAMS,
+        name="largest_value",
+    )(stay, near, far, cross, *core)
     piece = pl.pallas_call(
         fold_kernel,
         out_shape=jax.ShapeDtypeStruct((1, *folded_shape(2 * count, share)), sketch.dtype),

time: 63.8 us -> 63.7 us (level)
  starting transfers between devices: 25.6 us -> 28.4 us
  waiting for transfers between devices: 22.6 us -> 19.9 us
    ppermute x22, starting transfers between devices: 25.6 us -> 28.4 us  [swap(): return lax.ppermute(value, 'rcv', [(i, i ^ mask) for i in range(size)])]
    ppermute x22, waiting for transfers between devices: 22.6 us -> 19.9 us  [swap(): return lax.ppermute(value, 'rcv', [(i, i ^ mask) for i in range(size)])]
  transfers between devices with their start and end apart: 22 -> 22, of which waited for: 10 -> 12; matrix products, arithmetic and copies ran while one was open for 1% -> 1% of each run, Pallas kernels for 11% -> 11%
where the time goes in v10:
time: 63.7 us; the launch traced here: 63.6 us
  starting transfers between devices  28.4 us (45%)
  waiting for transfers between devices  19.9 us (31%)
  Pallas kernels  9.74 us (15%)
  local copies, waits for them, and re-layouts  3.16 us (5%)
  between operations  1.41 us (2%)
  other arithmetic  0.98 us (2%)
    ppermute x22, starting transfers between devices, swap(): return lax.ppermute(value, 'rcv', [(i, i ^ mask) for i in range(size)])  28.4 us
    ppermute x22, waiting for transfers between devices, swap(): return lax.ppermute(value, 'rcv', [(i, i ^ mask) for i in range(size)])  19.9 us
    pallas_call x1, Pallas kernels, per_device(): pl.pallas_call(functools.partial(basis_kernel, math.sqrt(rows * size)), o...  5.18 us
    unnamed x4, local copies, waits for them, and re-layouts  2.48 us
  transfers between devices with their start and end apart: 22, of which 12 were waited for; matrix products, arithmetic and copies ran while one was open for 1% of the time, Pallas kernels for 11%

profile of v10, /device:TPU:0, one launch (start us, length us, event | category | flops | bytes accessed | tf_op | source)
XLA Modules:
  0.0 63.6 jit_solution(18186766760383198358)
XLA Ops:
  0.6 0.9 %copy-done.1 = bf16[2,96,336]{2,1,0:T(8,128)(2,1)S(1)} copy-done((bf16[2,96,336]{2,1,0:T(8,128)(2,1)S(1)}, bf16[2,96,336]{2,1,0:T(8,128)(2,1)}, u32[]{:S(2)}) %copy-start.1) | copy-done | bytes 129048
  1.6 4.0 %collective-permute-start.4 = (bf16[1,256,256]{2,1,0:T(8,128)(2,1)S(1)}, bf16[1,256,256]{2,1,0:T(8,128)(2,1)S(1)}, u32[]{:S(2)}, u32[]{:S(2)}) collective-permute-start(bf16[1,256,256]{2,1,0:T(8,128)(2,1)S(1)} %fold_columns.1.refs_4_), channel_id=1, source_target_pairs={{0,8},{1,9},{2,10},{3,11},{4,12},{5,13},{6,14},{7,15},{8,0},{9,1},... | collective-permute-start | bytes 393224 | tf_op jit(solution)/shard_map/ppermute | solution.py:21
  5.7 1.6 %collective-permute-start.5 = (bf16[1,256,256]{2,1,0:T(8,128)(2,1)S(1)}, bf16[1,256,256]{2,1,0:T(8,128)(2,1)S(1)}, u32[]{:S(2)}, u32[]{:S(2)}) collective-permute-start(bf16[1,256,256]{2,1,0:T(8,128)(2,1)S(1)} %fold_columns.1.refs_4_), channel_id=1, source_target_pairs={{0,4},{1,5},{2,6},{3,7},{4,0},{5,1},{6,2},{7,3},{8,12},{9,13},{10,... | collective-permute-start | bytes 393224 | tf_op jit(solution)/shard_map/ppermute | solution.py:21
  7.2 1.5 %collective-permute-start.6 = (bf16[1,256,256]{2,1,0:T(8,128)(2,1)S(1)}, bf16[1,256,256]{2,1,0:T(8,128)(2,1)S(1)}, u32[]{:S(2)}, u32[]{:S(2)}) collective-permute-start(bf16[1,256,256]{2,1,0:T(8,128)(2,1)S(1)} %fold_columns.1.refs_4_), channel_id=1, source_target_pairs={{0,2},{1,3},{2,0},{3,1},{4,6},{5,7},{6,4},{7,5},{8,10},{9,11},{10,... | collective-permute-start | bytes 393224 | tf_op jit(solution)/shard_map/ppermute | solution.py:21
  8.7 1.6 %copy-done = bf16[2,96,5376]{2,1,0:T(8,128)(2,1)S(1)} copy-done((bf16[2,96,5376]{2,1,0:T(8,128)(2,1)S(1)}, bf16[2,96,5376]{2,1,0:T(8,128)(2,1)}, u32[]{:S(2)}) %copy-start) | copy-done | bytes 2064408
  10.3 1.0 %source_chunks.1 = (bf16[4,192,336]{2,1,0:T(8,128)(2,1)S(1)}, bf16[2,192,336]{2,1,0:T(8,128)(2,1)S(1)}, bf16[2,192,336]{2,1,0:T(8,128)(2,1)S(1)}, bf16[2,192,336...) custom-call(s32[1]{0:T(128)} %bitcast.me_ref, ...), custom_call_target="tpu_custom_call" | custom-call | tf_op jit(solution)/shard_map/source_chunks/pallas_call | solution.py:346
  12.3 1.4 %collective-permute-start.9 = (bf16[1,256,256]{2,1,0:T(8,128)(2,1)S(1)}, bf16[1,256,256]{2,1,0:T(8,128)(2,1)S(1)}, u32[]{:S(2)}, u32[]{:S(2)}) collective-permute-start(bf16[1,256,256]{2,1,0:T(8,128)(2,1)S(1)} %collective-permute-done.4.refs_7_), channel_id=1, source_target_pairs={{0,4},{1,5},{2,6},{3,7},{4,0},{5,1},{6,2},{7,3},{8,12},{9,13},{10,... | collective-permute-start | bytes 393224 | tf_op jit(solution)/shard_map/ppermute | solution.py:21
  14.2 1.5 %collective-permute-start.8 = (bf16[1,256,256]{2,1,0:T(8,128)(2,1)S(1)}, bf16[1,256,256]{2,1,0:T(8,128)(2,1)S(1)}, u32[]{:S(2)}, u32[]{:S(2)}) collective-permute-start(bf16[1,256,256]{2,1,0:T(8,128)(2,1)S(1)} %collective-permute-done.4.refs_7_), channel_id=1, source_target_pairs={{0,2},{1,3},{2,0},{3,1},{4,6},{5,7},{6,4},{7,5},{8,10},{9,11},{10,... | collective-permute-start | bytes 393224 | tf_op jit(solution)/shard_map/ppermute | solution.py:21
  15.7 0.6 %collective-permute-start.7 = (bf16[1,256,256]{2,1,0:T(8,128)(2,1)S(1)}, bf16[1,256,256]{2,1,0:T(8,128)(2,1)S(1)}, u32[]{:S(2)}, u32[]{:S(2)}) collective-permute-start(bf16[1,256,256]{2,1,0:T(8,128)(2,1)S(1)} %collective-permute-done.6.refs_5_), channel_id=1, source_target_pairs={{0,4},{1,5},{2,6},{3,7},{4,0},{5,1},{6,2},{7,3},{8,12},{9,13},{10,... | collective-permute-start | bytes 393224 | tf_op jit(solution)/shard_map/ppermute | solution.py:21
  16.4 1.1 %collective-permute-done.9.refs_10_ = bf16[1,256,256]{2,1,0:T(8,128)(2,1)S(1)} collective-permute-done((bf16[1,256,256]{2,1,0:T(8,128)(2,1)S(1)}, bf16[1,256,256]{2,1,0:T(8,128)(2,1)S(1)}, u32[]{:S(2)}, u32[]{:S(2)}) %collective-permute-start.9) | collective-permute-done | bytes 131104 | tf_op jit(solution)/shard_map/ppermute | solution.py:21
  17.5 1.5 %collective-permute-start.10 = (bf16[1,256,256]{2,1,0:T(8,128)(2,1)S(1)}, bf16[1,256,256]{2,1,0:T(8,128)(2,1)S(1)}, u32[]{:S(2)}, u32[]{:S(2)}) collective-permute-start(bf16[1,256,256]{2,1,0:T(8,128)(2,1)S(1)} %collective-permute-done.9.refs_10_), channel_id=1, source_target_pairs={{0,2},{1,3},{2,0},{3,1},{4,6},{5,7},{6,4},{7,5},{8,10},{9,11},{10,... | collective-permute-start | bytes 393224 | tf_op jit(solution)/shard_map/ppermute | solution.py:21
  19.5 1.4 %collective-permute-done.7.refs_8_ = bf16[1,256,256]{2,1,0:T(8,128)(2,1)S(1)} collective-permute-done((bf16[1,256,256]{2,1,0:T(8,128)(2,1)S(1)}, bf16[1,256,256]{2,1,0:T(8,128)(2,1)S(1)}, u32[]{:S(2)}, u32[]{:S(2)}) %collective-permute-start.7) | collective-permute-done | bytes 131104 | tf_op jit(solution)/shard_map/ppermute | solution.py:21
  20.9 1.6 %collective-permute-done.10.refs_11_ = bf16[1,256,256]{2,1,0:T(8,128)(2,1)S(1)} collective-permute-done((bf16[1,256,256]{2,1,0:T(8,128)(2,1)S(1)}, bf16[1,256,256]{2,1,0:T(8,128)(2,1)S(1)}, u32[]{:S(2)}, u32[]{:S(2)}) %collective-permute-start.10) | collective-permute-done | bytes 131104 | tf_op jit(solution)/shard_map/ppermute | solution.py:21
  22.4 1.2 %sketch_rows.1.part_ref = f32[2,2,96,97]{3,2,1,0:T(8,128)S(1)} custom-call(f32[1,336]{1,0:T(1,128)S(1)} %largest_value.1.peak_ref, bf16[4,192,336]{2,1,0:T(8,128)(2,1)S(1)} %get-tuple-element.26.refs_0_.stay_ref.refs_4_, bf16[2,192,336]{2,1,0:T(8,128)(2,1)S(1)} %get-tuple-element.27.refs_1_.near_ref.refs_5_, ...), custom_call_target="tpu_custom_call" | custom-call | tf_op jit(solution)/shard_map/sketch_rows/pallas_call | solution.py:381
  23.7 1.4 %collective-permute-done.11.other_ref = f32[2,2,96,97]{3,2,1,0:T(8,128)S(1)} collective-permute-done((f32[2,2,96,97]{3,2,1,0:T(8,128)S(1)}, f32[2,2,96,97]{3,2,1,0:T(8,128)S(1)}, u32[]{:S(2)}, u32[]{:S(2)}) %collective-permute-start.11) | collective-permute-done | bytes 149024 | tf_op jit(solution)/shard_map/ppermute | solution.py:21
  25.1 0.7 %chip_gram.1 = (f32[288,97]{1,0:T(8,128)S(1)}, f32[288,97]{1,0:T(8,128)S(1)}) custom-call(f32[2,2,96,97]{3,2,1,0:T(8,128)S(1)} %sketch_rows.1.part_ref, f32[2,2,96,97]{3,2,1,0:T(8,128)S(1)} %collective-permute-done.11.other_ref), custom_call_target="tpu_custom_call" | custom-call | tf_op jit(solution)/shard_map/chip_gram/pallas_call | solution.py:390
  25.9 1.5 %collective-permute-start.12 = (f32[288,97]{1,0:T(8,128)S(1)}, f32[288,97]{1,0:T(8,128)S(1)}, u32[]{:S(2)}, u32[]{:S(2)}) collective-permute-start(f32[288,97]{1,0:T(8,128)S(1)} %get-tuple-element.37.refs_0_), channel_id=1, source_target_pairs={{0,2},{1,3},{2,0},{3,1},{4,6},{5,7},{6,4},{7,5},{8,10},{9,11},{10,... | collective-permute-start | bytes 335240 | tf_op jit(solution)/shard_map/ppermute | solution.py:21
  28.0 0.7 %collective-permute-start.17 = (bf16[2,192,336]{2,1,0:T(8,128)(2,1)S(1)}, bf16[2,192,336]{2,1,0:T(8,128)(2,1)S(1)}, u32[]{:S(2)}, u32[]{:S(2)}) collective-permute-start(bf16[2,192,336]{2,1,0:T(8,128)(2,1)S(1)} %get-tuple-element.45.refs_3_), channel_id=1, source_target_pairs={{0,3},{1,2},{2,1},{3,0},{4,7},{5,6},{6,5},{7,4},{8,11},{9,10},{10,... | collective-permute-start | bytes 774152 | tf_op jit(solution)/shard_map/ppermute | solution.py:21
  28.6 4.0 %collective-permute-done.12.refs_2_ = f32[288,97]{1,0:T(8,128)S(1)} collective-permute-done((f32[288,97]{1,0:T(8,128)S(1)}, f32[288,97]{1,0:T(8,128)S(1)}, u32[]{:S(2)}, u32[]{:S(2)}) %collective-permute-start.12) | collective-permute-done | bytes 111776 | tf_op jit(solution)/shard_map/ppermute | solution.py:21
  32.7 1.8 %collective-permute-start.14 = (f32[96,97]{1,0:T(8,128)S(1)}, f32[96,97]{1,0:T(8,128)S(1)}, u32[]{:S(2)}, u32[]{:S(2)}) collective-permute-start(f32[96,97]{1,0:T(8,128)S(1)} %slice_add_fusion.2), channel_id=1, source_target_pairs={{0,4},{1,5},{2,6},{3,7},{4,0},{5,1},{6,2},{7,3},{8,12},{9,13},{10,... | collective-permute-start | bytes 111752 | tf_op jit(solution)/shard_map/ppermute | solution.py:21
  34.5 2.4 %collective-permute-done.14 = f32[96,97]{1,0:T(8,128)S(1)} collective-permute-done((f32[96,97]{1,0:T(8,128)S(1)}, f32[96,97]{1,0:T(8,128)S(1)}, u32[]{:S(2)}, u32[]{:S(2)}) %collective-permute-start.14) | collective-permute-done | bytes 37280 | tf_op jit(solution)/shard_map/ppermute | solution.py:21
  36.8 3.1 %collective-permute-start.15 = (f32[96,97]{1,0:T(8,128)S(1)}, f32[96,97]{1,0:T(8,128)S(1)}, u32[]{:S(2)}, u32[]{:S(2)}) collective-permute-start(f32[96,97]{1,0:T(8,128)S(1)} %add.29), channel_id=1, source_target_pairs={{0,8},{1,9},{2,10},{3,11},{4,12},{5,13},{6,14},{7,15},{8,0},{9,1},... | collective-permute-start | bytes 111752 | tf_op jit(solution)/shard_map/ppermute | solution.py:21
  40.0 2.6 %collective-permute-done.15 = f32[96,97]{1,0:T(8,128)S(1)} collective-permute-done((f32[96,97]{1,0:T(8,128)S(1)}, f32[96,97]{1,0:T(8,128)S(1)}, u32[]{:S(2)}, u32[]{:S(2)}) %collective-permute-start.15) | collective-permute-done | bytes 37280 | tf_op jit(solution)/shard_map/ppermute | solution.py:21
  42.6 5.2 %orthonormal_basis.1 = (f32[2,96,96]{2,1,0:T(8,128)}, bf16[192,192]{1,0:T(8,128)(2,1)S(1)}, bf16[192,192]{1,0:T(8,128)(2,1)S(1)}, bf16[192,192]{1,0:T(8,128)(2,1)S(1)}, bf16[192,192]{1,0:T(8,128)(2,1)S(1)}) custom-call(f32[288,97]{1,0:T(8,128)S(1)} %get-tuple-element.37.refs_0_, f32[288,97]{1,0:T(8,128)S(1)} %get-tuple-element.38.refs_1_, ...), custom_call_target="tpu_custom_call" | custom-call | flops 1500000000 | bytes 1000000 | tf_op jit(solution)/shard_map/orthonormal_basis/pallas_call | solution.py:407
  47.8 1.1 %project_rows.1 = (f32[2,256,256]{2,1,0:T(8,128)S(1)}, f32[2,256,256]{2,1,0:T(8,128)S(1)}, f32[256,256]{1,0:T(8,128)S(1)}, f32[256,256]{1,0:T(8,128)S(1)}) custom-call(f32[96,97]{1,0:T(8,128)S(1)} %add.30.refs_4_.gram_ref, bf16[192,192]{1,0:T(8,128)(2,1)S(1)} %get-tuple-element.40.refs_0_, bf16[192,192]{1,0:T(8,128)(2,1)S(1)} %get-tuple-element.41.refs_1_, ...), custom_call_target="tpu_custom_call" | custom-call | tf_op jit(solution)/shard_map/project_rows/pallas_call | solution.py:419
  48.9 1.8 %collective-permute-start.18 = (f16[2,256,256]{2,1,0:T(8,128)(2,1)S(1)}, f16[2,256,256]{2,1,0:T(8,128)(2,1)S(1)}, u32[]{:S(2)}, u32[]{:S(2)}) collective-permute-start(f16[2,256,256]{2,1,0:T(8,128)(2,1)S(1)} %convert_element_type.27), channel_id=1, source_target_pairs={{0,2},{1,3},{2,0},{3,1},{4,6},{5,7},{6,4},{7,5},{8,10},{9,11},{10,... | collective-permute-start | bytes 786440 | tf_op jit(solution)/shard_map/ppermute | solution.py:21
  50.7 2.4 %collective-permute-start.20 = (f16[256,256]{1,0:T(8,128)(2,1)S(1)}, f16[256,256]{1,0:T(8,128)(2,1)S(1)}, u32[]{:S(2)}, u32[]{:S(2)}) collective-permute-start(f16[256,256]{1,0:T(8,128)(2,1)S(1)} %convert_element_type.31), channel_id=1, source_target_pairs={{0,8},{1,9},{2,10},{3,11},{4,12},{5,13},{6,14},{7,15},{8,0},{9,1},... | collective-permute-start | bytes 393224 | tf_op jit(solution)/shard_map/ppermute | solution.py:21
  53.1 1.5 %collective-permute-start.19 = (f16[256,256]{1,0:T(8,128)(2,1)S(1)}, f16[256,256]{1,0:T(8,128)(2,1)S(1)}, u32[]{:S(2)}, u32[]{:S(2)}) collective-permute-start(f16[256,256]{1,0:T(8,128)(2,1)S(1)} %convert_element_type.29), channel_id=1, source_target_pairs={{0,12},{1,13},{2,14},{3,15},{4,8},{5,9},{6,10},{7,11},{8,4},{9,5},... | collective-permute-start | bytes 393224 | tf_op jit(solution)/shard_map/ppermute | solution.py:21
  54.6 1.0 %collective-permute-done.18 = f16[2,256,256]{2,1,0:T(8,128)(2,1)S(1)} collective-permute-done((f16[2,256,256]{2,1,0:T(8,128)(2,1)S(1)}, f16[2,256,256]{2,1,0:T(8,128)(2,1)S(1)}, u32[]{:S(2)}, u32[]{:S(2)}) %collective-permute-start.18) | collective-permute-done | bytes 262176 | tf_op jit(solution)/shard_map/ppermute | solution.py:21
  55.7 1.6 %collective-permute-start.21 = (f16[256,256]{1,0:T(8,128)(2,1)S(1)}, f16[256,256]{1,0:T(8,128)(2,1)S(1)}, u32[]{:S(2)}, u32[]{:S(2)}) collective-permute-start(f16[256,256]{1,0:T(8,128)(2,1)S(1)} %fusion.4), channel_id=1, source_target_pairs={{0,4},{1,5},{2,6},{3,7},{4,0},{5,1},{6,2},{7,3},{8,12},{9,13},{10,... | collective-permute-start | bytes 393224 | tf_op jit(solution)/shard_map/ppermute | solution.py:21
  58.6 3.5 %collective-permute-done.20 = f16[256,256]{1,0:T(8,128)(2,1)S(1)} collective-permute-done((f16[256,256]{1,0:T(8,128)(2,1)S(1)}, f16[256,256]{1,0:T(8,128)(2,1)S(1)}, u32[]{:S(2)}, u32[]{:S(2)}) %collective-permute-start.20) | collective-permute-done | bytes 131104 | tf_op jit(solution)/shard_map/ppermute | solution.py:21
  62.8 0.7 %maximum_maximum_fusion = f32[192,336]{1,0:T(8,128)} fusion(f32[64,80]{1,0:T(8,128)S(1)} %get-tuple-element.51, f32[64,80]{1,0:T(8,128)S(1)} %get-tuple-element.52, f32[64,80]{1,0:T(8,128)S(1)} %get-tuple-element.50, f32[192,256]{1,0:T(8,128)S(1)} %slice.48), kind=kLoop, calls=%fused_computation | loop fusion | flops 193536 | bytes 516096 | tf_op jit(solution)/shard_map/concatenate | solution.py:283
  (36 shorter events, 4.1 us)
Async XLA Ops:
  0.6 0.9 %copy-start.1 = (bf16[2,96,336]{2,1,0:T(8,128)(2,1)S(1)}, bf16[2,96,336]{2,1,0:T(8,128)(2,1)}, u32[]{:S(2)}) copy-start(bf16[2,96,336]{2,1,0:T(8,128)(2,1)} %sketch_ref.1) | copy-start | bytes 387076
  1.6 10.5 %collective-permute-start.4 = (bf16[1,256,256]{2,1,0:T(8,128)(2,1)S(1)}, bf16[1,256,256]{2,1,0:T(8,128)(2,1)S(1)}, u32[]{:S(2)}, u32[]{:S(2)}) collective-permute-start(bf16[1,256,256]{2,1,0:T(8,128)(2,1)S(1)} %fold_columns.1.refs_4_), channel_id=1, source_target_pairs={{0,8},{1,9},{2,10},{3,11},{4,12},{5,13},{6,14},{7,15},{8,0},{9,1},... | collective-permute-start | bytes 393224 | tf_op jit(solution)/shard_map/ppermute | solution.py:21
  5.7 6.6 %collective-permute-start.5 = (bf16[1,256,256]{2,1,0:T(8,128)(2,1)S(1)}, bf16[1,256,256]{2,1,0:T(8,128)(2,1)S(1)}, u32[]{:S(2)}, u32[]{:S(2)}) collective-permute-start(bf16[1,256,256]{2,1,0:T(8,128)(2,1)S(1)} %fold_columns.1.refs_4_), channel_id=1, source_target_pairs={{0,4},{1,5},{2,6},{3,7},{4,0},{5,1},{6,2},{7,3},{8,12},{9,13},{10,... | collective-permute-start | bytes 393224 | tf_op jit(solution)/shard_map/ppermute | solution.py:21
  7.2 5.0 %collective-permute-start.6 = (bf16[1,256,256]{2,1,0:T(8,128)(2,1)S(1)}, bf16[1,256,256]{2,1,0:T(8,128)(2,1)S(1)}, u32[]{:S(2)}, u32[]{:S(2)}) collective-permute-start(bf16[1,256,256]{2,1,0:T(8,128)(2,1)S(1)} %fold_columns.1.refs_4_), channel_id=1, source_target_pairs={{0,2},{1,3},{2,0},{3,1},{4,6},{5,7},{6,4},{7,5},{8,10},{9,11},{10,... | collective-permute-start | bytes 393224 | tf_op jit(solution)/shard_map/ppermute | solution.py:21
  8.7 1.6 %copy-start = (bf16[2,96,5376]{2,1,0:T(8,128)(2,1)S(1)}, bf16[2,96,5376]{2,1,0:T(8,128)(2,1)}, u32[]{:S(2)}) copy-start(bf16[2,96,5376]{2,1,0:T(8,128)(2,1)} %traces_ref.1) | copy-start | bytes 6193156
  11.3 2.9 %collective-permute-start = (bf16[2,192,336]{2,1,0:T(8,128)(2,1)S(1)}, bf16[2,192,336]{2,1,0:T(8,128)(2,1)S(1)}, u32[]{:S(2)}, u32[]{:S(2)}) collective-permute-start(bf16[2,192,336]{2,1,0:T(8,128)(2,1)S(1)} %get-tuple-element.30.refs_4_), channel_id=1, source_target_pairs={{0,1},{1,0},{2,3},{3,2},{4,5},{5,4},{6,7},{7,6},{8,9},{9,8},{10,11... | collective-permute-start | bytes 774152 | tf_op jit(solution)/shard_map/ppermute | solution.py:21
  11.4 4.3 %collective-permute-start.1 = (bf16[2,192,336]{2,1,0:T(8,128)(2,1)S(1)}, bf16[2,192,336]{2,1,0:T(8,128)(2,1)S(1)}, u32[]{:S(2)}, u32[]{:S(2)}) collective-permute-start(bf16[2,192,336]{2,1,0:T(8,128)(2,1)S(1)} %get-tuple-element.31.refs_5_), channel_id=1, source_target_pairs={{0,1},{1,0},{2,3},{3,2},{4,5},{5,4},{6,7},{7,6},{8,9},{9,8},{10,11... | collective-permute-start | bytes 774152 | tf_op jit(solution)/shard_map/ppermute | solution.py:21
  12.3 5.2 %collective-permute-start.9 = (bf16[1,256,256]{2,1,0:T(8,128)(2,1)S(1)}, bf16[1,256,256]{2,1,0:T(8,128)(2,1)S(1)}, u32[]{:S(2)}, u32[]{:S(2)}) collective-permute-start(bf16[1,256,256]{2,1,0:T(8,128)(2,1)S(1)} %collective-permute-done.4.refs_7_), channel_id=1, source_target_pairs={{0,4},{1,5},{2,6},{3,7},{4,0},{5,1},{6,2},{7,3},{8,12},{9,13},{10,... | collective-permute-start | bytes 393224 | tf_op jit(solution)/shard_map/ppermute | solution.py:21
  13.7 5.8 %collective-permute-start.2 = (bf16[2,192,336]{2,1,0:T(8,128)(2,1)S(1)}, bf16[2,192,336]{2,1,0:T(8,128)(2,1)S(1)}, u32[]{:S(2)}, u32[]{:S(2)}) collective-permute-start(bf16[2,192,336]{2,1,0:T(8,128)(2,1)S(1)} %get-tuple-element.32.refs_6_), channel_id=1, source_target_pairs={{0,1},{1,0},{2,3},{3,2},{4,5},{5,4},{6,7},{7,6},{8,9},{9,8},{10,11... | collective-permute-start | bytes 774152 | tf_op jit(solution)/shard_map/ppermute | solution.py:21
  13.7 5.8 %collective-permute-start.3 = (bf16[2,192,336]{2,1,0:T(8,128)(2,1)S(1)}, bf16[2,192,336]{2,1,0:T(8,128)(2,1)S(1)}, u32[]{:S(2)}, u32[]{:S(2)}) collective-permute-start(bf16[2,192,336]{2,1,0:T(8,128)(2,1)S(1)} %get-tuple-element.33.refs_7_), channel_id=1, source_target_pairs={{0,1},{1,0},{2,3},{3,2},{4,5},{5,4},{6,7},{7,6},{8,9},{9,8},{10,11... | collective-permute-start | bytes 774152 | tf_op jit(solution)/shard_map/ppermute | solution.py:21
  14.2 6.6 %collective-permute-start.8 = (bf16[1,256,256]{2,1,0:T(8,128)(2,1)S(1)}, bf16[1,256,256]{2,1,0:T(8,128)(2,1)S(1)}, u32[]{:S(2)}, u32[]{:S(2)}) collective-permute-start(bf16[1,256,256]{2,1,0:T(8,128)(2,1)S(1)} %collective-permute-done.4.refs_7_), channel_id=1, source_target_pairs={{0,2},{1,3},{2,0},{3,1},{4,6},{5,7},{6,4},{7,5},{8,10},{9,11},{10,... | collective-permute-start | bytes 393224 | tf_op jit(solution)/shard_map/ppermute | solution.py:21
  15.7 5.1 %collective-permute-start.7 = (bf16[1,256,256]{2,1,0:T(8,128)(2,1)S(1)}, bf16[1,256,256]{2,1,0:T(8,128)(2,1)S(1)}, u32[]{:S(2)}, u32[]{:S(2)}) collective-permute-start(bf16[1,256,256]{2,1,0:T(8,128)(2,1)S(1)} %collective-permute-done.6.refs_5_), channel_id=1, source_target_pairs={{0,4},{1,5},{2,6},{3,7},{4,0},{5,1},{6,2},{7,3},{8,12},{9,13},{10,... | collective-permute-start | bytes 393224 | tf_op jit(solution)/shard_map/ppermute | solution.py:21
  17.5 5.0 %collective-permute-start.10 = (bf16[1,256,256]{2,1,0:T(8,128)(2,1)S(1)}, bf16[1,256,256]{2,1,0:T(8,128)(2,1)S(1)}, u32[]{:S(2)}, u32[]{:S(2)}) collective-permute-start(bf16[1,256,256]{2,1,0:T(8,128)(2,1)S(1)} %collective-permute-done.9.refs_10_), channel_id=1, source_target_pairs={{0,2},{1,3},{2,0},{3,1},{4,6},{5,7},{6,4},{7,5},{8,10},{9,11},{10,... | collective-permute-start | bytes 393224 | tf_op jit(solution)/shard_map/ppermute | solution.py:21
  23.6 1.5 %collective-permute-start.11 = (f32[2,2,96,97]{3,2,1,0:T(8,128)S(1)}, f32[2,2,96,97]{3,2,1,0:T(8,128)S(1)}, u32[]{:S(2)}, u32[]{:S(2)}) collective-permute-start(f32[2,2,96,97]{3,2,1,0:T(8,128)S(1)} %sketch_rows.1.part_ref), channel_id=1, source_target_pairs={{0,1},{1,0},{2,3},{3,2},{4,5},{5,4},{6,7},{7,6},{8,9},{9,8},{10,11... | collective-permute-start | bytes 446984 | tf_op jit(solution)/shard_map/ppermute | solution.py:21
  25.9 6.8 %collective-permute-start.12 = (f32[288,97]{1,0:T(8,128)S(1)}, f32[288,97]{1,0:T(8,128)S(1)}, u32[]{:S(2)}, u32[]{:S(2)}) collective-permute-start(f32[288,97]{1,0:T(8,128)S(1)} %get-tuple-element.37.refs_0_), channel_id=1, source_target_pairs={{0,2},{1,3},{2,0},{3,1},{4,6},{5,7},{6,4},{7,5},{8,10},{9,11},{10,... | collective-permute-start | bytes 335240 | tf_op jit(solution)/shard_map/ppermute | solution.py:21
  27.4 20.3 %collective-permute-start.16 = (bf16[2,192,336]{2,1,0:T(8,128)(2,1)S(1)}, bf16[2,192,336]{2,1,0:T(8,128)(2,1)S(1)}, u32[]{:S(2)}, u32[]{:S(2)}) collective-permute-start(bf16[2,192,336]{2,1,0:T(8,128)(2,1)S(1)} %get-tuple-element.44.refs_2_.far_ref), channel_id=1, source_target_pairs={{0,2},{1,3},{2,0},{3,1},{4,6},{5,7},{6,4},{7,5},{8,10},{9,11},{10,... | collective-permute-start | bytes 774152 | tf_op jit(solution)/shard_map/ppermute | solution.py:21
  28.0 19.8 %collective-permute-start.17 = (bf16[2,192,336]{2,1,0:T(8,128)(2,1)S(1)}, bf16[2,192,336]{2,1,0:T(8,128)(2,1)S(1)}, u32[]{:S(2)}, u32[]{:S(2)}) collective-permute-start(bf16[2,192,336]{2,1,0:T(8,128)(2,1)S(1)} %get-tuple-element.45.refs_3_), channel_id=1, source_target_pairs={{0,3},{1,2},{2,1},{3,0},{4,7},{5,6},{6,5},{7,4},{8,11},{9,10},{10,... | collective-permute-start | bytes 774152 | tf_op jit(solution)/shard_map/ppermute | solution.py:21
  32.6 9.9 %collective-permute-start.13 = (f32[288,97]{1,0:T(8,128)S(1)}, f32[288,97]{1,0:T(8,128)S(1)}, u32[]{:S(2)}, u32[]{:S(2)}) collective-permute-start(f32[288,97]{1,0:T(8,128)S(1)} %collective-permute-done.12.refs_2_), channel_id=1, source_target_pairs={{0,1},{1,0},{2,3},{3,2},{4,5},{5,4},{6,7},{7,6},{8,9},{9,8},{10,11... | collective-permute-start | bytes 335240 | tf_op jit(solution)/shard_map/ppermute | solution.py:21
  32.7 4.2 %collective-permute-start.14 = (f32[96,97]{1,0:T(8,128)S(1)}, f32[96,97]{1,0:T(8,128)S(1)}, u32[]{:S(2)}, u32[]{:S(2)}) collective-permute-start(f32[96,97]{1,0:T(8,128)S(1)} %slice_add_fusion.2), channel_id=1, source_target_pairs={{0,4},{1,5},{2,6},{3,7},{4,0},{5,1},{6,2},{7,3},{8,12},{9,13},{10,... | collective-permute-start | bytes 111752 | tf_op jit(solution)/shard_map/ppermute | solution.py:21
  36.8 5.7 %collective-permute-start.15 = (f32[96,97]{1,0:T(8,128)S(1)}, f32[96,97]{1,0:T(8,128)S(1)}, u32[]{:S(2)}, u32[]{:S(2)}) collective-permute-start(f32[96,97]{1,0:T(8,128)S(1)} %add.29), channel_id=1, source_target_pairs={{0,8},{1,9},{2,10},{3,11},{4,12},{5,13},{6,14},{7,15},{8,0},{9,1},... | collective-permute-start | bytes 111752 | tf_op jit(solution)/shard_map/ppermute | solution.py:21
  48.9 6.7 %collective-permute-start.18 = (f16[2,256,256]{2,1,0:T(8,128)(2,1)S(1)}, f16[2,256,256]{2,1,0:T(8,128)(2,1)S(1)}, u32[]{:S(2)}, u32[]{:S(2)}) collective-permute-start(f16[2,256,256]{2,1,0:T(8,128)(2,1)S(1)} %convert_element_type.27), channel_id=1, source_target_pairs={{0,2},{1,3},{2,0},{3,1},{4,6},{5,7},{6,4},{7,5},{8,10},{9,11},{10,... | collective-permute-start | bytes 786440 | tf_op jit(solution)/shard_map/ppermute | solution.py:21
  50.7 11.4 %collective-permute-start.20 = (f16[256,256]{1,0:T(8,128)(2,1)S(1)}, f16[256,256]{1,0:T(8,128)(2,1)S(1)}, u32[]{:S(2)}, u32[]{:S(2)}) collective-permute-start(f16[256,256]{1,0:T(8,128)(2,1)S(1)} %convert_element_type.31), channel_id=1, source_target_pairs={{0,8},{1,9},{2,10},{3,11},{4,12},{5,13},{6,14},{7,15},{8,0},{9,1},... | collective-permute-start | bytes 393224 | tf_op jit(solution)/shard_map/ppermute | solution.py:21
  53.1 9.0 %collective-permute-start.19 = (f16[256,256]{1,0:T(8,128)(2,1)S(1)}, f16[256,256]{1,0:T(8,128)(2,1)S(1)}, u32[]{:S(2)}, u32[]{:S(2)}) collective-permute-start(f16[256,256]{1,0:T(8,128)(2,1)S(1)} %convert_element_type.29), channel_id=1, source_target_pairs={{0,12},{1,13},{2,14},{3,15},{4,8},{5,9},{6,10},{7,11},{8,4},{9,5},... | collective-permute-start | bytes 393224 | tf_op jit(solution)/shard_map/ppermute | solution.py:21
  55.7 6.9 %collective-permute-start.21 = (f16[256,256]{1,0:T(8,128)(2,1)S(1)}, f16[256,256]{1,0:T(8,128)(2,1)S(1)}, u32[]{:S(2)}, u32[]{:S(2)}) collective-permute-start(f16[256,256]{1,0:T(8,128)(2,1)S(1)} %fusion.4), channel_id=1, source_target_pairs={{0,4},{1,5},{2,6},{3,7},{4,0},{5,1},{6,2},{7,3},{8,12},{9,13},{10,... | collective-permute-start | bytes 393224 | tf_op jit(solution)/shard_map/ppermute | solution.py:21

commit v11 on v9

--- a/solution.py
+++ b/solution.py
@@ -224,8 +224,9 @@
     low_re = jnp.where(row >= column, low_re[:, :count] * across, 0.0)
     low_im = jnp.where(row >= column, low_im[:, :count] * across, 0.0)
     stacked = jnp.concatenate([ref[count:, :count] for ref in sketched], axis=0)
-    by_re = exact(stacked, low_re, ((1,), (1,)))
-    by_im = exact(stacked, low_im, ((1,), (1,)))
+    spare = jnp.zeros((-count % 128, count), jnp.float32)
+    both = exact(stacked, jnp.concatenate([low_re, spare, low_im], axis=0), ((1,), (1,)))
+    by_re, by_im = both[:, :count], both[:, count + spare.shape[0] :]
     for group in range(GROUPS):
         real = slice(2 * rows * group, 2 * rows * group + rows)
         imag = slice(2 * rows * group + rows, 2 * rows * (group + 1))

time: 63.8 us -> 63.8 us (level)
  no operation moved by 1% of the time
where the time goes in v11:
time: 63.8 us; the launch traced here: 63.6 us
  starting transfers between devices  25.6 us (40%)
  waiting for transfers between devices  22.6 us (35%)
  Pallas kernels  9.81 us (15%)
  local copies, waits for them, and re-layouts  3.16 us (5%)
  between operations  1.4 us (2%)
  other arithmetic  0.98 us (2%)
    ppermute x22, starting transfers between devices, swap(): return lax.ppermute(value, 'rcv', [(i, i ^ mask) for i in range(size)])  25.6 us
    ppermute x22, waiting for transfers between devices, swap(): return lax.ppermute(value, 'rcv', [(i, i ^ mask) for i in range(size)])  22.6 us
    pallas_call x1, Pallas kernels, per_device(): pl.pallas_call(functools.partial(basis_kernel, math.sqrt(rows * size)), o...  5.19 us
    unnamed x4, local copies, waits for them, and re-layouts  2.48 us
    pallas_call x1, Pallas kernels, per_device(): pl.pallas_call(functools.partial(chunk_kernel, share), out_shape=(chunk(z...  1.56 us
  transfers between devices with their start and end apart: 22, of which 10 were waited for; matrix products, arithmetic and copies ran while one was open for 1% of the time, Pallas kernels for 11%

profile of v11, /device:TPU:0, one launch (start us, length us, event | category | flops | bytes accessed | tf_op | source)
XLA Modules:
  0.0 63.6 jit_solution(5222234950440958617)
XLA Ops:
  0.6 0.9 %copy-done.1 = bf16[2,96,336]{2,1,0:T(8,128)(2,1)S(1)} copy-done((bf16[2,96,336]{2,1,0:T(8,128)(2,1)S(1)}, bf16[2,96,336]{2,1,0:T(8,128)(2,1)}, u32[]{:S(2)}) %copy-start.1) | copy-done | bytes 129048
  1.6 4.0 %collective-permute-start.4 = (bf16[1,256,256]{2,1,0:T(8,128)(2,1)S(1)}, bf16[1,256,256]{2,1,0:T(8,128)(2,1)S(1)}, u32[]{:S(2)}, u32[]{:S(2)}) collective-permute-start(bf16[1,256,256]{2,1,0:T(8,128)(2,1)S(1)} %fold_columns.1.refs_4_), channel_id=1, source_target_pairs={{0,8},{1,9},{2,10},{3,11},{4,12},{5,13},{6,14},{7,15},{8,0},{9,1},... | collective-permute-start | bytes 393224 | tf_op jit(solution)/shard_map/ppermute | solution.py:21
  5.7 1.6 %collective-permute-start.5 = (bf16[1,256,256]{2,1,0:T(8,128)(2,1)S(1)}, bf16[1,256,256]{2,1,0:T(8,128)(2,1)S(1)}, u32[]{:S(2)}, u32[]{:S(2)}) collective-permute-start(bf16[1,256,256]{2,1,0:T(8,128)(2,1)S(1)} %fold_columns.1.refs_4_), channel_id=1, source_target_pairs={{0,4},{1,5},{2,6},{3,7},{4,0},{5,1},{6,2},{7,3},{8,12},{9,13},{10,... | collective-permute-start | bytes 393224 | tf_op jit(solution)/shard_map/ppermute | solution.py:21
  7.2 1.5 %collective-permute-start.6 = (bf16[1,256,256]{2,1,0:T(8,128)(2,1)S(1)}, bf16[1,256,256]{2,1,0:T(8,128)(2,1)S(1)}, u32[]{:S(2)}, u32[]{:S(2)}) collective-permute-start(bf16[1,256,256]{2,1,0:T(8,128)(2,1)S(1)} %fold_columns.1.refs_4_), channel_id=1, source_target_pairs={{0,2},{1,3},{2,0},{3,1},{4,6},{5,7},{6,4},{7,5},{8,10},{9,11},{10,... | collective-permute-start | bytes 393224 | tf_op jit(solution)/shard_map/ppermute | solution.py:21
  8.7 1.6 %copy-done = bf16[2,96,5376]{2,1,0:T(8,128)(2,1)S(1)} copy-done((bf16[2,96,5376]{2,1,0:T(8,128)(2,1)S(1)}, bf16[2,96,5376]{2,1,0:T(8,128)(2,1)}, u32[]{:S(2)}) %copy-start) | copy-done | bytes 2064408
  10.3 1.6 %source_chunks.1 = (bf16[4,192,336]{2,1,0:T(8,128)(2,1)S(1)}, bf16[2,192,336]{2,1,0:T(8,128)(2,1)S(1)}, bf16[2,192,336]{2,1,0:T(8,128)(2,1)S(1)}, bf16[2,192,336...) custom-call(s32[1]{0:T(128)} %bitcast.me_ref, ...), custom_call_target="tpu_custom_call" | custom-call | tf_op jit(solution)/shard_map/source_chunks/pallas_call | solution.py:342
  12.5 1.3 %collective-permute-start.9 = (bf16[1,256,256]{2,1,0:T(8,128)(2,1)S(1)}, bf16[1,256,256]{2,1,0:T(8,128)(2,1)S(1)}, u32[]{:S(2)}, u32[]{:S(2)}) collective-permute-start(bf16[1,256,256]{2,1,0:T(8,128)(2,1)S(1)} %collective-permute-done.4.refs_7_), channel_id=1, source_target_pairs={{0,4},{1,5},{2,6},{3,7},{4,0},{5,1},{6,2},{7,3},{8,12},{9,13},{10,... | collective-permute-start | bytes 393224 | tf_op jit(solution)/shard_map/ppermute | solution.py:21
  14.2 1.5 %collective-permute-start.8 = (bf16[1,256,256]{2,1,0:T(8,128)(2,1)S(1)}, bf16[1,256,256]{2,1,0:T(8,128)(2,1)S(1)}, u32[]{:S(2)}, u32[]{:S(2)}) collective-permute-start(bf16[1,256,256]{2,1,0:T(8,128)(2,1)S(1)} %collective-permute-done.4.refs_7_), channel_id=1, source_target_pairs={{0,2},{1,3},{2,0},{3,1},{4,6},{5,7},{6,4},{7,5},{8,10},{9,11},{10,... | collective-permute-start | bytes 393224 | tf_op jit(solution)/shard_map/ppermute | solution.py:21
  15.7 0.6 %collective-permute-start.7 = (bf16[1,256,256]{2,1,0:T(8,128)(2,1)S(1)}, bf16[1,256,256]{2,1,0:T(8,128)(2,1)S(1)}, u32[]{:S(2)}, u32[]{:S(2)}) collective-permute-start(bf16[1,256,256]{2,1,0:T(8,128)(2,1)S(1)} %collective-permute-done.6.refs_5_), channel_id=1, source_target_pairs={{0,4},{1,5},{2,6},{3,7},{4,0},{5,1},{6,2},{7,3},{8,12},{9,13},{10,... | collective-permute-start | bytes 393224 | tf_op jit(solution)/shard_map/ppermute | solution.py:21
  16.4 1.6 %collective-permute-done.9.refs_10_ = bf16[1,256,256]{2,1,0:T(8,128)(2,1)S(1)} collective-permute-done((bf16[1,256,256]{2,1,0:T(8,128)(2,1)S(1)}, bf16[1,256,256]{2,1,0:T(8,128)(2,1)S(1)}, u32[]{:S(2)}, u32[]{:S(2)}) %collective-permute-start.9) | collective-permute-done | bytes 131104 | tf_op jit(solution)/shard_map/ppermute | solution.py:21
  18.0 1.0 %collective-permute-start.10 = (bf16[1,256,256]{2,1,0:T(8,128)(2,1)S(1)}, bf16[1,256,256]{2,1,0:T(8,128)(2,1)S(1)}, u32[]{:S(2)}, u32[]{:S(2)}) collective-permute-start(bf16[1,256,256]{2,1,0:T(8,128)(2,1)S(1)} %collective-permute-done.9.refs_10_), channel_id=1, source_target_pairs={{0,2},{1,3},{2,0},{3,1},{4,6},{5,7},{6,4},{7,5},{8,10},{9,11},{10,... | collective-permute-start | bytes 393224 | tf_op jit(solution)/shard_map/ppermute | solution.py:21
  19.0 1.9 %collective-permute-done.7.refs_8_ = bf16[1,256,256]{2,1,0:T(8,128)(2,1)S(1)} collective-permute-done((bf16[1,256,256]{2,1,0:T(8,128)(2,1)S(1)}, bf16[1,256,256]{2,1,0:T(8,128)(2,1)S(1)}, u32[]{:S(2)}, u32[]{:S(2)}) %collective-permute-start.7) | collective-permute-done | bytes 131104 | tf_op jit(solution)/shard_map/ppermute | solution.py:21
  20.9 2.1 %collective-permute-done.10.refs_11_ = bf16[1,256,256]{2,1,0:T(8,128)(2,1)S(1)} collective-permute-done((bf16[1,256,256]{2,1,0:T(8,128)(2,1)S(1)}, bf16[1,256,256]{2,1,0:T(8,128)(2,1)S(1)}, u32[]{:S(2)}, u32[]{:S(2)}) %collective-permute-start.10) | collective-permute-done | bytes 131104 | tf_op jit(solution)/shard_map/ppermute | solution.py:21
  23.0 1.2 %sketch_rows.1.part_ref = f32[2,2,96,97]{3,2,1,0:T(8,128)S(1)} custom-call(f32[1,5376]{1,0:T(1,128)S(1)} %get-tuple-element.27.peak_ref, bf16[4,192,336]{2,1,0:T(8,128)(2,1)S(1)} %get-tuple-element.28.stay_ref.refs_4_, bf16[2,192,336]{2,1,0:T(8,128)(2,1)S(1)} %get-tuple-element.29.near_ref.refs_5_, bf16[2,192,336]{2,1,0:T(8,128)(2,1)S(1)} %get-tuple-element.46.far_ref, ...), custom_call_target="tpu_custom_call" | custom-call | tf_op jit(solution)/shard_map/sketch_rows/pallas_call | solution.py:370
  24.2 1.4 %collective-permute-done.11.other_ref = f32[2,2,96,97]{3,2,1,0:T(8,128)S(1)} collective-permute-done((f32[2,2,96,97]{3,2,1,0:T(8,128)S(1)}, f32[2,2,96,97]{3,2,1,0:T(8,128)S(1)}, u32[]{:S(2)}, u32[]{:S(2)}) %collective-permute-start.11) | collective-permute-done | bytes 149024 | tf_op jit(solution)/shard_map/ppermute | solution.py:21
  25.7 0.7 %chip_gram.1 = (f32[288,97]{1,0:T(8,128)S(1)}, f32[288,97]{1,0:T(8,128)S(1)}) custom-call(f32[2,2,96,97]{3,2,1,0:T(8,128)S(1)} %sketch_rows.1.part_ref, f32[2,2,96,97]{3,2,1,0:T(8,128)S(1)} %collective-permute-done.11.other_ref), custom_call_target="tpu_custom_call" | custom-call | tf_op jit(solution)/shard_map/chip_gram/pallas_call | solution.py:379
  26.4 1.0 %collective-permute-start.12 = (f32[288,97]{1,0:T(8,128)S(1)}, f32[288,97]{1,0:T(8,128)S(1)}, u32[]{:S(2)}, u32[]{:S(2)}) collective-permute-start(f32[288,97]{1,0:T(8,128)S(1)} %get-tuple-element.38.refs_0_), channel_id=1, source_target_pairs={{0,2},{1,3},{2,0},{3,1},{4,6},{5,7},{6,4},{7,5},{8,10},{9,11},{10,... | collective-permute-start | bytes 335240 | tf_op jit(solution)/shard_map/ppermute | solution.py:21
  27.4 1.1 %collective-permute-start.16 = (bf16[2,192,336]{2,1,0:T(8,128)(2,1)S(1)}, bf16[2,192,336]{2,1,0:T(8,128)(2,1)S(1)}, u32[]{:S(2)}, u32[]{:S(2)}) collective-permute-start(bf16[2,192,336]{2,1,0:T(8,128)(2,1)S(1)} %get-tuple-element.46.far_ref), channel_id=1, source_target_pairs={{0,2},{1,3},{2,0},{3,1},{4,6},{5,7},{6,4},{7,5},{8,10},{9,11},{10,... | collective-permute-start | bytes 774152 | tf_op jit(solution)/shard_map/ppermute | solution.py:21
  28.6 4.5 %collective-permute-done.12.refs_2_ = f32[288,97]{1,0:T(8,128)S(1)} collective-permute-done((f32[288,97]{1,0:T(8,128)S(1)}, f32[288,97]{1,0:T(8,128)S(1)}, u32[]{:S(2)}, u32[]{:S(2)}) %collective-permute-start.12) | collective-permute-done | bytes 111776 | tf_op jit(solution)/shard_map/ppermute | solution.py:21
  33.2 1.0 %collective-permute-start.14 = (f32[96,97]{1,0:T(8,128)S(1)}, f32[96,97]{1,0:T(8,128)S(1)}, u32[]{:S(2)}, u32[]{:S(2)}) collective-permute-start(f32[96,97]{1,0:T(8,128)S(1)} %slice_add_fusion.2), channel_id=1, source_target_pairs={{0,4},{1,5},{2,6},{3,7},{4,0},{5,1},{6,2},{7,3},{8,12},{9,13},{10,... | collective-permute-start | bytes 111752 | tf_op jit(solution)/shard_map/ppermute | solution.py:21
  34.2 3.2 %collective-permute-done.14 = f32[96,97]{1,0:T(8,128)S(1)} collective-permute-done((f32[96,97]{1,0:T(8,128)S(1)}, f32[96,97]{1,0:T(8,128)S(1)}, u32[]{:S(2)}, u32[]{:S(2)}) %collective-permute-start.14) | collective-permute-done | bytes 37280 | tf_op jit(solution)/shard_map/ppermute | solution.py:21
  37.3 2.6 %collective-permute-start.15 = (f32[96,97]{1,0:T(8,128)S(1)}, f32[96,97]{1,0:T(8,128)S(1)}, u32[]{:S(2)}, u32[]{:S(2)}) collective-permute-start(f32[96,97]{1,0:T(8,128)S(1)} %add.29), channel_id=1, source_target_pairs={{0,8},{1,9},{2,10},{3,11},{4,12},{5,13},{6,14},{7,15},{8,0},{9,1},... | collective-permute-start | bytes 111752 | tf_op jit(solution)/shard_map/ppermute | solution.py:21
  39.9 2.7 %collective-permute-done.15 = f32[96,97]{1,0:T(8,128)S(1)} collective-permute-done((f32[96,97]{1,0:T(8,128)S(1)}, f32[96,97]{1,0:T(8,128)S(1)}, u32[]{:S(2)}, u32[]{:S(2)}) %collective-permute-start.15) | collective-permute-done | bytes 37280 | tf_op jit(solution)/shard_map/ppermute | solution.py:21
  42.6 5.2 %orthonormal_basis.1 = (f32[2,96,96]{2,1,0:T(8,128)}, bf16[192,192]{1,0:T(8,128)(2,1)S(1)}, bf16[192,192]{1,0:T(8,128)(2,1)S(1)}, bf16[192,192]{1,0:T(8,128)(2,1)S(1)}, bf16[192,192]{1,0:T(8,128)(2,1)S(1)}) custom-call(f32[288,97]{1,0:T(8,128)S(1)} %get-tuple-element.38.refs_0_, f32[288,97]{1,0:T(8,128)S(1)} %get-tuple-element.39.refs_1_, ...), custom_call_target="tpu_custom_call" | custom-call | flops 1500000000 | bytes 1000000 | tf_op jit(solution)/shard_map/orthonormal_basis/pallas_call | solution.py:396
  47.8 1.1 %project_rows.1 = (f32[2,256,256]{2,1,0:T(8,128)S(1)}, f32[2,256,256]{2,1,0:T(8,128)S(1)}, f32[256,256]{1,0:T(8,128)S(1)}, f32[256,256]{1,0:T(8,128)S(1)}) custom-call(f32[96,97]{1,0:T(8,128)S(1)} %add.30.refs_4_.gram_ref, bf16[192,192]{1,0:T(8,128)(2,1)S(1)} %get-tuple-element.41.refs_0_, bf16[192,192]{1,0:T(8,128)(2,1)S(1)} %get-tuple-element.42.refs_1_, ...), custom_call_target="tpu_custom_call" | custom-call | tf_op jit(solution)/shard_map/project_rows/pallas_call | solution.py:408
  49.0 1.6 %collective-permute-start.18 = (f16[2,256,256]{2,1,0:T(8,128)(2,1)S(1)}, f16[2,256,256]{2,1,0:T(8,128)(2,1)S(1)}, u32[]{:S(2)}, u32[]{:S(2)}) collective-permute-start(f16[2,256,256]{2,1,0:T(8,128)(2,1)S(1)} %convert_element_type.27), channel_id=1, source_target_pairs={{0,2},{1,3},{2,0},{3,1},{4,6},{5,7},{6,4},{7,5},{8,10},{9,11},{10,... | collective-permute-start | bytes 786440 | tf_op jit(solution)/shard_map/ppermute | solution.py:21
  50.6 2.5 %collective-permute-start.20 = (f16[256,256]{1,0:T(8,128)(2,1)S(1)}, f16[256,256]{1,0:T(8,128)(2,1)S(1)}, u32[]{:S(2)}, u32[]{:S(2)}) collective-permute-start(f16[256,256]{1,0:T(8,128)(2,1)S(1)} %convert_element_type.31), channel_id=1, source_target_pairs={{0,8},{1,9},{2,10},{3,11},{4,12},{5,13},{6,14},{7,15},{8,0},{9,1},... | collective-permute-start | bytes 393224 | tf_op jit(solution)/shard_map/ppermute | solution.py:21
  53.1 1.5 %collective-permute-start.19 = (f16[256,256]{1,0:T(8,128)(2,1)S(1)}, f16[256,256]{1,0:T(8,128)(2,1)S(1)}, u32[]{:S(2)}, u32[]{:S(2)}) collective-permute-start(f16[256,256]{1,0:T(8,128)(2,1)S(1)} %convert_element_type.29), channel_id=1, source_target_pairs={{0,12},{1,13},{2,14},{3,15},{4,8},{5,9},{6,10},{7,11},{8,4},{9,5},... | collective-permute-start | bytes 393224 | tf_op jit(solution)/shard_map/ppermute | solution.py:21
  54.6 1.0 %collective-permute-done.18 = f16[2,256,256]{2,1,0:T(8,128)(2,1)S(1)} collective-permute-done((f16[2,256,256]{2,1,0:T(8,128)(2,1)S(1)}, f16[2,256,256]{2,1,0:T(8,128)(2,1)S(1)}, u32[]{:S(2)}, u32[]{:S(2)}) %collective-permute-start.18) | collective-permute-done | bytes 262176 | tf_op jit(solution)/shard_map/ppermute | solution.py:21
  55.7 1.6 %collective-permute-start.21 = (f16[256,256]{1,0:T(8,128)(2,1)S(1)}, f16[256,256]{1,0:T(8,128)(2,1)S(1)}, u32[]{:S(2)}, u32[]{:S(2)}) collective-permute-start(f16[256,256]{1,0:T(8,128)(2,1)S(1)} %fusion.4), channel_id=1, source_target_pairs={{0,4},{1,5},{2,6},{3,7},{4,0},{5,1},{6,2},{7,3},{8,12},{9,13},{10,... | collective-permute-start | bytes 393224 | tf_op jit(solution)/shard_map/ppermute | solution.py:21
  58.5 3.6 %collective-permute-done.20 = f16[256,256]{1,0:T(8,128)(2,1)S(1)} collective-permute-done((f16[256,256]{1,0:T(8,128)(2,1)S(1)}, f16[256,256]{1,0:T(8,128)(2,1)S(1)}, u32[]{:S(2)}, u32[]{:S(2)}) %collective-permute-start.20) | collective-permute-done | bytes 131104 | tf_op jit(solution)/shard_map/ppermute | solution.py:21
  62.8 0.7 %maximum_maximum_fusion = f32[192,336]{1,0:T(8,128)} fusion(f32[64,80]{1,0:T(8,128)S(1)} %get-tuple-element.53, f32[64,80]{1,0:T(8,128)S(1)} %get-tuple-element.54, f32[64,80]{1,0:T(8,128)S(1)} %get-tuple-element.52, f32[192,256]{1,0:T(8,128)S(1)} %slice.48), kind=kLoop, calls=%fused_computation | loop fusion | flops 193536 | bytes 516096 | tf_op jit(solution)/shard_map/concatenate | solution.py:279
  (35 shorter events, 2.9 us)
Async XLA Ops:
  0.6 0.9 %copy-start.1 = (bf16[2,96,336]{2,1,0:T(8,128)(2,1)S(1)}, bf16[2,96,336]{2,1,0:T(8,128)(2,1)}, u32[]{:S(2)}) copy-start(bf16[2,96,336]{2,1,0:T(8,128)(2,1)} %sketch_ref.1) | copy-start | bytes 387076
  1.6 10.8 %collective-permute-start.4 = (bf16[1,256,256]{2,1,0:T(8,128)(2,1)S(1)}, bf16[1,256,256]{2,1,0:T(8,128)(2,1)S(1)}, u32[]{:S(2)}, u32[]{:S(2)}) collective-permute-start(bf16[1,256,256]{2,1,0:T(8,128)(2,1)S(1)} %fold_columns.1.refs_4_), channel_id=1, source_target_pairs={{0,8},{1,9},{2,10},{3,11},{4,12},{5,13},{6,14},{7,15},{8,0},{9,1},... | collective-permute-start | bytes 393224 | tf_op jit(solution)/shard_map/ppermute | solution.py:21
  5.7 6.8 %collective-permute-start.5 = (bf16[1,256,256]{2,1,0:T(8,128)(2,1)S(1)}, bf16[1,256,256]{2,1,0:T(8,128)(2,1)S(1)}, u32[]{:S(2)}, u32[]{:S(2)}) collective-permute-start(bf16[1,256,256]{2,1,0:T(8,128)(2,1)S(1)} %fold_columns.1.refs_4_), channel_id=1, source_target_pairs={{0,4},{1,5},{2,6},{3,7},{4,0},{5,1},{6,2},{7,3},{8,12},{9,13},{10,... | collective-permute-start | bytes 393224 | tf_op jit(solution)/shard_map/ppermute | solution.py:21
  7.2 5.2 %collective-permute-start.6 = (bf16[1,256,256]{2,1,0:T(8,128)(2,1)S(1)}, bf16[1,256,256]{2,1,0:T(8,128)(2,1)S(1)}, u32[]{:S(2)}, u32[]{:S(2)}) collective-permute-start(bf16[1,256,256]{2,1,0:T(8,128)(2,1)S(1)} %fold_columns.1.refs_4_), channel_id=1, source_target_pairs={{0,2},{1,3},{2,0},{3,1},{4,6},{5,7},{6,4},{7,5},{8,10},{9,11},{10,... | collective-permute-start | bytes 393224 | tf_op jit(solution)/shard_map/ppermute | solution.py:21
  8.7 1.6 %copy-start = (bf16[2,96,5376]{2,1,0:T(8,128)(2,1)S(1)}, bf16[2,96,5376]{2,1,0:T(8,128)(2,1)}, u32[]{:S(2)}) copy-start(bf16[2,96,5376]{2,1,0:T(8,128)(2,1)} %traces_ref.1) | copy-start | bytes 6193156
  11.9 2.4 %collective-permute-start = (bf16[2,192,336]{2,1,0:T(8,128)(2,1)S(1)}, bf16[2,192,336]{2,1,0:T(8,128)(2,1)S(1)}, u32[]{:S(2)}, u32[]{:S(2)}) collective-permute-start(bf16[2,192,336]{2,1,0:T(8,128)(2,1)S(1)} %get-tuple-element.31), channel_id=1, source_target_pairs={{0,1},{1,0},{2,3},{3,2},{4,5},{5,4},{6,7},{7,6},{8,9},{9,8},{10,11... | collective-permute-start | bytes 774152 | tf_op jit(solution)/shard_map/ppermute | solution.py:21
  12.0 3.8 %collective-permute-start.1 = (bf16[2,192,336]{2,1,0:T(8,128)(2,1)S(1)}, bf16[2,192,336]{2,1,0:T(8,128)(2,1)S(1)}, u32[]{:S(2)}, u32[]{:S(2)}) collective-permute-start(bf16[2,192,336]{2,1,0:T(8,128)(2,1)S(1)} %get-tuple-element.32), channel_id=1, source_target_pairs={{0,1},{1,0},{2,3},{3,2},{4,5},{5,4},{6,7},{7,6},{8,9},{9,8},{10,11... | collective-permute-start | bytes 774152 | tf_op jit(solution)/shard_map/ppermute | solution.py:21
  12.5 5.5 %collective-permute-start.9 = (bf16[1,256,256]{2,1,0:T(8,128)(2,1)S(1)}, bf16[1,256,256]{2,1,0:T(8,128)(2,1)S(1)}, u32[]{:S(2)}, u32[]{:S(2)}) collective-permute-start(bf16[1,256,256]{2,1,0:T(8,128)(2,1)S(1)} %collective-permute-done.4.refs_7_), channel_id=1, source_target_pairs={{0,4},{1,5},{2,6},{3,7},{4,0},{5,1},{6,2},{7,3},{8,12},{9,13},{10,... | collective-permute-start | bytes 393224 | tf_op jit(solution)/shard_map/ppermute | solution.py:21
  13.7 5.3 %collective-permute-start.2 = (bf16[2,192,336]{2,1,0:T(8,128)(2,1)S(1)}, bf16[2,192,336]{2,1,0:T(8,128)(2,1)S(1)}, u32[]{:S(2)}, u32[]{:S(2)}) collective-permute-start(bf16[2,192,336]{2,1,0:T(8,128)(2,1)S(1)} %get-tuple-element.33), channel_id=1, source_target_pairs={{0,1},{1,0},{2,3},{3,2},{4,5},{5,4},{6,7},{7,6},{8,9},{9,8},{10,11... | collective-permute-start | bytes 774152 | tf_op jit(solution)/shard_map/ppermute | solution.py:21
  13.7 5.3 %collective-permute-start.3 = (bf16[2,192,336]{2,1,0:T(8,128)(2,1)S(1)}, bf16[2,192,336]{2,1,0:T(8,128)(2,1)S(1)}, u32[]{:S(2)}, u32[]{:S(2)}) collective-permute-start(bf16[2,192,336]{2,1,0:T(8,128)(2,1)S(1)} %get-tuple-element.34), channel_id=1, source_target_pairs={{0,1},{1,0},{2,3},{3,2},{4,5},{5,4},{6,7},{7,6},{8,9},{9,8},{10,11... | collective-permute-start | bytes 774152 | tf_op jit(solution)/shard_map/ppermute | solution.py:21
  14.2 6.6 %collective-permute-start.8 = (bf16[1,256,256]{2,1,0:T(8,128)(2,1)S(1)}, bf16[1,256,256]{2,1,0:T(8,128)(2,1)S(1)}, u32[]{:S(2)}, u32[]{:S(2)}) collective-permute-start(bf16[1,256,256]{2,1,0:T(8,128)(2,1)S(1)} %collective-permute-done.4.refs_7_), channel_id=1, source_target_pairs={{0,2},{1,3},{2,0},{3,1},{4,6},{5,7},{6,4},{7,5},{8,10},{9,11},{10,... | collective-permute-start | bytes 393224 | tf_op jit(solution)/shard_map/ppermute | solution.py:21
  15.7 5.1 %collective-permute-start.7 = (bf16[1,256,256]{2,1,0:T(8,128)(2,1)S(1)}, bf16[1,256,256]{2,1,0:T(8,128)(2,1)S(1)}, u32[]{:S(2)}, u32[]{:S(2)}) collective-permute-start(bf16[1,256,256]{2,1,0:T(8,128)(2,1)S(1)} %collective-permute-done.6.refs_5_), channel_id=1, source_target_pairs={{0,4},{1,5},{2,6},{3,7},{4,0},{5,1},{6,2},{7,3},{8,12},{9,13},{10,... | collective-permute-start | bytes 393224 | tf_op jit(solution)/shard_map/ppermute | solution.py:21
  18.0 5.0 %collective-permute-start.10 = (bf16[1,256,256]{2,1,0:T(8,128)(2,1)S(1)}, bf16[1,256,256]{2,1,0:T(8,128)(2,1)S(1)}, u32[]{:S(2)}, u32[]{:S(2)}) collective-permute-start(bf16[1,256,256]{2,1,0:T(8,128)(2,1)S(1)} %collective-permute-done.9.refs_10_), channel_id=1, source_target_pairs={{0,2},{1,3},{2,0},{3,1},{4,6},{5,7},{6,4},{7,5},{8,10},{9,11},{10,... | collective-permute-start | bytes 393224 | tf_op jit(solution)/shard_map/ppermute | solution.py:21
  24.2 1.5 %collective-permute-start.11 = (f32[2,2,96,97]{3,2,1,0:T(8,128)S(1)}, f32[2,2,96,97]{3,2,1,0:T(8,128)S(1)}, u32[]{:S(2)}, u32[]{:S(2)}) collective-permute-start(f32[2,2,96,97]{3,2,1,0:T(8,128)S(1)} %sketch_rows.1.part_ref), channel_id=1, source_target_pairs={{0,1},{1,0},{2,3},{3,2},{4,5},{5,4},{6,7},{7,6},{8,9},{9,8},{10,11... | collective-permute-start | bytes 446984 | tf_op jit(solution)/shard_map/ppermute | solution.py:21
  26.4 6.8 %collective-permute-start.12 = (f32[288,97]{1,0:T(8,128)S(1)}, f32[288,97]{1,0:T(8,128)S(1)}, u32[]{:S(2)}, u32[]{:S(2)}) collective-permute-start(f32[288,97]{1,0:T(8,128)S(1)} %get-tuple-element.38.refs_0_), channel_id=1, source_target_pairs={{0,2},{1,3},{2,0},{3,1},{4,6},{5,7},{6,4},{7,5},{8,10},{9,11},{10,... | collective-permute-start | bytes 335240 | tf_op jit(solution)/shard_map/ppermute | solution.py:21
  27.4 20.4 %collective-permute-start.16 = (bf16[2,192,336]{2,1,0:T(8,128)(2,1)S(1)}, bf16[2,192,336]{2,1,0:T(8,128)(2,1)S(1)}, u32[]{:S(2)}, u32[]{:S(2)}) collective-permute-start(bf16[2,192,336]{2,1,0:T(8,128)(2,1)S(1)} %get-tuple-element.46.far_ref), channel_id=1, source_target_pairs={{0,2},{1,3},{2,0},{3,1},{4,6},{5,7},{6,4},{7,5},{8,10},{9,11},{10,... | collective-permute-start | bytes 774152 | tf_op jit(solution)/shard_map/ppermute | solution.py:21
  28.5 19.3 %collective-permute-start.17 = (bf16[2,192,336]{2,1,0:T(8,128)(2,1)S(1)}, bf16[2,192,336]{2,1,0:T(8,128)(2,1)S(1)}, u32[]{:S(2)}, u32[]{:S(2)}) collective-permute-start(bf16[2,192,336]{2,1,0:T(8,128)(2,1)S(1)} %get-tuple-element.47), channel_id=1, source_target_pairs={{0,3},{1,2},{2,1},{3,0},{4,7},{5,6},{6,5},{7,4},{8,11},{9,10},{10,... | collective-permute-start | bytes 774152 | tf_op jit(solution)/shard_map/ppermute | solution.py:21
  33.2 9.5 %collective-permute-start.13 = (f32[288,97]{1,0:T(8,128)S(1)}, f32[288,97]{1,0:T(8,128)S(1)}, u32[]{:S(2)}, u32[]{:S(2)}) collective-permute-start(f32[288,97]{1,0:T(8,128)S(1)} %collective-permute-done.12.refs_2_), channel_id=1, source_target_pairs={{0,1},{1,0},{2,3},{3,2},{4,5},{5,4},{6,7},{7,6},{8,9},{9,8},{10,11... | collective-permute-start | bytes 335240 | tf_op jit(solution)/shard_map/ppermute | solution.py:21
  33.2 4.2 %collective-permute-start.14 = (f32[96,97]{1,0:T(8,128)S(1)}, f32[96,97]{1,0:T(8,128)S(1)}, u32[]{:S(2)}, u32[]{:S(2)}) collective-permute-start(f32[96,97]{1,0:T(8,128)S(1)} %slice_add_fusion.2), channel_id=1, source_target_pairs={{0,4},{1,5},{2,6},{3,7},{4,0},{5,1},{6,2},{7,3},{8,12},{9,13},{10,... | collective-permute-start | bytes 111752 | tf_op jit(solution)/shard_map/ppermute | solution.py:21
  37.3 5.3 %collective-permute-start.15 = (f32[96,97]{1,0:T(8,128)S(1)}, f32[96,97]{1,0:T(8,128)S(1)}, u32[]{:S(2)}, u32[]{:S(2)}) collective-permute-start(f32[96,97]{1,0:T(8,128)S(1)} %add.29), channel_id=1, source_target_pairs={{0,8},{1,9},{2,10},{3,11},{4,12},{5,13},{6,14},{7,15},{8,0},{9,1},... | collective-permute-start | bytes 111752 | tf_op jit(solution)/shard_map/ppermute | solution.py:21
  49.0 6.7 %collective-permute-start.18 = (f16[2,256,256]{2,1,0:T(8,128)(2,1)S(1)}, f16[2,256,256]{2,1,0:T(8,128)(2,1)S(1)}, u32[]{:S(2)}, u32[]{:S(2)}) collective-permute-start(f16[2,256,256]{2,1,0:T(8,128)(2,1)S(1)} %convert_element_type.27), channel_id=1, source_target_pairs={{0,2},{1,3},{2,0},{3,1},{4,6},{5,7},{6,4},{7,5},{8,10},{9,11},{10,... | collective-permute-start | bytes 786440 | tf_op jit(solution)/shard_map/ppermute | solution.py:21
  50.6 11.5 %collective-permute-start.20 = (f16[256,256]{1,0:T(8,128)(2,1)S(1)}, f16[256,256]{1,0:T(8,128)(2,1)S(1)}, u32[]{:S(2)}, u32[]{:S(2)}) collective-permute-start(f16[256,256]{1,0:T(8,128)(2,1)S(1)} %convert_element_type.31), channel_id=1, source_target_pairs={{0,8},{1,9},{2,10},{3,11},{4,12},{5,13},{6,14},{7,15},{8,0},{9,1},... | collective-permute-start | bytes 393224 | tf_op jit(solution)/shard_map/ppermute | solution.py:21
  53.1 9.0 %collective-permute-start.19 = (f16[256,256]{1,0:T(8,128)(2,1)S(1)}, f16[256,256]{1,0:T(8,128)(2,1)S(1)}, u32[]{:S(2)}, u32[]{:S(2)}) collective-permute-start(f16[256,256]{1,0:T(8,128)(2,1)S(1)} %convert_element_type.29), channel_id=1, source_target_pairs={{0,12},{1,13},{2,14},{3,15},{4,8},{5,9},{6,10},{7,11},{8,4},{9,5},... | collective-permute-start | bytes 393224 | tf_op jit(solution)/shard_map/ppermute | solution.py:21
  55.7 7.0 %collective-permute-start.21 = (f16[256,256]{1,0:T(8,128)(2,1)S(1)}, f16[256,256]{1,0:T(8,128)(2,1)S(1)}, u32[]{:S(2)}, u32[]{:S(2)}) collective-permute-start(f16[256,256]{1,0:T(8,128)(2,1)S(1)} %fusion.4), channel_id=1, source_target_pairs={{0,4},{1,5},{2,6},{3,7},{4,0},{5,1},{6,2},{7,3},{8,12},{9,13},{10,... | collective-permute-start | bytes 393224 | tf_op jit(solution)/shard_map/ppermute | solution.py:21
